TPU v7x, 32 devices: a whole 2x2x4 slice. The times are simulated.
32 devices in a mesh: dp: 4 (over z), blk: 4 (over y, x), tensor: 2 (over core).
Axes of the slice: x: 2, y: 2, z: 4, core: 2. Of those that a mesh axis runs over, the one named last changes fastest.
Arguments:
- tokens: bfloat16 [8192, 896], P(('dp', 'blk')), may hold values from -6 to 6
- lengths: int32 [4, 3], P('dp'), may hold values from 1 to 1537, 2016 in all within a row
- norm1_gain: bfloat16 [896], replicated, may hold values from 0.5 to 1.5
- w_query: bfloat16 [896, 896], P(None, 'tensor'), may hold values from -0.1875 to 0.1875
- b_query: bfloat16 [896], P('tensor'), may hold values from -3 to 3
- w_key: bfloat16 [896, 128], P(None, 'tensor'), may hold values from -0.1875 to 0.1875
- b_key: bfloat16 [128], P('tensor'), may hold values from -3 to 3
- w_value: bfloat16 [896, 128], P(None, 'tensor'), may hold values from -0.1875 to 0.1875
- b_value: bfloat16 [128], P('tensor'), may hold values from -3 to 3
- w_out: bfloat16 [896, 896], P('tensor'), may hold values from -6 to 6
- norm2_gain: bfloat16 [896], replicated, may hold values from 0.5 to 1.5
- w_gate: bfloat16 [896, 4864], P(None, 'tensor'), may hold values from -0.1875 to 0.1875
- w_up: bfloat16 [896, 4864], P(None, 'tensor'), may hold values from -0.1875 to 0.1875
- w_down: bfloat16 [4864, 896], P('tensor'), may hold values from -0.078125 to 0.078125
- cotangent: bfloat16 [8192, 896], P(('dp', 'blk')), may hold values from -6 to 6
Outputs:
- layer_out: bfloat16 [8192, 896], P(('dp', 'blk'))
- grad_tokens: float32 [8192, 896], P(('dp', 'blk'))
- grad_norm1: float32 [896], replicated
- grad_w_query: float32 [896, 896], P(None, 'tensor')
- grad_b_query: float32 [896], P('tensor')
- grad_w_key: float32 [896, 128], P(None, 'tensor')
- grad_b_key: float32 [128], P('tensor')
- grad_w_value: float32 [896, 128], P(None, 'tensor')
- grad_b_value: float32 [128], P('tensor')
- grad_w_out: float32 [896, 896], P('tensor')
- grad_norm2: float32 [896], replicated
- grad_w_gate: float32 [896, 4864], P(None, 'tensor')
- grad_w_up: float32 [896, 4864], P(None, 'tensor')
- grad_w_down: float32 [4864, 896], P('tensor')
Inputs may be any that keep to these rules, and one draw needn't show every extreme that they name: Row g lists the lengths of group g's sequences in packing order; they sum to 2016, the remaining rows of the group being padding, and the longest is exactly 1537.
All inputs are finite; a program needn't handle non-finite values.
Results may differ from a plain program's by a relative error of at most 0.03.
Values may be sent and summed in bfloat16 or wider, within the bound.
No kernel may reach another device: no remote copies, remote signals or barrier semaphores. Data moves between devices by JAX's collectives and lax.ppermute only.
A program may use at most 192 MiB of HBM per device.

v0:
```python
import math

import jax
import jax.numpy as jnp
from jax import lax
from jax.sharding import PartitionSpec as P

HEAD_DIM = 64


epsilon = 1e-06
rope_base = 1000000.0
masked_value = -1e30


def layout(length_row, row_index):
    seq_ends = jnp.cumsum(length_row, dtype=jnp.int32)
    passed = (row_index[:, None] >= seq_ends[None, :]).astype(jnp.int32)
    segment = jnp.sum(passed, axis=1, dtype=jnp.int32)
    offset = jnp.sum(passed * length_row[None, :], axis=1, dtype=jnp.int32)
    return (segment, row_index - offset)


def rotary(vector, position, direction):
    half_dim = vector.shape[-1] // 2
    frequency = rope_base ** (-2.0 * jnp.arange(half_dim, dtype=jnp.float32) / vector.shape[-1])
    angles = position.astype(jnp.float32)[:, None] * frequency[None, :]
    cosine = jnp.cos(angles)[:, None, :]
    sine_part = direction * jnp.sin(angles)[:, None, :]
    first_half = vector[..., :half_dim]
    second_half = vector[..., half_dim:]
    return jnp.concatenate(
        [
            first_half * cosine - second_half * sine_part,
            second_half * cosine + first_half * sine_part,
        ],
        axis=-1,
    )


def normalize(vector, scale_gain):
    inverse = lax.rsqrt(jnp.mean(vector * vector, axis=1, keepdims=True) + epsilon)
    return (vector * inverse * scale_gain, inverse)


def norm_back(vector, inverse, scale_gain, grad_normed):
    weighted = scale_gain * grad_normed
    inner_mean = jnp.mean(weighted * vector, axis=1, keepdims=True)
    grad_vector = inverse * weighted - vector * (inverse * inverse * inverse) * inner_mean
    grad_gain = jnp.sum(grad_normed * vector * inverse, axis=0)
    return (grad_vector, grad_gain)


def product(left_side, right_side):
    return jnp.dot(left_side, right_side, preferred_element_type=jnp.float32)


def outer_sum(left_side, right_side):
    return lax.dot_general(
        left_side, right_side, (((0,), (0,)), ((), ())), preferred_element_type=jnp.float32
    )


def inner_sum(left_side, right_side):
    return lax.dot_general(
        left_side, right_side, (((1,), (1,)), ((), ())), preferred_element_type=jnp.float32
    )


def block_scores(queries, key_rows, q_segment, q_index, k_segment, k_index, factor):
    raw_scores = (
        jnp.einsum("qcgd,kcd->qcgk", queries, key_rows, preferred_element_type=jnp.float32) * factor
    )
    allowed = (q_segment[:, None] == k_segment[None, :]) & (k_index[None, :] <= q_index[:, None])
    allowed = allowed[:, None, None, :]
    return (jnp.where(allowed, raw_scores, masked_value), allowed)


def is_live(q_segment, q_index, k_segment, k_index):
    return (
        (k_index[0] <= q_index[-1])
        & (k_segment[0] <= q_segment[-1])
        & (q_segment[0] <= k_segment[-1])
    )


def split_pair(key_block, kv_local, head_size):
    half_width = kv_local * head_size
    key_rows = key_block[:, :half_width].reshape(key_block.shape[0], kv_local, head_size)
    value_rows = key_block[:, half_width:].reshape(key_block.shape[0], kv_local, head_size)
    return (key_rows, value_rows)


def sweep_keys(state_now, key_piece, context):
    queries, q_segment, q_index, length_row, kv_local, head_size = context
    piece_rows = key_piece.shape[0]
    block_rows = math.gcd(piece_rows, 512)
    blocks = key_piece.reshape(piece_rows // block_rows, block_rows, key_piece.shape[1])
    offsets = block_rows * jnp.arange(piece_rows // block_rows, dtype=jnp.int32)
    factor = head_size ** (-0.5)

    def absorb(state_in, key_block, k_index, k_segment):
        accumulated, row_max, row_total = state_in
        key_rows, value_rows = split_pair(key_block, kv_local, head_size)
        scores, allowed = block_scores(
            queries, key_rows, q_segment, q_index, k_segment, k_index, factor
        )
        new_max = jnp.maximum(row_max, jnp.max(scores, axis=-1))
        shrink = jnp.exp(row_max - new_max)
        weight = jnp.where(allowed, jnp.exp(scores - new_max[..., None]), 0.0)
        update = jnp.einsum(
            "qcgk,kcd->qcgd",
            weight.astype(jnp.bfloat16),
            value_rows,
            preferred_element_type=jnp.float32,
        )
        return (
            accumulated * shrink[..., None] + update,
            new_max,
            row_total * shrink + jnp.sum(weight, axis=-1),
        )

    def visit_block(state_in, block_item):
        key_block, block_start = block_item
        k_index = block_start + jnp.arange(block_rows, dtype=jnp.int32)
        k_segment, unused = layout(length_row, k_index)
        live = is_live(q_segment, q_index, k_segment, k_index)
        state_next = lax.cond(
            live,
            lambda held_state: absorb(held_state, key_block, k_index, k_segment),
            lambda held_state: held_state,
            state_in,
        )
        return (state_next, None)

    state_out, unused = lax.scan(visit_block, state_now, (blocks, offsets))
    return state_out


def sweep_back(grad_start, whole_kv, context, grad_attn, log_total, row_delta):
    queries, q_segment, q_index, length_row, kv_local, head_size = context
    whole_rows = whole_kv.shape[0]
    block_rows = math.gcd(whole_rows, 512)
    blocks = whole_kv.reshape(whole_rows // block_rows, block_rows, whole_kv.shape[1])
    offsets = block_rows * jnp.arange(whole_rows // block_rows, dtype=jnp.int32)
    factor = head_size ** (-0.5)

    def visit_block(grad_now, block_item):
        key_block, block_start = block_item
        k_index = block_start + jnp.arange(block_rows, dtype=jnp.int32)
        k_segment, unused = layout(length_row, k_index)
        live = is_live(q_segment, q_index, k_segment, k_index)

        def live_branch(grad_in):
            key_rows, value_rows = split_pair(key_block, kv_local, head_size)
            scores, allowed = block_scores(
                queries, key_rows, q_segment, q_index, k_segment, k_index, factor
            )
            probability = jnp.where(allowed, jnp.exp(scores - log_total[..., None]), 0.0)
            grad_probs = jnp.einsum(
                "qcgd,kcd->qcgk", grad_attn, value_rows, preferred_element_type=jnp.float32
            )
            grad_scores = (probability * (grad_probs - row_delta[..., None])).astype(jnp.bfloat16)
            grad_next = (
                grad_in
                + jnp.einsum(
                    "qcgk,kcd->qcgd", grad_scores, key_rows, preferred_element_type=jnp.float32
                )
                * factor
            )
            grad_keys = (
                jnp.einsum(
                    "qcgk,qcgd->kcd", grad_scores, queries, preferred_element_type=jnp.float32
                )
                * factor
            )
            grad_values = jnp.einsum(
                "qcgk,qcgd->kcd",
                probability.astype(jnp.bfloat16),
                grad_attn,
                preferred_element_type=jnp.float32,
            )
            return (
                grad_next,
                jnp.concatenate(
                    [grad_keys.reshape(block_rows, -1), grad_values.reshape(block_rows, -1)], axis=1
                ),
            )

        def dead_branch(grad_in):
            return (grad_in, jnp.zeros((block_rows, key_block.shape[1]), jnp.float32))

        return lax.cond(live, live_branch, dead_branch, grad_now)

    grad_query, pieces = lax.scan(visit_block, grad_start, (blocks, offsets))
    return (grad_query, pieces.reshape(whole_rows, whole_kv.shape[1]))


def local(
    tokens,
    lengths,
    norm1_gain,
    w_query,
    b_query,
    w_key,
    b_key,
    w_value,
    b_value,
    w_out,
    norm2_gain,
    w_gate,
    w_up,
    w_down,
    cotangent,
):
    row_count = tokens.shape[0]
    kv_local = w_key.shape[1] // HEAD_DIM
    group_share = w_query.shape[1] // w_key.shape[1]
    length_row = lengths[0]
    q_index = lax.axis_index("blk") * row_count + jnp.arange(row_count, dtype=jnp.int32)
    q_segment, position = layout(length_row, q_index)
    valid_rows = (q_segment < length_row.shape[0]).astype(jnp.float32)
    hidden_in = tokens.astype(jnp.float32)
    gain_one = norm1_gain.astype(jnp.float32)
    normed_one, inverse_one = normalize(hidden_in, gain_one)
    normed_one = normed_one.astype(jnp.bfloat16)
    q_lin = product(normed_one, w_query) + b_query.astype(jnp.float32)
    k_lin = product(normed_one, w_key) + b_key.astype(jnp.float32)
    v_lin = product(normed_one, w_value) + b_value.astype(jnp.float32)
    q_rot = rotary(
        q_lin.reshape(row_count, kv_local * group_share, HEAD_DIM), position, 1.0
    ).astype(jnp.bfloat16)
    q_rot = q_rot.reshape(row_count, kv_local, group_share, HEAD_DIM)
    k_rot = rotary(k_lin.reshape(row_count, kv_local, HEAD_DIM), position, 1.0).astype(jnp.bfloat16)
    key_value = jnp.concatenate([k_rot.reshape(row_count, -1), v_lin.astype(jnp.bfloat16)], axis=1)
    context = (q_rot, q_segment, q_index, length_row, kv_local, HEAD_DIM)
    start_state = (
        jnp.zeros((row_count, kv_local, group_share, HEAD_DIM), jnp.float32),
        jnp.full((row_count, kv_local, group_share), masked_value, jnp.float32),
        jnp.zeros((row_count, kv_local, group_share), jnp.float32),
    )
    accumulated, row_max, row_total = sweep_keys(
        start_state, lax.all_gather(key_value, "blk", axis=0, tiled=True), context
    )
    whole_kv = lax.all_gather(key_value, "blk", axis=0, tiled=True)
    attention = accumulated / row_total[..., None]
    log_total = row_max + jnp.log(row_total)
    out_low = attention.reshape(row_count, -1).astype(jnp.bfloat16)
    hidden_mid = hidden_in + lax.psum(
        product(out_low, w_out).astype(jnp.bfloat16), "tensor"
    ).astype(jnp.float32)
    gain_two = norm2_gain.astype(jnp.float32)
    normed_two, inverse_two = normalize(hidden_mid, gain_two)
    normed_two = normed_two.astype(jnp.bfloat16)
    gate_val = product(normed_two, w_gate)
    up_val = product(normed_two, w_up)
    gate_sigmoid = jax.nn.sigmoid(gate_val)
    silu_val = gate_val * gate_sigmoid
    mixed_low = (silu_val * up_val).astype(jnp.bfloat16)
    layer_out = (
        hidden_mid
        + lax.psum(product(mixed_low, w_down).astype(jnp.bfloat16), "tensor").astype(jnp.float32)
    ).astype(jnp.bfloat16)
    grad_y = cotangent.astype(jnp.float32) * valid_rows[:, None]
    grad_y_low = grad_y.astype(jnp.bfloat16)
    grad_w_down = outer_sum(mixed_low, grad_y_low)
    grad_mixed = inner_sum(grad_y_low, w_down)
    grad_gate = (
        grad_mixed * up_val * gate_sigmoid * (1.0 + gate_val * (1.0 - gate_sigmoid))
    ).astype(jnp.bfloat16)
    grad_up = (grad_mixed * silu_val).astype(jnp.bfloat16)
    grad_w_gate = outer_sum(normed_two, grad_gate)
    grad_w_up = outer_sum(normed_two, grad_up)
    grad_normed_two = lax.psum(
        (inner_sum(grad_gate, w_gate) + inner_sum(grad_up, w_up)).astype(jnp.bfloat16), "tensor"
    ).astype(jnp.float32)
    grad_mid_norm, grad_gain_two = norm_back(hidden_mid, inverse_two, gain_two, grad_normed_two)
    grad_mid = grad_y + grad_mid_norm
    grad_mid_low = grad_mid.astype(jnp.bfloat16)
    grad_w_out = outer_sum(out_low, grad_mid_low)
    grad_attn = (
        inner_sum(grad_mid_low, w_out)
        .astype(jnp.bfloat16)
        .reshape(row_count, kv_local, group_share, HEAD_DIM)
    )
    row_delta = jnp.sum(grad_attn.astype(jnp.float32) * attention, axis=-1)
    grad_q_rot, grad_kv_whole = sweep_back(
        jnp.zeros_like(accumulated), whole_kv, context, grad_attn, log_total, row_delta
    )
    grad_kv = lax.psum_scatter(
        grad_kv_whole.astype(jnp.bfloat16), "blk", scatter_dimension=0, tiled=True
    ).astype(jnp.float32)
    half_width = kv_local * HEAD_DIM
    grad_q = (
        rotary(grad_q_rot.reshape(row_count, kv_local * group_share, HEAD_DIM), position, -1.0)
        .reshape(row_count, -1)
        .astype(jnp.bfloat16)
    )
    grad_k = (
        rotary(grad_kv[:, :half_width].reshape(row_count, kv_local, HEAD_DIM), position, -1.0)
        .reshape(row_count, -1)
        .astype(jnp.bfloat16)
    )
    grad_v = grad_kv[:, half_width:].astype(jnp.bfloat16)
    grad_w_query = outer_sum(normed_one, grad_q)
    grad_w_key = outer_sum(normed_one, grad_k)
    grad_w_value = outer_sum(normed_one, grad_v)
    grad_b_query = jnp.sum(grad_q.astype(jnp.float32), axis=0)
    grad_b_key = jnp.sum(grad_k.astype(jnp.float32), axis=0)
    grad_b_value = jnp.sum(grad_v.astype(jnp.float32), axis=0)
    grad_normed_one = lax.psum(
        (inner_sum(grad_q, w_query) + inner_sum(grad_k, w_key) + inner_sum(grad_v, w_value)).astype(
            jnp.bfloat16
        ),
        "tensor",
    ).astype(jnp.float32)
    grad_in_norm, grad_gain_one = norm_back(hidden_in, inverse_one, gain_one, grad_normed_one)
    grad_tokens = grad_mid + grad_in_norm
    (
        grad_gain_one,
        grad_w_query,
        grad_b_query,
        grad_w_key,
        grad_b_key,
        grad_w_value,
        grad_b_value,
        grad_w_out,
        grad_gain_two,
        grad_w_gate,
        grad_w_up,
        grad_w_down,
    ) = lax.psum(
        (
            grad_gain_one,
            grad_w_query,
            grad_b_query,
            grad_w_key,
            grad_b_key,
            grad_w_value,
            grad_b_value,
            grad_w_out,
            grad_gain_two,
            grad_w_gate,
            grad_w_up,
            grad_w_down,
        ),
        ("dp", "blk"),
    )
    return (
        layer_out,
        grad_tokens,
        grad_gain_one,
        grad_w_query,
        grad_b_query,
        grad_w_key,
        grad_b_key,
        grad_w_value,
        grad_b_value,
        grad_w_out,
        grad_gain_two,
        grad_w_gate,
        grad_w_up,
        grad_w_down,
    )


def solution(mesh):
    placed = (
        P(("dp", "blk"), None),
        P("dp", None),
        P(),
        P(None, "tensor"),
        P("tensor"),
        P(None, "tensor"),
        P("tensor"),
        P(None, "tensor"),
        P("tensor"),
        P("tensor", None),
        P(),
        P(None, "tensor"),
        P(None, "tensor"),
        P("tensor", None),
        P(("dp", "blk"), None),
    )
    return jax.shard_map(
        local,
        mesh=mesh,
        in_specs=placed,
        out_specs=(
            P(("dp", "blk"), None),
            P(("dp", "blk"), None),
            P(),
            P(None, "tensor"),
            P("tensor"),
            P(None, "tensor"),
            P("tensor"),
            P(None, "tensor"),
            P("tensor"),
            P("tensor", None),
            P(),
            P(None, "tensor"),
            P(None, "tensor"),
            P("tensor", None),
        ),
        check_vma=False,
    )
```

profile of v0, /device:TPU:0, one launch (start us, length us, event | category | flops | bytes accessed | tf_op | source)
XLA Modules:
  0.0 1122.0 jit_solution(2312310157196220996)
XLA Ops:
  7.3 0.9 broadcast_in_dim.78
  11.1 1.4 fusion.54
  14.5 0.9 broadcast_multiply_fusion
  15.4 1.7 fusion.62
  18.0 11.5 %all_gather.4 = bf16[2048,128]{0,1:T(8,128)(2,1)S(1)} all-gather(bf16[512,128]{0,1:T(8,128)(2,1)S(1)} %pad_maximum_fusion.1), channel_id=1, replica_groups=mesh['dp'=4,'blk'=4,'tensor'=2] {'blk'}, dimensions={0}, use_global_device_ids=true | all-gather | bytes 655360 | tf_op jit(solution)/shard_map/all_gather | solution.py:243
  31.5 34.5 %while.33 = (s32[]{:T(128)}, f32[512,1,7,64]{0,3,2,1:T(8,128)S(1)}, f32[512,1,7]{0,2,1:T(8,128)S(1)}, f32[512,1,7]{0,2,1:T(8,128)S(1)}, s32[4]{0:T(128)S(1)}, /*...) while((s32[]{:T(128)}, f32[512,1,7,64]{0,3,2,1:T(8,128)S(1)}, ...), condition=%wide.region_11.12_spmd, body=%wide.region_5.11_spmd.sunk | while | flops 494877696 | bytes 26003828 | solution.py:136
  38.4 6.8 conditional.4
  39.6 1.3 fusion
  41.0 1.7 fusion.1
  42.7 2.4 fusion.10
  67.1 1.7 convolution_convert_fusion.1
  69.1 39.8 %all-reduce.8.cloned.1.call-done = bf16[512,896]{1,0:T(8,128)(2,1)} async-done(((bf16[512,896]{1,0:T(8,128)(2,1)}), bf16[512,896]{1,0:T(8,128)(2,1)}) %all-reduce.8.cloned.1.call-update) | async-done | bytes 917520 | tf_op jit(solution)/shard_map/psum | solution.py:249
  108.9 1.6 multiply_reduce_fusion
  110.5 1.7 multiply_convert_fusion.3
  112.2 7.1 fusion.115
  119.4 4.5 fusion.114
  123.9 9.0 multiply_convert_fusion
  132.9 4.7 fusion.116
  137.6 3.8 add_convert_fusion.1
  142.3 6.8 convolution_convert_fusion
  149.1 13.0 %all-reduce.10.cloned.1.call-done = bf16[512,896]{1,0:T(8,128)(2,1)} async-done(((bf16[512,896]{1,0:T(8,128)(2,1)}), bf16[512,896]{1,0:T(8,128)(2,1)}) %all-reduce.10.cloned.1.call-update) | async-done | bytes 917520 | tf_op jit(solution)/shard_map/psum | solution.py:274
  162.2 2.7 fusion.53
  166.4 1.1 copy-done.9
  167.9 51.9 %while.34 = (s32[]{:T(128)}, f32[512,1,7,64]{0,3,2,1:T(8,128)S(1)}, bf16[4,512,128]{1,2,0:T(8,128)(2,1)}, s32[4]{0:T(128)}, s32[512]{0:T(512)}, /*index=5*/s32[1...) while((s32[]{:T(128)}, f32[512,1,7,64]{0,3,2,1:T(8,128)S(1)}, ...), condition=%wide.region_22.23_spmd, body=%wide.region_18.22_spmd.sunk | while | flops 1198002688 | bytes 38720384 | solution.py:195
  167.9 1.3 slice.206
  169.2 1.2 dynamic_slice.31
  173.7 1.4 fusion.153
  177.6 10.1 conditional.5
  178.6 1.0 compare_and_fusion.1
  179.5 1.1 fusion.38
  180.7 2.2 fusion.31
  182.9 2.8 fusion.25
  185.6 1.2 fusion.34
  188.4 1.3 slice.206
  189.7 1.2 dynamic_slice.31
  194.1 1.4 fusion.153
  198.8 1.3 slice.206
  200.2 1.2 dynamic_slice.31
  204.6 1.4 fusion.153
  209.3 1.3 slice.206
  210.6 1.2 dynamic_slice.31
  215.1 1.4 fusion.153
  219.7 1.9 copy.48
  222.0 8.1 fusion.119
  231.2 2.0 fusion.117
  233.2 44.7 %reduce-scatter.2.cloned.1.call-done = bf16[512,128]{0,1:T(8,128)(2,1)} async-done(((bf16[2048,128]{0,1:T(8,128)(2,1)}), bf16[512,128]{0,1:T(8,128)(2,1)}) %reduce-scatter.2.cloned.1.call-update) | async-done | bytes 131088 | tf_op jit(solution)/shard_map/reduce_scatter | solution.py:290
  277.8 1.0 fusion.91
  279.6 2.2 add_convert_fusion
  281.9 8.4 fusion.118
  290.4 6.4 fusion.67
  296.8 1.9 fusion.103
  298.7 1.8 fusion.64
  300.5 1.1 fusion.97
  301.6 1.1 fusion.92
  303.0 2.0 fusion.60
  305.1 80.3 %all-reduce = (f32[896]{0:T(1024)}, f32[448]{0:T(512)}, f32[64]{0:T(128)}, f32[64]{0:T(128)}, f32[896]{0:T(1024)}) all-reduce(f32[896]{0:T(1024)S(1)} %get-tuple-element.451, f32[448]{0:T(512)S(1)} %reduce_sum.155, f32[64]{0:T(128)S(1)} %get-tuple-element.552, ...), channel_id=1, replica_groups=mesh['dp'=4,'blk'=4,'tensor'=2] {'dp','blk'}, use_global_device_ids=true, to_apply=%region_27.28 | all-reduce | flops 2368 | bytes 18944 | tf_op jit(solution)/shard_map/psum | solution.py:332
  385.4 4.3 fusion.48
  389.7 701.7 %all-reduce.12.cloned.1.call-done = (f32[896,448]{0,1:T(8,128)}, f32[896,64]{0,1:T(8,128)}, f32[896,64]{0,1:T(8,128)}, f32[448,896]{1,0:T(8,128)}, f32[896,2432]...) async-done(((f32[896,448]{0,1:T(8,128)}, f32[896,64]{0,1:T(8,128)}, f32[896,64]{0,1:T(8,128)}, f32[448,896]{1,0:T(8,128)}, f32[896,2432]{1,0:T(8,128)}, ...) | async-done | bytes 29818896 | tf_op jit(solution)/shard_map/psum | solution.py:332
  1091.5 2.8 copy.96
  1095.7 1.2 copy.99
  1096.9 8.6 copy.100
  1105.5 4.4 copy.101
  1109.9 1.6 slice-done.1
  1111.6 3.5 copy.102
  (233 shorter events, 41.1 us)
Async XLA Ops:
  7.2 60.0 %copy-start = (bf16[448,896]{1,0:T(8,128)(2,1)S(1)}, bf16[448,896]{1,0:T(8,128)(2,1)}, u32[]{:S(2)}) copy-start(bf16[448,896]{1,0:T(8,128)(2,1)} %param.32) | copy-start | bytes 2408452
  7.2 10.3 copy-start.2
  7.2 10.3 copy-start.32
  7.2 101.7 %all-reduce.8.cloned.1.call-start = ((), (), s32[]{:S(2)}) async-start(), calls=%async_computation.1 | async-start | bytes 1835008 | tf_op jit(solution)/shard_map/psum | solution.py:249
  7.3 10.7 copy-start.46
  13.0 17.4 %copy-start.39 = (f32[512]{0:T(512)}, f32[512]{0:T(512)S(1)}, u32[]{:S(2)}) copy-start(f32[512]{0:T(512)S(1)} %get-tuple-element.548) | copy-start | bytes 6148
  13.8 15.7 %copy-start.37 = (f32[512]{0:T(512)}, f32[512]{0:T(512)S(1)}, u32[]{:S(2)}) copy-start(f32[512]{0:T(512)S(1)} %subtract_convert_fusion.1) | copy-start | bytes 6148
  14.5 15.9 %copy-start.34 = (f32[896]{0:T(1024)}, f32[896]{0:T(1024)S(1)}, u32[]{:S(2)}) copy-start(f32[896]{0:T(1024)S(1)} %convert_element_type.193) | copy-start | bytes 10756
  15.4 15.7 %copy-start.24 = (f32[512,32]{0,1:T(8,128)}, f32[512,32]{0,1:T(8,128)S(1)}, u32[]{:S(2)}) copy-start(f32[512,32]{0,1:T(8,128)S(1)} %get-tuple-element.546) | copy-start | bytes 196612
  15.4 14.9 %copy-start.21 = (bf16[896,448]{0,1:T(8,128)(2,1)S(1)}, bf16[896,448]{0,1:T(8,128)(2,1)}, u32[]{:S(2)}) copy-start(bf16[896,448]{0,1:T(8,128)(2,1)} %param.26) | copy-start | bytes 2408452
  66.0 42.9 %copy-start.49 = (s32[4]{0:T(128)}, s32[4]{0:T(128)S(1)}, u32[]{:S(2)}) copy-start(s32[4]{0:T(128)S(1)} %get-tuple-element.870) | copy-start | bytes 52
  66.0 44.4 %copy-start.8 = (f32[512,1,7,64]{0,3,2,1:T(8,128)}, f32[512,1,7,64]{0,3,2,1:T(8,128)S(1)}, u32[]{:S(2)}) copy-start(f32[512,1,7,64]{0,3,2,1:T(8,128)S(1)} %get-tuple-element.400) | copy-start | bytes 2752516
  66.1 44.4 %copy-start.23 = (s32[512]{0:T(512)}, s32[512]{0:T(512)S(1)}, u32[]{:S(2)}) copy-start(s32[512]{0:T(512)S(1)} %get-tuple-element.862) | copy-start | bytes 6148
  66.1 44.4 %copy-start.26 = (s32[512]{0:T(512)}, s32[512]{0:T(512)S(1)}, u32[]{:S(2)}) copy-start(s32[512]{0:T(512)S(1)} %get-tuple-element.863) | copy-start | bytes 6148
  66.1 44.4 %copy-start.36 = (s32[1,3]{1,0:T(1,128)}, s32[1,3]{1,0:T(1,128)S(1)}, u32[]{:S(2)}) copy-start(s32[1,3]{1,0:T(1,128)S(1)} %get-tuple-element.869) | copy-start | bytes 40
  66.1 75.6 %copy-start.15 = (f32[512,1,7]{0,2,1:T(8,128)}, f32[512,1,7]{0,2,1:T(8,128)S(1)}, u32[]{:S(2)}) copy-start(f32[512,1,7]{0,2,1:T(8,128)S(1)} %get-tuple-element.401) | copy-start | bytes 43012
  66.1 2.9 copy-start.48
  68.8 93.4 %all-reduce.10.cloned.1.call-start = ((), (), s32[]{:S(2)}) async-start(), calls=%async_computation.2 | async-start | bytes 1835008 | tf_op jit(solution)/shard_map/psum | solution.py:274
  69.1 95.8 %copy-start.43 = (f32[512]{0:T(512)}, f32[512]{0:T(512)S(1)}, u32[]{:S(2)}) copy-start(f32[512]{0:T(512)S(1)} %compare_convert_fusion.1) | copy-start | bytes 6148
  110.5 8.8 slice-start.3
  112.2 7.1 copy-start.20
  112.2 7.1 slice-start.4
  112.2 11.6 %slice-start.7 = ((s8[4358144]{0:T(1024)(128)(4,1)}), s8[4194304]{0:T(1024)(128)(4,1)S(1)}, s32[]{:S(2)}) async-start(s8[4358144]{0:T(1024)(128)(4,1)} %bitcast.248), calls=%async_computation.13 | async-start | bytes 8388608
  119.3 4.5 copy-start.17
  119.3 4.5 slice-start.8
  119.4 18.2 %slice-start.5 = ((s8[4358144]{0:T(1024)(128)(4,1)}), s8[4194304]{0:T(1024)(128)(4,1)S(1)}, s32[]{:S(2)}) async-start(s8[4358144]{0:T(1024)(128)(4,1)} %bitcast.246), calls=%async_computation.11 | async-start | bytes 8388608
  123.9 13.7 %slice-start.6 = ((s8[4358144]{0:T(1024)(128)(4,1)}), s8[163840]{0:T(1024)(128)(4,1)S(1)}, s32[]{:S(2)}) async-start(s8[4358144]{0:T(1024)(128)(4,1)} %bitcast.246), calls=%async_computation.12 | async-start | bytes 327680
  132.9 4.7 copy-start.51
  141.4 136.4 %reduce-scatter.2.cloned.1.call-start = ((), (), s32[]{:S(2)}) async-start(), calls=%async_computation.3 | async-start | bytes 655360 | tf_op jit(solution)/shard_map/reduce_scatter | solution.py:290
  142.3 19.9 %copy-start.5 = (bf16[512,896]{1,0:T(8,128)(2,1)S(1)}, bf16[512,896]{1,0:T(8,128)(2,1)}, u32[]{:S(2)}) copy-start(bf16[512,896]{1,0:T(8,128)(2,1)} %all-reduce.8.cloned.1.call-done) | copy-start | bytes 2752516
  162.2 2.7 copy-start.11
  162.2 2.7 copy-start.18
  165.7 2.1 copy-start.3
  165.7 1.8 copy-start.9
  165.7 1.8 copy-start.16
  179.5 1.2 copy-start.42
  221.7 8.4 copy-start.25
  221.7 8.4 copy-start.28
  221.7 81.3 %all-reduce.14.cloned.1.call-start = ((), (), s32[]{:S(2)}) async-start(), calls=%async_computation.5 | async-start | bytes 3670016 | tf_op jit(solution)/shard_map/psum | solution.py:262
  230.1 48.8 %copy-start.38 = (f32[512]{0:T(512)S(1)}, f32[512]{0:T(512)}, u32[]{:S(2)}) copy-start(f32[512]{0:T(512)} %copy-done.37) | copy-start | bytes 6148
  230.1 48.8 %copy-start.47 = (f32[32]{0:T(128)S(1)}, f32[32]{0:T(128)}, u32[]{:S(2)}) copy-start(f32[32]{0:T(128)} %copy-done.46) | copy-start | bytes 388
  230.2 48.9 %copy-start.31 = (bf16[896,64]{0,1:T(8,128)(2,1)S(1)}, bf16[896,64]{0,1:T(8,128)(2,1)}, u32[]{:S(2)}) copy-start(bf16[896,64]{0,1:T(8,128)(2,1)} %param.28) | copy-start | bytes 344068
  231.2 48.4 %copy-start.33 = (bf16[896,64]{0,1:T(8,128)(2,1)S(1)}, bf16[896,64]{0,1:T(8,128)(2,1)}, u32[]{:S(2)}) copy-start(bf16[896,64]{0,1:T(8,128)(2,1)} %param.30) | copy-start | bytes 344068
  277.8 1.8 copy-start.10
  281.8 8.5 copy-start.19
  281.8 8.5 copy-start.44
  281.9 809.6 %all-reduce.12.cloned.1.call-start = ((), (), s32[]{:S(2)}) async-start(), calls=%async_computation.4 | async-start | bytes 59637760 | tf_op jit(solution)/shard_map/psum | solution.py:332
  281.9 8.4 copy-start.50
  290.4 6.4 copy-start.35
  290.4 6.4 copy-start.40
  296.8 1.9 copy-start.4
  296.8 1.9 copy-start.13
  298.7 2.9 copy-start.27
  302.7 2.3 copy-start.41
  302.7 82.6 %copy-start.45 = (f32[512]{0:T(512)S(1)}, f32[512]{0:T(512)}, u32[]{:S(2)}) copy-start(f32[512]{0:T(512)} %get-tuple-element.547) | copy-start | bytes 6148
  302.8 82.6 %copy-start.6 = (bf16[512,896]{1,0:T(8,128)(2,1)S(1)}, bf16[512,896]{1,0:T(8,128)(2,1)}, u32[]{:S(2)}) copy-start(bf16[512,896]{1,0:T(8,128)(2,1)} %all-reduce.8.cloned.1.call-done) | copy-start | bytes 2752516
  1091.5 2.8 copy-start.30
  1091.5 3.5 copy-start.29
  1091.5 4.2 copy-start.14
  1096.8 8.6 copy-start.7
  1096.8 13.0 %slice-start = ((s8[8716288]{0:T(1024)(128)(4,1)}), s8[4194304]{0:T(1024)(128)(4,1)S(1)}, s32[]{:S(2)}) async-start(s8[8716288]{0:T(1024)(128)(4,1)} %bitcast.218), calls=%async_computation.6 | async-start | bytes 8388608
  1096.9 14.6 %slice-start.1 = ((s8[8716288]{0:T(1024)(128)(4,1)}), s8[4194304]{0:T(1024)(128)(4,1)S(1)}, s32[]{:S(2)}) async-start(s8[8716288]{0:T(1024)(128)(4,1)} %bitcast.218), calls=%async_computation.7 | async-start | bytes 8388608
  1105.5 6.1 slice-start.2
  1111.6 3.5 copy-start.1
  (2 other events, 2.0 us)
Sparse Core Ops, SparseCore 0:
  68.9 39.9 all-reduce.7
  141.5 20.5 all-reduce.9
  221.8 56.0 reduce-scatter.1
  282.0 20.8 all-reduce.13
  310.3 781.1 all-reduce.11
where the time goes:
time: 1130 us; the launch traced here: 1120 us
  waiting for transfers between devices  799 us (71%)
  blocking collectives  91.8 us (8%)
  matrix products  86.4 us (8%)
  local copies, waits for them, and re-layouts  61.1 us (5%)
  other arithmetic  36 us (3%)
  loops' own time  31.6 us (3%)
  between operations  15 us (1%)
    psum x1, waiting for transfers between devices, local(): lax.psum((grad_gain_one, grad_w_query, grad_b_query, grad_w_key, grad_b_k...  702 us
    psum x1, blocking collectives, local(): lax.psum((grad_gain_one, grad_w_query, grad_b_query, grad_w_key, grad_b_k...  80.3 us
    reduce_scatter x1, waiting for transfers between devices, local(): lax.psum_scatter(grad_kv_whole.astype(jnp.bfloat16), 'blk', scatter_dimen...  44.7 us
    psum x1, waiting for transfers between devices, local(): lax.psum(product(out_low, w_out).astype(jnp.bfloat16), 'tensor')  39.8 us
    dot_general x7, matrix products, outer_sum(): lax.dot_general(left_side, right_side, (((0,), (0,)), ((), ())), preferre...  28.9 us
    unnamed x127, local copies, waits for them, and re-layouts  26.7 us
    dot_general x7, matrix products, product(): return jnp.dot(left_side, right_side, preferred_element_type=jnp.float32)  23 us
    dot_general x7, matrix products, inner_sum(): lax.dot_general(left_side, right_side, (((1,), (1,)), ((), ())), preferre...  22.7 us
  transfers between devices with their start and end apart: 5, of which 4 were waited for; matrix products, arithmetic and copies ran while one was open for 4% of the time, Pallas kernels for 0%

commit v1 on v0

v1 whole, which is shorter than its diff:
```python
import functools
import math

import jax
import jax.numpy as jnp
from jax import lax
from jax.experimental import pallas as pl
from jax.experimental.pallas import tpu as pltpu
from jax.sharding import PartitionSpec as P

HEAD_DIM = 64

epsilon = 1e-06
rope_base = 1000000.0
masked_value = -1e30

low = jnp.bfloat16
wide = jnp.float32
vmem_limit = 50 * 1024 * 1024


def dot_nn(left, right):
    return lax.dot_general(left, right, (((1,), (0,)), ((), ())), preferred_element_type=wide)


def dot_nt(left, right):
    return lax.dot_general(left, right, (((1,), (1,)), ((), ())), preferred_element_type=wide)


def dot_tn(left, right):
    return lax.dot_general(left, right, (((0,), (0,)), ((), ())), preferred_element_type=wide)


def partner(value, axis, step):
    count = lax.axis_size(axis)
    return lax.ppermute(value, axis, [(i, i ^ step) for i in range(count)])


def gather_blocks(piece):
    count = lax.axis_size("blk")
    return [piece] + [partner(piece, "blk", r) for r in range(1, count)]


def gather_relayed(piece):
    count = lax.axis_size("blk")
    rows = piece.shape[0] // 2
    first, second = [piece[:rows]], [piece[rows:]]
    for r in range(1, count):
        low_bit = r & -r
        high_bit = 1 << (r.bit_length() - 1)
        if low_bit == r:
            whole = partner(piece, "blk", r)
            first.append(whole[:rows])
            second.append(whole[rows:])
        else:
            first.append(partner(first[r ^ high_bit], "blk", high_bit))
            second.append(partner(second[r ^ low_bit], "blk", low_bit))
    return first, second


def scatter_blocks(stacked):
    return [stacked[0]] + [partner(stacked[r], "blk", r) for r in range(1, stacked.shape[0])]


def line_sum(value):
    count = lax.axis_size("dp")
    middle = count // 2
    index = lax.axis_index("dp")
    total = value.astype(low)
    for s in range(middle - 1):
        passed = lax.ppermute(total, "dp", [(s, s + 1), (count - 1 - s, count - 2 - s)])
        total = (total.astype(wide) + passed.astype(wide)).astype(low)
    passed = lax.ppermute(total, "dp", [(middle - 1, middle), (middle, middle - 1)])
    total = (total.astype(wide) + passed.astype(wide)).astype(low)
    for s in range(middle - 1):
        passed = lax.ppermute(
            total, "dp", [(middle - 1 - s, middle - 2 - s), (middle + s, middle + s + 1)]
        )
        arrived = (index == middle - 2 - s) | (index == middle + s + 1)
        total = jnp.where(arrived, passed, total)
    return total


def call(body, outs, ins, scratch=(), grid=None, in_specs=None, out_specs=None, flops=0):
    whole = pl.BlockSpec(memory_space=pltpu.VMEM)
    moved = sum(math.prod(v.shape) * v.dtype.itemsize for v in list(outs) + list(ins))
    extra = {} if grid is None else {"grid": grid}
    return pl.pallas_call(
        body,
        out_shape=tuple(outs),
        in_specs=in_specs or [whole] * len(ins),
        out_specs=out_specs or tuple([whole] * len(outs)),
        scratch_shapes=list(scratch),
        cost_estimate=pl.CostEstimate(flops=flops, bytes_accessed=moved, transcendentals=0),
        compiler_params=pltpu.CompilerParams(vmem_limit_bytes=vmem_limit),
        **extra,
    )(*ins)


def shape(dims, kind):
    return jax.ShapeDtypeStruct(dims, kind)


in_smem = pl.BlockSpec(memory_space=pltpu.SMEM)
in_vmem = pl.BlockSpec(memory_space=pltpu.VMEM)


def segment_start(lengths_ref, rows):
    start = jnp.zeros_like(rows)
    end = jnp.int32(0)
    for i in range(lengths_ref.shape[1]):
        end = end + lengths_ref[0, i]
        start = jnp.where(rows >= end, end, start)
    return start


def rotate(pair, cosine, sine):
    half = HEAD_DIM // 2
    first, second = pair[:half], pair[half:]
    return jnp.concatenate(
        [first * cosine - second * sine, second * cosine + first * sine], axis=0
    )


def enter_kernel(
    lengths_ref, place_ref, tokens_ref, gain_ref, wq_ref, wk_ref, wv_ref, bq_ref, bk_ref, bv_ref,
    turn_ref, q_ref, kv_ref, normed_ref, tokens_t_ref, cos_ref, sin_ref,
):
    rows = tokens_ref.shape[0]
    hidden = tokens_ref[...].astype(wide)
    inverse = lax.rsqrt(jnp.mean(hidden * hidden, axis=1, keepdims=True) + epsilon)
    normed = (hidden * inverse * gain_ref[...].astype(wide)).astype(low)
    tokens_t_ref[...] = hidden.T.astype(low)
    normed_ref[...] = normed.astype(wide).T.astype(low)
    index = place_ref[0] * rows + lax.broadcasted_iota(jnp.int32, (1, rows), 1)
    position = (index - segment_start(lengths_ref, index)).astype(wide)
    angles = turn_ref[...] * position
    cosine, sine = jnp.cos(angles), jnp.sin(angles)
    cos_ref[...] = cosine
    sin_ref[...] = sine
    q_lin = dot_nn(normed, wq_ref[...]) + bq_ref[...].astype(wide)
    width = q_lin.shape[1]
    padded = -(-width // 128) * 128
    if padded != width:
        q_lin = jnp.concatenate([q_lin, jnp.zeros((rows, padded - width), wide)], axis=1)
    q_turned = q_lin.T
    for h in range(width // HEAD_DIM):
        head = rotate(q_turned[h * HEAD_DIM : (h + 1) * HEAD_DIM], cosine, sine)
        q_ref[h * HEAD_DIM : (h + 1) * HEAD_DIM, :] = head.astype(low) * low(HEAD_DIM**-0.5)
    k_lin = dot_nn(normed, wk_ref[...]) + bk_ref[...].astype(wide)
    v_lin = dot_nn(normed, wv_ref[...]) + bv_ref[...].astype(wide)
    both = jnp.concatenate([k_lin, v_lin], axis=1).T
    both = jnp.concatenate([rotate(both[:HEAD_DIM], cosine, sine), both[HEAD_DIM:]], axis=0)
    kv_ref[...] = both.T.astype(low)


def mask_bias(key_base, key_rows, q_index, q_start):
    keys = key_base + lax.broadcasted_iota(jnp.int32, (key_rows, q_index.shape[1]), 0)
    return jnp.where((keys >= q_start) & (keys <= q_index), 0.0, masked_value)


def attend_kernel(
    lengths_ref, place_ref, q_ref, kv_ref, w_out_ref,
    out_ref, log_ref, part_ref,
    acc_ref, max_ref, bias_ref,
):
    rows = q_ref.shape[1]
    heads = q_ref.shape[0] // HEAD_DIM
    own = place_ref[0]
    q_index = own * rows + lax.broadcasted_iota(jnp.int32, (1, rows), 1)
    q_start = segment_start(lengths_ref, q_index)
    base = own * rows
    first_key = jnp.int32(0)
    end = jnp.int32(0)
    for i in range(lengths_ref.shape[1]):
        end = end + lengths_ref[0, i]
        first_key = jnp.where(base >= end, end, first_key)
    acc_ref[...] = jnp.zeros_like(acc_ref)
    max_ref[...] = jnp.full_like(max_ref, masked_value)

    def visit(block, carry):
        key_base = pl.multiple_of(block * rows, rows)
        pair = kv_ref[pl.ds(key_base, rows), :]
        keys = pair[:, :HEAD_DIM]
        values = pair.astype(wide).T[HEAD_DIM:].astype(low)
        values = jnp.concatenate([values, jnp.ones((16, rows), low)], axis=0)
        bias_ref[...] = mask_bias(key_base, rows, q_index, q_start)
        for h in range(heads):
            scores = dot_nn(keys, q_ref[h * HEAD_DIM : (h + 1) * HEAD_DIM, :]) + bias_ref[...]
            old = max_ref[h : h + 1, :]
            new = jnp.maximum(old, jnp.max(scores, axis=0, keepdims=True))
            weight = jnp.exp(scores - new).astype(low)
            acc_ref[h] = acc_ref[h] * jnp.exp(old - new) + dot_nn(values, weight)
            max_ref[h : h + 1, :] = new
        return carry

    lax.fori_loop(first_key // rows, own + 1, visit, 0)
    for h in range(heads):
        total = acc_ref[h, HEAD_DIM : HEAD_DIM + 1, :]
        out_ref[h * HEAD_DIM : (h + 1) * HEAD_DIM, :] = acc_ref[h, :HEAD_DIM, :] / total
        log_ref[h : h + 1, :] = max_ref[h : h + 1, :] + jnp.log(total)
    part_ref[...] = dot_tn(w_out_ref[...], out_ref[...].astype(low))


def middle_kernel(place_ref, tokens_ref, part_ref, passed_ref, gain_ref, hidden_ref, normed_ref):
    half = hidden_ref.shape[1]
    mine = pl.ds(pl.multiple_of(place_ref[1] * half, half), half)
    hidden = tokens_ref[:, mine].astype(wide) + part_ref[:, mine] + passed_ref[...].astype(wide)
    hidden_ref[...] = hidden
    inverse = lax.rsqrt(jnp.mean(hidden * hidden, axis=0, keepdims=True) + epsilon)
    normed_ref[...] = (hidden * inverse * gain_ref[...].astype(wide)).astype(low)


def hidden_kernel(
    x_ref, gy_ref, gate_t_ref, up_t_ref, down_ref, gate_ref, up_ref,
    mixed_ref, grad_gate_ref, grad_up_ref, grad_x_ref,
):
    x = x_ref[0]
    gate = dot_nn(gate_t_ref[...], x)
    up = dot_nn(up_t_ref[...], x)
    grad_mixed = dot_nt(down_ref[...], gy_ref[...])
    sigmoid = 1.0 / (1.0 + jnp.exp(-gate))
    silu = gate * sigmoid
    mixed_ref[0] = (silu * up).astype(low)
    grad_gate = (grad_mixed * up * sigmoid * (1.0 + gate * (1.0 - sigmoid))).astype(low)
    grad_up = (grad_mixed * silu).astype(low)
    grad_gate_ref[0] = grad_gate
    grad_up_ref[0] = grad_up
    grad_x_ref[0] = (dot_nn(gate_ref[...], grad_gate) + dot_nn(up_ref[...], grad_up)).astype(low)


def weight_kernel(dot, *refs):
    pairs, out_ref, acc_ref = refs[:-2], refs[-2], refs[-1]
    step = pl.program_id(0)

    def both(ref):
        return ref[0] if len(ref.shape) == 3 else ref[...]

    total = dot(both(pairs[0]), both(pairs[1]))
    for i in range(2, len(pairs), 2):
        total = total + dot(both(pairs[i]), both(pairs[i + 1]))

    @pl.when(step == 0)
    def _():
        acc_ref[...] = total

    @pl.when(step > 0)
    def _():
        acc_ref[...] += total

    @pl.when(step == pl.num_programs(0) - 1)
    def _():
        out_ref[...] = acc_ref[...].astype(low)


def project_kernel(weight_ref, mixed_ref, out_ref):
    out_ref[0] = dot_nn(weight_ref[...], mixed_ref[0]).astype(low)


def sum_blocks(refs):
    total = refs[0][...].astype(wide)
    for ref in refs[1:]:
        total = total + ref[...].astype(wide)
    return total


def layer_kernel(hidden_ref, *refs):
    out_ref = refs[-1]
    out_ref[...] = (hidden_ref[...] + sum_blocks(refs[:-1])).T.astype(low)


def grad_middle_kernel(hidden_ref, gain_ref, gy_ref, *refs):
    grad_ref, grad_low_ref, grad_gain_ref = refs[-3:]
    hidden = hidden_ref[...]
    inverse = lax.rsqrt(jnp.mean(hidden * hidden, axis=0, keepdims=True) + epsilon)
    grad_normed = sum_blocks(refs[:-3])
    weighted = gain_ref[...].astype(wide) * grad_normed
    inner = jnp.mean(weighted * hidden, axis=0, keepdims=True)
    grad = inverse * weighted - hidden * (inverse * inverse * inverse * inner)
    grad = grad + gy_ref[...].astype(wide).T
    grad_ref[...] = grad
    grad_low_ref[...] = grad.astype(low)
    grad_gain_ref[...] = jnp.sum(grad_normed * hidden * inverse, axis=1, keepdims=True)


def attend_back_kernel(
    lengths_ref, place_ref, gm_mine_ref, gm_other_ref, w_out_ref, out_ref, log_ref, q_ref, kv_ref, cos_ref, sin_ref,
    grad_w_out_ref, grad_q_ref, grad_kv_ref,
    gm_ref, go_ref, delta_ref, bias_ref, dq_ref, dk_ref, dv_ref,
):
    rows = q_ref.shape[1]
    half = rows // 2
    heads = q_ref.shape[0] // HEAD_DIM
    blocks = kv_ref.shape[0] // rows
    own, core = place_ref[0], place_ref[1]
    gm_ref[:, pl.ds(pl.multiple_of(core * half, half), half)] = gm_mine_ref[...]
    gm_ref[:, pl.ds(pl.multiple_of((1 - core) * half, half), half)] = gm_other_ref[...]
    grad_out = dot_nn(w_out_ref[...], gm_ref[...]).astype(low)
    go_ref[...] = grad_out
    grad_w_out_ref[...] = dot_nt(out_ref[...].astype(low), gm_ref[...]).astype(low)
    product = grad_out.astype(wide) * out_ref[...]
    for h in range(heads):
        delta_ref[h : h + 1, :] = jnp.sum(
            product[h * HEAD_DIM : (h + 1) * HEAD_DIM], axis=0, keepdims=True
        )
    dq_ref[...] = jnp.zeros_like(dq_ref)
    q_index = own * rows + lax.broadcasted_iota(jnp.int32, (1, rows), 1)
    q_start = segment_start(lengths_ref, q_index)
    base = own * rows
    first_key = jnp.int32(0)
    end = jnp.int32(0)
    for i in range(lengths_ref.shape[1]):
        end = end + lengths_ref[0, i]
        first_key = jnp.where(base >= end, end, first_key)
    first_block = first_key // rows

    def clear(block, carry):
        grad_kv_ref[block ^ own] = jnp.zeros((rows, 2 * HEAD_DIM), low)
        return carry

    lax.fori_loop(0, first_block, clear, 0)
    lax.fori_loop(own + 1, blocks, clear, 0)

    def visit(block, carry):
        key_base = pl.multiple_of(block * rows, rows)
        pair = kv_ref[pl.ds(key_base, rows), :]
        keys = pair[:, :HEAD_DIM]
        values = pair[:, HEAD_DIM:]
        keys_t = pair.astype(wide).T[:HEAD_DIM].astype(low)
        bias_ref[...] = mask_bias(key_base, rows, q_index, q_start)
        for h in range(heads):
            span = slice(h * HEAD_DIM, (h + 1) * HEAD_DIM)
            scores = dot_nn(keys, q_ref[span, :]) + bias_ref[...]
            weight = jnp.exp(scores - log_ref[h : h + 1, :])
            grad_weight = dot_nn(values, go_ref[span, :])
            grad_scores = (weight * (grad_weight - delta_ref[h : h + 1, :])).astype(low)
            dq_ref[span, :] += dot_nn(keys_t, grad_scores)
            dk = dot_nt(grad_scores, q_ref[span, :])
            dv = dot_nt(weight.astype(low), go_ref[span, :])
            if h == 0:
                dk_ref[...] = dk
                dv_ref[...] = dv
            else:
                dk_ref[...] += dk
                dv_ref[...] += dv
        grad_kv_ref[block ^ own] = jnp.concatenate([dk_ref[...], dv_ref[...]], axis=1).astype(low)
        return carry

    lax.fori_loop(first_block, own + 1, visit, 0)
    for h in range(heads):
        span = slice(h * HEAD_DIM, (h + 1) * HEAD_DIM)
        turned = rotate(dq_ref[span, :] * HEAD_DIM**-0.5, cos_ref[...], -sin_ref[...])
        grad_q_ref[span, :] = turned.astype(low)


def query_kernel(normed_ref, grad_q_ref, wq_ref, grad_wq_ref, part_ref, grad_bq_ref):
    grad_q = grad_q_ref[...]
    grad_wq_ref[...] = dot_nt(normed_ref[...], grad_q).astype(low)
    part_ref[...] = dot_nn(wq_ref[...], grad_q)
    grad_bq_ref[...] = jnp.sum(grad_q.astype(wide), axis=1, keepdims=True)


def key_kernel(place_ref, normed_ref, tokens_ref, part_ref, wk_ref, wv_ref, cos_ref, sin_ref, *refs):
    grad_wkv_ref, mine_ref, other_ref, grad_bkv_ref, grad_gain_ref, sum_ref = refs[-6:]
    both = sum_blocks(refs[:-6]).T
    both = jnp.concatenate(
        [rotate(both[:HEAD_DIM], cos_ref[...], -sin_ref[...]), both[HEAD_DIM:]], axis=0
    ).astype(low)
    grad_wkv_ref[...] = dot_nt(normed_ref[...], both).astype(low)
    grad_bkv_ref[...] = jnp.sum(both.astype(wide), axis=1, keepdims=True)
    total = part_ref[...] + dot_nn(wk_ref[...], both[:HEAD_DIM]) + dot_nn(wv_ref[...], both[HEAD_DIM:])
    sum_ref[...] = total
    hidden = tokens_ref[...].astype(wide)
    inverse = lax.rsqrt(jnp.mean(hidden * hidden, axis=0, keepdims=True) + epsilon)
    grad_gain_ref[...] = jnp.sum(total * (hidden * inverse), axis=1, keepdims=True)
    half = mine_ref.shape[1]
    core = place_ref[1]
    mine_ref[...] = sum_ref[:, pl.ds(pl.multiple_of(core * half, half), half)]
    other_ref[...] = sum_ref[:, pl.ds(pl.multiple_of((1 - core) * half, half), half)].astype(low)


def leave_kernel(place_ref, tokens_ref, mine_ref, passed_ref, gain_ref, grad_mid_ref, out_ref):
    half = mine_ref.shape[1]
    hidden = tokens_ref[:, pl.ds(pl.multiple_of(place_ref[1] * half, half), half)].astype(wide)
    inverse = lax.rsqrt(jnp.mean(hidden * hidden, axis=0, keepdims=True) + epsilon)
    weighted = gain_ref[...].astype(wide) * (mine_ref[...] + passed_ref[...].astype(wide))
    inner = jnp.mean(weighted * hidden, axis=0, keepdims=True)
    grad = grad_mid_ref[...] + inverse * weighted - hidden * (inverse * inverse * inverse * inner)
    out_ref[...] = grad.T.astype(low)


def rows_kernel(count, place_ref, *refs):
    out_ref = refs[-1]
    step = pl.program_id(0)
    half = refs[0].shape[0]
    for r in range(count):

        @pl.when((step ^ place_ref[0]) == r)
        def _(r=r):
            out_ref[:half, :] = refs[r][...].astype(wide)
            out_ref[half:, :] = refs[count + r][...].astype(wide)


def columns_kernel(count, place_ref, *refs):
    out_ref = refs[-1]
    step = pl.program_id(0)
    width = refs[0].shape[1]
    half_steps = pl.num_programs(0) // 2
    for k in range(count):
        for first in (True, False):

            @pl.when((place_ref[0] == k) & ((step < half_steps) == first))
            def _(k=k, first=first):
                for r in range(count):
                    j = k ^ r
                    ref = refs[r] if first else refs[count + r]
                    out_ref[:, j * width : (j + 1) * width] = ref[...].astype(wide)


def place_rows(place, piece):
    first, second = gather_relayed(piece)
    count = len(first)
    rows, width = piece.shape
    (whole,) = call(
        functools.partial(rows_kernel, count),
        [shape((count * rows, width), wide)],
        [place] + first + second,
        grid=(count,),
        in_specs=[in_smem] + [in_vmem] * (2 * count),
        out_specs=(pl.BlockSpec((rows, width), lambda i: (i, 0)),),
    )
    return whole


def place_columns(place, piece):
    first, second = gather_relayed(piece)
    count = len(first)
    rows, width = piece.shape
    tile = 64
    steps = rows // tile
    half = steps // 2
    early = pl.BlockSpec((tile, width), lambda i: (jnp.minimum(i, half - 1), 0))
    late = pl.BlockSpec((tile, width), lambda i: (jnp.maximum(i - half, 0), 0))
    (whole,) = call(
        functools.partial(columns_kernel, count),
        [shape((rows, count * width), wide)],
        [place] + first + second,
        grid=(steps,),
        in_specs=[in_smem] + [early] * count + [late] * count,
        out_specs=(pl.BlockSpec((tile, count * width), lambda i: (i, 0)),),
    )
    return whole


def local(
    tokens,
    lengths,
    norm1_gain,
    w_query,
    b_query,
    w_key,
    b_key,
    w_value,
    b_value,
    w_out,
    norm2_gain,
    w_gate,
    w_up,
    w_down,
    cotangent,
):
    rows, width = tokens.shape
    half = rows // 2
    blocks = lax.axis_size("blk")
    own_block = lax.axis_index("blk")
    own_core = lax.axis_index("tensor")
    q_width = w_query.shape[1]
    heads = q_width // HEAD_DIM
    units = w_gate.shape[1] // blocks
    place = jnp.stack([own_block, own_core]).astype(jnp.int32)
    gain_two = norm2_gain.reshape(width, 1)

    def whole_rows(mine):
        other = partner(mine, "tensor", 1)
        return jnp.where(
            own_core == 0,
            jnp.concatenate([mine, other], axis=0),
            jnp.concatenate([other, mine], axis=0),
        )

    half_dim = HEAD_DIM // 2
    turn = (rope_base ** (-2.0 * jnp.arange(half_dim, dtype=wide) / HEAD_DIM)).reshape(half_dim, 1)
    q_t, key_value, normed_t, tokens_t, cosine, sine = call(
        enter_kernel,
        [
            shape((q_width, rows), low),
            shape((rows, 2 * HEAD_DIM), low),
            shape((width, rows), low),
            shape((width, rows), low),
            shape((half_dim, rows), wide),
            shape((half_dim, rows), wide),
        ],
        [
            lengths, place, tokens, norm1_gain.reshape(1, width), w_query, w_key, w_value,
            b_query.reshape(1, -1), b_key.reshape(1, -1), b_value.reshape(1, -1), turn,
        ],
        in_specs=[in_smem] * 2 + [in_vmem] * 9,
        flops=2 * rows * width * (q_width + 2 * HEAD_DIM),
    )
    whole_kv = lax.all_gather(key_value, "blk", axis=0, tiled=True)

    row_index = own_block * rows + own_core * half + jnp.arange(half, dtype=jnp.int32)
    real = (row_index < jnp.sum(lengths)).astype(low)
    grad_y = lax.dynamic_slice_in_dim(cotangent, own_core * half, half, 0) * real[:, None]
    grad_y, whole_kv = lax.optimization_barrier((grad_y, whole_kv))
    grad_y_mine = jnp.concatenate(gather_blocks(grad_y), axis=0)
    grad_y_other = partner(grad_y_mine, "tensor", 1)

    out_t, log_total, part = call(
        attend_kernel,
        [
            shape((q_width, rows), wide),
            shape((heads + 1, rows), wide),
            shape((width, rows), wide),
        ],
        [lengths, place, q_t, whole_kv, w_out],
        [
            pltpu.VMEM((heads, HEAD_DIM + 16, rows), wide),
            pltpu.VMEM((heads + 1, rows), wide),
            pltpu.VMEM((rows, rows), wide),
        ],
        in_specs=[in_smem] * 2 + [in_vmem] * 3,
        flops=4 * rows * rows * q_width * blocks,
    )
    part_other = lax.dynamic_slice_in_dim(part, (1 - own_core) * half, half, 1).astype(low)
    hidden, normed_two = call(
        middle_kernel,
        [shape((width, half), wide), shape((width, half), low)],
        [place, tokens_t, part, partner(part_other, "tensor", 1), gain_two],
        in_specs=[in_smem] + [in_vmem] * 4,
    )

    x_mine = jnp.stack(gather_blocks(normed_two))
    x_other = partner(x_mine, "tensor", 1)
    gate_own = lax.dynamic_slice_in_dim(w_gate, own_block * units, units, 1)
    up_own = lax.dynamic_slice_in_dim(w_up, own_block * units, units, 1)
    down_own = lax.dynamic_slice_in_dim(w_down, own_block * units, units, 0)
    gate_t, up_t, down_t = gate_own.T, up_own.T, down_own.T

    def cut(dims):
        return pl.BlockSpec((1,) + dims, lambda i: (i, 0, 0))

    unit_cut, width_cut = cut((units, half)), cut((width, half))
    row_cut = pl.BlockSpec((half, width), lambda i: (i, 0))

    def hidden_units(x, grad_rows):
        kept = shape((blocks, units, half), low)
        return call(
            hidden_kernel,
            [kept, kept, kept, shape((blocks, width, half), low)],
            [x, grad_rows, gate_t, up_t, down_own, gate_own, up_own],
            grid=(blocks,),
            in_specs=[width_cut, row_cut] + [in_vmem] * 5,
            out_specs=(unit_cut, unit_cut, unit_cut, width_cut),
            flops=10 * rows * blocks * width * units // 2,
        )

    mixed_mine, gate_mine, up_mine, back_mine = hidden_units(x_mine, grad_y_mine)
    mixed_other, gate_other, up_other, back_other = hidden_units(x_other, grad_y_other)
    back_passed = partner(back_other, "tensor", 1)

    def hidden_weight(dot, dims, arrays, specs):
        (out,) = call(
            functools.partial(weight_kernel, dot),
            [shape(dims, low)],
            arrays,
            [pltpu.VMEM(dims, wide)],
            grid=(blocks,),
            in_specs=specs,
            out_specs=(pl.BlockSpec(dims, lambda i: (0, 0)),),
            flops=2 * rows * blocks * width * units,
        )
        return out

    grad_w_down = hidden_weight(
        dot_nn,
        (units, width),
        [mixed_mine, grad_y_mine, mixed_other, grad_y_other],
        [unit_cut, row_cut] * 2,
    )
    back = (back_mine.astype(wide) + back_passed.astype(wide)).astype(low)
    back_pieces = scatter_blocks(back)
    grad_w_gate = hidden_weight(
        dot_nt,
        (width, units),
        [x_mine, gate_mine, x_other, gate_other],
        [width_cut, unit_cut] * 2,
    )
    grad_w_up = hidden_weight(
        dot_nt,
        (width, units),
        [x_mine, up_mine, x_other, up_other],
        [width_cut, unit_cut] * 2,
    )

    def project(mixed):
        (out,) = call(
            project_kernel,
            [shape((blocks, width, half), low)],
            [down_t, mixed],
            grid=(blocks,),
            in_specs=[in_vmem, unit_cut],
            out_specs=(width_cut,),
            flops=rows * blocks * width * units,
        )
        return out

    layer_passed = partner(project(mixed_other), "tensor", 1)
    layer_sum = (project(mixed_mine).astype(wide) + layer_passed.astype(wide)).astype(low)
    (layer_half,) = call(
        layer_kernel, [shape((half, width), low)], [hidden] + scatter_blocks(layer_sum)
    )
    layer_out = whole_rows(layer_half)
    grad_w_down = place_rows(place, line_sum(grad_w_down))
    grad_w_gate = place_columns(place, line_sum(grad_w_gate))
    grad_w_up = place_columns(place, line_sum(grad_w_up))

    grad_mid, grad_mid_low, grad_gain_two = call(
        grad_middle_kernel,
        [shape((width, half), wide), shape((width, half), low), shape((width, 1), wide)],
        [hidden, gain_two, grad_y] + back_pieces,
    )
    grad_w_out, grad_q, grad_kv = call(
        attend_back_kernel,
        [
            shape((q_width, width), low),
            shape((q_width, rows), low),
            shape((blocks, rows, 2 * HEAD_DIM), low),
        ],
        [
            lengths, place, grad_mid_low, partner(grad_mid_low, "tensor", 1), w_out, out_t, log_total, q_t,
            whole_kv, cosine, sine,
        ],
        [
            pltpu.VMEM((width, rows), low),
            pltpu.VMEM((q_width, rows), low),
            pltpu.VMEM((heads + 1, rows), wide),
            pltpu.VMEM((rows, rows), wide),
            pltpu.VMEM((q_width, rows), wide),
            pltpu.VMEM((rows, HEAD_DIM), wide),
            pltpu.VMEM((rows, HEAD_DIM), wide),
        ],
        in_specs=[in_smem] * 2 + [in_vmem] * 9,
        flops=10 * rows * rows * q_width * blocks,
    )
    kv_pieces = scatter_blocks(grad_kv)
    grad_w_query, normed_part, grad_b_query = call(
        query_kernel,
        [shape((width, q_width), low), shape((width, rows), wide), shape((q_width, 1), wide)],
        [normed_t, grad_q, w_query],
        flops=4 * rows * width * q_width,
    )
    grad_w_kv, normed_mine, normed_other, grad_b_kv, grad_gain_one = call(
        key_kernel,
        [
            shape((width, 2 * HEAD_DIM), low),
            shape((width, half), wide),
            shape((width, half), low),
            shape((2 * HEAD_DIM, 1), wide),
            shape((width, 1), wide),
        ],
        [place, normed_t, tokens_t, normed_part, w_key, w_value, cosine, sine] + kv_pieces,
        [pltpu.VMEM((width, rows), wide)],
        in_specs=[in_smem] + [in_vmem] * (7 + blocks),
    )
    (grad_half,) = call(
        leave_kernel,
        [shape((half, width), low)],
        [
            place, tokens_t, normed_mine, partner(normed_other, "tensor", 1),
            norm1_gain.reshape(width, 1), grad_mid,
        ],
        in_specs=[in_smem] + [in_vmem] * 5,
    )
    grad_tokens = whole_rows(grad_half).astype(wide)

    def total_blocks(partial):
        share = partial.shape[0] // blocks
        parts = jnp.stack(
            [
                lax.dynamic_slice_in_dim(partial, (own_block ^ r) * share, share, 0)
                for r in range(blocks)
            ]
        )
        pieces = scatter_blocks(parts)
        total = pieces[0].astype(wide)
        for piece in pieces[1:]:
            total = total + piece.astype(wide)
        stacked = jnp.stack(gather_blocks(line_sum(total)))
        ordered = [
            lax.dynamic_index_in_dim(stacked, own_block ^ j, 0, keepdims=False)
            for j in range(blocks)
        ]
        return jnp.concatenate(ordered, axis=0).astype(wide)

    grad_w_out = total_blocks(grad_w_out)
    grad_w_qkv = total_blocks(jnp.concatenate([grad_w_query, grad_w_kv], axis=1))
    gains = jnp.concatenate([grad_gain_one, grad_gain_two], axis=0).reshape(-1)
    gains = gains + partner(gains, "tensor", 1)
    small = jnp.concatenate([gains, grad_b_query.reshape(-1), grad_b_kv.reshape(-1)])
    for axis in ("blk", "dp"):
        step = 1
        while step < lax.axis_size(axis):
            small = small + partner(small, axis, step)
            step = 2 * step
    grad_b = small[2 * width :]
    return (
        layer_out,
        grad_tokens,
        small[:width],
        grad_w_qkv[:, :q_width],
        grad_b[:q_width],
        grad_w_qkv[:, q_width : q_width + HEAD_DIM],
        grad_b[q_width : q_width + HEAD_DIM],
        grad_w_qkv[:, q_width + HEAD_DIM :],
        grad_b[q_width + HEAD_DIM :],
        grad_w_out,
        small[width : 2 * width],
        grad_w_gate,
        grad_w_up,
        grad_w_down,
    )


def solution(mesh):
    placed = (
        P(("dp", "blk"), None),
        P("dp", None),
        P(),
        P(None, "tensor"),
        P("tensor"),
        P(None, "tensor"),
        P("tensor"),
        P(None, "tensor"),
        P("tensor"),
        P("tensor", None),
        P(),
        P(None, "tensor"),
        P(None, "tensor"),
        P("tensor", None),
        P(("dp", "blk"), None),
    )
    return jax.shard_map(
        local,
        mesh=mesh,
        in_specs=placed,
        out_specs=(
            P(("dp", "blk"), None),
            P(("dp", "blk"), None),
            P(),
            P(None, "tensor"),
            P("tensor"),
            P(None, "tensor"),
            P("tensor"),
            P(None, "tensor"),
            P("tensor"),
            P("tensor", None),
            P(),
            P(None, "tensor"),
            P(None, "tensor"),
            P("tensor", None),
        ),
        check_vma=False,
    )
```

time: 1130 us -> 567 us (0.50)
  waiting for transfers between devices: 799 us -> 171 us
  Pallas kernels: 0 us -> 110 us
  starting transfers between devices: 0.84 us -> 108 us
  matrix products: 86.4 us -> 0 us
  blocking collectives: 91.8 us -> 11.6 us
  local copies, waits for them, and re-layouts: 61.1 us -> 115 us
  loops' own time: 31.6 us -> 0 us
  between operations: 15 us -> 2.05 us
    psum x4 -> x0, waiting for transfers between devices: 755 us -> none  [the longest x1 702 us: local(): lax.psum((grad_gain_one, grad_w_query, grad_b_query, grad_w_key, grad_b_k...]
    ppermute x0 -> x68, waiting for transfers between devices: none -> 171 us  [the longest x53 142 us: partner(): return lax.ppermute(value, axis, [(i, i ^ step) for i in range(count)])]
    pallas_call x0 -> x19, Pallas kernels: none -> 110 us  [call(): pl.pallas_call(body, out_shape=tuple(outs), in_specs=in_specs or [whole]...]
    ppermute x0 -> x68, starting transfers between devices: none -> 108 us  [the longest x53 77.4 us: partner(): return lax.ppermute(value, axis, [(i, i ^ step) for i in range(count)])]
    dot_general x28 -> x0, matrix products: 86.4 us -> none  [the longest x7 28.9 us: outer_sum(): lax.dot_general(left_side, right_side, (((0,), (0,)), ((), ())), preferre...]
    psum x1 -> x0, blocking collectives: 80.3 us -> none  [local(): lax.psum((grad_gain_one, grad_w_query, grad_b_query, grad_w_key, grad_b_k...]
    reduce_scatter x1 -> x0, waiting for transfers between devices: 44.7 us -> none  [local(): lax.psum_scatter(grad_kv_whole.astype(jnp.bfloat16), 'blk', scatter_dimen...]
    another operation x10 -> x0, loops' own time: 31.6 us -> none  [the longest x1 15.7 us: sweep_keys(): state_out, unused = lax.scan(visit_block, state_now, (blocks, offsets))]
  transfers between devices with their start and end apart: 5 -> 68, of which waited for: 4 -> 20; matrix products, arithmetic and copies ran while one was open for 4% -> 23% of each run, Pallas kernels for 0% -> 15%
where the time goes in v1:
time: 567 us; the launch traced here: 559 us
  waiting for transfers between devices  171 us (30%)
  local copies, waits for them, and re-layouts  115 us (20%)
  Pallas kernels  110 us (19%)
  starting transfers between devices  108 us (19%)
  other arithmetic  41.7 us (7%)
  blocking collectives  11.6 us (2%)
    ppermute x53, waiting for transfers between devices, partner(): return lax.ppermute(value, axis, [(i, i ^ step) for i in range(count)])  142 us
    pallas_call x19, Pallas kernels, call(): pl.pallas_call(body, out_shape=tuple(outs), in_specs=in_specs or [whole]...  110 us
    ppermute x53, starting transfers between devices, partner(): return lax.ppermute(value, axis, [(i, i ^ step) for i in range(count)])  77.4 us
    unnamed x158, local copies, waits for them, and re-layouts  46.4 us
    ppermute x5, waiting for transfers between devices, line_sum(): lax.ppermute(total, 'dp', [(s, s + 1), (count - 1 - s, count - 2 - s)])  25.8 us
    ppermute x5, starting transfers between devices, line_sum(): lax.ppermute(total, 'dp', [(s, s + 1), (count - 1 - s, count - 2 - s)])  16.5 us
    convert_element_type x10, other arithmetic, line_sum(): total = (total.astype(wide) + passed.astype(wide)).astype(low)  15.6 us
    slice x6, local copies, waits for them, and re-layouts, gather_relayed(): second.append(whole[rows:])  13.6 us
  transfers between devices with their start and end apart: 68, of which 20 were waited for; matrix products, arithmetic and copies ran while one was open for 23% of the time, Pallas kernels for 15%

profile of v1, /device:TPU:0, one launch (start us, length us, event | category | flops | bytes accessed | tf_op | source)
XLA Modules:
  0.0 559.2 jit_solution(15156110291123774368)
XLA Ops:
  8.1 3.1 shard_map.254
  12.8 11.6 %all_gather.3.kv_ref = bf16[2048,128]{1,0:T(8,128)(2,1)S(1)} all-gather(bf16[512,128]{1,0:T(8,128)(2,1)S(1)} %get-tuple-element.51), channel_id=1, replica_groups=mesh['dp'=4,'blk'=4,'tensor'=2] {'blk'}, dimensions={0}, use_global_device_ids=true | all-gather | bytes 655360 | tf_op jit(solution)/shard_map/all_gather | solution.py:510
  26.3 6.5 %shard_map.255 = (f32[448,512]{1,0:T(8,128)S(1)}, f32[8,512]{1,0:T(8,128)S(1)}, f32[896,512]{1,0:T(8,128)}) custom-call(s32[1,3]{1,0:T(1,128)S(1)} %copy-done.42, s32[2]{0:T(128)S(1)} %pad_add_fusion.place_ref, bf16[448,512]{1,0:T(8,128)(2,1)S(1)} %get-tuple-element.50.q_ref, bf16[2048,128]{1,0:T(8,128)(2,1)S(1)} %all_gather.3.kv_ref, ...), custom_call_target="tpu_custom_call" | custom-call | flops 1879048192 | bytes 4554772 | tf_op jit(solution)/shard_map/pallas_call | solution.py:88
  34.5 5.0 collective-permute-start.4
  39.5 7.6 %collective-permute-start.5 = (bf16[256,896]{1,0:T(8,128)(2,1)S(1)}, bf16[256,896]{1,0:T(8,128)(2,1)S(1)}, u32[]{:S(2)}, u32[]{:S(2)}) collective-permute-start(bf16[256,896]{1,0:T(8,128)(2,1)S(1)} %dynamic-slice_multiply_fusion.gy_ref), channel_id=1, source_target_pairs={{0,4},{2,6},{4,0},{6,2},{1,5},{3,7},{5,1},{7,3},{8,12},{10,14},{12... | collective-permute-start | bytes 1376264 | tf_op jit(solution)/shard_map/ppermute | solution.py:36
  49.4 3.0 collective-permute-start.3
  54.7 23.4 %collective-permute-done.5 = bf16[256,896]{1,0:T(8,128)(2,1)S(1)} collective-permute-done((bf16[256,896]{1,0:T(8,128)(2,1)S(1)}, bf16[256,896]{1,0:T(8,128)(2,1)S(1)}, u32[]{:S(2)}, u32[]{:S(2)}) %collective-permute-start.5) | collective-permute-done | bytes 458784 | tf_op jit(solution)/shard_map/ppermute | solution.py:36
  79.7 7.8 %collective-permute-done.2 = bf16[896,256]{1,0:T(8,128)(2,1)S(1)} collective-permute-done((bf16[896,256]{1,0:T(8,128)(2,1)S(1)}, bf16[896,256]{1,0:T(8,128)(2,1)S(1)}, u32[]{:S(2)}, u32[]{:S(2)}) %collective-permute-start.2) | collective-permute-done | bytes 458784 | tf_op jit(solution)/shard_map/ppermute | solution.py:36
  88.9 3.9 constant_dynamic-slice_fusion.3
  97.5 13.6 %shard_map.259 = (bf16[4,608,256]{2,1,0:T(8,128)(2,1)}, bf16[4,608,256]{2,1,0:T(8,128)(2,1)}, bf16[4,608,256]{2,1,0:T(8,128)(2,1)}, bf16[4,896,256]{2,1,0:T(8,128)(2,1)}) custom-call(bf16[4,896,256]{2,1,0:T(8,128)(2,1)} %collective-permute-done.7.x_ref.refs_2_, bf16[1024,896]{1,0:T(8,128)(2,1)} %collective-permute-done.8.gy_ref.refs_3_, ...), custom_call_target="tpu_custom_call" | custom-call | flops 5578424320 | bytes 14688256 | tf_op jit(solution)/shard_map/pallas_call | solution.py:88
  111.7 13.3 %shard_map.257 = (bf16[4,608,256]{2,1,0:T(8,128)(2,1)}, bf16[4,608,256]{2,1,0:T(8,128)(2,1)}, bf16[4,608,256]{2,1,0:T(8,128)(2,1)}, bf16[4,896,256]{2,1,0:T(8,128)(2,1)}) custom-call(bf16[4,896,256]{2,1,0:T(8,128)(2,1)} %pad_maximum_fusion.x_ref.refs_0_, bf16[1024,896]{1,0:T(8,128)(2,1)} %constant_dynamic-update-slice_fusion.gy_ref.refs_1_, ...), custom_call_target="tpu_custom_call" | custom-call | flops 5578424320 | bytes 14688256 | tf_op jit(solution)/shard_map/pallas_call | solution.py:88
  126.3 5.8 %shard_map.269 = bf16[896,608]{1,0:T(8,128)(2,1)S(1)} custom-call(bf16[4,896,256]{2,1,0:T(8,128)(2,1)} %pad_maximum_fusion.x_ref.refs_0_, bf16[4,608,256]{2,1,0:T(8,128)(2,1)S(1)} %copy-done.51, bf16[4,896,256]{2,1,0:T(8,128)(2,1)} %collective-permute-done.7.x_ref.refs_2_, bf16[4,608,256]{2,1,0:T(8,128)(2,1)S(1)} %copy-done.50), custom_call_target="tpu_custom_call" | custom-call | flops 2231369728 | bytes 7249920 | tf_op jit(solution)/shard_map/pallas_call | solution.py:88
  133.8 4.5 collective-permute-start.54
  140.9 5.8 %shard_map.267 = bf16[896,608]{1,0:T(8,128)(2,1)S(1)} custom-call(bf16[4,896,256]{2,1,0:T(8,128)(2,1)} %pad_maximum_fusion.x_ref.refs_0_, bf16[4,608,256]{2,1,0:T(8,128)(2,1)S(1)} %copy-done.49, bf16[4,896,256]{2,1,0:T(8,128)(2,1)} %collective-permute-done.7.x_ref.refs_2_, bf16[4,608,256]{2,1,0:T(8,128)(2,1)S(1)} %copy-done.48), custom_call_target="tpu_custom_call" | custom-call | flops 2231369728 | bytes 7249920 | tf_op jit(solution)/shard_map/pallas_call | solution.py:88
  148.4 2.4 collective-permute-start.47
  154.2 3.1 shard_map.260
  157.3 6.5 %shard_map.271 = bf16[608,896]{1,0:T(8,128)(2,1)} custom-call(bf16[4,608,256]{2,1,0:T(8,128)(2,1)S(1)} %copy-done.22, bf16[1024,896]{1,0:T(8,128)(2,1)} %constant_dynamic-update-slice_fusion.gy_ref.refs_1_, bf16[4,608,256]{2,1,0:T(8,128)(2,1)S(1)} %copy-done.24, bf16[1024,896]{1,0:T(8,128)(2,1)} %collective-permute-done.8.gy_ref.refs_3_), custom_call_target="tpu_custom_call" | custom-call | flops 2231369728 | bytes 7249920 | tf_op jit(solution)/shard_map/pallas_call | solution.py:88
  168.3 3.1 shard_map.258
  171.4 2.4 copy.92
  178.8 6.6 %collective-permute-done.47 = bf16[896,608]{0,1:T(8,128)(2,1)} collective-permute-done((bf16[896,608]{0,1:T(8,128)(2,1)}, bf16[896,608]{0,1:T(8,128)(2,1)}, u32[]{:S(2)}, u32[]{:S(2)}) %collective-permute-start.47) | collective-permute-done | bytes 1089568 | tf_op jit(solution)/shard_map/ppermute | solution.py:71
  185.3 2.4 copy.80
  187.7 2.5 add_convert_fusion
  193.1 14.8 %collective-permute-done.61 = bf16[608,896]{1,0:T(8,128)(2,1)} collective-permute-done((bf16[608,896]{1,0:T(8,128)(2,1)}, bf16[608,896]{1,0:T(8,128)(2,1)}, u32[]{:S(2)}, u32[]{:S(2)}) %collective-permute-start.61) | collective-permute-done | bytes 1089568 | tf_op jit(solution)/shard_map/ppermute | solution.py:71
  209.4 2.3 copy.81
  211.7 2.9 add_convert_fusion.7
  219.7 3.2 shard_map.262
  228.0 2.4 copy.94
  233.8 8.9 %shard_map.263 = (bf16[448,896]{1,0:T(8,128)(2,1)S(1)}, bf16[448,512]{1,0:T(8,128)(2,1)S(1)}, bf16[4,512,128]{2,1,0:T(8,128)(2,1)S(1)}) custom-call(s32[1,3]{1,0:T(1,128)S(1)} %copy-done.42, s32[2]{0:T(128)S(1)} %pad_add_fusion.place_ref, bf16[896,256]{1,0:T(8,128)(2,1)} %get-tuple-element.62.gm_mine_ref, bf16[896,256]{1,0:T(8,128)(2,1)S(1)} %copy-done.47, ...), custom_call_target="tpu_custom_call" | custom-call | flops 4697620480 | bytes 5554196 | tf_op jit(solution)/shard_map/pallas_call | solution.py:88
  244.5 17.9 %collective-permute-start.21 = (bf16[512,128]{1,0:T(8,128)(2,1)}, bf16[512,128]{1,0:T(8,128)(2,1)S(1)}, u32[]{:S(2)}, u32[]{:S(2)}) collective-permute-start(bf16[512,128]{1,0:T(8,128)(2,1)} %get-tuple-element.154), channel_id=1, source_target_pairs={{0,6},{2,4},{4,2},{6,0},{1,7},{3,5},{5,3},{7,1},{8,14},{10,12},{12... | collective-permute-start | bytes 393224 | tf_op jit(solution)/shard_map/ppermute | solution.py:36
  264.3 2.3 copy.95
  266.7 2.5 copy.82
  272.2 2.4 shard_map.264
  274.6 4.1 shard_map.265
  281.3 2.9 add_convert_fusion.4
  284.2 2.3 copy.83
  289.7 2.8 add_convert_fusion.6
  298.5 6.8 %collective-permute-start.27 = (f32[2368]{0:T(1024)S(1)}, f32[2368]{0:T(1024)S(1)}, u32[]{:S(2)}, u32[]{:S(2)}) collective-permute-start(f32[2368]{0:T(1024)S(1)} %add.145), channel_id=1, source_target_pairs={{0,8},{8,0},{16,24},{24,16},{1,9},{9,1},{17,25},{25,17},{2,10},{10... | collective-permute-start | bytes 28424 | tf_op jit(solution)/shard_map/ppermute | solution.py:36
  307.6 14.8 %collective-permute-done.27 = f32[2368]{0:T(1024)S(1)} collective-permute-done((f32[2368]{0:T(1024)S(1)}, f32[2368]{0:T(1024)S(1)}, u32[]{:S(2)}, u32[]{:S(2)}) %collective-permute-start.27) | collective-permute-done | bytes 9504 | tf_op jit(solution)/shard_map/ppermute | solution.py:36
  323.1 3.9 collective-permute-done.28
  331.1 6.6 %collective-permute-done.39 = bf16[112,896]{1,0:T(8,128)(2,1)S(1)} collective-permute-done((bf16[112,896]{1,0:T(8,128)(2,1)S(1)}, bf16[112,896]{1,0:T(8,128)(2,1)S(1)}, u32[]{:S(2)}, u32[]{:S(2)}) %collective-permute-start.39) | collective-permute-done | bytes 200736 | tf_op jit(solution)/shard_map/ppermute | solution.py:36
  341.6 3.6 collective-permute-done.31
  347.6 4.4 collective-permute-done.41
  352.0 5.1 collective-permute-start.32
  359.3 2.4 copy.96
  364.8 2.5 copy.84
  367.2 2.4 broadcast_select_fusion.1
  369.6 2.3 copy.85
  373.3 2.4 broadcast_select_fusion.2
  388.7 5.2 collective-permute-done.46
  394.5 13.3 %collective-permute-done.45 = bf16[112,896]{1,0:T(8,128)(2,1)S(1)} collective-permute-done((bf16[112,896]{1,0:T(8,128)(2,1)S(1)}, bf16[112,896]{1,0:T(8,128)(2,1)S(1)}, u32[]{:S(2)}, u32[]{:S(2)}) %collective-permute-start.45) | collective-permute-done | bytes 200736 | tf_op jit(solution)/shard_map/ppermute | solution.py:36
  414.1 2.5 collective-permute-done.34
  421.0 10.3 %collective-permute-done.58 = bf16[896,608]{0,1:T(8,128)(2,1)} collective-permute-done((bf16[896,608]{0,1:T(8,128)(2,1)}, bf16[896,608]{0,1:T(8,128)(2,1)}, u32[]{:S(2)}, u32[]{:S(2)}) %collective-permute-start.58) | collective-permute-done | bytes 1089568 | tf_op jit(solution)/shard_map/ppermute | solution.py:36
  432.9 2.7 fusion.10
  435.7 2.6 fusion.11
  438.3 20.1 %collective-permute-done.50 = bf16[896,608]{0,1:T(8,128)(2,1)} collective-permute-done((bf16[896,608]{0,1:T(8,128)(2,1)}, bf16[896,608]{0,1:T(8,128)(2,1)}, u32[]{:S(2)}, u32[]{:S(2)}) %collective-permute-start.50) | collective-permute-done | bytes 1089568 | tf_op jit(solution)/shard_map/ppermute | solution.py:36
  458.8 2.6 fusion.13
  468.7 2.3 fusion.7
  471.0 10.7 %collective-permute-done.64 = bf16[608,896]{1,0:T(8,128)(2,1)} collective-permute-done((bf16[608,896]{1,0:T(8,128)(2,1)}, bf16[608,896]{1,0:T(8,128)(2,1)}, u32[]{:S(2)}, u32[]{:S(2)}) %collective-permute-start.64) | collective-permute-done | bytes 1089568 | tf_op jit(solution)/shard_map/ppermute | solution.py:36
  484.4 3.3 collective-permute-done.37
  489.8 16.4 %collective-permute-done.35 = bf16[224,576]{1,0:T(8,128)(2,1)S(1)} collective-permute-done((bf16[224,576]{1,0:T(8,128)(2,1)}, bf16[224,576]{1,0:T(8,128)(2,1)S(1)}, u32[]{:S(2)}, u32[]{:S(2)}) %collective-permute-start.35) | collective-permute-done | bytes 258080 | tf_op jit(solution)/shard_map/ppermute | solution.py:36
  518.3 2.6 copy.103
  531.7 10.8 %shard_map.268 = f32[896,2432]{1,0:T(8,128)} custom-call(s32[2]{0:T(128)S(1)} %pad_add_fusion.place_ref, bf16[448,608]{1,0:T(8,128)(2,1)S(1)} %get-tuple-element.123.refs_0_, bf16[448,608]{1,0:T(8,128)(2,1)} %copy.107.refs_1_, bf16[448,608]{1,0:T(8,128)(2,1)S(1)} %copy-done.10, bf16[448,608]{1,0:T(8,128)(2,1)} %collective-permute-done.52.refs_3_, ...), custom_call_target="tpu_custom_call" | custom-call | bytes 13074440 | tf_op jit(solution)/shard_map/pallas_call | solution.py:88
  542.6 10.8 %shard_map.270 = f32[896,2432]{1,0:T(8,128)} custom-call(s32[2]{0:T(128)S(1)} %pad_add_fusion.place_ref, bf16[448,608]{1,0:T(8,128)(2,1)S(1)} %get-tuple-element.121.refs_0_, bf16[448,608]{1,0:T(8,128)(2,1)} %copy.111.refs_1_, bf16[448,608]{1,0:T(8,128)(2,1)S(1)} %copy-done.8, bf16[448,608]{1,0:T(8,128)(2,1)} %collective-permute-done.59.refs_3_, ...), custom_call_target="tpu_custom_call" | custom-call | bytes 13074440 | tf_op jit(solution)/shard_map/pallas_call | solution.py:88
  553.4 5.3 shard_map.272
  (337 shorter events, 163.0 us)
Async XLA Ops:
  34.4 12.9 %collective-permute-start = (bf16[896,256]{1,0:T(8,128)(2,1)S(1)}, bf16[896,256]{1,0:T(8,128)(2,1)S(1)}, u32[]{:S(2)}, u32[]{:S(2)}) collective-permute-start(bf16[896,256]{1,0:T(8,128)(2,1)S(1)} %dynamic-slice_convert_fusion), channel_id=1, source_target_pairs={{0,1},{1,0},{2,3},{3,2},{4,5},{5,4},{6,7},{7,6},{8,9},{9,8},{10,11... | collective-permute-start | bytes 1376264 | tf_op jit(solution)/shard_map/ppermute | solution.py:36
  34.5 18.0 %collective-permute-start.4 = (bf16[256,896]{1,0:T(8,128)(2,1)S(1)}, bf16[256,896]{1,0:T(8,128)(2,1)S(1)}, u32[]{:S(2)}, u32[]{:S(2)}) collective-permute-start(bf16[256,896]{1,0:T(8,128)(2,1)S(1)} %dynamic-slice_multiply_fusion.gy_ref), channel_id=1, source_target_pairs={{0,2},{2,0},{4,6},{6,4},{1,3},{3,1},{5,7},{7,5},{8,10},{10,8},{12,... | collective-permute-start | bytes 1376264 | tf_op jit(solution)/shard_map/ppermute | solution.py:36
  39.5 38.5 %collective-permute-start.5 = (bf16[256,896]{1,0:T(8,128)(2,1)S(1)}, bf16[256,896]{1,0:T(8,128)(2,1)S(1)}, u32[]{:S(2)}, u32[]{:S(2)}) collective-permute-start(bf16[256,896]{1,0:T(8,128)(2,1)S(1)} %dynamic-slice_multiply_fusion.gy_ref), channel_id=1, source_target_pairs={{0,4},{2,6},{4,0},{6,2},{1,5},{3,7},{5,1},{7,3},{8,12},{10,14},{12... | collective-permute-start | bytes 1376264 | tf_op jit(solution)/shard_map/ppermute | solution.py:36
  47.1 31.8 %collective-permute-start.6 = (bf16[256,896]{1,0:T(8,128)(2,1)S(1)}, bf16[256,896]{1,0:T(8,128)(2,1)S(1)}, u32[]{:S(2)}, u32[]{:S(2)}) collective-permute-start(bf16[256,896]{1,0:T(8,128)(2,1)S(1)} %dynamic-slice_multiply_fusion.gy_ref), channel_id=1, source_target_pairs={{0,6},{2,4},{4,2},{6,0},{1,7},{3,5},{5,3},{7,1},{8,14},{10,12},{12... | collective-permute-start | bytes 1376264 | tf_op jit(solution)/shard_map/ppermute | solution.py:36
  49.4 30.2 %collective-permute-start.3 = (bf16[896,256]{1,0:T(8,128)(2,1)S(1)}, bf16[896,256]{1,0:T(8,128)(2,1)S(1)}, u32[]{:S(2)}, u32[]{:S(2)}) collective-permute-start(bf16[896,256]{1,0:T(8,128)(2,1)S(1)} %get-tuple-element.55), channel_id=1, source_target_pairs={{0,6},{2,4},{4,2},{6,0},{1,7},{3,5},{5,3},{7,1},{8,14},{10,12},{12... | collective-permute-start | bytes 1376264 | tf_op jit(solution)/shard_map/ppermute | solution.py:36
  52.4 35.0 %collective-permute-start.2 = (bf16[896,256]{1,0:T(8,128)(2,1)S(1)}, bf16[896,256]{1,0:T(8,128)(2,1)S(1)}, u32[]{:S(2)}, u32[]{:S(2)}) collective-permute-start(bf16[896,256]{1,0:T(8,128)(2,1)S(1)} %get-tuple-element.55), channel_id=1, source_target_pairs={{0,4},{2,6},{4,0},{6,2},{1,5},{3,7},{5,1},{7,3},{8,12},{10,14},{12... | collective-permute-start | bytes 1376264 | tf_op jit(solution)/shard_map/ppermute | solution.py:36
  52.4 35.0 %collective-permute-start.1 = (bf16[896,256]{1,0:T(8,128)(2,1)S(1)}, bf16[896,256]{1,0:T(8,128)(2,1)S(1)}, u32[]{:S(2)}, u32[]{:S(2)}) collective-permute-start(bf16[896,256]{1,0:T(8,128)(2,1)S(1)} %get-tuple-element.55), channel_id=1, source_target_pairs={{0,2},{2,0},{4,6},{6,4},{1,3},{3,1},{5,7},{7,5},{8,10},{10,8},{12,... | collective-permute-start | bytes 1376264 | tf_op jit(solution)/shard_map/ppermute | solution.py:36
  79.7 17.8 %collective-permute-start.8 = (bf16[1024,896]{1,0:T(8,128)(2,1)}, bf16[1024,896]{1,0:T(8,128)(2,1)}, u32[]{:S(2)}, u32[]{:S(2)}) collective-permute-start(bf16[1024,896]{1,0:T(8,128)(2,1)} %constant_dynamic-update-slice_fusion.gy_ref.refs_1_), channel_id=1, source_target_pairs={{0,1},{1,0},{2,3},{3,2},{4,5},{5,4},{6,7},{7,6},{8,9},{9,8},{10,11... | collective-permute-start | bytes 5505032 | tf_op jit(solution)/shard_map/ppermute | solution.py:36
  88.9 8.6 %collective-permute-start.7 = (bf16[4,896,256]{2,1,0:T(8,128)(2,1)}, bf16[4,896,256]{2,1,0:T(8,128)(2,1)}, u32[]{:S(2)}, u32[]{:S(2)}) collective-permute-start(bf16[4,896,256]{2,1,0:T(8,128)(2,1)} %pad_maximum_fusion.x_ref.refs_0_), channel_id=1, source_target_pairs={{0,1},{1,0},{2,3},{3,2},{4,5},{5,4},{6,7},{7,6},{8,9},{9,8},{10,11... | collective-permute-start | bytes 5505032 | tf_op jit(solution)/shard_map/ppermute | solution.py:36
  111.1 76.6 %collective-permute-start.14 = (bf16[4,896,256]{2,1,0:T(8,128)(2,1)}, bf16[4,896,256]{2,1,0:T(8,128)(2,1)}, u32[]{:S(2)}, u32[]{:S(2)}) collective-permute-start(bf16[4,896,256]{2,1,0:T(8,128)(2,1)} %get-tuple-element.61), channel_id=1, source_target_pairs={{0,1},{1,0},{2,3},{3,2},{4,5},{5,4},{6,7},{7,6},{8,9},{9,8},{10,11... | collective-permute-start | bytes 5505032 | tf_op jit(solution)/shard_map/ppermute | solution.py:36
  133.8 37.6 %collective-permute-start.54 = (bf16[896,608]{0,1:T(8,128)(2,1)}, bf16[896,608]{0,1:T(8,128)(2,1)}, u32[]{:S(2)}, u32[]{:S(2)}) collective-permute-start(bf16[896,608]{0,1:T(8,128)(2,1)} %copy.91), channel_id=1, source_target_pairs={{0,8},{24,16},{1,9},{25,17},{2,10},{26,18},{3,11},{27,19},{4,12},{... | collective-permute-start | bytes 3268616 | tf_op jit(solution)/shard_map/ppermute | solution.py:71
  148.4 37.0 %collective-permute-start.47 = (bf16[896,608]{0,1:T(8,128)(2,1)}, bf16[896,608]{0,1:T(8,128)(2,1)}, u32[]{:S(2)}, u32[]{:S(2)}) collective-permute-start(bf16[896,608]{0,1:T(8,128)(2,1)} %copy.79), channel_id=1, source_target_pairs={{0,8},{24,16},{1,9},{25,17},{2,10},{26,18},{3,11},{27,19},{4,12},{... | collective-permute-start | bytes 3268616 | tf_op jit(solution)/shard_map/ppermute | solution.py:71
  157.3 65.6 %collective-permute-start.9 = (bf16[4,896,256]{2,1,0:T(8,128)(2,1)}, bf16[4,896,256]{2,1,0:T(8,128)(2,1)}, u32[]{:S(2)}, u32[]{:S(2)}) collective-permute-start(bf16[4,896,256]{2,1,0:T(8,128)(2,1)} %shard_map.260), channel_id=1, source_target_pairs={{0,1},{1,0},{2,3},{3,2},{4,5},{5,4},{6,7},{7,6},{8,9},{9,8},{10,11... | collective-permute-start | bytes 5505032 | tf_op jit(solution)/shard_map/ppermute | solution.py:36
  163.8 44.0 %collective-permute-start.61 = (bf16[608,896]{1,0:T(8,128)(2,1)}, bf16[608,896]{1,0:T(8,128)(2,1)}, u32[]{:S(2)}, u32[]{:S(2)}) collective-permute-start(bf16[608,896]{1,0:T(8,128)(2,1)} %shard_map.271), channel_id=1, source_target_pairs={{0,8},{24,16},{1,9},{25,17},{2,10},{26,18},{3,11},{27,19},{4,12},{... | collective-permute-start | bytes 3268616 | tf_op jit(solution)/shard_map/ppermute | solution.py:71
  177.1 50.5 %collective-permute-start.55 = (bf16[896,608]{0,1:T(8,128)(2,1)}, bf16[896,608]{0,1:T(8,128)(2,1)}, u32[]{:S(2)}, u32[]{:S(2)}) collective-permute-start(bf16[896,608]{0,1:T(8,128)(2,1)} %copy.93), channel_id=1, source_target_pairs={{8,16},{16,8},{9,17},{17,9},{10,18},{18,10},{11,19},{19,11},{12,20... | collective-permute-start | bytes 3268616 | tf_op jit(solution)/shard_map/ppermute | solution.py:73
  191.3 23.3 %collective-permute-start.17 = (bf16[896,256]{1,0:T(8,128)(2,1)}, bf16[896,256]{1,0:T(8,128)(2,1)S(1)}, u32[]{:S(2)}, u32[]{:S(2)}) collective-permute-start(bf16[896,256]{1,0:T(8,128)(2,1)} %get-tuple-element.112), channel_id=1, source_target_pairs={{0,6},{2,4},{4,2},{6,0},{1,7},{3,5},{5,3},{7,1},{8,14},{10,12},{12... | collective-permute-start | bytes 1376264 | tf_op jit(solution)/shard_map/ppermute | solution.py:36
  192.7 23.6 %collective-permute-start.16 = (bf16[896,256]{1,0:T(8,128)(2,1)}, bf16[896,256]{1,0:T(8,128)(2,1)S(1)}, u32[]{:S(2)}, u32[]{:S(2)}) collective-permute-start(bf16[896,256]{1,0:T(8,128)(2,1)} %get-tuple-element.113), channel_id=1, source_target_pairs={{0,4},{2,6},{4,0},{6,2},{1,5},{3,7},{5,1},{7,3},{8,12},{10,14},{12... | collective-permute-start | bytes 1376264 | tf_op jit(solution)/shard_map/ppermute | solution.py:36
  207.8 11.9 %collective-permute-start.15 = (bf16[896,256]{1,0:T(8,128)(2,1)}, bf16[896,256]{1,0:T(8,128)(2,1)S(1)}, u32[]{:S(2)}, u32[]{:S(2)}) collective-permute-start(bf16[896,256]{1,0:T(8,128)(2,1)} %get-tuple-element.114), channel_id=1, source_target_pairs={{0,2},{2,0},{4,6},{6,4},{1,3},{3,1},{5,7},{7,5},{8,10},{10,8},{12,... | collective-permute-start | bytes 1376264 | tf_op jit(solution)/shard_map/ppermute | solution.py:36
  214.6 29.9 %collective-permute-start.48 = (bf16[896,608]{0,1:T(8,128)(2,1)}, bf16[896,608]{0,1:T(8,128)(2,1)}, u32[]{:S(2)}, u32[]{:S(2)}) collective-permute-start(bf16[896,608]{0,1:T(8,128)(2,1)} %copy.81), channel_id=1, source_target_pairs={{8,16},{16,8},{9,17},{17,9},{10,18},{18,10},{11,19},{19,11},{12,20... | collective-permute-start | bytes 3268616 | tf_op jit(solution)/shard_map/ppermute | solution.py:73
  216.3 73.4 %collective-permute-start.62 = (bf16[608,896]{1,0:T(8,128)(2,1)}, bf16[608,896]{1,0:T(8,128)(2,1)}, u32[]{:S(2)}, u32[]{:S(2)}) collective-permute-start(bf16[608,896]{1,0:T(8,128)(2,1)} %add_convert_fusion.7), channel_id=1, source_target_pairs={{8,16},{16,8},{9,17},{17,9},{10,18},{18,10},{11,19},{19,11},{12,20... | collective-permute-start | bytes 3268616 | tf_op jit(solution)/shard_map/ppermute | solution.py:73
  222.9 7.4 %collective-permute-start.18 = (bf16[896,256]{1,0:T(8,128)(2,1)}, bf16[896,256]{1,0:T(8,128)(2,1)S(1)}, u32[]{:S(2)}, u32[]{:S(2)}) collective-permute-start(bf16[896,256]{1,0:T(8,128)(2,1)} %get-tuple-element.62.gm_mine_ref), channel_id=1, source_target_pairs={{0,1},{1,0},{2,3},{3,2},{4,5},{5,4},{6,7},{7,6},{8,9},{9,8},{10,11... | collective-permute-start | bytes 1376264 | tf_op jit(solution)/shard_map/ppermute | solution.py:36
  226.2 36.2 %collective-permute-start.12 = (bf16[896,256]{1,0:T(8,128)(2,1)}, bf16[896,256]{1,0:T(8,128)(2,1)S(1)}, u32[]{:S(2)}, u32[]{:S(2)}) collective-permute-start(bf16[896,256]{1,0:T(8,128)(2,1)} %get-tuple-element.116), channel_id=1, source_target_pairs={{0,6},{2,4},{4,2},{6,0},{1,7},{3,5},{5,3},{7,1},{8,14},{10,12},{12... | collective-permute-start | bytes 1376264 | tf_op jit(solution)/shard_map/ppermute | solution.py:36
  227.6 34.8 %collective-permute-start.11 = (bf16[896,256]{1,0:T(8,128)(2,1)}, bf16[896,256]{1,0:T(8,128)(2,1)S(1)}, u32[]{:S(2)}, u32[]{:S(2)}) collective-permute-start(bf16[896,256]{1,0:T(8,128)(2,1)} %get-tuple-element.117), channel_id=1, source_target_pairs={{0,4},{2,6},{4,0},{6,2},{1,5},{3,7},{5,1},{7,3},{8,12},{10,14},{12... | collective-permute-start | bytes 1376264 | tf_op jit(solution)/shard_map/ppermute | solution.py:36
  231.1 38.2 %collective-permute-start.10 = (bf16[896,256]{1,0:T(8,128)(2,1)}, bf16[896,256]{1,0:T(8,128)(2,1)S(1)}, u32[]{:S(2)}, u32[]{:S(2)}) collective-permute-start(bf16[896,256]{1,0:T(8,128)(2,1)} %get-tuple-element.118), channel_id=1, source_target_pairs={{0,2},{2,0},{4,6},{6,4},{1,3},{3,1},{5,7},{7,5},{8,10},{10,8},{12,... | collective-permute-start | bytes 1376264 | tf_op jit(solution)/shard_map/ppermute | solution.py:36
  244.5 30.1 %collective-permute-start.21 = (bf16[512,128]{1,0:T(8,128)(2,1)}, bf16[512,128]{1,0:T(8,128)(2,1)S(1)}, u32[]{:S(2)}, u32[]{:S(2)}) collective-permute-start(bf16[512,128]{1,0:T(8,128)(2,1)} %get-tuple-element.154), channel_id=1, source_target_pairs={{0,6},{2,4},{4,2},{6,0},{1,7},{3,5},{5,3},{7,1},{8,14},{10,12},{12... | collective-permute-start | bytes 393224 | tf_op jit(solution)/shard_map/ppermute | solution.py:36
  262.4 12.2 %collective-permute-start.20 = (bf16[512,128]{1,0:T(8,128)(2,1)}, bf16[512,128]{1,0:T(8,128)(2,1)}, u32[]{:S(2)}, u32[]{:S(2)}) collective-permute-start(bf16[512,128]{1,0:T(8,128)(2,1)} %get-tuple-element.155), channel_id=1, source_target_pairs={{0,4},{2,6},{4,0},{6,2},{1,5},{3,7},{5,1},{7,3},{8,12},{10,14},{12... | collective-permute-start | bytes 393224 | tf_op jit(solution)/shard_map/ppermute | solution.py:36
  262.4 12.2 %collective-permute-start.19 = (bf16[512,128]{1,0:T(8,128)(2,1)}, bf16[512,128]{1,0:T(8,128)(2,1)}, u32[]{:S(2)}, u32[]{:S(2)}) collective-permute-start(bf16[512,128]{1,0:T(8,128)(2,1)} %get-tuple-element.156), channel_id=1, source_target_pairs={{0,2},{2,0},{4,6},{6,4},{1,3},{3,1},{5,7},{7,5},{8,10},{10,8},{12,... | collective-permute-start | bytes 393224 | tf_op jit(solution)/shard_map/ppermute | solution.py:36
  269.3 88.5 %collective-permute-start.56 = (bf16[896,608]{0,1:T(8,128)(2,1)}, bf16[896,608]{0,1:T(8,128)(2,1)}, u32[]{:S(2)}, u32[]{:S(2)}) collective-permute-start(bf16[896,608]{0,1:T(8,128)(2,1)} %copy.95), channel_id=1, source_target_pairs={{8,0},{16,24},{9,1},{17,25},{10,2},{18,26},{11,3},{19,27},{12,4},{... | collective-permute-start | bytes 3268616 | tf_op jit(solution)/shard_map/ppermute | solution.py:76
  274.6 23.9 %collective-permute-start.13 = (bf16[256,896]{1,0:T(8,128)(2,1)S(1)}, bf16[256,896]{1,0:T(8,128)(2,1)}, u32[]{:S(2)}, u32[]{:S(2)}) collective-permute-start(bf16[256,896]{1,0:T(8,128)(2,1)S(1)} %shard_map.261), channel_id=1, source_target_pairs={{0,1},{1,0},{2,3},{3,2},{4,5},{5,4},{6,7},{7,6},{8,9},{9,8},{10,11... | collective-permute-start | bytes 1376264 | tf_op jit(solution)/shard_map/ppermute | solution.py:36
  280.8 7.3 %collective-permute-start.24 = (f32[1792]{0:T(1024)S(1)}, f32[1792]{0:T(1024)S(1)}, u32[]{:S(2)}, u32[]{:S(2)}) collective-permute-start(f32[1792]{0:T(1024)S(1)} %maximum_reduce_fusion), channel_id=1, source_target_pairs={{0,1},{1,0},{2,3},{3,2},{4,5},{5,4},{6,7},{7,6},{8,9},{9,8},{10,11... | collective-permute-start | bytes 21512 | tf_op jit(solution)/shard_map/ppermute | solution.py:36
  286.5 78.2 %collective-permute-start.49 = (bf16[896,608]{0,1:T(8,128)(2,1)}, bf16[896,608]{0,1:T(8,128)(2,1)}, u32[]{:S(2)}, u32[]{:S(2)}) collective-permute-start(bf16[896,608]{0,1:T(8,128)(2,1)} %copy.83), channel_id=1, source_target_pairs={{8,0},{16,24},{9,1},{17,25},{10,2},{18,26},{11,3},{19,27},{12,4},{... | collective-permute-start | bytes 3268616 | tf_op jit(solution)/shard_map/ppermute | solution.py:76
  294.6 34.4 %collective-permute-start.38 = (bf16[112,896]{1,0:T(8,128)(2,1)S(1)}, bf16[112,896]{1,0:T(8,128)(2,1)S(1)}, u32[]{:S(2)}, u32[]{:S(2)}) collective-permute-start(bf16[112,896]{1,0:T(8,128)(2,1)S(1)} %get-tuple-element.151), channel_id=1, source_target_pairs={{0,2},{2,0},{4,6},{6,4},{1,3},{3,1},{5,7},{7,5},{8,10},{10,8},{12,... | collective-permute-start | bytes 602120 | tf_op jit(solution)/shard_map/ppermute | solution.py:36
  296.2 34.5 %collective-permute-start.40 = (bf16[112,896]{1,0:T(8,128)(2,1)S(1)}, bf16[112,896]{1,0:T(8,128)(2,1)S(1)}, u32[]{:S(2)}, u32[]{:S(2)}) collective-permute-start(bf16[112,896]{1,0:T(8,128)(2,1)S(1)} %get-tuple-element.152), channel_id=1, source_target_pairs={{0,6},{2,4},{4,2},{6,0},{1,7},{3,5},{5,3},{7,1},{8,14},{10,12},{12... | collective-permute-start | bytes 602120 | tf_op jit(solution)/shard_map/ppermute | solution.py:36
  298.5 23.9 %collective-permute-start.27 = (f32[2368]{0:T(1024)S(1)}, f32[2368]{0:T(1024)S(1)}, u32[]{:S(2)}, u32[]{:S(2)}) collective-permute-start(f32[2368]{0:T(1024)S(1)} %add.145), channel_id=1, source_target_pairs={{0,8},{8,0},{16,24},{24,16},{1,9},{9,1},{17,25},{25,17},{2,10},{10... | collective-permute-start | bytes 28424 | tf_op jit(solution)/shard_map/ppermute | solution.py:36
  327.0 10.7 %collective-permute-start.39 = (bf16[112,896]{1,0:T(8,128)(2,1)S(1)}, bf16[112,896]{1,0:T(8,128)(2,1)S(1)}, u32[]{:S(2)}, u32[]{:S(2)}) collective-permute-start(bf16[112,896]{1,0:T(8,128)(2,1)S(1)} %get-tuple-element.153), channel_id=1, source_target_pairs={{0,4},{2,6},{4,0},{6,2},{1,5},{3,7},{5,1},{7,3},{8,12},{10,14},{12... | collective-permute-start | bytes 602120 | tf_op jit(solution)/shard_map/ppermute | solution.py:36
  329.0 11.2 %collective-permute-start.29 = (bf16[224,576]{1,0:T(8,128)(2,1)S(1)}, bf16[224,576]{1,0:T(8,128)(2,1)S(1)}, u32[]{:S(2)}, u32[]{:S(2)}) collective-permute-start(bf16[224,576]{1,0:T(8,128)(2,1)S(1)} %get-tuple-element.130), channel_id=1, source_target_pairs={{0,2},{2,0},{4,6},{6,4},{1,3},{3,1},{5,7},{7,5},{8,10},{10,8},{12,... | collective-permute-start | bytes 774152 | tf_op jit(solution)/shard_map/ppermute | solution.py:36
  330.7 10.8 %collective-permute-start.30 = (bf16[224,576]{1,0:T(8,128)(2,1)S(1)}, bf16[224,576]{1,0:T(8,128)(2,1)S(1)}, u32[]{:S(2)}, u32[]{:S(2)}) collective-permute-start(bf16[224,576]{1,0:T(8,128)(2,1)S(1)} %get-tuple-element.131), channel_id=1, source_target_pairs={{0,4},{2,6},{4,0},{6,2},{1,5},{3,7},{5,1},{7,3},{8,12},{10,14},{12... | collective-permute-start | bytes 774152 | tf_op jit(solution)/shard_map/ppermute | solution.py:36
  337.7 7.5 %collective-permute-start.31 = (bf16[224,576]{1,0:T(8,128)(2,1)S(1)}, bf16[224,576]{1,0:T(8,128)(2,1)S(1)}, u32[]{:S(2)}, u32[]{:S(2)}) collective-permute-start(bf16[224,576]{1,0:T(8,128)(2,1)S(1)} %get-tuple-element.132), channel_id=1, source_target_pairs={{0,6},{2,4},{4,2},{6,0},{1,7},{3,5},{5,3},{7,1},{8,14},{10,12},{12... | collective-permute-start | bytes 774152 | tf_op jit(solution)/shard_map/ppermute | solution.py:36
  340.2 33.1 %collective-permute-start.63 = (bf16[608,896]{1,0:T(8,128)(2,1)}, bf16[608,896]{1,0:T(8,128)(2,1)}, u32[]{:S(2)}, u32[]{:S(2)}) collective-permute-start(bf16[608,896]{1,0:T(8,128)(2,1)} %add_convert_fusion.6), channel_id=1, source_target_pairs={{8,0},{16,24},{9,1},{17,25},{10,2},{18,26},{11,3},{19,27},{12,4},{... | collective-permute-start | bytes 3268616 | tf_op jit(solution)/shard_map/ppermute | solution.py:76
  341.5 40.7 %collective-permute-start.22 = (bf16[896,256]{1,0:T(8,128)(2,1)}, bf16[896,256]{1,0:T(8,128)(2,1)}, u32[]{:S(2)}, u32[]{:S(2)}) collective-permute-start(bf16[896,256]{1,0:T(8,128)(2,1)} %get-tuple-element.71), channel_id=1, source_target_pairs={{0,1},{1,0},{2,3},{3,2},{4,5},{5,4},{6,7},{7,6},{8,9},{9,8},{10,11... | collective-permute-start | bytes 1376264 | tf_op jit(solution)/shard_map/ppermute | solution.py:36
  352.0 26.1 %collective-permute-start.32 = (bf16[224,576]{1,0:T(8,128)(2,1)S(1)}, bf16[224,576]{1,0:T(8,128)(2,1)}, u32[]{:S(2)}, u32[]{:S(2)}) collective-permute-start(bf16[224,576]{1,0:T(8,128)(2,1)S(1)} %add_convert_fusion.10), channel_id=1, source_target_pairs={{0,8},{24,16},{1,9},{25,17},{2,10},{26,18},{3,11},{27,19},{4,12},{... | collective-permute-start | bytes 774152 | tf_op jit(solution)/shard_map/ppermute | solution.py:71
  357.8 17.9 %collective-permute-start.42 = (bf16[112,896]{1,0:T(8,128)(2,1)}, bf16[112,896]{1,0:T(8,128)(2,1)}, u32[]{:S(2)}, u32[]{:S(2)}) collective-permute-start(bf16[112,896]{1,0:T(8,128)(2,1)} %add_convert_fusion.12), channel_id=1, source_target_pairs={{8,16},{16,8},{9,17},{17,9},{10,18},{18,10},{11,19},{19,11},{12,20... | collective-permute-start | bytes 602120 | tf_op jit(solution)/shard_map/ppermute | solution.py:73
  372.0 47.3 %collective-permute-start.51 = (bf16[896,608]{0,1:T(8,128)(2,1)}, bf16[896,608]{0,1:T(8,128)(2,1)S(1)}, u32[]{:S(2)}, u32[]{:S(2)}) collective-permute-start(bf16[896,608]{0,1:T(8,128)(2,1)} %copy.85), channel_id=1, source_target_pairs={{0,4},{2,6},{4,0},{6,2},{1,5},{3,7},{5,1},{7,3},{8,12},{10,14},{12... | collective-permute-start | bytes 3268616 | tf_op jit(solution)/shard_map/ppermute | solution.py:36
  376.8 8.2 %collective-permute-start.43 = (bf16[112,896]{1,0:T(8,128)(2,1)S(1)}, bf16[112,896]{1,0:T(8,128)(2,1)S(1)}, u32[]{:S(2)}, u32[]{:S(2)}) collective-permute-start(bf16[112,896]{1,0:T(8,128)(2,1)S(1)} %add_convert_fusion.11), channel_id=1, source_target_pairs={{8,0},{16,24},{9,1},{17,25},{10,2},{18,26},{11,3},{19,27},{12,4},{... | collective-permute-start | bytes 602120 | tf_op jit(solution)/shard_map/ppermute | solution.py:76
  379.2 8.2 %collective-permute-start.33 = (bf16[224,576]{1,0:T(8,128)(2,1)S(1)}, bf16[224,576]{1,0:T(8,128)(2,1)S(1)}, u32[]{:S(2)}, u32[]{:S(2)}) collective-permute-start(bf16[224,576]{1,0:T(8,128)(2,1)S(1)} %add_convert_fusion.9), channel_id=1, source_target_pairs={{8,16},{16,8},{9,17},{17,9},{10,18},{18,10},{11,19},{19,11},{12,20... | collective-permute-start | bytes 774152 | tf_op jit(solution)/shard_map/ppermute | solution.py:73
  383.9 26.9 %collective-permute-start.23 = (bf16[256,896]{1,0:T(8,128)(2,1)S(1)}, bf16[256,896]{1,0:T(8,128)(2,1)S(1)}, u32[]{:S(2)}, u32[]{:S(2)}) collective-permute-start(bf16[256,896]{1,0:T(8,128)(2,1)S(1)} %shard_map.266), channel_id=1, source_target_pairs={{0,1},{1,0},{2,3},{3,2},{4,5},{5,4},{6,7},{7,6},{8,9},{9,8},{10,11... | collective-permute-start | bytes 1376264 | tf_op jit(solution)/shard_map/ppermute | solution.py:36
  385.0 8.9 %collective-permute-start.46 = (bf16[112,896]{1,0:T(8,128)(2,1)S(1)}, bf16[112,896]{1,0:T(8,128)(2,1)S(1)}, u32[]{:S(2)}, u32[]{:S(2)}) collective-permute-start(bf16[112,896]{1,0:T(8,128)(2,1)S(1)} %broadcast_select_fusion.4), channel_id=1, source_target_pairs={{0,6},{2,4},{4,2},{6,0},{1,7},{3,5},{5,3},{7,1},{8,14},{10,12},{12... | collective-permute-start | bytes 602120 | tf_op jit(solution)/shard_map/ppermute | solution.py:36
  386.7 21.0 %collective-permute-start.45 = (bf16[112,896]{1,0:T(8,128)(2,1)S(1)}, bf16[112,896]{1,0:T(8,128)(2,1)S(1)}, u32[]{:S(2)}, u32[]{:S(2)}) collective-permute-start(bf16[112,896]{1,0:T(8,128)(2,1)S(1)} %broadcast_select_fusion.4), channel_id=1, source_target_pairs={{0,4},{2,6},{4,0},{6,2},{1,5},{3,7},{5,1},{7,3},{8,12},{10,14},{12... | collective-permute-start | bytes 602120 | tf_op jit(solution)/shard_map/ppermute | solution.py:36
  387.4 20.8 %collective-permute-start.44 = (bf16[112,896]{1,0:T(8,128)(2,1)S(1)}, bf16[112,896]{1,0:T(8,128)(2,1)S(1)}, u32[]{:S(2)}, u32[]{:S(2)}) collective-permute-start(bf16[112,896]{1,0:T(8,128)(2,1)S(1)} %broadcast_select_fusion.4), channel_id=1, source_target_pairs={{0,2},{2,0},{4,6},{6,4},{1,3},{3,1},{5,7},{7,5},{8,10},{10,8},{12,... | collective-permute-start | bytes 602120 | tf_op jit(solution)/shard_map/ppermute | solution.py:36
  393.9 37.3 %collective-permute-start.58 = (bf16[896,608]{0,1:T(8,128)(2,1)}, bf16[896,608]{0,1:T(8,128)(2,1)}, u32[]{:S(2)}, u32[]{:S(2)}) collective-permute-start(bf16[896,608]{0,1:T(8,128)(2,1)} %copy.97), channel_id=1, source_target_pairs={{0,4},{2,6},{4,0},{6,2},{1,5},{3,7},{5,1},{7,3},{8,12},{10,14},{12... | collective-permute-start | bytes 3268616 | tf_op jit(solution)/shard_map/ppermute | solution.py:36
  407.8 27.8 %collective-permute-start.57 = (bf16[896,608]{0,1:T(8,128)(2,1)}, bf16[896,608]{0,1:T(8,128)(2,1)}, u32[]{:S(2)}, u32[]{:S(2)}) collective-permute-start(bf16[896,608]{0,1:T(8,128)(2,1)} %copy.97), channel_id=1, source_target_pairs={{0,2},{2,0},{4,6},{6,4},{1,3},{3,1},{5,7},{7,5},{8,10},{10,8},{12,... | collective-permute-start | bytes 3268616 | tf_op jit(solution)/shard_map/ppermute | solution.py:36
  408.1 8.5 %collective-permute-start.34 = (bf16[224,576]{1,0:T(8,128)(2,1)S(1)}, bf16[224,576]{1,0:T(8,128)(2,1)S(1)}, u32[]{:S(2)}, u32[]{:S(2)}) collective-permute-start(bf16[224,576]{1,0:T(8,128)(2,1)S(1)} %add_convert_fusion.8), channel_id=1, source_target_pairs={{8,0},{16,24},{9,1},{17,25},{10,2},{18,26},{11,3},{19,27},{12,4},{... | collective-permute-start | bytes 774152 | tf_op jit(solution)/shard_map/ppermute | solution.py:76
  410.9 47.5 %collective-permute-start.50 = (bf16[896,608]{0,1:T(8,128)(2,1)}, bf16[896,608]{0,1:T(8,128)(2,1)}, u32[]{:S(2)}, u32[]{:S(2)}) collective-permute-start(bf16[896,608]{0,1:T(8,128)(2,1)} %copy.85), channel_id=1, source_target_pairs={{0,2},{2,0},{4,6},{6,4},{1,3},{3,1},{5,7},{7,5},{8,10},{10,8},{12,... | collective-permute-start | bytes 3268616 | tf_op jit(solution)/shard_map/ppermute | solution.py:36
  416.6 50.4 %collective-permute-start.65 = (bf16[608,896]{1,0:T(8,128)(2,1)}, bf16[608,896]{1,0:T(8,128)(2,1)}, u32[]{:S(2)}, u32[]{:S(2)}) collective-permute-start(bf16[608,896]{1,0:T(8,128)(2,1)} %broadcast_select_fusion.2), channel_id=1, source_target_pairs={{0,4},{2,6},{4,0},{6,2},{1,5},{3,7},{5,1},{7,3},{8,12},{10,14},{12... | collective-permute-start | bytes 3268616 | tf_op jit(solution)/shard_map/ppermute | solution.py:36
  419.3 62.5 %collective-permute-start.64 = (bf16[608,896]{1,0:T(8,128)(2,1)}, bf16[608,896]{1,0:T(8,128)(2,1)}, u32[]{:S(2)}, u32[]{:S(2)}) collective-permute-start(bf16[608,896]{1,0:T(8,128)(2,1)} %broadcast_select_fusion.2), channel_id=1, source_target_pairs={{0,2},{2,0},{4,6},{6,4},{1,3},{3,1},{5,7},{7,5},{8,10},{10,8},{12,... | collective-permute-start | bytes 3268616 | tf_op jit(solution)/shard_map/ppermute | solution.py:36
  431.2 56.5 %collective-permute-start.37 = (bf16[224,576]{1,0:T(8,128)(2,1)}, bf16[224,576]{1,0:T(8,128)(2,1)}, u32[]{:S(2)}, u32[]{:S(2)}) collective-permute-start(bf16[224,576]{1,0:T(8,128)(2,1)} %broadcast_select_fusion.3), channel_id=1, source_target_pairs={{0,6},{2,4},{4,2},{6,0},{1,7},{3,5},{5,3},{7,1},{8,14},{10,12},{12... | collective-permute-start | bytes 774152 | tf_op jit(solution)/shard_map/ppermute | solution.py:36
  435.5 53.8 %collective-permute-start.36 = (bf16[224,576]{1,0:T(8,128)(2,1)}, bf16[224,576]{1,0:T(8,128)(2,1)}, u32[]{:S(2)}, u32[]{:S(2)}) collective-permute-start(bf16[224,576]{1,0:T(8,128)(2,1)} %broadcast_select_fusion.3), channel_id=1, source_target_pairs={{0,4},{2,6},{4,0},{6,2},{1,5},{3,7},{5,1},{7,3},{8,12},{10,14},{12... | collective-permute-start | bytes 774152 | tf_op jit(solution)/shard_map/ppermute | solution.py:36
  458.4 48.2 %collective-permute-start.53 = (bf16[448,608]{1,0:T(8,128)(2,1)S(1)}, bf16[448,608]{1,0:T(8,128)(2,1)}, u32[]{:S(2)}, u32[]{:S(2)}) collective-permute-start(bf16[448,608]{1,0:T(8,128)(2,1)S(1)} %copy.110.refs_6_), channel_id=1, source_target_pairs={{0,2},{2,0},{4,6},{6,4},{1,3},{3,1},{5,7},{7,5},{8,10},{10,8},{12,... | collective-permute-start | bytes 1634312 | tf_op jit(solution)/shard_map/ppermute | solution.py:36
  467.0 39.2 %collective-permute-start.35 = (bf16[224,576]{1,0:T(8,128)(2,1)}, bf16[224,576]{1,0:T(8,128)(2,1)S(1)}, u32[]{:S(2)}, u32[]{:S(2)}) collective-permute-start(bf16[224,576]{1,0:T(8,128)(2,1)} %broadcast_select_fusion.3), channel_id=1, source_target_pairs={{0,2},{2,0},{4,6},{6,4},{1,3},{3,1},{5,7},{7,5},{8,10},{10,8},{12,... | collective-permute-start | bytes 774152 | tf_op jit(solution)/shard_map/ppermute | solution.py:36
  481.7 60.8 %collective-permute-start.60 = (bf16[448,608]{1,0:T(8,128)(2,1)S(1)}, bf16[448,608]{1,0:T(8,128)(2,1)}, u32[]{:S(2)}, u32[]{:S(2)}) collective-permute-start(bf16[448,608]{1,0:T(8,128)(2,1)S(1)} %copy.114.refs_6_), channel_id=1, source_target_pairs={{0,2},{2,0},{4,6},{6,4},{1,3},{3,1},{5,7},{7,5},{8,10},{10,8},{12,... | collective-permute-start | bytes 1634312 | tf_op jit(solution)/shard_map/ppermute | solution.py:36
  487.8 54.8 %collective-permute-start.59 = (bf16[448,608]{1,0:T(8,128)(2,1)}, bf16[448,608]{1,0:T(8,128)(2,1)}, u32[]{:S(2)}, u32[]{:S(2)}) collective-permute-start(bf16[448,608]{1,0:T(8,128)(2,1)} %copy.111.refs_1_), channel_id=1, source_target_pairs={{0,4},{2,6},{4,0},{6,2},{1,5},{3,7},{5,1},{7,3},{8,12},{10,14},{12... | collective-permute-start | bytes 1634312 | tf_op jit(solution)/shard_map/ppermute | solution.py:36
  489.4 40.2 %collective-permute-start.52 = (bf16[448,608]{1,0:T(8,128)(2,1)}, bf16[448,608]{1,0:T(8,128)(2,1)}, u32[]{:S(2)}, u32[]{:S(2)}) collective-permute-start(bf16[448,608]{1,0:T(8,128)(2,1)} %copy.107.refs_1_), channel_id=1, source_target_pairs={{0,4},{2,6},{4,0},{6,2},{1,5},{3,7},{5,1},{7,3},{8,12},{10,14},{12... | collective-permute-start | bytes 1634312 | tf_op jit(solution)/shard_map/ppermute | solution.py:36
  506.2 47.2 %collective-permute-start.67 = (bf16[304,896]{1,0:T(8,128)(2,1)}, bf16[304,896]{1,0:T(8,128)(2,1)}, u32[]{:S(2)}, u32[]{:S(2)}) collective-permute-start(bf16[304,896]{1,0:T(8,128)(2,1)} %get-tuple-element.133.refs_6_), channel_id=1, source_target_pairs={{0,2},{2,0},{4,6},{6,4},{1,3},{3,1},{5,7},{7,5},{8,10},{10,8},{12,... | collective-permute-start | bytes 1634312 | tf_op jit(solution)/shard_map/ppermute | solution.py:36
  506.6 46.8 %collective-permute-start.66 = (bf16[304,896]{1,0:T(8,128)(2,1)}, bf16[304,896]{1,0:T(8,128)(2,1)}, u32[]{:S(2)}, u32[]{:S(2)}) collective-permute-start(bf16[304,896]{1,0:T(8,128)(2,1)} %get-tuple-element.136.refs_1_), channel_id=1, source_target_pairs={{0,4},{2,6},{4,0},{6,2},{1,5},{3,7},{5,1},{7,3},{8,12},{10,14},{12... | collective-permute-start | bytes 1634312 | tf_op jit(solution)/shard_map/ppermute | solution.py:36
  (74 other events, 549.2 us)

commit v2 on v1

v2 whole, which is shorter than its diff:
```python
import functools
import math

import jax
import jax.numpy as jnp
from jax import lax
from jax.experimental import pallas as pl
from jax.experimental.pallas import tpu as pltpu
from jax.sharding import PartitionSpec as P

HEAD_DIM = 64

epsilon = 1e-06
rope_base = 1000000.0
masked_value = -1e30

low = jnp.bfloat16
wide = jnp.float32
vmem_limit = 50 * 1024 * 1024


def dot_nn(left, right):
    return lax.dot_general(left, right, (((1,), (0,)), ((), ())), preferred_element_type=wide)


def dot_nt(left, right):
    return lax.dot_general(left, right, (((1,), (1,)), ((), ())), preferred_element_type=wide)


def dot_tn(left, right):
    return lax.dot_general(left, right, (((0,), (0,)), ((), ())), preferred_element_type=wide)


def partner(value, axis, step, name):
    count = lax.axis_size(axis)
    with jax.named_scope(name):
        return lax.ppermute(value, axis, [(i, i ^ step) for i in range(count)])


def gather_blocks(piece, name):
    count = lax.axis_size("blk")
    return [piece] + [partner(piece, "blk", r, name) for r in range(1, count)]


def relay_far(near, own, name):
    count = lax.axis_size("blk")
    rows = own.shape[0]
    halved = rows % 32 == 0
    cuts = [slice(0, rows // 2), slice(rows // 2, rows)] if halved else [slice(0, rows)]
    pieces = {}
    for r in range(1, count):
        if r in near:
            pieces[r] = [near[r]]
            continue
        low_bit = r & -r
        high_bit = 1 << (r.bit_length() - 1)
        pieces[r] = []
        for i, (bit, rows_cut) in enumerate(zip((high_bit, low_bit), cuts)):
            source = pieces[r ^ bit]
            part = source[i] if len(source) > 1 else source[0][rows_cut]
            pieces[r].append(partner(part, "blk", bit, name + "_relay"))
    return pieces


def gather_relayed(piece, name):
    count = lax.axis_size("blk")
    near = {r: partner(piece, "blk", r, name) for r in range(1, count) if r & (r - 1) == 0}
    pieces = relay_far(near, piece, name)
    return [[piece]] + [pieces[r] for r in range(1, count)]


def scatter_blocks(pieces, name):
    return [pieces[0]] + [partner(pieces[r], "blk", r, name) for r in range(1, len(pieces))]


def hop(value, stage, name):
    routes = ([(0, 1), (3, 2)], [(1, 2), (2, 1)], [(1, 0), (2, 3)])
    with jax.named_scope(f"{name}_hop{stage}"):
        return lax.ppermute(value, "dp", routes[stage])


def call(body, outs, ins, scratch=(), in_specs=None, after=(), carry=()):
    whole = pl.BlockSpec(memory_space=pltpu.VMEM)
    anywhere = pl.BlockSpec(memory_space=pl.ANY)
    in_specs = list(in_specs or [whole] * len(ins))
    given, waited, made = len(ins), len(after) + len(carry), len(outs)

    def run(*refs):
        results = given + waited
        body(*refs[:given], *refs[results : results + made], *refs[results + made + len(carry) :])

    return pl.pallas_call(
        run,
        name=getattr(body, "func", body).__name__,
        out_shape=tuple(outs) + tuple(shape(value.shape, value.dtype) for value in carry),
        in_specs=in_specs + [anywhere] * waited,
        out_specs=tuple([whole] * made + [anywhere] * len(carry)),
        scratch_shapes=list(scratch),
        input_output_aliases={given + len(after) + i: made + i for i in range(len(carry))},
        cost_estimate=pl.CostEstimate(flops=0, bytes_accessed=0, transcendentals=0),
        compiler_params=pltpu.CompilerParams(vmem_limit_bytes=vmem_limit),
    )(*ins, *after, *carry)


def shape(dims, kind):
    return jax.ShapeDtypeStruct(dims, kind)


in_smem = pl.BlockSpec(memory_space=pltpu.SMEM)
in_vmem = pl.BlockSpec(memory_space=pltpu.VMEM)


def as_row(column):
    return jnp.broadcast_to(column, (column.shape[0], 128)).T[:1]


def as_column(row):
    width = row.shape[1]
    padded = -(-width // 128) * 128
    row = row.astype(wide)
    if padded != width:
        row = jnp.concatenate([row, jnp.zeros((1, padded - width), wide)], axis=1)
    return jnp.broadcast_to(row, (128, padded)).T[:width, :1]


def segment_start(lengths_ref, rows):
    start = jnp.zeros_like(rows)
    end = jnp.int32(0)
    for i in range(lengths_ref.shape[1]):
        end = end + lengths_ref[0, i]
        start = jnp.where(rows >= end, end, start)
    return start


def rotate(pair, cosine, sine):
    half = HEAD_DIM // 2
    first, second = pair[:half], pair[half:]
    return jnp.concatenate(
        [first * cosine - second * sine, second * cosine + first * sine], axis=0
    )


def enter_kernel(
    lengths_ref, place_ref, tokens_ref, gain_ref, wq_ref, wk_ref, wv_ref, bq_ref, bk_ref, bv_ref,
    turn_ref, q_ref, kv_ref, normed_ref, tokens_t_ref, cos_ref, sin_ref,
):
    rows = tokens_ref.shape[0]
    hidden = tokens_ref[...].astype(wide)
    inverse = lax.rsqrt(jnp.mean(hidden * hidden, axis=1, keepdims=True) + epsilon)
    normed = (hidden * inverse * gain_ref[...].astype(wide)).astype(low)
    tokens_t_ref[...] = hidden.T.astype(low)
    normed_ref[...] = normed.astype(wide).T.astype(low)
    index = place_ref[0] * rows + lax.broadcasted_iota(jnp.int32, (1, rows), 1)
    position = (index - segment_start(lengths_ref, index)).astype(wide)
    angles = turn_ref[...] * position
    cosine, sine = jnp.cos(angles), jnp.sin(angles)
    cos_ref[...] = cosine
    sin_ref[...] = sine
    q_lin = dot_nt(wq_ref[...], normed) + as_column(bq_ref[...])
    for h in range(q_lin.shape[0] // HEAD_DIM):
        head = rotate(q_lin[h * HEAD_DIM : (h + 1) * HEAD_DIM], cosine, sine)
        q_ref[h * HEAD_DIM : (h + 1) * HEAD_DIM, :] = head.astype(low) * low(HEAD_DIM**-0.5)
    k_lin = dot_nt(wk_ref[...], normed) + as_column(bk_ref[...])
    v_lin = dot_nt(wv_ref[...], normed) + as_column(bv_ref[...])
    kv_ref[...] = jnp.concatenate([rotate(k_lin, cosine, sine), v_lin], axis=0).T.astype(low)


def weights_kernel(
    lengths_ref, place_ref, gate_ref, up_ref, down_ref, cotangent_ref,
    gate_t_ref, gate_own_ref, up_t_ref, up_own_ref, down_t_ref, mine_ref, other_ref, turned_ref, grad_ref,
):
    units = gate_t_ref.shape[0]
    width, hidden = gate_ref.shape
    window = turned_ref.shape[0]
    first = place_ref[0] * units
    base = pl.multiple_of(jnp.minimum(first // 128 * 128, hidden - window), 128)
    for ref, turned, own in ((gate_ref, gate_t_ref, gate_own_ref), (up_ref, up_t_ref, up_own_ref)):
        turned_ref[...] = ref[:, pl.ds(base, window)].astype(wide).T
        part = turned_ref[pl.ds(pl.multiple_of(first - base, 8), units), :]
        turned[...] = part.astype(low)
        own[...] = part.T.astype(low)
    down_t_ref[...] = down_ref[...].astype(wide).T.astype(low)
    rows = cotangent_ref.shape[0]
    half = rows // 2
    row = place_ref[0] * rows + lax.broadcasted_iota(jnp.int32, (rows, 1), 0)
    end = jnp.int32(0)
    for i in range(lengths_ref.shape[1]):
        end = end + lengths_ref[0, i]
    grad_ref[...] = jnp.where(row < end, cotangent_ref[...].astype(wide), 0.0)
    core = place_ref[1]
    mine_ref[...] = grad_ref[pl.ds(pl.multiple_of(core * half, half), half), :].astype(low)
    other_ref[...] = grad_ref[pl.ds(pl.multiple_of((1 - core) * half, half), half), :].astype(low)


def mask_bias(key_base, key_rows, q_index, q_start):
    keys = key_base + lax.broadcasted_iota(jnp.int32, (key_rows, q_index.shape[1]), 0)
    return jnp.where((keys >= q_start) & (keys <= q_index), 0.0, masked_value)


def first_row(lengths_ref, row):
    start = jnp.int32(0)
    end = jnp.int32(0)
    for i in range(lengths_ref.shape[1]):
        end = end + lengths_ref[0, i]
        start = jnp.where(row >= end, end, start)
    return start


def attend_kernel(blocks, lengths_ref, place_ref, q_ref, w_out_ref, *refs):
    kv_refs = refs[:blocks]
    out_ref, log_ref, mine_ref, other_ref, kv_ref, acc_ref, max_ref, bias_ref, part_ref = refs[blocks:]
    rows = q_ref.shape[1]
    heads = q_ref.shape[0] // HEAD_DIM
    own, core = place_ref[0], place_ref[1]
    for r in range(blocks):
        kv_ref[r] = kv_refs[r][...]
    q_index = own * rows + lax.broadcasted_iota(jnp.int32, (1, rows), 1)
    q_start = segment_start(lengths_ref, q_index)
    acc_ref[...] = jnp.zeros_like(acc_ref)
    max_ref[...] = jnp.full_like(max_ref, masked_value)

    def visit(block, carry):
        pair = kv_ref[block ^ own]
        keys = pair[:, :HEAD_DIM]
        values = pair.astype(wide).T[HEAD_DIM:].astype(low)
        values = jnp.concatenate([values, jnp.ones((16, rows), low)], axis=0)
        bias_ref[...] = mask_bias(block * rows, rows, q_index, q_start)
        for h in range(heads):
            scores = dot_nn(keys, q_ref[h * HEAD_DIM : (h + 1) * HEAD_DIM, :]) + bias_ref[...]
            old = max_ref[h : h + 1, :]
            new = jnp.maximum(old, jnp.max(scores, axis=0, keepdims=True))
            weight = jnp.exp(scores - new).astype(low)
            acc_ref[h] = acc_ref[h] * jnp.exp(old - new) + dot_nn(values, weight)
            max_ref[h : h + 1, :] = new
        return carry

    lax.fori_loop(first_row(lengths_ref, own * rows) // rows, own + 1, visit, 0)
    for h in range(heads):
        total = acc_ref[h, HEAD_DIM : HEAD_DIM + 1, :]
        out_ref[h * HEAD_DIM : (h + 1) * HEAD_DIM, :] = acc_ref[h, :HEAD_DIM, :] / total
        log_ref[h : h + 1, :] = max_ref[h : h + 1, :] + jnp.log(total)
    part_ref[...] = dot_tn(w_out_ref[...], out_ref[...].astype(low))
    half = mine_ref.shape[1]
    mine_ref[...] = part_ref[:, pl.ds(pl.multiple_of(core * half, half), half)]
    other_ref[...] = part_ref[:, pl.ds(pl.multiple_of((1 - core) * half, half), half)].astype(low)


def middle_kernel(place_ref, tokens_ref, part_ref, passed_ref, gain_ref, hidden_ref, normed_ref):
    half = hidden_ref.shape[1]
    mine = pl.ds(pl.multiple_of(place_ref[1] * half, half), half)
    hidden = tokens_ref[:, mine].astype(wide) + part_ref[...] + passed_ref[...].astype(wide)
    hidden_ref[...] = hidden
    inverse = lax.rsqrt(jnp.mean(hidden * hidden, axis=0, keepdims=True) + epsilon)
    normed_ref[...] = (hidden * inverse * as_column(gain_ref[...])).astype(low)


def hidden_kernel(parts, *refs):
    gy_refs, x_refs, refs = refs[: 2 * parts], refs[2 * parts : 4 * parts], refs[4 * parts :]
    gate_t_ref, up_t_ref, down_ref, gate_ref, up_ref = refs[:5]
    x_ref, gy_ref, mixed_ref, grad_gate_ref, grad_up_ref, other_ref, mine_ref = refs[5:]
    half = other_ref.shape[1]
    for k in range(2):
        at = 0
        for part in x_refs[k * parts : (k + 1) * parts]:
            x_ref[at : at + part.shape[0], k * half : (k + 1) * half] = part[...]
            at += part.shape[0]
    at = 0
    for part in gy_refs:
        gy_ref[at : at + part.shape[0], :] = part[...]
        at += part.shape[0]
    x = x_ref[...]
    gate = dot_nn(gate_t_ref[...], x)
    up = dot_nn(up_t_ref[...], x)
    grad_mixed = dot_nt(down_ref[...], gy_ref[...])
    sigmoid = 1.0 / (1.0 + jnp.exp(-gate))
    silu = gate * sigmoid
    mixed_ref[...] = (silu * up).astype(low)
    grad_gate = (grad_mixed * up * sigmoid * (1.0 + gate * (1.0 - sigmoid))).astype(low)
    grad_up = (grad_mixed * silu).astype(low)
    grad_gate_ref[...] = grad_gate
    grad_up_ref[...] = grad_up
    back = (dot_nn(gate_ref[...], grad_gate) + dot_nn(up_ref[...], grad_up)).astype(low)
    other_ref[...] = back[:, :half]
    mine_ref[...] = back[:, half:]


def weight_kernel(transposed, *refs):
    pairs, out_refs = refs[:-2], refs[-2:]
    at = 0
    for out_ref in out_refs:
        rows, columns = out_ref.shape
        tile = rows // 2 if rows % 32 == 0 else rows
        cols = slice(at, at + columns)
        for t in range(0, rows, tile):
            span = slice(t, t + tile)
            total = None
            for i in range(0, len(pairs), 2):
                left = pairs[i][span, :]
                part = dot_nt(left, pairs[i + 1][cols, :]) if transposed else dot_nn(left, pairs[i + 1][:, cols])
                total = part if total is None else total + part
            out_ref[span, :] = total.astype(low)
        at += columns


def wait_kernel(*refs):
    pass


def step_kernel(adds, place_ref, *refs):
    count = len(refs) // 3
    end = (place_ref[2] == 0) | (place_ref[2] == 3)
    for i in range(count):
        left, right, out_ref = refs[2 * i], refs[2 * i + 1], refs[2 * count + i]
        if i < adds:
            out_ref[...] = (left[...].astype(wide) + right[...].astype(wide)).astype(low)
        else:
            out_ref[...] = jnp.where(end, left[...], right[...])


def project_kernel(blocks, weight_ref, *refs):
    other_ref, mine_refs = refs[blocks], refs[blocks + 1 :]
    half = other_ref.shape[2]
    for r in range(blocks):
        part = dot_nn(weight_ref[...], refs[r][...]).astype(low)
        other_ref[r] = part[:, :half]
        mine_refs[r][...] = part[:, half:]


def add_kernel(*refs):
    count = (len(refs) - 1) // 2
    for i in range(count):
        own = refs[1 + i][...] if len(refs[1 + i].shape) == 2 else refs[1 + i][0]
        refs[1 + count + i][...] = (own.astype(wide) + refs[0][i].astype(wide)).astype(low)


def pair_kernel(*refs):
    count = len(refs) // 3
    for i in range(count):
        refs[2 * count + i][...] = (refs[2 * i][...].astype(wide) + refs[2 * i + 1][...].astype(wide)).astype(low)


def sum_blocks(refs):
    total = refs[0][...].astype(wide)
    for ref in refs[1:]:
        total = total + ref[...].astype(wide)
    return total


def layer_kernel(hidden_ref, *refs):
    out_ref = refs[-1]
    out_ref[...] = (hidden_ref[...] + sum_blocks(refs[:-1])).T.astype(low)


def grad_middle_kernel(hidden_ref, gain_ref, gy_ref, *refs):
    grad_ref, grad_low_ref, grad_gain_ref = refs[-3:]
    hidden = hidden_ref[...]
    inverse = lax.rsqrt(jnp.mean(hidden * hidden, axis=0, keepdims=True) + epsilon)
    grad_normed = sum_blocks(refs[:-3])
    weighted = as_column(gain_ref[...]) * grad_normed
    inner = jnp.mean(weighted * hidden, axis=0, keepdims=True)
    grad = inverse * weighted - hidden * (inverse * inverse * inverse * inner)
    grad = grad + gy_ref[...].astype(wide).T
    grad_ref[...] = grad
    grad_low_ref[...] = grad.astype(low)
    grad_gain_ref[...] = as_row(jnp.sum(grad_normed * hidden * inverse, axis=1, keepdims=True))


def back_enter_kernel(
    place_ref, gm_mine_ref, gm_other_ref, w_out_ref, out_ref, go_ref, delta_ref, gm_ref
):
    half = gm_mine_ref.shape[1]
    core = place_ref[1]
    gm_ref[:, pl.ds(pl.multiple_of(core * half, half), half)] = gm_mine_ref[...]
    gm_ref[:, pl.ds(pl.multiple_of((1 - core) * half, half), half)] = gm_other_ref[...]
    grad_out = dot_nn(w_out_ref[...], gm_ref[...]).astype(low)
    go_ref[...] = grad_out
    product = grad_out.astype(wide) * out_ref[...]
    for h in range(product.shape[0] // HEAD_DIM):
        delta_ref[h : h + 1, :] = jnp.sum(
            product[h * HEAD_DIM : (h + 1) * HEAD_DIM], axis=0, keepdims=True
        )


def attend_back_kernel(
    blocks, first_head, earlier, lengths_ref, place_ref, go_ref, delta_ref, log_ref, q_ref, cos_ref, sin_ref, *refs,
):
    kv_refs, refs = refs[:blocks], refs[blocks:]
    if earlier:
        earlier_refs, refs = refs[:blocks], refs[blocks:]
    (grad_q_ref, *grad_kv_refs), refs = refs[: blocks + 1], refs[blocks + 1 :]
    kv_ref, bias_ref, dq_ref, dk_ref, dv_ref, grad_kv_ref = refs
    rows = q_ref.shape[1]
    heads = grad_q_ref.shape[0] // HEAD_DIM
    own = place_ref[0]
    for r in range(blocks):
        kv_ref[r] = kv_refs[r][...]
        if earlier:
            grad_kv_ref[r] = earlier_refs[r][...].astype(wide)
        else:
            grad_kv_ref[r] = jnp.zeros_like(grad_kv_ref[r])
    dq_ref[...] = jnp.zeros_like(dq_ref)
    q_index = own * rows + lax.broadcasted_iota(jnp.int32, (1, rows), 1)
    q_start = segment_start(lengths_ref, q_index)

    def visit(block, carry):
        pair = kv_ref[block ^ own]
        keys = pair[:, :HEAD_DIM]
        values = pair[:, HEAD_DIM:]
        keys_t = pair.astype(wide).T[:HEAD_DIM].astype(low)
        bias_ref[...] = mask_bias(block * rows, rows, q_index, q_start)
        for i in range(heads):
            h = first_head + i
            span = slice(h * HEAD_DIM, (h + 1) * HEAD_DIM)
            scores = dot_nn(keys, q_ref[span, :]) + bias_ref[...]
            weight = jnp.exp(scores - log_ref[h : h + 1, :])
            grad_weight = dot_nn(values, go_ref[span, :])
            grad_scores = (weight * (grad_weight - delta_ref[h : h + 1, :])).astype(low)
            dq_ref[i * HEAD_DIM : (i + 1) * HEAD_DIM, :] += dot_nn(keys_t, grad_scores)
            dk = dot_nt(grad_scores, q_ref[span, :])
            dv = dot_nt(weight.astype(low), go_ref[span, :])
            if i == 0:
                dk_ref[...] = dk
                dv_ref[...] = dv
            else:
                dk_ref[...] += dk
                dv_ref[...] += dv
        grad_kv_ref[block ^ own] += jnp.concatenate([dk_ref[...], dv_ref[...]], axis=1)
        return carry

    lax.fori_loop(first_row(lengths_ref, own * rows) // rows, own + 1, visit, 0)
    for r in range(blocks):
        grad_kv_refs[r][...] = grad_kv_ref[r].astype(grad_kv_refs[r].dtype)
    for i in range(heads):
        span = slice(i * HEAD_DIM, (i + 1) * HEAD_DIM)
        turned = rotate(dq_ref[span, :] * HEAD_DIM**-0.5, cos_ref[...], -sin_ref[...])
        grad_q_ref[span, :] = turned.astype(low)


def query_kernel(
    place_ref, normed_ref, grad_q_a_ref, grad_q_b_ref, wq_ref, gm_mine_ref, gm_other_ref, out_ref,
    grad_wq_ref, part_ref, grad_bq_ref, grad_w_out_ref, gm_ref,
):
    half = gm_mine_ref.shape[1]
    core = place_ref[1]
    gm_ref[:, pl.ds(pl.multiple_of(core * half, half), half)] = gm_mine_ref[...]
    gm_ref[:, pl.ds(pl.multiple_of((1 - core) * half, half), half)] = gm_other_ref[...]
    grad_w_out_ref[...] = dot_nt(out_ref[...].astype(low), gm_ref[...]).astype(low)
    grad_q = jnp.concatenate([grad_q_a_ref[...], grad_q_b_ref[...]], axis=0)
    grad_wq_ref[...] = dot_nt(grad_q, normed_ref[...]).astype(low)
    part_ref[...] = dot_tn(wq_ref[...], grad_q)
    grad_bq_ref[...] = dot_nt(jnp.ones((16, grad_q.shape[1]), low), grad_q)


def key_kernel(
    blocks, place_ref, normed_ref, tokens_ref, part_ref, wk_ref, wv_ref, cos_ref, sin_ref,
    grad_wq_ref, grad_bq_ref, grad_w_out_ref, grad_gain_two_ref, *refs,
):
    kv_refs, share_refs, (mine_ref, other_ref, sum_ref, pack_ref) = refs[:blocks], refs[blocks : 2 * blocks], refs[2 * blocks :]
    both = sum_blocks(kv_refs).T
    both = jnp.concatenate(
        [rotate(both[:HEAD_DIM], cos_ref[...], -sin_ref[...]), both[HEAD_DIM:]], axis=0
    ).astype(low)
    total = part_ref[...] + dot_tn(wk_ref[...], both[:HEAD_DIM]) + dot_tn(wv_ref[...], both[HEAD_DIM:])
    sum_ref[...] = total
    half = mine_ref.shape[1]
    core = place_ref[1]
    mine_ref[...] = sum_ref[:, pl.ds(pl.multiple_of(core * half, half), half)]
    other_ref[...] = sum_ref[:, pl.ds(pl.multiple_of((1 - core) * half, half), half)].astype(low)
    hidden = tokens_ref[...].astype(wide)
    inverse = lax.rsqrt(jnp.mean(hidden * hidden, axis=0, keepdims=True) + epsilon)
    q_width, width = grad_wq_ref.shape
    kv_width = both.shape[0]
    at = 0
    pack_ref[at : at + q_width, :] = grad_wq_ref[...]
    at += q_width
    pack_ref[at : at + kv_width, :] = dot_nt(both, normed_ref[...]).astype(low)
    at += kv_width
    pack_ref[at : at + q_width, :] = grad_w_out_ref[...]
    at += q_width
    grad_gain = as_row(jnp.sum(total * (hidden * inverse), axis=1, keepdims=True))
    grad_bkv = dot_nt(jnp.ones((16, both.shape[1]), low), both)[:1]
    biases = jnp.concatenate(
        [grad_bq_ref[:1, :], grad_bkv, jnp.zeros((1, width - q_width - kv_width), wide)], axis=1
    )
    small = jnp.concatenate(
        [grad_gain, grad_gain_two_ref[...], biases, jnp.zeros((pack_ref.shape[0] - at - 3, width), wide)], axis=0
    )
    pack_ref[at:, :] = small.astype(low)
    share = pack_ref.shape[0] // blocks
    for r in range(blocks):
        start = pl.multiple_of((place_ref[0] ^ r) * share, share)
        share_refs[r][...] = pack_ref[pl.ds(start, share), :]


def share_kernel(*refs):
    refs[-1][...] = sum_blocks(refs[:-1]).astype(low)


def unpack_kernel(counts, place_ref, *refs):
    total = sum(counts)
    pieces, outs, pack_ref = refs[:total], refs[total:-1], refs[-1]
    share = pack_ref.shape[0] // len(counts)
    at = 0
    for r, count in enumerate(counts):
        start = (place_ref[0] ^ r) * share
        for ref in pieces[at : at + count]:
            pack_ref[pl.ds(pl.multiple_of(start, 8), ref.shape[0]), :] = ref[...].astype(wide)
            start = start + ref.shape[0]
        at += count
    at = 0
    for out_ref in outs:
        out_ref[...] = pack_ref[at : at + out_ref.shape[0], :]
        at += out_ref.shape[0]


def leave_kernel(place_ref, tokens_ref, mine_ref, passed_ref, gain_ref, grad_mid_ref, out_ref):
    half = mine_ref.shape[1]
    hidden = tokens_ref[:, pl.ds(pl.multiple_of(place_ref[1] * half, half), half)].astype(wide)
    inverse = lax.rsqrt(jnp.mean(hidden * hidden, axis=0, keepdims=True) + epsilon)
    weighted = as_column(gain_ref[...]) * (mine_ref[...] + passed_ref[...].astype(wide))
    inner = jnp.mean(weighted * hidden, axis=0, keepdims=True)
    grad = grad_mid_ref[...] + inverse * weighted - hidden * (inverse * inverse * inverse * inner)
    out_ref[...] = grad.T.astype(low)


def put_pieces(counts, place_ref, refs, all_ref):
    rows = all_ref.shape[0] // len(counts)
    at = 0
    for r, count in enumerate(counts):
        start = (place_ref[0] ^ r) * rows
        for ref in refs[at : at + count]:
            all_ref[pl.ds(pl.multiple_of(start, 8), ref.shape[0]), :] = ref[...].astype(wide)
            start = start + ref.shape[0]
        at += count


def rows_kernel(counts, place_ref, *refs):
    put_pieces(counts, place_ref, refs[:-1], refs[-1])


def columns_kernel(counts, place_ref, *refs):
    put_pieces(counts, place_ref, refs[:-2], refs[-1])
    refs[-2][...] = refs[-1][...].T


def place_share(place, share, transposed, width, at, whole, last):
    tile = 128
    counts = [len(parts) for parts in share]
    pieces = sum(share, [])
    whole_rows = sum(p.shape[0] for p in pieces)
    first = at // tile
    total = len(pieces)
    ins = [place] + pieces + last
    specs = (
        [in_smem]
        + [pl.BlockSpec((p.shape[0], tile), lambda i: (0, i)) for p in pieces]
        + [pl.BlockSpec(memory_space=pl.ANY)] * len(last)
    )
    aliases = {}
    if whole is not None:
        aliases = {len(ins): 0}
        ins.append(whole)
        specs.append(pl.BlockSpec(memory_space=pl.ANY))
    kernel = columns_kernel if transposed else rows_kernel

    def body(*refs):
        kernel(counts, *refs[: total + 1], *refs[len(ins) :])

    if transposed:
        dims = (width, whole_rows)
        out_spec = pl.BlockSpec((tile, whole_rows), lambda i: (i + first, 0))
        scratch = [pltpu.VMEM((whole_rows, tile), wide)]
    else:
        dims = (whole_rows, width)
        out_spec = pl.BlockSpec((whole_rows, tile), lambda i: (0, i + first))
        scratch = []
    return pl.pallas_call(
        body,
        name=kernel.__name__,
        out_shape=shape(dims, wide),
        grid=(pieces[0].shape[1] // tile,),
        in_specs=specs,
        out_specs=out_spec,
        scratch_shapes=scratch,
        input_output_aliases=aliases,
        cost_estimate=pl.CostEstimate(flops=0, bytes_accessed=0, transcendentals=0),
        compiler_params=pltpu.CompilerParams(vmem_limit_bytes=vmem_limit),
    )(*ins)


def local(
    tokens,
    lengths,
    norm1_gain,
    w_query,
    b_query,
    w_key,
    b_key,
    w_value,
    b_value,
    w_out,
    norm2_gain,
    w_gate,
    w_up,
    w_down,
    cotangent,
):
    rows, width = tokens.shape
    half = rows // 2
    blocks = lax.axis_size("blk")
    own_block = lax.axis_index("blk")
    own_core = lax.axis_index("tensor")
    q_width = w_query.shape[1]
    heads = q_width // HEAD_DIM
    units = w_gate.shape[1] // blocks
    place = jnp.stack([own_block, own_core, lax.axis_index("dp")]).astype(jnp.int32)
    gain_two = norm2_gain.reshape(1, width)

    def whole_rows(mine):
        other = partner(mine, "tensor", 1, "rows_core")
        return jnp.where(
            own_core == 0,
            jnp.concatenate([mine, other], axis=0),
            jnp.concatenate([other, mine], axis=0),
        )

    half_dim = HEAD_DIM // 2
    turn = (rope_base ** (-2.0 * jnp.arange(half_dim, dtype=wide) / HEAD_DIM)).reshape(half_dim, 1)
    q_t, key_value, normed_t, tokens_t, cosine, sine = call(
        enter_kernel,
        [
            shape((q_width, rows), low),
            shape((rows, 2 * HEAD_DIM), low),
            shape((width, rows), low),
            shape((width, rows), low),
            shape((half_dim, rows), wide),
            shape((half_dim, rows), wide),
        ],
        [
            lengths, place, tokens, norm1_gain.reshape(1, width), w_query.T, w_key.T, w_value.T,
            b_query.reshape(1, -1), b_key.reshape(1, -1), b_value.reshape(1, -1), turn,
        ],
        in_specs=[in_smem] * 2 + [in_vmem] * 9,
    )
    kv_blocks = gather_blocks(key_value, "kv")

    down_own = lax.dynamic_slice_in_dim(w_down, own_block * units, units, 0)
    window = -(-(units + 127) // 128) * 128
    gate_t, gate_own, up_t, up_own, down_t, grad_y_mine, grad_y_other = call(
        weights_kernel,
        [
            shape((units, width), low),
            shape((width, units), low),
            shape((units, width), low),
            shape((width, units), low),
            shape((width, units), low),
            shape((half, width), low),
            shape((half, width), low),
        ],
        [lengths, place, w_gate, w_up, down_own, cotangent],
        [pltpu.VMEM((window, width), wide), pltpu.VMEM((rows, width), wide)],
        in_specs=[in_smem] * 2 + [in_vmem] * 4,
        after=[q_t],
    )
    gy_near = {r: partner(grad_y_mine, "blk", r, "gy") for r in range(1, blocks) if r & (r - 1) == 0}

    out_t, log_total, part_mine, part_other = call(
        functools.partial(attend_kernel, blocks),
        [
            shape((q_width, rows), wide),
            shape((heads + 1, rows), wide),
            shape((width, half), wide),
            shape((width, half), low),
        ],
        [lengths, place, q_t, w_out] + kv_blocks,
        [
            pltpu.VMEM((blocks, rows, 2 * HEAD_DIM), low),
            pltpu.VMEM((heads, HEAD_DIM + 16, rows), wide),
            pltpu.VMEM((heads + 1, rows), wide),
            pltpu.VMEM((rows, rows), wide),
            pltpu.VMEM((width, rows), wide),
        ],
        in_specs=[in_smem] * 2 + [in_vmem] * (2 + blocks),
        after=[gate_t],
    )
    hidden, normed_two = call(
        middle_kernel,
        [shape((width, half), wide), shape((width, half), low)],
        [place, tokens_t, part_mine, partner(part_other, "tensor", 1, "part_core"), gain_two],
        in_specs=[in_smem] + [in_vmem] * 4,
        after=list(gy_near.values()),
    )

    last = [normed_two]

    def ordered(body, outs, ins, needs=(), **more):
        nonlocal last
        carry = more.get("carry", ())
        after = [v for v in last + list(needs) if not any(v is c for c in carry)]
        results = call(body, outs, ins, after=after, **more)
        last = [results[0]]
        return results

    def wait(carry, needs=()):
        return list(ordered(wait_kernel, [], [], needs=needs, carry=carry))

    def near(pieces):
        return [p for r, parts in enumerate(pieces) if r and r & (r - 1) == 0 for p in parts]

    def far(pieces):
        return [p for r, parts in enumerate(pieces) if r & (r - 1) for p in parts]

    kept = shape((units, rows), low)
    piece = shape((width, half), low)
    runs, back, passed = [], [None] * blocks, [None] * blocks

    def cores(parts, name):
        return [partner(part, "tensor", 1, name) for part in parts]

    def hidden_units(r, x_mine, x_other, gy_mine, gy_other):
        runs.append(
            ordered(
                functools.partial(hidden_kernel, len(x_mine)),
                [shape((width, rows), low), shape((rows, width), low), kept, kept, kept, piece, piece],
                gy_other + gy_mine + x_other + x_mine + [gate_t, up_t, down_own, gate_own, up_own],
            )
        )
        return runs[-1][5]

    def add_back(members, carry, needs=()):
        results = ordered(
            pair_kernel,
            [piece] * len(members),
            [value for r in members for value in (runs[r][6], passed[r])],
            needs=needs,
            carry=carry,
        )
        for r, value in zip(members, results):
            back[r] = partner(value, "blk", r, "back") if r else value
        return results[len(members) :]

    def hidden_weight(transposed, left, right, cuts):
        return ordered(
            functools.partial(weight_kernel, transposed),
            [shape((units, columns), low) for columns in cuts],
            [run[k] for run in runs for k in (left, right)],
        )

    def step(adds, takes, needs=(), carry=()):
        pairs = list(adds) + list(takes)
        return ordered(
            functools.partial(step_kernel, len(adds)),
            [shape(pair[0].shape, low) for pair in pairs],
            [place] + [value for pair in pairs for value in pair],
            in_specs=[in_smem] + [in_vmem] * (2 * len(pairs)),
            needs=needs,
            carry=carry,
        )

    x_near = {r: partner(normed_two, "blk", r, "x") for r in range(1, blocks) if r & (r - 1) == 0}
    other = hidden_units(
        0, [normed_two], cores([normed_two], "x_core"), [grad_y_mine], [grad_y_other]
    )
    other, *arrived = wait([other] + list(x_near.values()))
    passed[0] = partner(other, "tensor", 1, "back_core")
    x_near = dict(zip(x_near, arrived))
    x_mine = relay_far(x_near, normed_two, "x")
    gy_mine = relay_far(gy_near, grad_y_mine, "gy")
    x_other = {r: cores(parts, "x_core") for r, parts in x_mine.items() if r in x_near}
    gy_other = {r: cores(parts, "gy_core") for r, parts in gy_mine.items() if r in x_near}
    waiting, out_of = [], list(range(1, blocks))
    for i, r in enumerate(out_of):
        other = hidden_units(r, x_mine[r], x_other[r], gy_mine[r], gy_other[r])
        ready = [k for k in out_of if k not in x_near] if i == 0 else []
        fars = [part for k in ready for part in x_mine[k] + gy_mine[k]]
        if i == 0:
            other, *fars = wait([other] + fars)
        else:
            other, *fars = add_back([out_of[i - 1]], [other])
        passed[r] = partner(other, "tensor", 1, "back_core")
        for k in ready:
            count = len(x_mine[k])
            x_mine[k], fars = fars[:count], fars[count:]
            count = len(gy_mine[k])
            gy_mine[k], fars = fars[:count], fars[count:]
            x_other[k] = cores(x_mine[k], "x_core")
            gy_other[k] = cores(gy_mine[k], "gy_core")
    d1, d2 = hidden_weight(False, 2, 1, [384, width - 384])
    layer_other, *layer_mine = ordered(
        functools.partial(project_kernel, blocks),
        [shape((blocks, width, half), low)] + [piece] * blocks,
        [down_t] + [run[2] for run in runs],
    )
    d1, d2, layer_other = add_back([blocks - 1, 0], [d1, d2, layer_other], needs=back[1 : blocks - 1])
    d1_in, d2_in = hop(d1, 0, "d1"), hop(d2, 0, "d2")
    layer_passed = partner(layer_other, "tensor", 1, "layer_core")
    g1, g2 = hidden_weight(True, 3, 0, [512, width - 512])
    u1, u2 = hidden_weight(True, 4, 0, [512, width - 512])
    (d1,) = step([(d1, d1_in)], [], needs=back[1:])
    grad_mid, grad_mid_low, grad_gain_two = ordered(
        grad_middle_kernel,
        [shape((width, half), wide), piece, shape((1, width), wide)],
        [hidden, gain_two, grad_y_mine] + back,
    )
    *layer_pieces, grad_mid_low, d1, g1 = ordered(
        add_kernel, [piece] * blocks, [layer_passed] + layer_mine, carry=[grad_mid_low, d1, g1]
    )
    grad_mid_other = partner(grad_mid_low, "tensor", 1, "mid_core")
    layer_pieces = scatter_blocks(layer_pieces, "layer")
    d1_in, g1_in = hop(d1, 1, "d1"), hop(g1, 0, "g1")

    grad_out, delta = ordered(
        back_enter_kernel,
        [shape((q_width, rows), low), shape((heads + 1, rows), wide)],
        [place, grad_mid_low, grad_mid_other, w_out, out_t],
        scratch=[pltpu.VMEM((width, rows), low)],
        in_specs=[in_smem] + [in_vmem] * 4,
    )

    def attend_back(first, count, earlier, kind):
        return ordered(
            functools.partial(attend_back_kernel, blocks, first, bool(earlier)),
            [shape((count * HEAD_DIM, rows), low)] + [shape((rows, 2 * HEAD_DIM), kind)] * blocks,
            [lengths, place, grad_out, delta, log_total, q_t, cosine, sine] + kv_blocks + earlier,
            scratch=[
                pltpu.VMEM((blocks, rows, 2 * HEAD_DIM), low),
                pltpu.VMEM((rows, rows), wide),
                pltpu.VMEM((count * HEAD_DIM, rows), wide),
                pltpu.VMEM((rows, HEAD_DIM), wide),
                pltpu.VMEM((rows, HEAD_DIM), wide),
                pltpu.VMEM((blocks, rows, 2 * HEAD_DIM), wide),
            ],
            in_specs=[in_smem] * 2 + [in_vmem] * (6 + blocks + len(earlier)),
        )

    early_heads = (heads + 1) // 2
    grad_q_a, *grad_kv = attend_back(0, early_heads, [], wide)
    d1, d2 = step([(d1, d1_in), (d2, d2_in)], [], needs=layer_pieces[1:])
    d1_in, d2_in = hop(d1, 2, "d1"), hop(d2, 1, "d2")
    grad_q_b, *grad_kv = attend_back(early_heads, heads - early_heads, grad_kv, low)
    d2, g1, d1, g2, *grad_kv = step(
        [(d2, d2_in), (g1, g1_in)], [(d1_in, d1)], carry=[g2] + grad_kv
    )
    d1_all = gather_relayed(d1, "all_d1")
    kv_pieces = scatter_blocks(grad_kv, "grad_kv")
    d2_in, g1_in, g2_in = hop(d2, 2, "d2"), hop(g1, 1, "g1"), hop(g2, 0, "g2")
    grad_w_query, normed_part, grad_b_query, grad_w_out = ordered(
        query_kernel,
        [
            shape((q_width, width), low),
            shape((width, rows), wide),
            shape((16, q_width), wide),
            shape((q_width, width), low),
        ],
        [place, normed_t, grad_q_a, grad_q_b, w_query.T, grad_mid_low, grad_mid_other, out_t],
        scratch=[pltpu.VMEM((width, rows), low)],
        in_specs=[in_smem] + [in_vmem] * 7,
    )
    (layer_half,) = ordered(layer_kernel, [shape((half, width), low)], [hidden] + layer_pieces)
    g1, g2, d2, layer_half, u1 = step(
        [(g1, g1_in), (g2, g2_in)], [(d2_in, d2)], needs=near(d1_all) + kv_pieces[1:], carry=[layer_half, u1]
    )
    d2_all = gather_relayed(d2, "all_d2")
    g1_in, g2_in, u1_in = hop(g1, 2, "g1"), hop(g2, 1, "g2"), hop(u1, 0, "u1")
    layer_out = whole_rows(layer_half)
    pack_rows = -(-(2 * q_width + 2 * HEAD_DIM + 3) // (16 * blocks)) * 16 * blocks
    share = pack_rows // blocks
    *shares, normed_mine, normed_other = ordered(
        functools.partial(key_kernel, blocks),
        [shape((share, width), low)] * blocks + [shape((width, half), wide), shape((width, half), low)],
        [
            place, normed_t, tokens_t, normed_part, w_key.T, w_value.T, cosine, sine,
            grad_w_query, grad_b_query, grad_w_out, grad_gain_two,
        ] + kv_pieces,
        scratch=[pltpu.VMEM((width, rows), wide), pltpu.VMEM((pack_rows, width), low)],
        in_specs=[in_smem] + [in_vmem] * (11 + blocks),
    )
    g2, u1, g1, u2, normed_other, *shares = step(
        [(g2, g2_in), (u1, u1_in)],
        [(g1_in, g1)],
        needs=far(d1_all) + near(d2_all),
        carry=[u2, normed_other] + shares,
    )
    g1_all = gather_relayed(g1, "all_g1")
    shares = scatter_blocks(shares, "shares")
    g2_in, u1_in, u2_in = hop(g2, 2, "g2"), hop(u1, 1, "u1"), hop(u2, 0, "u2")
    normed_passed = partner(normed_other, "tensor", 1, "normed_core")
    grad_w_down = place_share(place, d1_all, False, width, 0, None, last)
    last = [grad_w_down]
    (own_share,) = ordered(share_kernel, [shape((share, width), low)], shares)
    u1, u2, g2, own_share = step(
        [(u1, u1_in), (u2, u2_in)],
        [(g2_in, g2)],
        needs=far(d2_all) + near(g1_all),
        carry=[own_share],
    )
    g2_all = gather_relayed(g2, "all_g2")
    u1_in, u2_in, share_in = hop(u1, 2, "u1"), hop(u2, 1, "u2"), hop(own_share, 0, "share")
    (grad_half,) = ordered(
        leave_kernel,
        [shape((half, width), low)],
        [place, tokens_t, normed_mine, normed_passed, norm1_gain.reshape(1, width), grad_mid],
        in_specs=[in_smem] + [in_vmem] * 5,
    )
    grad_w_down = place_share(place, d2_all, False, width, d1.shape[1], grad_w_down, [grad_half])
    last = [grad_w_down]
    u2, own_share, u1, grad_half = step(
        [(u2, u2_in), (own_share, share_in)],
        [(u1_in, u1)],
        needs=far(g1_all) + near(g2_all),
        carry=[grad_half],
    )
    u1_all = gather_relayed(u1, "all_u1")
    u2_in, share_in = hop(u2, 2, "u2"), hop(own_share, 1, "share")
    grad_tokens = whole_rows(grad_half).astype(wide)
    grad_w_gate = place_share(place, g1_all, True, width, 0, None, last)
    last = [grad_w_gate]
    own_share, u2 = step(
        [(own_share, share_in)], [(u2_in, u2)], needs=far(g2_all) + near(u1_all)
    )
    u2_all = gather_relayed(u2, "all_u2")
    share_in = hop(own_share, 2, "share")
    grad_w_gate = place_share(place, g2_all, True, width, g1.shape[1], grad_w_gate, last)
    last = [grad_w_gate]
    (own_share,) = step([], [(share_in, own_share)], needs=far(u1_all) + near(u2_all))
    pieces = gather_relayed(own_share, "all_share")
    grad_w_up = place_share(place, u1_all, True, width, 0, None, last)
    last = [grad_w_up]
    grad_w_up = place_share(
        place, u2_all, True, width, u1.shape[1], grad_w_up, near(pieces)
    )

    counts = [len(parts) for parts in pieces]
    small_rows = pack_rows - 2 * q_width - 2 * HEAD_DIM
    grad_w_query, grad_w_key, grad_w_value, grad_w_out, small = call(
        functools.partial(unpack_kernel, counts),
        [
            shape((q_width, width), wide),
            shape((HEAD_DIM, width), wide),
            shape((HEAD_DIM, width), wide),
            shape((q_width, width), wide),
            shape((small_rows, width), wide),
        ],
        [place] + sum(pieces, []),
        [pltpu.VMEM((pack_rows, width), wide)],
        in_specs=[in_smem] + [in_vmem] * sum(counts),
    )
    gains = small[:2]
    gains = gains + partner(gains, "tensor", 1, "gains_core")
    grad_b = small[2]
    return (
        layer_out,
        grad_tokens,
        gains[0],
        grad_w_query.T,
        grad_b[:q_width],
        grad_w_key.T,
        grad_b[q_width : q_width + HEAD_DIM],
        grad_w_value.T,
        grad_b[q_width + HEAD_DIM : q_width + 2 * HEAD_DIM],
        grad_w_out,
        gains[1],
        grad_w_gate,
        grad_w_up,
        grad_w_down,
    )


def solution(mesh):
    placed = (
        P(("dp", "blk"), None),
        P("dp", None),
        P(),
        P(None, "tensor"),
        P("tensor"),
        P(None, "tensor"),
        P("tensor"),
        P(None, "tensor"),
        P("tensor"),
        P("tensor", None),
        P(),
        P(None, "tensor"),
        P(None, "tensor"),
        P("tensor", None),
        P(("dp", "blk"), None),
    )
    return jax.shard_map(
        local,
        mesh=mesh,
        in_specs=placed,
        out_specs=(
            P(("dp", "blk"), None),
            P(("dp", "blk"), None),
            P(),
            P(None, "tensor"),
            P("tensor"),
            P(None, "tensor"),
            P("tensor"),
            P(None, "tensor"),
            P("tensor"),
            P("tensor", None),
            P(),
            P(None, "tensor"),
            P(None, "tensor"),
            P("tensor", None),
        ),
        check_vma=False,
    )
```

time: 567 us -> 412 us (0.73)
  local copies, waits for them, and re-layouts: 115 us -> 38.7 us
  waiting for transfers between devices: 171 us -> 118 us
  other arithmetic: 41.7 us -> 5.09 us
  Pallas kernels: 110 us -> 134 us
  blocking collectives: 11.6 us -> 0 us
    ppermute x53 -> x70, waiting for transfers between devices: 142 us -> 104 us  [partner(): return lax.ppermute(value, axis, [(i, i ^ step) for i in range(count)])]
    convert_element_type x17 -> x0, other arithmetic: 23.8 us -> none  [the longest x10 15.6 us: line_sum(): total = (total.astype(wide) + passed.astype(wide)).astype(low)]
    pallas_call x19 -> x43, Pallas kernels: 110 us -> 134 us  [the longest x37 111 us: call(): pl.pallas_call(run, name=getattr(body, 'func', body).__name__, out_shape=...]
    unnamed x158 -> x184, local copies, waits for them, and re-layouts: 46.4 us -> 30.9 us
    slice x12 -> x19, local copies, waits for them, and re-layouts: 18.8 us -> 3.48 us  [the longest x16 2.28 us: relay_far(): part = source[i] if len(source) > 1 else source[0][rows_cut]]
    ppermute x15 -> x21, waiting for transfers between devices: 29.3 us -> 14.5 us  [hop(): return lax.ppermute(value, 'dp', routes[stage])]
    ppermute x6 -> x0, local copies, waits for them, and re-layouts: 14.3 us -> none  [the longest x2 4.82 us: line_sum(): lax.ppermute(total, 'dp', [(middle - 1, middle), (middle, middle - 1)])]
    ppermute x53 -> x70, starting transfers between devices: 77.4 us -> 65 us  [partner(): return lax.ppermute(value, axis, [(i, i ^ step) for i in range(count)])]
  transfers between devices with their start and end apart: 68 -> 91, of which waited for: 20 -> 30; matrix products, arithmetic and copies ran while one was open for 23% -> 3% of each run, Pallas kernels for 15% -> 28%
where the time goes in v2:
time: 412 us; the launch traced here: 405 us
  Pallas kernels  134 us (33%)
  waiting for transfers between devices  118 us (29%)
  starting transfers between devices  108 us (26%)
  local copies, waits for them, and re-layouts  38.7 us (9%)
  other arithmetic  5.09 us (1%)
    pallas_call x37, Pallas kernels, call(): pl.pallas_call(run, name=getattr(body, 'func', body).__name__, out_shape=...  111 us
    ppermute x70, waiting for transfers between devices, partner(): return lax.ppermute(value, axis, [(i, i ^ step) for i in range(count)])  104 us
    ppermute x70, starting transfers between devices, partner(): return lax.ppermute(value, axis, [(i, i ^ step) for i in range(count)])  65 us
    ppermute x21, starting transfers between devices, hop(): return lax.ppermute(value, 'dp', routes[stage])  42.5 us
    unnamed x184, local copies, waits for them, and re-layouts  30.9 us
    pallas_call x6, Pallas kernels, place_share(): pl.pallas_call(body, name=kernel.__name__, out_shape=shape(dims, wide), g...  22.6 us
    ppermute x21, waiting for transfers between devices, hop(): return lax.ppermute(value, 'dp', routes[stage])  14.5 us
  transfers between devices with their start and end apart: 91, of which 30 were waited for; matrix products, arithmetic and copies ran while one was open for 3% of the time, Pallas kernels for 28%

profile of v2, /device:TPU:0, one launch (start us, length us, event | category | flops | bytes accessed | tf_op | source)
XLA Modules:
  0.0 405.0 jit_solution(4069445470155386000)
XLA Ops:
  7.0 3.0 enter_kernel.1
  11.0 2.9 collective-permute-start.2
  15.5 2.3 constant_dynamic-slice_fusion.refs_4_.refs_6_.refs_10_
  17.8 7.5 %weights_kernel.1 = (bf16[608,896]{1,0:T(8,128)(2,1)S(1)}, bf16[896,608]{1,0:T(8,128)(2,1)}, bf16[608,896]{1,0:T(8,128)(2,1)}, bf16[896,608]{1,0:T(8,128)(2,1)},...) custom-call(s32[1,3]{1,0:T(1,128)S(1)} %copy-done.78, ...), custom_call_target="tpu_custom_call" | custom-call | tf_op jit(solution)/shard_map/weights_kernel/pallas_call | solution.py:92
  26.3 2.0 collective-permute-start
  29.8 5.4 %attend_kernel.1 = (f32[448,512]{1,0:T(8,128)S(1)}, f32[8,512]{1,0:T(8,128)S(1)}, f32[896,256]{1,0:T(8,128)S(1)}, bf16[896,256]{1,0:T(8,128)(2,1)S(1)}) custom-call(s32[1,3]{1,0:T(1,128)S(1)} %copy-done.78, s32[3]{0:T(128)S(1)} %pad_add_fusion.refs_1_.refs_0_, bf16[448,512]{1,0:T(8,128)(2,1)S(1)} %get-tuple-element.160.refs_6_.refs_2_.refs_5_, ...), custom_call_target="tpu_custom_call" | custom-call | tf_op jit(solution)/shard_map/attend_kernel/pallas_call | solution.py:92
  41.9 2.8 collective-permute-start.8
  44.7 7.1 %collective-permute-start.9 = (bf16[896,256]{1,0:T(8,128)(2,1)S(1)}, bf16[896,256]{1,0:T(8,128)(2,1)S(1)}, u32[]{:S(2)}, u32[]{:S(2)}) collective-permute-start(bf16[896,256]{1,0:T(8,128)(2,1)S(1)} %get-tuple-element.168.refs_3_.refs_9_), channel_id=1, source_target_pairs={{0,4},{2,6},{4,0},{6,2},{1,5},{3,7},{5,1},{7,3},{8,12},{10,14},{12... | collective-permute-start | bytes 1376264 | tf_op jit(solution)/shard_map/x/ppermute | solution.py:37
  51.8 6.4 %hidden_kernel.4 = (bf16[896,512]{1,0:T(8,128)(2,1)}, bf16[512,896]{1,0:T(8,128)(2,1)}, bf16[608,512]{1,0:T(8,128)(2,1)S(1)}, bf16[608,512]{1,0:T(8,128)(2,1)S(1...) custom-call(bf16[256,896]{1,0:T(8,128)(2,1)S(1)} %get-tuple-element.162.refs_0_, ...), custom_call_target="tpu_custom_call" | custom-call | tf_op jit(solution)/shard_map/hidden_kernel/pallas_call | solution.py:92
  58.9 3.6 collective-permute-done.9.refs_3_
  68.1 6.4 %hidden_kernel.5 = (bf16[896,512]{1,0:T(8,128)(2,1)}, bf16[512,896]{1,0:T(8,128)(2,1)}, bf16[608,512]{1,0:T(8,128)(2,1)S(1)}, bf16[608,512]{1,0:T(8,128)(2,1)}, ...) custom-call(bf16[256,896]{1,0:T(8,128)(2,1)S(1)} %collective-permute-done.1.refs_0_, ...), custom_call_target="tpu_custom_call" | custom-call | tf_op jit(solution)/shard_map/hidden_kernel/pallas_call | solution.py:92
  79.4 6.4 %hidden_kernel.6 = (bf16[896,512]{1,0:T(8,128)(2,1)}, bf16[512,896]{1,0:T(8,128)(2,1)}, bf16[608,512]{1,0:T(8,128)(2,1)S(1)}, bf16[608,512]{1,0:T(8,128)(2,1)}, ...) custom-call(bf16[256,896]{1,0:T(8,128)(2,1)S(1)} %collective-permute-done.20.refs_0_, ...), custom_call_target="tpu_custom_call" | custom-call | tf_op jit(solution)/shard_map/hidden_kernel/pallas_call | solution.py:92
  90.7 7.3 %hidden_kernel.7 = (bf16[896,512]{1,0:T(8,128)(2,1)}, bf16[512,896]{1,0:T(8,128)(2,1)}, bf16[608,512]{1,0:T(8,128)(2,1)S(1)}, bf16[608,512]{1,0:T(8,128)(2,1)}, ...) custom-call(bf16[128,896]{1,0:T(8,128)(2,1)S(1)} %collective-permute-done.15.refs_0_, ...), custom_call_target="tpu_custom_call" | custom-call | tf_op jit(solution)/shard_map/hidden_kernel/pallas_call | solution.py:92
  101.1 4.7 %weight_kernel.3 = (bf16[608,384]{1,0:T(8,128)(2,1)S(1)}, bf16[608,512]{1,0:T(8,128)(2,1)S(1)}) custom-call(bf16[608,512]{1,0:T(8,128)(2,1)S(1)} %get-tuple-element.196.refs_0_.refs_1_, bf16[512,896]{1,0:T(8,128)(2,1)} %get-tuple-element.197.refs_1_, bf16[608,512]{1,0:T(8,128)(2,1)S(1)} %get-tuple-element.198.refs_2_, ...), custom_call_target="tpu_custom_call" | custom-call | tf_op jit(solution)/shard_map/weight_kernel/pallas_call | solution.py:92
  106.7 6.1 %project_kernel.1 = (bf16[4,896,256]{2,1,0:T(8,128)(2,1)}, bf16[896,256]{1,0:T(8,128)(2,1)S(1)}, bf16[896,256]{1,0:T(8,128)(2,1)S(1)}, bf16[896,256]{1,0:T(8,128)(2,1)S(1)}, bf16[896,256]{1,0:T(8,128)(2,1)S(1)}) custom-call(bf16[896,608]{1,0:T(8,128)(2,1)} %get-tuple-element.206.refs_0_, bf16[608,512]{1,0:T(8,128)(2,1)S(1)} %get-tuple-element.196.refs_0_.refs_1_, ...), custom_call_target="tpu_custom_call" | custom-call | tf_op jit(solution)/shard_map/project_kernel/pallas_call | solution.py:92
  116.3 4.0 collective-permute-start.29
  120.3 2.5 collective-permute-start.28
  122.8 4.9 %weight_kernel.4 = (bf16[608,512]{1,0:T(8,128)(2,1)S(1)}, bf16[608,384]{1,0:T(8,128)(2,1)S(1)}) custom-call(bf16[608,512]{1,0:T(8,128)(2,1)S(1)} %get-tuple-element.221.refs_0_, bf16[896,512]{1,0:T(8,128)(2,1)} %get-tuple-element.172.refs_0_.refs_1_, bf16[608,512]{1,0:T(8,128)(2,1)S(1)} %copy-done.52, bf16[896,512]{1,0:T(8,128)(2,1)} %get-tuple-element.176.refs_0_.refs_3_, ...), custom_call_target="tpu_custom_call" | custom-call | tf_op jit(solution)/shard_map/weight_kernel/pallas_call | solution.py:92
  128.6 4.8 %weight_kernel.5 = (bf16[608,512]{1,0:T(8,128)(2,1)S(1)}, bf16[608,384]{1,0:T(8,128)(2,1)S(1)}) custom-call(bf16[608,512]{1,0:T(8,128)(2,1)S(1)} %copy-done.50, bf16[896,512]{1,0:T(8,128)(2,1)} %get-tuple-element.172.refs_0_.refs_1_, bf16[608,512]{1,0:T(8,128)(2,1)S(1)} %copy-done.51, bf16[896,512]{1,0:T(8,128)(2,1)} %get-tuple-element.176.refs_0_.refs_3_, ...), custom_call_target="tpu_custom_call" | custom-call | tf_op jit(solution)/shard_map/weight_kernel/pallas_call | solution.py:92
  134.8 3.2 grad_middle_kernel.1
  138.0 2.0 add_kernel.1
  147.2 4.3 %attend_back_kernel.2 = (bf16[256,512]{1,0:T(8,128)(2,1)S(1)}, f32[512,128]{1,0:T(8,128)S(1)}, f32[512,128]{1,0:T(8,128)S(1)}, f32[512,128]{1,0:T(8,128)S(1)}, f32[512,128]{1,0:T(8,128)S(1)}) custom-call(s32[1,3]{1,0:T(1,128)S(1)} %copy-done.78, s32[3]{0:T(128)S(1)} %pad_add_fusion.refs_1_.refs_0_, bf16[448,512]{1,0:T(8,128)(2,1)S(1)} %get-tuple-element.234.refs_2_.refs_12_, ...), custom_call_target="tpu_custom_call" | custom-call | tf_op jit(solution)/shard_map/attend_back_kernel/pallas_call | solution.py:92
  151.5 4.0 collective-permute-done.31.refs_4_
  156.4 4.4 %collective-permute-start.37 = (bf16[608,512]{1,0:T(8,128)(2,1)S(1)}, bf16[608,512]{1,0:T(8,128)(2,1)S(1)}, u32[]{:S(2)}, u32[]{:S(2)}) collective-permute-start(bf16[608,512]{1,0:T(8,128)(2,1)S(1)} %copy-done.11), channel_id=1, source_target_pairs={{0,8},{24,16},{1,9},{25,17},{2,10},{26,18},{3,11},{27,19},{4,12},{... | collective-permute-start | bytes 1867784 | tf_op jit(solution)/shard_map/g1_hop0/ppermute | solution.py:79
  160.8 4.2 %collective-permute-done.34.refs_7_.refs_3_ = bf16[896,256]{1,0:T(8,128)(2,1)S(1)} collective-permute-done((bf16[896,256]{1,0:T(8,128)(2,1)S(1)}, bf16[896,256]{1,0:T(8,128)(2,1)S(1)}, u32[]{:S(2)}, u32[]{:S(2)}) %collective-permute-start.34) | collective-permute-done | bytes 458784 | tf_op jit(solution)/shard_map/layer/ppermute | solution.py:37
  169.6 3.3 attend_back_kernel.3
  173.9 9.4 %collective-permute-done.38.refs_5_ = bf16[608,384]{1,0:T(8,128)(2,1)S(1)} collective-permute-done((bf16[608,384]{1,0:T(8,128)(2,1)S(1)}, bf16[608,384]{1,0:T(8,128)(2,1)S(1)}, u32[]{:S(2)}, u32[]{:S(2)}) %collective-permute-start.38) | collective-permute-done | bytes 466976 | tf_op jit(solution)/shard_map/d1_hop2/ppermute | solution.py:79
  184.1 2.0 step_kernel.11
  189.8 1.9 collective-permute-start.46
  191.7 2.4 collective-permute-done.44.refs_9_.refs_13_
  194.1 6.9 %collective-permute-start.40 = (bf16[608,384]{1,0:T(8,128)(2,1)S(1)}, bf16[608,384]{1,0:T(8,128)(2,1)S(1)}, u32[]{:S(2)}, u32[]{:S(2)}) collective-permute-start(bf16[608,384]{1,0:T(8,128)(2,1)S(1)} %get-tuple-element.257.refs_3_), channel_id=1, source_target_pairs={{0,8},{24,16},{1,9},{25,17},{2,10},{26,18},{3,11},{27,19},{4,12},{... | collective-permute-start | bytes 1400840 | tf_op jit(solution)/shard_map/g2_hop0/ppermute | solution.py:79
  202.4 4.7 %query_kernel.1 = (bf16[448,896]{1,0:T(8,128)(2,1)S(1)}, f32[896,512]{1,0:T(8,128)}, f32[16,448]{1,0:T(8,128)S(1)}, bf16[448,896]{1,0:T(8,128)(2,1)S(1)}) custom-call(s32[3]{0:T(128)S(1)} %pad_add_fusion.refs_1_.refs_0_, bf16[896,512]{1,0:T(8,128)(2,1)} %copy-done.26, bf16[256,512]{1,0:T(8,128)(2,1)S(1)} %get-tuple-element.239.refs_5_.refs_2_, ...), custom_call_target="tpu_custom_call" | custom-call | tf_op jit(solution)/shard_map/query_kernel/pallas_call | solution.py:92
  212.7 2.5 step_kernel.12
  216.5 3.2 collective-permute-start.49
  222.3 2.4 collective-permute-done.51.refs_7_.refs_4_
  225.7 3.6 collective-permute-done.53.refs_9_.refs_2_
  230.0 5.4 %collective-permute-done.52.refs_8_.refs_5_ = bf16[304,384]{1,0:T(8,128)(2,1)S(1)} collective-permute-done((bf16[304,384]{1,0:T(8,128)(2,1)S(1)}, bf16[304,384]{1,0:T(8,128)(2,1)S(1)}, u32[]{:S(2)}, u32[]{:S(2)}) %collective-permute-start.52) | collective-permute-done | bytes 233504 | tf_op jit(solution)/shard_map/all_d1_relay/ppermute | solution.py:37
  235.6 4.8 %key_kernel.1 = (bf16[272,896]{1,0:T(8,128)(2,1)S(1)}, bf16[272,896]{1,0:T(8,128)(2,1)S(1)}, bf16[272,896]{1,0:T(8,128)(2,1)S(1)}, bf16[272,896]{1,0:T(8,128)(2,...) custom-call(s32[3]{0:T(128)S(1)} %pad_add_fusion.refs_1_.refs_0_, bf16[896,512]{1,0:T(8,128)(2,1)} %copy-done.26, ...), custom_call_target="tpu_custom_call" | custom-call | tf_op jit(solution)/shard_map/key_kernel/pallas_call | solution.py:92
  243.2 2.8 step_kernel.13
  246.0 3.7 collective-permute-start.56
  254.9 15.7 %collective-permute-done.59.refs_8_.refs_5_ = bf16[304,512]{1,0:T(8,128)(2,1)S(1)} collective-permute-done((bf16[304,512]{1,0:T(8,128)(2,1)S(1)}, bf16[304,512]{1,0:T(8,128)(2,1)S(1)}, u32[]{:S(2)}, u32[]{:S(2)}) %collective-permute-start.59) | collective-permute-done | bytes 311328 | tf_op jit(solution)/shard_map/all_d2_relay/ppermute | solution.py:37
  274.5 7.4 %collective-permute-done.60.refs_9_.refs_2_ = bf16[608,512]{1,0:T(8,128)(2,1)S(1)} collective-permute-done((bf16[608,512]{1,0:T(8,128)(2,1)}, bf16[608,512]{1,0:T(8,128)(2,1)S(1)}, u32[]{:S(2)}, u32[]{:S(2)}) %collective-permute-start.60) | collective-permute-done | bytes 622624 | tf_op jit(solution)/shard_map/all_g1/ppermute | solution.py:37
  281.9 9.1 %collective-permute-done.61.refs_10_.refs_3_ = bf16[608,512]{1,0:T(8,128)(2,1)S(1)} collective-permute-done((bf16[608,512]{1,0:T(8,128)(2,1)}, bf16[608,512]{1,0:T(8,128)(2,1)S(1)}, u32[]{:S(2)}, u32[]{:S(2)}) %collective-permute-start.61) | collective-permute-done | bytes 622624 | tf_op jit(solution)/shard_map/all_g1/ppermute | solution.py:37
  293.1 2.9 rows_kernel.2.refs_4_.refs_7_
  297.1 2.2 step_kernel.14
  300.6 4.6 %collective-permute-start.66 = (bf16[272,896]{1,0:T(8,128)(2,1)S(1)}, bf16[272,896]{1,0:T(8,128)(2,1)S(1)}, u32[]{:S(2)}, u32[]{:S(2)}) collective-permute-start(bf16[272,896]{1,0:T(8,128)(2,1)S(1)} %get-tuple-element.290.refs_3_), channel_id=1, source_target_pairs={{0,8},{24,16},{1,9},{25,17},{2,10},{26,18},{3,11},{27,19},{4,12},{... | collective-permute-start | bytes 1462280 | tf_op jit(solution)/shard_map/share_hop0/ppermute | solution.py:79
  309.2 2.1 leave_kernel.1.refs_6_.refs_12_
  311.4 3.5 rows_kernel.3.refs_7_
  314.9 2.0 collective-permute-done.71.refs_10_.refs_2_
  319.8 2.5 step_kernel.15
  327.4 8.8 %collective-permute-done.76.refs_6_.refs_4_ = bf16[304,384]{1,0:T(8,128)(2,1)S(1)} collective-permute-done((bf16[304,384]{1,0:T(8,128)(2,1)S(1)}, bf16[304,384]{1,0:T(8,128)(2,1)S(1)}, u32[]{:S(2)}, u32[]{:S(2)}) %collective-permute-start.76) | collective-permute-done | bytes 233504 | tf_op jit(solution)/shard_map/all_g2_relay/ppermute | solution.py:37
  337.3 4.4 %columns_kernel.4.refs_5_.refs_7_ = f32[896,2432]{1,0:T(8,128)} custom-call(s32[3]{0:T(128)S(1)} %pad_add_fusion.refs_1_.refs_0_, bf16[608,512]{1,0:T(8,128)(2,1)S(1)} %copy-done.48, bf16[608,512]{1,0:T(8,128)(2,1)S(1)} %copy-done.22, bf16[608,512]{1,0:T(8,128)(2,1)S(1)} %copy-done.24, bf16[304,512]{1,0:T(8,128)(2,1)S(1)} %collective-permute-done.69.refs_8_.refs_4_, ...), custom_call_target="tpu_custom_call" | custom-call | tf_op jit(solution)/shard_map/columns_kernel/pallas_call | solution.py:577
  341.6 3.2 collective-permute-done.77.refs_7_.refs_5_
  353.0 3.7 columns_kernel.5.refs_3_
  356.7 4.0 collective-permute-done.81.refs_4_
  360.7 4.2 %collective-permute-done.82.refs_5_ = bf16[304,512]{1,0:T(8,128)(2,1)S(1)} collective-permute-done((bf16[304,512]{1,0:T(8,128)(2,1)S(1)}, bf16[304,512]{1,0:T(8,128)(2,1)S(1)}, u32[]{:S(2)}, u32[]{:S(2)}) %collective-permute-start.82) | collective-permute-done | bytes 311328 | tf_op jit(solution)/shard_map/all_u1_relay/ppermute | solution.py:37
  368.3 8.2 %collective-permute-done.85.refs_2_.refs_6_ = bf16[272,896]{1,0:T(8,128)(2,1)S(1)} collective-permute-done((bf16[272,896]{1,0:T(8,128)(2,1)S(1)}, bf16[272,896]{1,0:T(8,128)(2,1)S(1)}, u32[]{:S(2)}, u32[]{:S(2)}) %collective-permute-start.85) | collective-permute-done | bytes 487456 | tf_op jit(solution)/shard_map/all_share/ppermute | solution.py:37
  376.6 2.0 collective-permute-start.89
  380.2 2.3 maximum_select_fusion
  382.5 2.7 fusion
  385.2 4.4 %columns_kernel.6.refs_8_ = f32[896,2432]{1,0:T(8,128)} custom-call(s32[3]{0:T(128)S(1)} %pad_add_fusion.refs_1_.refs_0_, bf16[608,512]{1,0:T(8,128)(2,1)S(1)} %copy-done.49, bf16[608,512]{1,0:T(8,128)(2,1)S(1)} %collective-permute-done.78.refs_8_.refs_2_, bf16[608,512]{1,0:T(8,128)(2,1)S(1)} %copy-done.20, bf16[304,512]{1,0:T(8,128)(2,1)S(1)} %copy-done.40, ...), custom_call_target="tpu_custom_call" | custom-call | tf_op jit(solution)/shard_map/columns_kernel/pallas_call | solution.py:577
  389.6 6.1 %collective-permute-done.89.refs_4_ = bf16[304,384]{1,0:T(8,128)(2,1)S(1)} collective-permute-done((bf16[304,384]{1,0:T(8,128)(2,1)S(1)}, bf16[304,384]{1,0:T(8,128)(2,1)S(1)}, u32[]{:S(2)}, u32[]{:S(2)}) %collective-permute-start.89) | collective-permute-done | bytes 233504 | tf_op jit(solution)/shard_map/all_u2_relay/ppermute | solution.py:37
  395.7 3.7 columns_kernel.7
  399.5 3.3 unpack_kernel.1
  (374 shorter events, 118.4 us)
Async XLA Ops:
  11.0 18.8 %collective-permute-start.2 = (bf16[512,128]{1,0:T(8,128)(2,1)S(1)}, bf16[512,128]{1,0:T(8,128)(2,1)S(1)}, u32[]{:S(2)}, u32[]{:S(2)}) collective-permute-start(bf16[512,128]{1,0:T(8,128)(2,1)S(1)} %get-tuple-element.164.refs_4_.refs_8_), channel_id=1, source_target_pairs={{0,2},{2,0},{4,6},{6,4},{1,3},{3,1},{5,7},{7,5},{8,10},{10,8},{12,... | collective-permute-start | bytes 393224 | tf_op jit(solution)/shard_map/kv/ppermute | solution.py:37
  13.9 15.8 %collective-permute-start.3 = (bf16[512,128]{1,0:T(8,128)(2,1)S(1)}, bf16[512,128]{1,0:T(8,128)(2,1)S(1)}, u32[]{:S(2)}, u32[]{:S(2)}) collective-permute-start(bf16[512,128]{1,0:T(8,128)(2,1)S(1)} %get-tuple-element.164.refs_4_.refs_8_), channel_id=1, source_target_pairs={{0,4},{2,6},{4,0},{6,2},{1,5},{3,7},{5,1},{7,3},{8,12},{10,14},{12... | collective-permute-start | bytes 393224 | tf_op jit(solution)/shard_map/kv/ppermute | solution.py:37
  15.5 14.3 %collective-permute-start.4 = (bf16[512,128]{1,0:T(8,128)(2,1)S(1)}, bf16[512,128]{1,0:T(8,128)(2,1)S(1)}, u32[]{:S(2)}, u32[]{:S(2)}) collective-permute-start(bf16[512,128]{1,0:T(8,128)(2,1)S(1)} %get-tuple-element.164.refs_4_.refs_8_), channel_id=1, source_target_pairs={{0,6},{2,4},{4,2},{6,0},{1,7},{3,5},{5,3},{7,1},{8,14},{10,12},{12... | collective-permute-start | bytes 393224 | tf_op jit(solution)/shard_map/kv/ppermute | solution.py:37
  26.3 11.7 %collective-permute-start = (bf16[256,896]{1,0:T(8,128)(2,1)S(1)}, bf16[256,896]{1,0:T(8,128)(2,1)S(1)}, u32[]{:S(2)}, u32[]{:S(2)}) collective-permute-start(bf16[256,896]{1,0:T(8,128)(2,1)S(1)} %get-tuple-element.161.refs_1_.refs_2_), channel_id=1, source_target_pairs={{0,2},{2,0},{4,6},{6,4},{1,3},{3,1},{5,7},{7,5},{8,10},{10,8},{12,... | collective-permute-start | bytes 1376264 | tf_op jit(solution)/shard_map/gy/ppermute | solution.py:37
  41.9 17.0 %collective-permute-start.8 = (bf16[896,256]{1,0:T(8,128)(2,1)S(1)}, bf16[896,256]{1,0:T(8,128)(2,1)S(1)}, u32[]{:S(2)}, u32[]{:S(2)}) collective-permute-start(bf16[896,256]{1,0:T(8,128)(2,1)S(1)} %get-tuple-element.168.refs_3_.refs_9_), channel_id=1, source_target_pairs={{0,2},{2,0},{4,6},{6,4},{1,3},{3,1},{5,7},{7,5},{8,10},{10,8},{12,... | collective-permute-start | bytes 1376264 | tf_op jit(solution)/shard_map/x/ppermute | solution.py:37
  44.7 17.8 %collective-permute-start.9 = (bf16[896,256]{1,0:T(8,128)(2,1)S(1)}, bf16[896,256]{1,0:T(8,128)(2,1)S(1)}, u32[]{:S(2)}, u32[]{:S(2)}) collective-permute-start(bf16[896,256]{1,0:T(8,128)(2,1)S(1)} %get-tuple-element.168.refs_3_.refs_9_), channel_id=1, source_target_pairs={{0,4},{2,6},{4,0},{6,2},{1,5},{3,7},{5,1},{7,3},{8,12},{10,14},{12... | collective-permute-start | bytes 1376264 | tf_op jit(solution)/shard_map/x/ppermute | solution.py:37
  51.7 14.5 %collective-permute-start.1 = (bf16[256,896]{1,0:T(8,128)(2,1)S(1)}, bf16[256,896]{1,0:T(8,128)(2,1)S(1)}, u32[]{:S(2)}, u32[]{:S(2)}) collective-permute-start(bf16[256,896]{1,0:T(8,128)(2,1)S(1)} %collective-permute-done.refs_5_.refs_1_), channel_id=1, source_target_pairs={{0,1},{1,0},{2,3},{3,2},{4,5},{5,4},{6,7},{7,6},{8,9},{9,8},{10,11... | collective-permute-start | bytes 1376264 | tf_op jit(solution)/shard_map/gy_core/ppermute | solution.py:37
  66.3 12.0 %collective-permute-start.12 = (bf16[448,256]{1,0:T(8,128)(2,1)S(1)}, bf16[448,256]{1,0:T(8,128)(2,1)S(1)}, u32[]{:S(2)}, u32[]{:S(2)}) collective-permute-start(bf16[448,256]{1,0:T(8,128)(2,1)S(1)} %slice.80), channel_id=1, source_target_pairs={{0,2},{2,0},{4,6},{6,4},{1,3},{3,1},{5,7},{7,5},{8,10},{10,8},{12,... | collective-permute-start | bytes 688136 | tf_op jit(solution)/shard_map/x_relay/ppermute | solution.py:37
  87.4 11.4 %collective-permute-start.22 = (bf16[896,256]{1,0:T(8,128)(2,1)S(1)}, bf16[896,256]{1,0:T(8,128)(2,1)S(1)}, u32[]{:S(2)}, u32[]{:S(2)}) collective-permute-start(bf16[896,256]{1,0:T(8,128)(2,1)S(1)} %get-tuple-element.190), channel_id=1, source_target_pairs={{0,1},{1,0},{2,3},{3,2},{4,5},{5,4},{6,7},{7,6},{8,9},{9,8},{10,11... | collective-permute-start | bytes 1376264 | tf_op jit(solution)/shard_map/back_core/ppermute | solution.py:37
  89.7 23.0 %collective-permute-start.24 = (bf16[896,256]{1,0:T(8,128)(2,1)S(1)}, bf16[896,256]{1,0:T(8,128)(2,1)S(1)}, u32[]{:S(2)}, u32[]{:S(2)}) collective-permute-start(bf16[896,256]{1,0:T(8,128)(2,1)S(1)} %get-tuple-element.175.refs_9_), channel_id=1, source_target_pairs={{0,1},{1,0},{2,3},{3,2},{4,5},{5,4},{6,7},{7,6},{8,9},{9,8},{10,11... | collective-permute-start | bytes 1376264 | tf_op jit(solution)/shard_map/back_core/ppermute | solution.py:37
  90.1 23.5 %collective-permute-start.25 = (bf16[896,256]{1,0:T(8,128)(2,1)S(1)}, bf16[896,256]{1,0:T(8,128)(2,1)S(1)}, u32[]{:S(2)}, u32[]{:S(2)}) collective-permute-start(bf16[896,256]{1,0:T(8,128)(2,1)S(1)} %get-tuple-element.187.refs_13_), channel_id=1, source_target_pairs={{0,2},{2,0},{4,6},{6,4},{1,3},{3,1},{5,7},{7,5},{8,10},{10,8},{12,... | collective-permute-start | bytes 1376264 | tf_op jit(solution)/shard_map/back/ppermute | solution.py:37
  100.3 13.2 %collective-permute-start.23 = (bf16[896,256]{1,0:T(8,128)(2,1)}, bf16[896,256]{1,0:T(8,128)(2,1)S(1)}, u32[]{:S(2)}, u32[]{:S(2)}) collective-permute-start(bf16[896,256]{1,0:T(8,128)(2,1)} %get-tuple-element.193), channel_id=1, source_target_pairs={{0,1},{1,0},{2,3},{3,2},{4,5},{5,4},{6,7},{7,6},{8,9},{9,8},{10,11... | collective-permute-start | bytes 1376264 | tf_op jit(solution)/shard_map/back_core/ppermute | solution.py:37
  100.8 12.8 %collective-permute-start.26 = (bf16[896,256]{1,0:T(8,128)(2,1)S(1)}, bf16[896,256]{1,0:T(8,128)(2,1)S(1)}, u32[]{:S(2)}, u32[]{:S(2)}) collective-permute-start(bf16[896,256]{1,0:T(8,128)(2,1)S(1)} %get-tuple-element.195.refs_8_), channel_id=1, source_target_pairs={{0,4},{2,6},{4,0},{6,2},{1,5},{3,7},{5,1},{7,3},{8,12},{10,14},{12... | collective-permute-start | bytes 1376264 | tf_op jit(solution)/shard_map/back/ppermute | solution.py:37
  116.3 21.7 %collective-permute-start.27 = (bf16[4,896,256]{2,1,0:T(8,128)(2,1)}, bf16[4,896,256]{2,1,0:T(8,128)(2,1)}, u32[]{:S(2)}, u32[]{:S(2)}) collective-permute-start(bf16[4,896,256]{2,1,0:T(8,128)(2,1)} %get-tuple-element.208), channel_id=1, source_target_pairs={{0,1},{1,0},{2,3},{3,2},{4,5},{5,4},{6,7},{7,6},{8,9},{9,8},{10,11... | collective-permute-start | bytes 5505032 | tf_op jit(solution)/shard_map/layer_core/ppermute | solution.py:37
  116.3 17.8 %collective-permute-start.29 = (bf16[608,384]{1,0:T(8,128)(2,1)}, bf16[608,384]{1,0:T(8,128)(2,1)S(1)}, u32[]{:S(2)}, u32[]{:S(2)}) collective-permute-start(bf16[608,384]{1,0:T(8,128)(2,1)} %get-tuple-element.216.refs_1_), channel_id=1, source_target_pairs={{0,8},{24,16},{1,9},{25,17},{2,10},{26,18},{3,11},{27,19},{4,12},{... | collective-permute-start | bytes 1400840 | tf_op jit(solution)/shard_map/d1_hop0/ppermute | solution.py:79
  120.3 13.8 %collective-permute-start.28 = (bf16[896,256]{1,0:T(8,128)(2,1)}, bf16[896,256]{1,0:T(8,128)(2,1)S(1)}, u32[]{:S(2)}, u32[]{:S(2)}) collective-permute-start(bf16[896,256]{1,0:T(8,128)(2,1)} %get-tuple-element.215.refs_8_), channel_id=1, source_target_pairs={{0,6},{2,4},{4,2},{6,0},{1,7},{3,5},{5,3},{7,1},{8,14},{10,12},{12... | collective-permute-start | bytes 1376264 | tf_op jit(solution)/shard_map/back/ppermute | solution.py:37
  140.0 15.5 %collective-permute-start.31 = (bf16[608,512]{1,0:T(8,128)(2,1)S(1)}, bf16[608,512]{1,0:T(8,128)(2,1)S(1)}, u32[]{:S(2)}, u32[]{:S(2)}) collective-permute-start(bf16[608,512]{1,0:T(8,128)(2,1)S(1)} %copy-done.38), channel_id=1, source_target_pairs={{0,8},{24,16},{1,9},{25,17},{2,10},{26,18},{3,11},{27,19},{4,12},{... | collective-permute-start | bytes 1867784 | tf_op jit(solution)/shard_map/d2_hop0/ppermute | solution.py:79
  141.6 24.4 %collective-permute-start.30 = (bf16[608,384]{1,0:T(8,128)(2,1)}, bf16[608,384]{1,0:T(8,128)(2,1)S(1)}, u32[]{:S(2)}, u32[]{:S(2)}) collective-permute-start(bf16[608,384]{1,0:T(8,128)(2,1)} %get-tuple-element.229.refs_1_), channel_id=1, source_target_pairs={{8,16},{16,8},{9,17},{17,9},{10,18},{18,10},{11,19},{19,11},{12,20... | collective-permute-start | bytes 1400840 | tf_op jit(solution)/shard_map/d1_hop1/ppermute | solution.py:79
  142.3 18.5 %collective-permute-start.33 = (bf16[896,256]{1,0:T(8,128)(2,1)S(1)}, bf16[896,256]{1,0:T(8,128)(2,1)S(1)}, u32[]{:S(2)}, u32[]{:S(2)}) collective-permute-start(bf16[896,256]{1,0:T(8,128)(2,1)S(1)} %get-tuple-element.240), channel_id=1, source_target_pairs={{0,2},{2,0},{4,6},{6,4},{1,3},{3,1},{5,7},{7,5},{8,10},{10,8},{12,... | collective-permute-start | bytes 1376264 | tf_op jit(solution)/shard_map/layer/ppermute | solution.py:37
  143.6 21.4 %collective-permute-start.34 = (bf16[896,256]{1,0:T(8,128)(2,1)S(1)}, bf16[896,256]{1,0:T(8,128)(2,1)S(1)}, u32[]{:S(2)}, u32[]{:S(2)}) collective-permute-start(bf16[896,256]{1,0:T(8,128)(2,1)S(1)} %get-tuple-element.241), channel_id=1, source_target_pairs={{0,4},{2,6},{4,0},{6,2},{1,5},{3,7},{5,1},{7,3},{8,12},{10,14},{12... | collective-permute-start | bytes 1376264 | tf_op jit(solution)/shard_map/layer/ppermute | solution.py:37
  145.3 20.8 %collective-permute-start.35 = (bf16[896,256]{1,0:T(8,128)(2,1)S(1)}, bf16[896,256]{1,0:T(8,128)(2,1)S(1)}, u32[]{:S(2)}, u32[]{:S(2)}) collective-permute-start(bf16[896,256]{1,0:T(8,128)(2,1)S(1)} %get-tuple-element.242), channel_id=1, source_target_pairs={{0,6},{2,4},{4,2},{6,0},{1,7},{3,5},{5,3},{7,1},{8,14},{10,12},{12... | collective-permute-start | bytes 1376264 | tf_op jit(solution)/shard_map/layer/ppermute | solution.py:37
  156.4 17.5 %collective-permute-start.37 = (bf16[608,512]{1,0:T(8,128)(2,1)S(1)}, bf16[608,512]{1,0:T(8,128)(2,1)S(1)}, u32[]{:S(2)}, u32[]{:S(2)}) collective-permute-start(bf16[608,512]{1,0:T(8,128)(2,1)S(1)} %copy-done.11), channel_id=1, source_target_pairs={{0,8},{24,16},{1,9},{25,17},{2,10},{26,18},{3,11},{27,19},{4,12},{... | collective-permute-start | bytes 1867784 | tf_op jit(solution)/shard_map/g1_hop0/ppermute | solution.py:79
  167.6 15.7 %collective-permute-start.36 = (bf16[608,512]{1,0:T(8,128)(2,1)S(1)}, bf16[608,512]{1,0:T(8,128)(2,1)S(1)}, u32[]{:S(2)}, u32[]{:S(2)}) collective-permute-start(bf16[608,512]{1,0:T(8,128)(2,1)S(1)} %get-tuple-element.243.refs_1_), channel_id=1, source_target_pairs={{8,16},{16,8},{9,17},{17,9},{10,18},{18,10},{11,19},{19,11},{12,20... | collective-permute-start | bytes 1867784 | tf_op jit(solution)/shard_map/d2_hop1/ppermute | solution.py:79
  168.3 15.0 %collective-permute-start.38 = (bf16[608,384]{1,0:T(8,128)(2,1)S(1)}, bf16[608,384]{1,0:T(8,128)(2,1)S(1)}, u32[]{:S(2)}, u32[]{:S(2)}) collective-permute-start(bf16[608,384]{1,0:T(8,128)(2,1)S(1)} %get-tuple-element.245.refs_16_.refs_6_), channel_id=1, source_target_pairs={{8,0},{16,24},{9,1},{17,25},{10,2},{18,26},{11,3},{19,27},{12,4},{... | collective-permute-start | bytes 1400840 | tf_op jit(solution)/shard_map/d1_hop2/ppermute | solution.py:79
  186.2 24.8 %collective-permute-start.39 = (bf16[608,512]{1,0:T(8,128)(2,1)S(1)}, bf16[608,512]{1,0:T(8,128)(2,1)S(1)}, u32[]{:S(2)}, u32[]{:S(2)}) collective-permute-start(bf16[608,512]{1,0:T(8,128)(2,1)S(1)} %get-tuple-element.256.refs_1_), channel_id=1, source_target_pairs={{8,16},{16,8},{9,17},{17,9},{10,18},{18,10},{11,19},{19,11},{12,20... | collective-permute-start | bytes 1867784 | tf_op jit(solution)/shard_map/g1_hop1/ppermute | solution.py:79
  186.9 24.1 %collective-permute-start.41 = (bf16[608,512]{1,0:T(8,128)(2,1)S(1)}, bf16[608,512]{1,0:T(8,128)(2,1)S(1)}, u32[]{:S(2)}, u32[]{:S(2)}) collective-permute-start(bf16[608,512]{1,0:T(8,128)(2,1)S(1)} %get-tuple-element.258.refs_8_.refs_6_), channel_id=1, source_target_pairs={{8,0},{16,24},{9,1},{17,25},{10,2},{18,26},{11,3},{19,27},{12,4},{... | collective-permute-start | bytes 1867784 | tf_op jit(solution)/shard_map/d2_hop2/ppermute | solution.py:79
  189.4 11.7 %collective-permute-start.45 = (bf16[512,128]{1,0:T(8,128)(2,1)S(1)}, bf16[512,128]{1,0:T(8,128)(2,1)S(1)}, u32[]{:S(2)}, u32[]{:S(2)}) collective-permute-start(bf16[512,128]{1,0:T(8,128)(2,1)S(1)} %get-tuple-element.261), channel_id=1, source_target_pairs={{0,4},{2,6},{4,0},{6,2},{1,5},{3,7},{5,1},{7,3},{8,12},{10,14},{12... | collective-permute-start | bytes 393224 | tf_op jit(solution)/shard_map/grad_kv/ppermute | solution.py:37
  189.8 12.2 %collective-permute-start.46 = (bf16[512,128]{1,0:T(8,128)(2,1)S(1)}, bf16[512,128]{1,0:T(8,128)(2,1)S(1)}, u32[]{:S(2)}, u32[]{:S(2)}) collective-permute-start(bf16[512,128]{1,0:T(8,128)(2,1)S(1)} %get-tuple-element.262), channel_id=1, source_target_pairs={{0,6},{2,4},{4,2},{6,0},{1,7},{3,5},{5,3},{7,1},{8,14},{10,12},{12... | collective-permute-start | bytes 393224 | tf_op jit(solution)/shard_map/grad_kv/ppermute | solution.py:37
  194.1 14.2 %collective-permute-start.40 = (bf16[608,384]{1,0:T(8,128)(2,1)S(1)}, bf16[608,384]{1,0:T(8,128)(2,1)S(1)}, u32[]{:S(2)}, u32[]{:S(2)}) collective-permute-start(bf16[608,384]{1,0:T(8,128)(2,1)S(1)} %get-tuple-element.257.refs_3_), channel_id=1, source_target_pairs={{0,8},{24,16},{1,9},{25,17},{2,10},{26,18},{3,11},{27,19},{4,12},{... | collective-permute-start | bytes 1400840 | tf_op jit(solution)/shard_map/g2_hop0/ppermute | solution.py:79
  215.2 14.1 %collective-permute-start.53 = (bf16[608,512]{1,0:T(8,128)(2,1)}, bf16[608,512]{1,0:T(8,128)(2,1)S(1)}, u32[]{:S(2)}, u32[]{:S(2)}) collective-permute-start(bf16[608,512]{1,0:T(8,128)(2,1)} %get-tuple-element.269.refs_1_), channel_id=1, source_target_pairs={{0,2},{2,0},{4,6},{6,4},{1,3},{3,1},{5,7},{7,5},{8,10},{10,8},{12,... | collective-permute-start | bytes 1867784 | tf_op jit(solution)/shard_map/all_d2/ppermute | solution.py:37
  216.5 25.5 %collective-permute-start.49 = (bf16[608,512]{1,0:T(8,128)(2,1)}, bf16[608,512]{1,0:T(8,128)(2,1)S(1)}, u32[]{:S(2)}, u32[]{:S(2)}) collective-permute-start(bf16[608,512]{1,0:T(8,128)(2,1)} %get-tuple-element.267.refs_3_), channel_id=1, source_target_pairs={{0,8},{24,16},{1,9},{25,17},{2,10},{26,18},{3,11},{27,19},{4,12},{... | collective-permute-start | bytes 1867784 | tf_op jit(solution)/shard_map/u1_hop0/ppermute | solution.py:79
  219.7 22.3 %collective-permute-start.50 = (bf16[608,512]{1,0:T(8,128)(2,1)S(1)}, bf16[608,512]{1,0:T(8,128)(2,1)S(1)}, u32[]{:S(2)}, u32[]{:S(2)}) collective-permute-start(bf16[608,512]{1,0:T(8,128)(2,1)S(1)} %get-tuple-element.268.refs_16_.refs_6_), channel_id=1, source_target_pairs={{8,0},{16,24},{9,1},{17,25},{10,2},{18,26},{11,3},{19,27},{12,4},{... | collective-permute-start | bytes 1867784 | tf_op jit(solution)/shard_map/g1_hop2/ppermute | solution.py:79
  221.0 21.0 %collective-permute-start.54 = (bf16[608,512]{1,0:T(8,128)(2,1)}, bf16[608,512]{1,0:T(8,128)(2,1)S(1)}, u32[]{:S(2)}, u32[]{:S(2)}) collective-permute-start(bf16[608,512]{1,0:T(8,128)(2,1)} %get-tuple-element.269.refs_1_), channel_id=1, source_target_pairs={{0,4},{2,6},{4,0},{6,2},{1,5},{3,7},{5,1},{7,3},{8,12},{10,14},{12... | collective-permute-start | bytes 1867784 | tf_op jit(solution)/shard_map/all_d2/ppermute | solution.py:37
  224.7 17.3 %collective-permute-start.48 = (bf16[608,384]{1,0:T(8,128)(2,1)S(1)}, bf16[608,384]{1,0:T(8,128)(2,1)S(1)}, u32[]{:S(2)}, u32[]{:S(2)}) collective-permute-start(bf16[608,384]{1,0:T(8,128)(2,1)S(1)} %get-tuple-element.266.refs_1_), channel_id=1, source_target_pairs={{8,16},{16,8},{9,17},{17,9},{10,18},{18,10},{11,19},{19,11},{12,20... | collective-permute-start | bytes 1400840 | tf_op jit(solution)/shard_map/g2_hop1/ppermute | solution.py:79
  235.3 18.7 %collective-permute-start.58 = (bf16[304,512]{1,0:T(8,128)(2,1)S(1)}, bf16[304,512]{1,0:T(8,128)(2,1)S(1)}, u32[]{:S(2)}, u32[]{:S(2)}) collective-permute-start(bf16[304,512]{1,0:T(8,128)(2,1)S(1)} %slice.108), channel_id=1, source_target_pairs={{0,4},{2,6},{4,0},{6,2},{1,5},{3,7},{5,1},{7,3},{8,12},{10,14},{12... | collective-permute-start | bytes 933896 | tf_op jit(solution)/shard_map/all_d2_relay/ppermute | solution.py:37
  246.0 25.7 %collective-permute-start.56 = (bf16[608,384]{1,0:T(8,128)(2,1)S(1)}, bf16[608,384]{1,0:T(8,128)(2,1)S(1)}, u32[]{:S(2)}, u32[]{:S(2)}) collective-permute-start(bf16[608,384]{1,0:T(8,128)(2,1)S(1)} %get-tuple-element.282.refs_3_), channel_id=1, source_target_pairs={{0,8},{24,16},{1,9},{25,17},{2,10},{26,18},{3,11},{27,19},{4,12},{... | collective-permute-start | bytes 1400840 | tf_op jit(solution)/shard_map/u2_hop0/ppermute | solution.py:79
  249.8 22.8 %collective-permute-start.62 = (bf16[272,896]{1,0:T(8,128)(2,1)S(1)}, bf16[272,896]{1,0:T(8,128)(2,1)S(1)}, u32[]{:S(2)}, u32[]{:S(2)}) collective-permute-start(bf16[272,896]{1,0:T(8,128)(2,1)S(1)} %get-tuple-element.286), channel_id=1, source_target_pairs={{0,2},{2,0},{4,6},{6,4},{1,3},{3,1},{5,7},{7,5},{8,10},{10,8},{12,... | collective-permute-start | bytes 1462280 | tf_op jit(solution)/shard_map/shares/ppermute | solution.py:37
  251.3 19.3 %collective-permute-start.59 = (bf16[304,512]{1,0:T(8,128)(2,1)S(1)}, bf16[304,512]{1,0:T(8,128)(2,1)S(1)}, u32[]{:S(2)}, u32[]{:S(2)}) collective-permute-start(bf16[304,512]{1,0:T(8,128)(2,1)S(1)} %slice.109), channel_id=1, source_target_pairs={{0,2},{2,0},{4,6},{6,4},{1,3},{3,1},{5,7},{7,5},{8,10},{10,8},{12,... | collective-permute-start | bytes 933896 | tf_op jit(solution)/shard_map/all_d2_relay/ppermute | solution.py:37
  252.9 20.3 %collective-permute-start.63 = (bf16[272,896]{1,0:T(8,128)(2,1)}, bf16[272,896]{1,0:T(8,128)(2,1)S(1)}, u32[]{:S(2)}, u32[]{:S(2)}) collective-permute-start(bf16[272,896]{1,0:T(8,128)(2,1)} %get-tuple-element.287), channel_id=1, source_target_pairs={{0,4},{2,6},{4,0},{6,2},{1,5},{3,7},{5,1},{7,3},{8,12},{10,14},{12... | collective-permute-start | bytes 1462280 | tf_op jit(solution)/shard_map/shares/ppermute | solution.py:37
  254.1 27.8 %collective-permute-start.60 = (bf16[608,512]{1,0:T(8,128)(2,1)}, bf16[608,512]{1,0:T(8,128)(2,1)S(1)}, u32[]{:S(2)}, u32[]{:S(2)}) collective-permute-start(bf16[608,512]{1,0:T(8,128)(2,1)} %get-tuple-element.284.refs_1_), channel_id=1, source_target_pairs={{0,2},{2,0},{4,6},{6,4},{1,3},{3,1},{5,7},{7,5},{8,10},{10,8},{12,... | collective-permute-start | bytes 1867784 | tf_op jit(solution)/shard_map/all_g1/ppermute | solution.py:37
  270.6 20.4 %collective-permute-start.61 = (bf16[608,512]{1,0:T(8,128)(2,1)}, bf16[608,512]{1,0:T(8,128)(2,1)S(1)}, u32[]{:S(2)}, u32[]{:S(2)}) collective-permute-start(bf16[608,512]{1,0:T(8,128)(2,1)} %get-tuple-element.284.refs_1_), channel_id=1, source_target_pairs={{0,4},{2,6},{4,0},{6,2},{1,5},{3,7},{5,1},{7,3},{8,12},{10,14},{12... | collective-permute-start | bytes 1867784 | tf_op jit(solution)/shard_map/all_g1/ppermute | solution.py:37
  271.7 20.2 %collective-permute-start.64 = (bf16[272,896]{1,0:T(8,128)(2,1)}, bf16[272,896]{1,0:T(8,128)(2,1)S(1)}, u32[]{:S(2)}, u32[]{:S(2)}) collective-permute-start(bf16[272,896]{1,0:T(8,128)(2,1)} %get-tuple-element.288), channel_id=1, source_target_pairs={{0,6},{2,4},{4,2},{6,0},{1,7},{3,5},{5,3},{7,1},{8,14},{10,12},{12... | collective-permute-start | bytes 1462280 | tf_op jit(solution)/shard_map/shares/ppermute | solution.py:37
  272.5 23.8 %collective-permute-start.55 = (bf16[608,512]{1,0:T(8,128)(2,1)}, bf16[608,512]{1,0:T(8,128)(2,1)S(1)}, u32[]{:S(2)}, u32[]{:S(2)}) collective-permute-start(bf16[608,512]{1,0:T(8,128)(2,1)} %get-tuple-element.281.refs_1_), channel_id=1, source_target_pairs={{8,16},{16,8},{9,17},{17,9},{10,18},{18,10},{11,19},{19,11},{12,20... | collective-permute-start | bytes 1867784 | tf_op jit(solution)/shard_map/u1_hop1/ppermute | solution.py:79
  273.2 23.0 %collective-permute-start.57 = (bf16[608,384]{1,0:T(8,128)(2,1)S(1)}, bf16[608,384]{1,0:T(8,128)(2,1)S(1)}, u32[]{:S(2)}, u32[]{:S(2)}) collective-permute-start(bf16[608,384]{1,0:T(8,128)(2,1)S(1)} %get-tuple-element.283.refs_6_), channel_id=1, source_target_pairs={{8,0},{16,24},{9,1},{17,25},{10,2},{18,26},{11,3},{19,27},{12,4},{... | collective-permute-start | bytes 1400840 | tf_op jit(solution)/shard_map/g2_hop2/ppermute | solution.py:79
  281.9 23.4 %collective-permute-start.68 = (bf16[896,256]{1,0:T(8,128)(2,1)S(1)}, bf16[896,256]{1,0:T(8,128)(2,1)S(1)}, u32[]{:S(2)}, u32[]{:S(2)}) collective-permute-start(bf16[896,256]{1,0:T(8,128)(2,1)S(1)} %get-tuple-element.293), channel_id=1, source_target_pairs={{0,1},{1,0},{2,3},{3,2},{4,5},{5,4},{6,7},{7,6},{8,9},{9,8},{10,11... | collective-permute-start | bytes 1376264 | tf_op jit(solution)/shard_map/normed_core/ppermute | solution.py:37
  291.0 15.0 %collective-permute-start.69 = (bf16[304,512]{1,0:T(8,128)(2,1)S(1)}, bf16[304,512]{1,0:T(8,128)(2,1)S(1)}, u32[]{:S(2)}, u32[]{:S(2)}) collective-permute-start(bf16[304,512]{1,0:T(8,128)(2,1)S(1)} %slice.110), channel_id=1, source_target_pairs={{0,4},{2,6},{4,0},{6,2},{1,5},{3,7},{5,1},{7,3},{8,12},{10,14},{12... | collective-permute-start | bytes 933896 | tf_op jit(solution)/shard_map/all_g1_relay/ppermute | solution.py:37
  291.9 15.1 %collective-permute-start.70 = (bf16[304,512]{1,0:T(8,128)(2,1)S(1)}, bf16[304,512]{1,0:T(8,128)(2,1)S(1)}, u32[]{:S(2)}, u32[]{:S(2)}) collective-permute-start(bf16[304,512]{1,0:T(8,128)(2,1)S(1)} %slice.111), channel_id=1, source_target_pairs={{0,2},{2,0},{4,6},{6,4},{1,3},{3,1},{5,7},{7,5},{8,10},{10,8},{12,... | collective-permute-start | bytes 933896 | tf_op jit(solution)/shard_map/all_g1_relay/ppermute | solution.py:37
  299.4 18.9 %collective-permute-start.67 = (bf16[608,512]{1,0:T(8,128)(2,1)}, bf16[608,512]{1,0:T(8,128)(2,1)S(1)}, u32[]{:S(2)}, u32[]{:S(2)}) collective-permute-start(bf16[608,512]{1,0:T(8,128)(2,1)} %get-tuple-element.291.refs_6_), channel_id=1, source_target_pairs={{8,0},{16,24},{9,1},{17,25},{10,2},{18,26},{11,3},{19,27},{12,4},{... | collective-permute-start | bytes 1867784 | tf_op jit(solution)/shard_map/u1_hop2/ppermute | solution.py:79
  300.6 17.6 %collective-permute-start.66 = (bf16[272,896]{1,0:T(8,128)(2,1)S(1)}, bf16[272,896]{1,0:T(8,128)(2,1)S(1)}, u32[]{:S(2)}, u32[]{:S(2)}) collective-permute-start(bf16[272,896]{1,0:T(8,128)(2,1)S(1)} %get-tuple-element.290.refs_3_), channel_id=1, source_target_pairs={{0,8},{24,16},{1,9},{25,17},{2,10},{26,18},{3,11},{27,19},{4,12},{... | collective-permute-start | bytes 1462280 | tf_op jit(solution)/shard_map/share_hop0/ppermute | solution.py:79
  322.3 22.6 %collective-permute-start.78 = (bf16[608,512]{1,0:T(8,128)(2,1)}, bf16[608,512]{1,0:T(8,128)(2,1)S(1)}, u32[]{:S(2)}, u32[]{:S(2)}) collective-permute-start(bf16[608,512]{1,0:T(8,128)(2,1)} %get-tuple-element.298.refs_1_), channel_id=1, source_target_pairs={{0,2},{2,0},{4,6},{6,4},{1,3},{3,1},{5,7},{7,5},{8,10},{10,8},{12,... | collective-permute-start | bytes 1867784 | tf_op jit(solution)/shard_map/all_u1/ppermute | solution.py:37
  323.3 21.6 %collective-permute-start.79 = (bf16[608,512]{1,0:T(8,128)(2,1)}, bf16[608,512]{1,0:T(8,128)(2,1)S(1)}, u32[]{:S(2)}, u32[]{:S(2)}) collective-permute-start(bf16[608,512]{1,0:T(8,128)(2,1)} %get-tuple-element.298.refs_1_), channel_id=1, source_target_pairs={{0,4},{2,6},{4,0},{6,2},{1,5},{3,7},{5,1},{7,3},{8,12},{10,14},{12... | collective-permute-start | bytes 1867784 | tf_op jit(solution)/shard_map/all_u1/ppermute | solution.py:37
  323.8 21.1 %collective-permute-start.74 = (bf16[272,896]{1,0:T(8,128)(2,1)S(1)}, bf16[272,896]{1,0:T(8,128)(2,1)S(1)}, u32[]{:S(2)}, u32[]{:S(2)}) collective-permute-start(bf16[272,896]{1,0:T(8,128)(2,1)S(1)} %get-tuple-element.296.refs_1_), channel_id=1, source_target_pairs={{8,16},{16,8},{9,17},{17,9},{10,18},{18,10},{11,19},{19,11},{12,20... | collective-permute-start | bytes 1462280 | tf_op jit(solution)/shard_map/share_hop1/ppermute | solution.py:79
  324.5 11.8 %collective-permute-start.76 = (bf16[304,384]{1,0:T(8,128)(2,1)S(1)}, bf16[304,384]{1,0:T(8,128)(2,1)S(1)}, u32[]{:S(2)}, u32[]{:S(2)}) collective-permute-start(bf16[304,384]{1,0:T(8,128)(2,1)S(1)} %slice.112), channel_id=1, source_target_pairs={{0,4},{2,6},{4,0},{6,2},{1,5},{3,7},{5,1},{7,3},{8,12},{10,14},{12... | collective-permute-start | bytes 700424 | tf_op jit(solution)/shard_map/all_g2_relay/ppermute | solution.py:37
  326.1 18.8 %collective-permute-start.75 = (bf16[608,384]{1,0:T(8,128)(2,1)S(1)}, bf16[608,384]{1,0:T(8,128)(2,1)S(1)}, u32[]{:S(2)}, u32[]{:S(2)}) collective-permute-start(bf16[608,384]{1,0:T(8,128)(2,1)S(1)} %get-tuple-element.297.refs_6_.refs_4_), channel_id=1, source_target_pairs={{8,0},{16,24},{9,1},{17,25},{10,2},{18,26},{11,3},{19,27},{12,4},{... | collective-permute-start | bytes 1400840 | tf_op jit(solution)/shard_map/u2_hop2/ppermute | solution.py:79
  346.5 18.5 %collective-permute-start.80 = (bf16[272,896]{1,0:T(8,128)(2,1)S(1)}, bf16[272,896]{1,0:T(8,128)(2,1)S(1)}, u32[]{:S(2)}, u32[]{:S(2)}) collective-permute-start(bf16[272,896]{1,0:T(8,128)(2,1)S(1)} %get-tuple-element.299.refs_6_.refs_2_), channel_id=1, source_target_pairs={{8,0},{16,24},{9,1},{17,25},{10,2},{18,26},{11,3},{19,27},{12,4},{... | collective-permute-start | bytes 1462280 | tf_op jit(solution)/shard_map/share_hop2/ppermute | solution.py:79
  347.8 17.2 %collective-permute-start.83 = (bf16[608,384]{1,0:T(8,128)(2,1)S(1)}, bf16[608,384]{1,0:T(8,128)(2,1)S(1)}, u32[]{:S(2)}, u32[]{:S(2)}) collective-permute-start(bf16[608,384]{1,0:T(8,128)(2,1)S(1)} %get-tuple-element.300.refs_1_), channel_id=1, source_target_pairs={{0,2},{2,0},{4,6},{6,4},{1,3},{3,1},{5,7},{7,5},{8,10},{10,8},{12,... | collective-permute-start | bytes 1400840 | tf_op jit(solution)/shard_map/all_u2/ppermute | solution.py:37
  348.8 16.1 %collective-permute-start.84 = (bf16[608,384]{1,0:T(8,128)(2,1)S(1)}, bf16[608,384]{1,0:T(8,128)(2,1)S(1)}, u32[]{:S(2)}, u32[]{:S(2)}) collective-permute-start(bf16[608,384]{1,0:T(8,128)(2,1)S(1)} %get-tuple-element.300.refs_1_), channel_id=1, source_target_pairs={{0,4},{2,6},{4,0},{6,2},{1,5},{3,7},{5,1},{7,3},{8,12},{10,14},{12... | collective-permute-start | bytes 1400840 | tf_op jit(solution)/shard_map/all_u2/ppermute | solution.py:37
  351.9 13.0 %collective-permute-start.82 = (bf16[304,512]{1,0:T(8,128)(2,1)S(1)}, bf16[304,512]{1,0:T(8,128)(2,1)S(1)}, u32[]{:S(2)}, u32[]{:S(2)}) collective-permute-start(bf16[304,512]{1,0:T(8,128)(2,1)S(1)} %slice.115), channel_id=1, source_target_pairs={{0,2},{2,0},{4,6},{6,4},{1,3},{3,1},{5,7},{7,5},{8,10},{10,8},{12,... | collective-permute-start | bytes 933896 | tf_op jit(solution)/shard_map/all_u1_relay/ppermute | solution.py:37
  366.7 12.0 %collective-permute-start.47 = (bf16[256,896]{1,0:T(8,128)(2,1)S(1)}, bf16[256,896]{1,0:T(8,128)(2,1)}, u32[]{:S(2)}, u32[]{:S(2)}) collective-permute-start(bf16[256,896]{1,0:T(8,128)(2,1)S(1)} %get-tuple-element.265), channel_id=1, source_target_pairs={{0,1},{1,0},{2,3},{3,2},{4,5},{5,4},{6,7},{7,6},{8,9},{9,8},{10,11... | collective-permute-start | bytes 1376264 | tf_op jit(solution)/shard_map/rows_core/ppermute | solution.py:37
  366.7 15.8 %collective-permute-start.73 = (bf16[256,896]{1,0:T(8,128)(2,1)S(1)}, bf16[256,896]{1,0:T(8,128)(2,1)}, u32[]{:S(2)}, u32[]{:S(2)}) collective-permute-start(bf16[256,896]{1,0:T(8,128)(2,1)S(1)} %get-tuple-element.295), channel_id=1, source_target_pairs={{0,1},{1,0},{2,3},{3,2},{4,5},{5,4},{6,7},{7,6},{8,9},{9,8},{10,11... | collective-permute-start | bytes 1376264 | tf_op jit(solution)/shard_map/rows_core/ppermute | solution.py:37
  367.2 28.5 %collective-permute-start.86 = (bf16[272,896]{1,0:T(8,128)(2,1)S(1)}, bf16[272,896]{1,0:T(8,128)(2,1)}, u32[]{:S(2)}, u32[]{:S(2)}) collective-permute-start(bf16[272,896]{1,0:T(8,128)(2,1)S(1)} %step_kernel.17.refs_1_.refs_6_), channel_id=1, source_target_pairs={{0,4},{2,6},{4,0},{6,2},{1,5},{3,7},{5,1},{7,3},{8,12},{10,14},{12... | collective-permute-start | bytes 1462280 | tf_op jit(solution)/shard_map/all_share/ppermute | solution.py:37
  376.5 22.9 %collective-permute-start.87 = (bf16[272,896]{1,0:T(8,128)(2,1)S(1)}, bf16[272,896]{1,0:T(8,128)(2,1)}, u32[]{:S(2)}, u32[]{:S(2)}) collective-permute-start(bf16[272,896]{1,0:T(8,128)(2,1)S(1)} %collective-permute-done.85.refs_2_.refs_6_), channel_id=1, source_target_pairs={{0,4},{2,6},{4,0},{6,2},{1,5},{3,7},{5,1},{7,3},{8,12},{10,14},{12... | collective-permute-start | bytes 1462280 | tf_op jit(solution)/shard_map/all_share_relay/ppermute | solution.py:37
  376.6 19.1 %collective-permute-start.89 = (bf16[304,384]{1,0:T(8,128)(2,1)S(1)}, bf16[304,384]{1,0:T(8,128)(2,1)S(1)}, u32[]{:S(2)}, u32[]{:S(2)}) collective-permute-start(bf16[304,384]{1,0:T(8,128)(2,1)S(1)} %slice.118), channel_id=1, source_target_pairs={{0,4},{2,6},{4,0},{6,2},{1,5},{3,7},{5,1},{7,3},{8,12},{10,14},{12... | collective-permute-start | bytes 700424 | tf_op jit(solution)/shard_map/all_u2_relay/ppermute | solution.py:37
  378.7 17.0 %collective-permute-start.90 = (bf16[304,384]{1,0:T(8,128)(2,1)S(1)}, bf16[304,384]{1,0:T(8,128)(2,1)S(1)}, u32[]{:S(2)}, u32[]{:S(2)}) collective-permute-start(bf16[304,384]{1,0:T(8,128)(2,1)S(1)} %slice.119), channel_id=1, source_target_pairs={{0,2},{2,0},{4,6},{6,4},{1,3},{3,1},{5,7},{7,5},{8,10},{10,8},{12,... | collective-permute-start | bytes 700424 | tf_op jit(solution)/shard_map/all_u2_relay/ppermute | solution.py:37
  (119 other events, 883.9 us)

commit v3 on v2

--- a/solution.py
+++ b/solution.py
@@ -16,7 +16,7 @@
 
 low = jnp.bfloat16
 wide = jnp.float32
-vmem_limit = 50 * 1024 * 1024
+vmem_limit = 40 * 1024 * 1024
 
 
 def dot_nn(left, right):
@@ -73,16 +73,20 @@
     return [pieces[0]] + [partner(pieces[r], "blk", r, name) for r in range(1, len(pieces))]
 
 
-def hop(value, stage, name):
-    routes = ([(0, 1), (3, 2)], [(1, 2), (2, 1)], [(1, 0), (2, 3)])
-    with jax.named_scope(f"{name}_hop{stage}"):
-        return lax.ppermute(value, "dp", routes[stage])
-
-
-def call(body, outs, ins, scratch=(), in_specs=None, after=(), carry=()):
+def swap(value, name):
+    with jax.named_scope(name):
+        return lax.ppermute(value, "dp", [(0, 1), (1, 0), (2, 3), (3, 2)])
+
+
+def cross(value, name):
+    with jax.named_scope(name):
+        return lax.ppermute(value, "dp", [(1, 2), (2, 1)])
+
+
+def call(body, outs, ins, scratch=(), in_specs=None, after=(), carry=(), moves=None):
+    anywhere = pl.BlockSpec(memory_space=pl.ANY)
     whole = pl.BlockSpec(memory_space=pltpu.VMEM)
-    anywhere = pl.BlockSpec(memory_space=pl.ANY)
-    in_specs = list(in_specs or [whole] * len(ins))
+    in_specs = list(in_specs or [anywhere if moves else whole] * len(ins))
     given, waited, made = len(ins), len(after) + len(carry), len(outs)
 
     def run(*refs):
@@ -94,7 +98,7 @@
         name=getattr(body, "func", body).__name__,
         out_shape=tuple(outs) + tuple(shape(value.shape, value.dtype) for value in carry),
         in_specs=in_specs + [anywhere] * waited,
-        out_specs=tuple([whole] * made + [anywhere] * len(carry)),
+        out_specs=tuple([anywhere if moves == "all" else whole] * made + [anywhere] * len(carry)),
         scratch_shapes=list(scratch),
         input_output_aliases={given + len(after) + i: made + i for i in range(len(carry))},
         cost_estimate=pl.CostEstimate(flops=0, bytes_accessed=0, transcendentals=0),
@@ -257,17 +261,16 @@
 def hidden_kernel(parts, *refs):
     gy_refs, x_refs, refs = refs[: 2 * parts], refs[2 * parts : 4 * parts], refs[4 * parts :]
     gate_t_ref, up_t_ref, down_ref, gate_ref, up_ref = refs[:5]
-    x_ref, gy_ref, mixed_ref, grad_gate_ref, grad_up_ref, other_ref, mine_ref = refs[5:]
+    mixed_ref, grad_gate_ref, grad_up_ref, other_ref, mine_ref, x_ref, gy_ref = refs[5:]
     half = other_ref.shape[1]
+    row = 0
     for k in range(2):
         at = 0
-        for part in x_refs[k * parts : (k + 1) * parts]:
-            x_ref[at : at + part.shape[0], k * half : (k + 1) * half] = part[...]
-            at += part.shape[0]
-    at = 0
-    for part in gy_refs:
-        gy_ref[at : at + part.shape[0], :] = part[...]
-        at += part.shape[0]
+        for x, gy in zip(x_refs[k * parts : (k + 1) * parts], gy_refs[k * parts : (k + 1) * parts]):
+            x_ref[at : at + x.shape[0], k * half : (k + 1) * half] = x[...]
+            gy_ref[row : row + gy.shape[0], :] = gy[...]
+            at += x.shape[0]
+            row += gy.shape[0]
     x = x_ref[...]
     gate = dot_nn(gate_t_ref[...], x)
     up = dot_nn(up_t_ref[...], x)
@@ -284,37 +287,38 @@
     mine_ref[...] = back[:, half:]
 
 
-def weight_kernel(transposed, *refs):
-    pairs, out_refs = refs[:-2], refs[-2:]
+def weight_kernel(transposed, first, counts, outputs, *refs):
+    blocks = len(counts)
+    lefts, parts, out_refs, right_ref = refs[:blocks], refs[blocks : -outputs - 1], refs[-outputs - 1 : -1], refs[-1]
+    units = lefts[0].shape[0]
+    columns = sum(ref.shape[0] for ref in out_refs) // units * 128
+    last = first + columns
+    total, at = None, 0
+    for r in range(blocks):
+        row = 0
+        for k in range(2):
+            place = 0
+            for part in parts[at : at + counts[r]]:
+                if transposed:
+                    half = part.shape[1]
+                    start, end = max(place, first), min(place + part.shape[0], last)
+                    if start < end:
+                        right_ref[r, start - first : end - first, k * half : (k + 1) * half] = part[
+                            start - place : end - place, :
+                        ]
+                    place += part.shape[0]
+                else:
+                    right_ref[r, row : row + part.shape[0], :] = part[:, first:last]
+                    row += part.shape[0]
+            at += counts[r]
+        left, right = lefts[r][...], right_ref[r]
+        product = dot_nt(left, right) if transposed else dot_nn(left, right)
+        total = product if total is None else total + product
     at = 0
     for out_ref in out_refs:
-        rows, columns = out_ref.shape
-        tile = rows // 2 if rows % 32 == 0 else rows
-        cols = slice(at, at + columns)
-        for t in range(0, rows, tile):
-            span = slice(t, t + tile)
-            total = None
-            for i in range(0, len(pairs), 2):
-                left = pairs[i][span, :]
-                part = dot_nt(left, pairs[i + 1][cols, :]) if transposed else dot_nn(left, pairs[i + 1][:, cols])
-                total = part if total is None else total + part
-            out_ref[span, :] = total.astype(low)
-        at += columns
-
-
-def wait_kernel(*refs):
-    pass
-
-
-def step_kernel(adds, place_ref, *refs):
-    count = len(refs) // 3
-    end = (place_ref[2] == 0) | (place_ref[2] == 3)
-    for i in range(count):
-        left, right, out_ref = refs[2 * i], refs[2 * i + 1], refs[2 * count + i]
-        if i < adds:
-            out_ref[...] = (left[...].astype(wide) + right[...].astype(wide)).astype(low)
-        else:
-            out_ref[...] = jnp.where(end, left[...], right[...])
+        for t in range(out_ref.shape[0] // units):
+            out_ref[t * units : (t + 1) * units, :] = total[:, at : at + 128].astype(low)
+            at += 128
 
 
 def project_kernel(blocks, weight_ref, *refs):
@@ -329,8 +333,7 @@
 def add_kernel(*refs):
     count = (len(refs) - 1) // 2
     for i in range(count):
-        own = refs[1 + i][...] if len(refs[1 + i].shape) == 2 else refs[1 + i][0]
-        refs[1 + count + i][...] = (own.astype(wide) + refs[0][i].astype(wide)).astype(low)
+        refs[1 + count + i][...] = (refs[1 + i][...].astype(wide) + refs[0][i].astype(wide)).astype(low)
 
 
 def pair_kernel(*refs):
@@ -339,10 +342,31 @@
         refs[2 * count + i][...] = (refs[2 * i][...].astype(wide) + refs[2 * i + 1][...].astype(wide)).astype(low)
 
 
-def sum_blocks(refs):
-    total = refs[0][...].astype(wide)
-    for ref in refs[1:]:
-        total = total + ref[...].astype(wide)
+def wait_kernel(*refs):
+    pass
+
+
+def tick_kernel(ops, place_ref, *refs):
+    ins, outs = refs[: -len(ops)], refs[-len(ops) :]
+    end = (place_ref[2] == 0) | (place_ref[2] == 3)
+    for (kind, args), out_ref in zip(ops, outs):
+        sources = [(ins if given else outs)[i] for given, i, *_ in args]
+        if kind == "add":
+            out_ref[...] = (sources[0][...].astype(wide) + sources[1][...].astype(wide)).astype(low)
+        elif kind == "pick":
+            out_ref[...] = jnp.where(end, sources[0][...], sources[1][...])
+        else:
+            at = 0
+            for source, (_, _, start, rows) in zip(sources, args):
+                out_ref[at : at + rows, :] = source[start : start + rows, :]
+                at += rows
+
+
+def sum_blocks(refs, starts=None, rows=None):
+    total = None
+    for i, ref in enumerate(refs):
+        value = ref[...] if starts is None else ref[starts[i] : starts[i] + rows, :]
+        total = value.astype(wide) if total is None else total + value.astype(wide)
     return total
 
 
@@ -382,11 +406,9 @@
 
 
 def attend_back_kernel(
-    blocks, first_head, earlier, lengths_ref, place_ref, go_ref, delta_ref, log_ref, q_ref, cos_ref, sin_ref, *refs,
+    blocks, lengths_ref, place_ref, go_ref, delta_ref, log_ref, q_ref, cos_ref, sin_ref, *refs,
 ):
     kv_refs, refs = refs[:blocks], refs[blocks:]
-    if earlier:
-        earlier_refs, refs = refs[:blocks], refs[blocks:]
     (grad_q_ref, *grad_kv_refs), refs = refs[: blocks + 1], refs[blocks + 1 :]
     kv_ref, bias_ref, dq_ref, dk_ref, dv_ref, grad_kv_ref = refs
     rows = q_ref.shape[1]
@@ -394,10 +416,7 @@
     own = place_ref[0]
     for r in range(blocks):
         kv_ref[r] = kv_refs[r][...]
-        if earlier:
-            grad_kv_ref[r] = earlier_refs[r][...].astype(wide)
-        else:
-            grad_kv_ref[r] = jnp.zeros_like(grad_kv_ref[r])
+        grad_kv_ref[r] = jnp.zeros_like(grad_kv_ref[r])
     dq_ref[...] = jnp.zeros_like(dq_ref)
     q_index = own * rows + lax.broadcasted_iota(jnp.int32, (1, rows), 1)
     q_start = segment_start(lengths_ref, q_index)
@@ -408,36 +427,35 @@
         values = pair[:, HEAD_DIM:]
         keys_t = pair.astype(wide).T[:HEAD_DIM].astype(low)
         bias_ref[...] = mask_bias(block * rows, rows, q_index, q_start)
-        for i in range(heads):
-            h = first_head + i
+        for h in range(heads):
             span = slice(h * HEAD_DIM, (h + 1) * HEAD_DIM)
             scores = dot_nn(keys, q_ref[span, :]) + bias_ref[...]
             weight = jnp.exp(scores - log_ref[h : h + 1, :])
             grad_weight = dot_nn(values, go_ref[span, :])
             grad_scores = (weight * (grad_weight - delta_ref[h : h + 1, :])).astype(low)
-            dq_ref[i * HEAD_DIM : (i + 1) * HEAD_DIM, :] += dot_nn(keys_t, grad_scores)
+            dq_ref[span, :] += dot_nn(keys_t, grad_scores)
             dk = dot_nt(grad_scores, q_ref[span, :])
             dv = dot_nt(weight.astype(low), go_ref[span, :])
-            if i == 0:
+            if h == 0:
                 dk_ref[...] = dk
                 dv_ref[...] = dv
             else:
                 dk_ref[...] += dk
                 dv_ref[...] += dv
-        grad_kv_ref[block ^ own] += jnp.concatenate([dk_ref[...], dv_ref[...]], axis=1)
+        grad_kv_ref[block ^ own] = jnp.concatenate([dk_ref[...], dv_ref[...]], axis=1).astype(low)
         return carry
 
     lax.fori_loop(first_row(lengths_ref, own * rows) // rows, own + 1, visit, 0)
     for r in range(blocks):
-        grad_kv_refs[r][...] = grad_kv_ref[r].astype(grad_kv_refs[r].dtype)
-    for i in range(heads):
-        span = slice(i * HEAD_DIM, (i + 1) * HEAD_DIM)
+        grad_kv_refs[r][...] = grad_kv_ref[r]
+    for h in range(heads):
+        span = slice(h * HEAD_DIM, (h + 1) * HEAD_DIM)
         turned = rotate(dq_ref[span, :] * HEAD_DIM**-0.5, cos_ref[...], -sin_ref[...])
         grad_q_ref[span, :] = turned.astype(low)
 
 
 def query_kernel(
-    place_ref, normed_ref, grad_q_a_ref, grad_q_b_ref, wq_ref, gm_mine_ref, gm_other_ref, out_ref,
+    place_ref, normed_ref, grad_q_ref, wq_ref, gm_mine_ref, gm_other_ref, out_ref,
     grad_wq_ref, part_ref, grad_bq_ref, grad_w_out_ref, gm_ref,
 ):
     half = gm_mine_ref.shape[1]
@@ -445,18 +463,18 @@
     gm_ref[:, pl.ds(pl.multiple_of(core * half, half), half)] = gm_mine_ref[...]
     gm_ref[:, pl.ds(pl.multiple_of((1 - core) * half, half), half)] = gm_other_ref[...]
     grad_w_out_ref[...] = dot_nt(out_ref[...].astype(low), gm_ref[...]).astype(low)
-    grad_q = jnp.concatenate([grad_q_a_ref[...], grad_q_b_ref[...]], axis=0)
+    grad_q = grad_q_ref[...]
     grad_wq_ref[...] = dot_nt(grad_q, normed_ref[...]).astype(low)
     part_ref[...] = dot_tn(wq_ref[...], grad_q)
     grad_bq_ref[...] = dot_nt(jnp.ones((16, grad_q.shape[1]), low), grad_q)
 
 
 def key_kernel(
-    blocks, place_ref, normed_ref, tokens_ref, part_ref, wk_ref, wv_ref, cos_ref, sin_ref,
+    blocks, starts, place_ref, normed_ref, tokens_ref, part_ref, wk_ref, wv_ref, cos_ref, sin_ref,
     grad_wq_ref, grad_bq_ref, grad_w_out_ref, grad_gain_two_ref, *refs,
 ):
     kv_refs, share_refs, (mine_ref, other_ref, sum_ref, pack_ref) = refs[:blocks], refs[blocks : 2 * blocks], refs[2 * blocks :]
-    both = sum_blocks(kv_refs).T
+    both = sum_blocks(kv_refs, starts, tokens_ref.shape[1]).T
     both = jnp.concatenate(
         [rotate(both[:HEAD_DIM], cos_ref[...], -sin_ref[...]), both[HEAD_DIM:]], axis=0
     ).astype(low)
@@ -489,24 +507,22 @@
     share = pack_ref.shape[0] // blocks
     for r in range(blocks):
         start = pl.multiple_of((place_ref[0] ^ r) * share, share)
-        share_refs[r][...] = pack_ref[pl.ds(start, share), :]
-
-
-def share_kernel(*refs):
-    refs[-1][...] = sum_blocks(refs[:-1]).astype(low)
-
-
-def unpack_kernel(counts, place_ref, *refs):
-    total = sum(counts)
-    pieces, outs, pack_ref = refs[:total], refs[total:-1], refs[-1]
-    share = pack_ref.shape[0] // len(counts)
-    at = 0
-    for r, count in enumerate(counts):
-        start = (place_ref[0] ^ r) * share
-        for ref in pieces[at : at + count]:
-            pack_ref[pl.ds(pl.multiple_of(start, 8), ref.shape[0]), :] = ref[...].astype(wide)
-            start = start + ref.shape[0]
-        at += count
+        for t in range(width // 128):
+            share_refs[r][t * share : (t + 1) * share, :] = pack_ref[pl.ds(start, share), t * 128 : (t + 1) * 128]
+
+
+def share_kernel(starts, *refs):
+    refs[-1][...] = sum_blocks(refs[:-1], starts, refs[-1].shape[0]).astype(low)
+
+
+def unpack_kernel(share, sources, place_ref, *refs):
+    pieces, outs, (stack_ref, pack_ref) = refs[: len(sources)], refs[len(sources) : -2], refs[-2:]
+    for ref, (r, first, rows, start) in zip(pieces, sources):
+        stack_ref[r, first : first + rows, :] = ref[start : start + rows, :].astype(wide)
+    for r in range(stack_ref.shape[0]):
+        at = pl.ds(pl.multiple_of((place_ref[0] ^ r) * share, 8), share)
+        for t in range(stack_ref.shape[1] // share):
+            pack_ref[at, t * 128 : (t + 1) * 128] = stack_ref[r, t * share : (t + 1) * share, :]
     at = 0
     for out_ref in outs:
         out_ref[...] = pack_ref[at : at + out_ref.shape[0], :]
@@ -523,37 +539,52 @@
     out_ref[...] = grad.T.astype(low)
 
 
-def put_pieces(counts, place_ref, refs, all_ref):
-    rows = all_ref.shape[0] // len(counts)
-    at = 0
-    for r, count in enumerate(counts):
-        start = (place_ref[0] ^ r) * rows
-        for ref in refs[at : at + count]:
-            all_ref[pl.ds(pl.multiple_of(start, 8), ref.shape[0]), :] = ref[...].astype(wide)
-            start = start + ref.shape[0]
-        at += count
-
-
-def rows_kernel(counts, place_ref, *refs):
-    put_pieces(counts, place_ref, refs[:-1], refs[-1])
-
-
-def columns_kernel(counts, place_ref, *refs):
-    put_pieces(counts, place_ref, refs[:-2], refs[-1])
-    refs[-2][...] = refs[-1][...].T
-
-
-def place_share(place, share, transposed, width, at, whole, last):
-    tile = 128
-    counts = [len(parts) for parts in share]
-    pieces = sum(share, [])
-    whole_rows = sum(p.shape[0] for p in pieces)
+def place_kernel(transposed, tiles, place_ref, *refs):
+    own_ref, near_x_ref, near_y_ref, *far_refs = refs[:7]
+    out_ref = refs[-2] if transposed else refs[-1]
+    all_ref = refs[-1]
+    step = pl.program_id(0)
+    units = own_ref.shape[0]
+    half = units // 2
+    for r, ref in enumerate((own_ref, near_x_ref, near_y_ref)):
+        start = pl.multiple_of((place_ref[0] ^ r) * units, 8)
+        all_ref[pl.ds(start, units), :] = ref[...].astype(wide)
+    for k in range(2):
+        start = pl.multiple_of((place_ref[0] ^ 3) * units + k * half, 8)
+        part = 2 * step + k
+
+        @pl.when(part < tiles)
+        def _(start=start, k=k):
+            all_ref[pl.ds(start, half), :] = far_refs[k][...].astype(wide)
+
+        @pl.when(part >= tiles)
+        def _(start=start, k=k):
+            all_ref[pl.ds(start, half), :] = far_refs[2 + k][...].astype(wide)
+
+    if transposed:
+        out_ref[...] = all_ref[...].T
+
+
+def place_share(place, own, near_x, near_y, far_y, far_x, units, transposed, width, at, whole, last):
+    tile, half = 128, units // 2
+    tiles = own.shape[0] // units
     first = at // tile
-    total = len(pieces)
-    ins = [place] + pieces + last
+    piece = pl.BlockSpec((units, tile), lambda i: (i, 0))
+
+    def halves(start, k, later):
+        base = start // half
+
+        def index(i):
+            part = 2 * i + k - (tiles if later else 0)
+            return (base + jnp.clip(part, 0, tiles - 1), 0)
+
+        return pl.BlockSpec((half, tile), index)
+
+    ins = [place, own, near_x, near_y, far_y[0], far_y[0], far_x[0], far_x[0]] + last
     specs = (
-        [in_smem]
-        + [pl.BlockSpec((p.shape[0], tile), lambda i: (0, i)) for p in pieces]
+        [in_smem, piece, piece, piece]
+        + [halves(far_y[1], k, False) for k in range(2)]
+        + [halves(far_x[1], k, True) for k in range(2)]
         + [pl.BlockSpec(memory_space=pl.ANY)] * len(last)
     )
     aliases = {}
@@ -561,24 +592,23 @@
         aliases = {len(ins): 0}
         ins.append(whole)
         specs.append(pl.BlockSpec(memory_space=pl.ANY))
-    kernel = columns_kernel if transposed else rows_kernel
 
     def body(*refs):
-        kernel(counts, *refs[: total + 1], *refs[len(ins) :])
+        place_kernel(transposed, tiles, *refs[:8], *refs[len(ins) :])
 
     if transposed:
-        dims = (width, whole_rows)
-        out_spec = pl.BlockSpec((tile, whole_rows), lambda i: (i + first, 0))
-        scratch = [pltpu.VMEM((whole_rows, tile), wide)]
+        dims = (width, 4 * units)
+        out_spec = pl.BlockSpec((tile, 4 * units), lambda i: (i + first, 0))
+        scratch = [pltpu.VMEM((4 * units, tile), wide)]
     else:
-        dims = (whole_rows, width)
-        out_spec = pl.BlockSpec((whole_rows, tile), lambda i: (0, i + first))
+        dims = (4 * units, width)
+        out_spec = pl.BlockSpec((4 * units, tile), lambda i: (0, i + first))
         scratch = []
     return pl.pallas_call(
         body,
-        name=kernel.__name__,
+        name="place_kernel",
         out_shape=shape(dims, wide),
-        grid=(pieces[0].shape[1] // tile,),
+        grid=(tiles,),
         in_specs=specs,
         out_specs=out_spec,
         scratch_shapes=scratch,
@@ -717,21 +747,26 @@
     def cores(parts, name):
         return [partner(part, "tensor", 1, name) for part in parts]
 
+    x_parts, gy_parts = [], []
+
     def hidden_units(r, x_mine, x_other, gy_mine, gy_other):
+        x_parts.append(x_other + x_mine)
+        gy_parts.append(gy_other + gy_mine)
         runs.append(
             ordered(
                 functools.partial(hidden_kernel, len(x_mine)),
-                [shape((width, rows), low), shape((rows, width), low), kept, kept, kept, piece, piece],
-                gy_other + gy_mine + x_other + x_mine + [gate_t, up_t, down_own, gate_own, up_own],
+                [kept, kept, kept, piece, piece],
+                gy_parts[-1] + x_parts[-1] + [gate_t, up_t, down_own, gate_own, up_own],
+                scratch=[pltpu.VMEM((width, rows), low), pltpu.VMEM((rows, width), low)],
             )
         )
-        return runs[-1][5]
+        return runs[-1][3]
 
     def add_back(members, carry, needs=()):
         results = ordered(
             pair_kernel,
             [piece] * len(members),
-            [value for r in members for value in (runs[r][6], passed[r])],
+            [value for r in members for value in (runs[r][4], passed[r])],
             needs=needs,
             carry=carry,
         )
@@ -739,20 +774,41 @@
             back[r] = partner(value, "blk", r, "back") if r else value
         return results[len(members) :]
 
-    def hidden_weight(transposed, left, right, cuts):
+    def hidden_weight(transposed, left, parts, first, shares):
+        counts = [len(part) // 2 for part in parts]
+        columns = sum(shares)
+        dims = (columns, rows) if transposed else (rows, columns)
         return ordered(
-            functools.partial(weight_kernel, transposed),
-            [shape((units, columns), low) for columns in cuts],
-            [run[k] for run in runs for k in (left, right)],
-        )
-
-    def step(adds, takes, needs=(), carry=()):
-        pairs = list(adds) + list(takes)
+            functools.partial(weight_kernel, transposed, first, counts, len(shares)),
+            [shape((share // 128 * units, 128), low) for share in shares],
+            [run[left] for run in runs] + sum(parts, []),
+            scratch=[pltpu.VMEM((blocks,) + dims, low)],
+        )
+
+    def tick(ops, needs=(), carry=()):
+        given, outs, listed = [], [], []
+        for kind, *args in ops:
+            spans = [arg if isinstance(arg, tuple) else (arg, 0, None) for arg in args]
+            named, size = [], 0
+            for value, start, count in spans:
+                if isinstance(value, int):
+                    entry, total = (False, value), outs[value].shape[0]
+                else:
+                    found = [i for i, known in enumerate(given) if known is value]
+                    if not found:
+                        given.append(value)
+                    entry = (True, found[0] if found else len(given) - 1)
+                    total = value.shape[0]
+                count = total if count is None else count
+                named.append(entry + (start, count))
+                size = size + count if kind == "cat" else count
+            listed.append((kind, named))
+            outs.append(shape((size, 128), low))
         return ordered(
-            functools.partial(step_kernel, len(adds)),
-            [shape(pair[0].shape, low) for pair in pairs],
-            [place] + [value for pair in pairs for value in pair],
-            in_specs=[in_smem] + [in_vmem] * (2 * len(pairs)),
+            functools.partial(tick_kernel, listed),
+            outs,
+            [place] + given,
+            in_specs=[in_smem] + [in_vmem] * len(given),
             needs=needs,
             carry=carry,
         )
@@ -785,29 +841,37 @@
             gy_mine[k], fars = fars[:count], fars[count:]
             x_other[k] = cores(x_mine[k], "x_core")
             gy_other[k] = cores(gy_mine[k], "gy_core")
-    d1, d2 = hidden_weight(False, 2, 1, [384, width - 384])
+    cut_at = width // 2 // 128 * 128
+    (d1,) = hidden_weight(False, 0, gy_parts, 0, [cut_at])
+    d1_swap = swap(d1, "swap_d1")
+    (d2,) = hidden_weight(False, 0, gy_parts, cut_at, [width - cut_at])
     layer_other, *layer_mine = ordered(
         functools.partial(project_kernel, blocks),
         [shape((blocks, width, half), low)] + [piece] * blocks,
-        [down_t] + [run[2] for run in runs],
-    )
-    d1, d2, layer_other = add_back([blocks - 1, 0], [d1, d2, layer_other], needs=back[1 : blocks - 1])
-    d1_in, d2_in = hop(d1, 0, "d1"), hop(d2, 0, "d2")
+        [down_t] + [run[0] for run in runs],
+    )
+    d2, layer_other = add_back(
+        [blocks - 1, 0], [d2, layer_other], needs=back[1 : blocks - 1] + [d1_swap]
+    )
+    (d1_sum,) = tick([("add", d1, d1_swap)])
+    d1_cross, d2_swap = cross(d1_sum, "cross_d1"), swap(d2, "swap_d2")
     layer_passed = partner(layer_other, "tensor", 1, "layer_core")
-    g1, g2 = hidden_weight(True, 3, 0, [512, width - 512])
-    u1, u2 = hidden_weight(True, 4, 0, [512, width - 512])
-    (d1,) = step([(d1, d1_in)], [], needs=back[1:])
+    g1, g2 = hidden_weight(True, 1, x_parts, 0, [cut_at, width - cut_at])
+    u1, u2 = hidden_weight(True, 2, x_parts, 0, [cut_at, width - cut_at])
+    d1_sum, d2_sum, d1_g1 = tick(
+        [("add", d1_sum, d1_cross), ("add", d2, d2_swap), ("pick", g1, 0)], needs=back[1:]
+    )
     grad_mid, grad_mid_low, grad_gain_two = ordered(
         grad_middle_kernel,
         [shape((width, half), wide), piece, shape((1, width), wide)],
         [hidden, gain_two, grad_y_mine] + back,
     )
-    *layer_pieces, grad_mid_low, d1, g1 = ordered(
-        add_kernel, [piece] * blocks, [layer_passed] + layer_mine, carry=[grad_mid_low, d1, g1]
+    *layer_pieces, grad_mid_low, d1_g1, d2_sum = ordered(
+        add_kernel, [piece] * blocks, [layer_passed] + layer_mine, carry=[grad_mid_low, d1_g1, d2_sum]
     )
     grad_mid_other = partner(grad_mid_low, "tensor", 1, "mid_core")
     layer_pieces = scatter_blocks(layer_pieces, "layer")
-    d1_in, g1_in = hop(d1, 1, "d1"), hop(g1, 0, "g1")
+    d1_g1_swap, d2_cross = swap(d1_g1, "swap_d1_g1"), cross(d2_sum, "cross_d2")
 
     grad_out, delta = ordered(
         back_enter_kernel,
@@ -817,134 +881,246 @@
         in_specs=[in_smem] + [in_vmem] * 4,
     )
 
-    def attend_back(first, count, earlier, kind):
-        return ordered(
-            functools.partial(attend_back_kernel, blocks, first, bool(earlier)),
-            [shape((count * HEAD_DIM, rows), low)] + [shape((rows, 2 * HEAD_DIM), kind)] * blocks,
-            [lengths, place, grad_out, delta, log_total, q_t, cosine, sine] + kv_blocks + earlier,
-            scratch=[
-                pltpu.VMEM((blocks, rows, 2 * HEAD_DIM), low),
-                pltpu.VMEM((rows, rows), wide),
-                pltpu.VMEM((count * HEAD_DIM, rows), wide),
-                pltpu.VMEM((rows, HEAD_DIM), wide),
-                pltpu.VMEM((rows, HEAD_DIM), wide),
-                pltpu.VMEM((blocks, rows, 2 * HEAD_DIM), wide),
-            ],
-            in_specs=[in_smem] * 2 + [in_vmem] * (6 + blocks + len(earlier)),
-        )
-
-    early_heads = (heads + 1) // 2
-    grad_q_a, *grad_kv = attend_back(0, early_heads, [], wide)
-    d1, d2 = step([(d1, d1_in), (d2, d2_in)], [], needs=layer_pieces[1:])
-    d1_in, d2_in = hop(d1, 2, "d1"), hop(d2, 1, "d2")
-    grad_q_b, *grad_kv = attend_back(early_heads, heads - early_heads, grad_kv, low)
-    d2, g1, d1, g2, *grad_kv = step(
-        [(d2, d2_in), (g1, g1_in)], [(d1_in, d1)], carry=[g2] + grad_kv
-    )
-    d1_all = gather_relayed(d1, "all_d1")
-    kv_pieces = scatter_blocks(grad_kv, "grad_kv")
-    d2_in, g1_in, g2_in = hop(d2, 2, "d2"), hop(g1, 1, "g1"), hop(g2, 0, "g2")
-    grad_w_query, normed_part, grad_b_query, grad_w_out = ordered(
-        query_kernel,
-        [
-            shape((q_width, width), low),
-            shape((width, rows), wide),
-            shape((16, q_width), wide),
-            shape((q_width, width), low),
+    grad_q, *grad_kv = ordered(
+        functools.partial(attend_back_kernel, blocks),
+        [shape((q_width, rows), low)] + [shape((rows, 2 * HEAD_DIM), low)] * blocks,
+        [lengths, place, grad_out, delta, log_total, q_t, cosine, sine] + kv_blocks,
+        scratch=[
+            pltpu.VMEM((blocks, rows, 2 * HEAD_DIM), low),
+            pltpu.VMEM((rows, rows), wide),
+            pltpu.VMEM((q_width, rows), wide),
+            pltpu.VMEM((rows, HEAD_DIM), wide),
+            pltpu.VMEM((rows, HEAD_DIM), wide),
+            pltpu.VMEM((blocks, rows, 2 * HEAD_DIM), low),
         ],
-        [place, normed_t, grad_q_a, grad_q_b, w_query.T, grad_mid_low, grad_mid_other, out_t],
-        scratch=[pltpu.VMEM((width, rows), low)],
-        in_specs=[in_smem] + [in_vmem] * 7,
-    )
-    (layer_half,) = ordered(layer_kernel, [shape((half, width), low)], [hidden] + layer_pieces)
-    g1, g2, d2, layer_half, u1 = step(
-        [(g1, g1_in), (g2, g2_in)], [(d2_in, d2)], needs=near(d1_all) + kv_pieces[1:], carry=[layer_half, u1]
-    )
-    d2_all = gather_relayed(d2, "all_d2")
-    g1_in, g2_in, u1_in = hop(g1, 2, "g1"), hop(g2, 1, "g2"), hop(u1, 0, "u1")
-    layer_out = whole_rows(layer_half)
+        in_specs=[in_smem] * 2 + [in_vmem] * (6 + blocks),
+    )
     pack_rows = -(-(2 * q_width + 2 * HEAD_DIM + 3) // (16 * blocks)) * 16 * blocks
     share = pack_rows // blocks
-    *shares, normed_mine, normed_other = ordered(
-        functools.partial(key_kernel, blocks),
-        [shape((share, width), low)] * blocks + [shape((width, half), wide), shape((width, half), low)],
-        [
-            place, normed_t, tokens_t, normed_part, w_key.T, w_value.T, cosine, sine,
-            grad_w_query, grad_b_query, grad_w_out, grad_gain_two,
-        ] + kv_pieces,
-        scratch=[pltpu.VMEM((width, rows), wide), pltpu.VMEM((pack_rows, width), low)],
-        in_specs=[in_smem] + [in_vmem] * (11 + blocks),
-    )
-    g2, u1, g1, u2, normed_other, *shares = step(
-        [(g2, g2_in), (u1, u1_in)],
-        [(g1_in, g1)],
-        needs=far(d1_all) + near(d2_all),
-        carry=[u2, normed_other] + shares,
-    )
-    g1_all = gather_relayed(g1, "all_g1")
-    shares = scatter_blocks(shares, "shares")
-    g2_in, u1_in, u2_in = hop(g2, 2, "g2"), hop(u1, 1, "u1"), hop(u2, 0, "u2")
-    normed_passed = partner(normed_other, "tensor", 1, "normed_core")
-    grad_w_down = place_share(place, d1_all, False, width, 0, None, last)
-    last = [grad_w_down]
-    (own_share,) = ordered(share_kernel, [shape((share, width), low)], shares)
-    u1, u2, g2, own_share = step(
-        [(u1, u1_in), (u2, u2_in)],
-        [(g2_in, g2)],
-        needs=far(d2_all) + near(g1_all),
-        carry=[own_share],
-    )
-    g2_all = gather_relayed(g2, "all_g2")
-    u1_in, u2_in, share_in = hop(u1, 2, "u1"), hop(u2, 1, "u2"), hop(own_share, 0, "share")
-    (grad_half,) = ordered(
-        leave_kernel,
-        [shape((half, width), low)],
-        [place, tokens_t, normed_mine, normed_passed, norm1_gain.reshape(1, width), grad_mid],
-        in_specs=[in_smem] + [in_vmem] * 5,
-    )
-    grad_w_down = place_share(place, d2_all, False, width, d1.shape[1], grad_w_down, [grad_half])
-    last = [grad_w_down]
-    u2, own_share, u1, grad_half = step(
-        [(u2, u2_in), (own_share, share_in)],
-        [(u1_in, u1)],
-        needs=far(g1_all) + near(g2_all),
-        carry=[grad_half],
-    )
-    u1_all = gather_relayed(u1, "all_u1")
-    u2_in, share_in = hop(u2, 2, "u2"), hop(own_share, 1, "share")
-    grad_tokens = whole_rows(grad_half).astype(wide)
-    grad_w_gate = place_share(place, g1_all, True, width, 0, None, last)
-    last = [grad_w_gate]
-    own_share, u2 = step(
-        [(own_share, share_in)], [(u2_in, u2)], needs=far(g2_all) + near(u1_all)
-    )
-    u2_all = gather_relayed(u2, "all_u2")
-    share_in = hop(own_share, 2, "share")
-    grad_w_gate = place_share(place, g2_all, True, width, g1.shape[1], grad_w_gate, last)
-    last = [grad_w_gate]
-    (own_share,) = step([], [(share_in, own_share)], needs=far(u1_all) + near(u2_all))
-    pieces = gather_relayed(own_share, "all_share")
-    grad_w_up = place_share(place, u1_all, True, width, 0, None, last)
-    last = [grad_w_up]
-    grad_w_up = place_share(
-        place, u2_all, True, width, u1.shape[1], grad_w_up, near(pieces)
-    )
-
-    counts = [len(parts) for parts in pieces]
-    small_rows = pack_rows - 2 * q_width - 2 * HEAD_DIM
-    grad_w_query, grad_w_key, grad_w_value, grad_w_out, small = call(
-        functools.partial(unpack_kernel, counts),
-        [
-            shape((q_width, width), wide),
-            shape((HEAD_DIM, width), wide),
-            shape((HEAD_DIM, width), wide),
-            shape((q_width, width), wide),
-            shape((small_rows, width), wide),
-        ],
-        [place] + sum(pieces, []),
-        [pltpu.VMEM((pack_rows, width), wide)],
-        in_specs=[in_smem] + [in_vmem] * sum(counts),
-    )
+    stack_rows = share * (width // 128)
+
+    def query_back():
+        return ordered(
+            query_kernel,
+            [
+                shape((q_width, width), low),
+                shape((width, rows), wide),
+                shape((16, q_width), wide),
+                shape((q_width, width), low),
+            ],
+            [place, normed_t, grad_q, w_query.T, grad_mid_low, grad_mid_other, out_t],
+            scratch=[pltpu.VMEM((width, rows), low)],
+            in_specs=[in_smem] + [in_vmem] * 6,
+        )
+
+    def key_back(kv_pieces, starts):
+        return ordered(
+            functools.partial(key_kernel, blocks, starts),
+            [shape((stack_rows, 128), low)] * blocks + [shape((width, half), wide), shape((width, half), low)],
+            [
+                place, normed_t, tokens_t, normed_part, w_key.T, w_value.T, cosine, sine,
+                grad_w_query, grad_b_query, grad_w_out, grad_gain_two,
+            ] + kv_pieces,
+            scratch=[pltpu.VMEM((width, rows), wide), pltpu.VMEM((pack_rows, width), low)],
+            in_specs=[in_smem] + [in_vmem] * (11 + blocks),
+        )
+
+    def sum_share(pieces, starts):
+        (own,) = ordered(
+            functools.partial(share_kernel, starts), [shape((stack_rows, 128), low)], pieces
+        )
+        return own
+
+    def leave(normed_mine, normed_passed):
+        (grad_half,) = ordered(
+            leave_kernel,
+            [shape((half, width), low)],
+            [place, tokens_t, normed_mine, normed_passed, norm1_gain.reshape(1, width), grad_mid],
+            in_specs=[in_smem] + [in_vmem] * 5,
+        )
+        return grad_half
+
+    def layer_leave():
+        (layer_half,) = ordered(layer_kernel, [shape((half, width), low)], [hidden] + layer_pieces)
+        return layer_half
+
+    def unpack(pieces, sources):
+        return ordered(
+            functools.partial(unpack_kernel, share, sources),
+            [
+                shape((q_width, width), wide),
+                shape((HEAD_DIM, width), wide),
+                shape((HEAD_DIM, width), wide),
+                shape((q_width, width), wide),
+                shape((pack_rows - 2 * q_width - 2 * HEAD_DIM, width), wide),
+            ],
+            [place] + pieces,
+            scratch=[pltpu.VMEM((blocks, stack_rows, 128), wide), pltpu.VMEM((pack_rows, width), wide)],
+            in_specs=[in_smem] + [in_vmem] * len(pieces),
+        )
+
+    if blocks != 4:
+        kv_pieces = scatter_blocks(grad_kv, "grad_kv")
+        grad_w_query, normed_part, grad_b_query, grad_w_out = query_back()
+        *shares, normed_mine, normed_other = key_back(kv_pieces, [0] * blocks)
+        layer_out = whole_rows(layer_leave())
+        grad_half = leave(normed_mine, partner(normed_other, "tensor", 1, "normed_core"))
+        own_share = sum_share(scatter_blocks(shares, "shares"), [0] * blocks)
+        own_share = lax.psum(own_share, "dp")
+        pieces = gather_blocks(own_share, "all_share")
+        grad_w_query, grad_w_key, grad_w_value, grad_w_out, small = unpack(
+            pieces, [(r, 0, stack_rows, 0) for r in range(blocks)]
+        )
+
+        def gather_weight(first, second, transposed):
+            stacked = lax.psum(jnp.concatenate([first, second], axis=0), "dp")
+            every = lax.all_gather(stacked, "blk").reshape(blocks, width // 128, units, 128)
+            order = (1, 3, 0, 2) if transposed else (0, 2, 1, 3)
+            dims = (width, blocks * units) if transposed else (blocks * units, width)
+            return every.transpose(order).reshape(dims).astype(wide)
+
+        grad_w_down = gather_weight(d1, d2, False)
+        grad_w_gate = gather_weight(g1, g2, True)
+        grad_w_up = gather_weight(u1, u2, True)
+    else:
+        r1, r2 = d1.shape[0], d2.shape[0]
+        h1, h2 = r1 // 2, r2 // 2
+
+        def both_ways(x_buffer, y_buffer, name):
+            return partner(x_buffer, "blk", 1, name + "_x"), partner(y_buffer, "blk", 2, name + "_y")
+
+        d1_all, g1_sum, d2_sum, d2_g2, x1, y1, kv_far = tick(
+            [
+                ("pick", d1_g1_swap, d1_sum),
+                ("add", g1, d1_g1_swap),
+                ("add", d2_sum, d2_cross),
+                ("pick", g2, 2),
+                ("cat", 0, grad_kv[1]),
+                ("cat", 0, grad_kv[2]),
+            ],
+            needs=layer_pieces[1:],
+            carry=[grad_kv[3]],
+        )
+        x1, y1 = both_ways(x1, y1, "d1")
+        kv_far = partner(kv_far, "blk", 3, "grad_kv")
+        d2_g2_swap, g1_cross = swap(d2_g2, "swap_d2_g2"), cross(g1_sum, "cross_g1")
+        grad_w_query, normed_part, grad_b_query, grad_w_out = query_back()
+        layer_half = layer_leave()
+        d2_all, g2_sum, g1_sum, g1_u1, x2, y2, layer_half = tick(
+            [
+                ("pick", d2_g2_swap, d2_sum),
+                ("add", g2, d2_g2_swap),
+                ("add", g1_sum, g1_cross),
+                ("pick", u1, 2),
+                ("cat", 0, (y1, h1, h1)),
+                ("cat", 0, (x1, 0, h1)),
+            ],
+            needs=[x1, y1, kv_far],
+            carry=[layer_half],
+        )
+        x2, y2 = both_ways(x2, y2, "d2")
+        g1_u1_swap, g2_cross = swap(g1_u1, "swap_g1_u1"), cross(g2_sum, "cross_g2")
+        layer_out = whole_rows(layer_half)
+        *shares, normed_mine, normed_other = key_back([grad_kv[0], x1, y1, kv_far], [0, r1, r1, 0])
+        g1_all, u1_sum, g2_sum, g2_u2, x3, y3, share_far, normed_other = tick(
+            [
+                ("pick", g1_u1_swap, g1_sum),
+                ("add", u1, g1_u1_swap),
+                ("add", g2_sum, g2_cross),
+                ("pick", u2, 2),
+                ("cat", 0, (y2, h2, h2), shares[1]),
+                ("cat", 0, (x2, 0, h2), shares[2]),
+            ],
+            needs=[x2, y2],
+            carry=[shares[3], normed_other],
+        )
+        x3, y3 = both_ways(x3, y3, "g1")
+        share_far = partner(share_far, "blk", 3, "shares")
+        g2_u2_swap, u1_cross = swap(g2_u2, "swap_g2_u2"), cross(u1_sum, "cross_u1")
+        normed_passed = partner(normed_other, "tensor", 1, "normed_core")
+        grad_w_down = place_share(
+            place, d1_all, x1, y1, (y2, r2), (x2, r2), units, False, width, 0, None, last
+        )
+        last = [grad_w_down]
+        grad_half = leave(normed_mine, normed_passed)
+        own_share = sum_share([shares[0], x3, y3, share_far], [0, r1 + h2, r1 + h2, 0])
+        g2_all, u2_sum, u1_sum, x4, y4, own_share, grad_half = tick(
+            [
+                ("pick", g2_u2_swap, g2_sum),
+                ("add", u2, g2_u2_swap),
+                ("add", u1_sum, u1_cross),
+                ("cat", 0, (y3, h1, h1)),
+                ("cat", 0, (x3, 0, h1)),
+            ],
+            carry=[own_share, grad_half],
+        )
+        x4, y4 = both_ways(x4, y4, "g2")
+        share_swap = swap(own_share, "swap_share")
+        u1_swap, u2_cross = swap(u1_sum, "swap_u1"), cross(u2_sum, "cross_u2")
+        grad_tokens = whole_rows(grad_half).astype(wide)
+        grad_w_down = place_share(
+            place, d2_all, x2, y2, (y3, r1), (x3, r1), units, False, width, cut_at, grad_w_down, [x3]
+        )
+        last = [grad_w_down]
+        u1_all, u2_sum, own_share, x5, y5 = tick(
+            [
+                ("pick", u1_swap, u1_sum),
+                ("add", u2_sum, u2_cross),
+                ("add", own_share, share_swap),
+                ("cat", 0, (y4, h2, h2)),
+                ("cat", 0, (x4, 0, h2)),
+            ],
+            needs=[x4, y4],
+        )
+        x5, y5 = both_ways(x5, y5, "u1")
+        u2_swap, share_swap = swap(u2_sum, "swap_u2"), partner(own_share, "dp", 2, "share_far")
+        grad_w_gate = place_share(
+            place, g1_all, x3, y3, (y4, r2), (x4, r2), units, True, width, 0, None, last
+        )
+        last = [grad_w_gate]
+        u2_all, own_share, x6, y6 = tick(
+            [
+                ("pick", u2_swap, u2_sum),
+                ("add", own_share, share_swap),
+                ("cat", 0, (y5, h1, h1), 1),
+                ("cat", 0, (x5, 0, h1), 1),
+            ],
+            needs=[x5, y5],
+        )
+        x6, y6 = both_ways(x6, y6, "u2")
+        grad_w_gate = place_share(
+            place, g2_all, x4, y4, (y5, r1), (x5, r1), units, True, width, cut_at, grad_w_gate, [x5]
+        )
+        last = [grad_w_gate]
+        first_half = stack_rows // 32 * 16
+        share_at = r2 + h1
+        x7, y7 = tick(
+            [
+                ("cat", (y6, h2, h2), (y6, share_at + first_half, stack_rows - first_half)),
+                ("cat", (x6, 0, h2), (x6, share_at, first_half)),
+            ],
+        )
+        x7, y7 = both_ways(x7, y7, "far")
+        grad_w_up = place_share(
+            place, u1_all, x5, y5, (y6, r2), (x6, r2), units, True, width, 0, None, last
+        )
+        last = [grad_w_up]
+        grad_w_up = place_share(
+            place, u2_all, x6, y6, (y7, 0), (x7, 0), units, True, width, cut_at, grad_w_up, []
+        )
+        last = [y7]
+        grad_w_query, grad_w_key, grad_w_value, grad_w_out, small = unpack(
+            [own_share, x6, y6, y7, x7],
+            [
+                (0, 0, stack_rows, 0),
+                (1, 0, stack_rows, share_at),
+                (2, 0, stack_rows, share_at),
+                (3, 0, first_half, h2),
+                (3, first_half, stack_rows - first_half, h2),
+            ],
+        )
+    if blocks != 4:
+        grad_tokens = whole_rows(grad_half).astype(wide)
     gains = small[:2]
     gains = gains + partner(gains, "tensor", 1, "gains_core")
     grad_b = small[2]

time: 412 us -> 350 us (0.85)
  Pallas kernels: 134 us -> 97.6 us
  starting transfers between devices: 108 us -> 87.3 us
  local copies, waits for them, and re-layouts: 38.7 us -> 27.4 us
  waiting for transfers between devices: 118 us -> 123 us
    pallas_call x37, Pallas kernels: 111 us -> 75 us  [call(): pl.pallas_call(run, name=getattr(body, 'func', body).__name__, out_shape=...]
    ppermute x21 -> x15, starting transfers between devices: 42.5 us -> 22.3 us  [the longest x9 17.6 us: swap(): return lax.ppermute(value, 'dp', [(0, 1), (1, 0), (2, 3), (3, 2)])]
    unnamed x184 -> x168, local copies, waits for them, and re-layouts: 30.9 us -> 22.9 us
    ppermute x21 -> x15, waiting for transfers between devices: 14.5 us -> 19.4 us  [the longest x9 19.4 us: swap(): return lax.ppermute(value, 'dp', [(0, 1), (1, 0), (2, 3), (3, 2)])]
    ppermute x70 -> x54, waiting for transfers between devices: 104 us -> 104 us  [partner(): return lax.ppermute(value, axis, [(i, i ^ step) for i in range(count)])]
    ppermute x70 -> x54, starting transfers between devices: 65 us -> 65 us  [partner(): return lax.ppermute(value, axis, [(i, i ^ step) for i in range(count)])]
  transfers between devices with their start and end apart: 91 -> 69, of which waited for: 30 -> 27; matrix products, arithmetic and copies ran while one was open for 3% -> 2% of each run, Pallas kernels for 28% -> 23%
where the time goes in v3:
time: 350 us; the launch traced here: 343 us
  waiting for transfers between devices  123 us (35%)
  Pallas kernels  97.6 us (28%)
  starting transfers between devices  87.3 us (25%)
  local copies, waits for them, and re-layouts  27.4 us (8%)
  other arithmetic  5.65 us (2%)
    ppermute x54, waiting for transfers between devices, partner(): return lax.ppermute(value, axis, [(i, i ^ step) for i in range(count)])  104 us
    pallas_call x37, Pallas kernels, call(): pl.pallas_call(run, name=getattr(body, 'func', body).__name__, out_shape=...  75 us
    ppermute x54, starting transfers between devices, partner(): return lax.ppermute(value, axis, [(i, i ^ step) for i in range(count)])  65 us
    unnamed x168, local copies, waits for them, and re-layouts  22.9 us
    pallas_call x6, Pallas kernels, place_share(): pl.pallas_call(body, name='place_kernel', out_shape=shape(dims, wide), gr...  22.7 us
    ppermute x9, waiting for transfers between devices, swap(): return lax.ppermute(value, 'dp', [(0, 1), (1, 0), (2, 3), (3, 2)])  19.4 us
    ppermute x9, starting transfers between devices, swap(): return lax.ppermute(value, 'dp', [(0, 1), (1, 0), (2, 3), (3, 2)])  17.6 us
  transfers between devices with their start and end apart: 69, of which 27 were waited for; matrix products, arithmetic and copies ran while one was open for 2% of the time, Pallas kernels for 23%

profile of v3, /device:TPU:0, one launch (start us, length us, event | category | flops | bytes accessed | tf_op | source)
XLA Modules:
  0.0 343.5 jit_solution(8577610526828220633)
XLA Ops:
  8.2 2.3 enter_kernel.1
  12.1 2.9 collective-permute-start.2
  17.9 2.2 copy-done.4
  20.1 4.6 %weights_kernel.1 = (bf16[608,896]{1,0:T(8,128)(2,1)S(1)}, bf16[896,608]{1,0:T(8,128)(2,1)S(1)}, bf16[608,896]{1,0:T(8,128)(2,1)S(1)}, bf16[896,608]{1,0:T(8,128...) custom-call(s32[1,3]{1,0:T(1,128)S(1)} %copy-done.80, ...), custom_call_target="tpu_custom_call" | custom-call | tf_op jit(solution)/shard_map/weights_kernel/pallas_call | solution.py:96
  24.8 2.0 collective-permute-start
  28.4 5.4 %attend_kernel.1 = (f32[448,512]{1,0:T(8,128)S(1)}, f32[8,512]{1,0:T(8,128)S(1)}, f32[896,256]{1,0:T(8,128)S(1)}, bf16[896,256]{1,0:T(8,128)(2,1)S(1)}) custom-call(s32[1,3]{1,0:T(1,128)S(1)} %copy-done.80, s32[3]{0:T(128)S(1)} %pad_add_fusion.refs_1_.refs_0_, bf16[448,512]{1,0:T(8,128)(2,1)S(1)} %get-tuple-element.153.refs_6_.refs_2_.refs_5_, ...), custom_call_target="tpu_custom_call" | custom-call | tf_op jit(solution)/shard_map/attend_kernel/pallas_call | solution.py:96
  34.7 1.8 collective-permute-done.refs_5_.refs_1_.refs_7_
  39.9 2.8 collective-permute-start.8
  42.7 7.1 %collective-permute-start.9 = (bf16[896,256]{1,0:T(8,128)(2,1)S(1)}, bf16[896,256]{1,0:T(8,128)(2,1)S(1)}, u32[]{:S(2)}, u32[]{:S(2)}) collective-permute-start(bf16[896,256]{1,0:T(8,128)(2,1)S(1)} %get-tuple-element.161.refs_3_.refs_9_.refs_5_), channel_id=1, source_target_pairs={{0,4},{2,6},{4,0},{6,2},{1,5},{3,7},{5,1},{7,3},{8,12},{10,14},{12... | collective-permute-start | bytes 1376264 | tf_op jit(solution)/shard_map/x/ppermute | solution.py:37
  49.8 3.8 %hidden_kernel.4 = (bf16[608,512]{1,0:T(8,128)(2,1)S(1)}, bf16[608,512]{1,0:T(8,128)(2,1)S(1)}, bf16[608,512]{1,0:T(8,128)(2,1)S(1)}, bf16[896,256]{1,0:T(8,128)(2,1)S(1)}, bf16[896,256]{1,0:T(8,128)(2,1)S(1)}) custom-call(bf16[256,896]{1,0:T(8,128)(2,1)S(1)} %get-tuple-element.155.refs_0_.refs_4_, ...), custom_call_target="tpu_custom_call" | custom-call | tf_op jit(solution)/shard_map/hidden_kernel/pallas_call | solution.py:96
  53.7 6.8 %collective-permute-done.9.refs_3_ = bf16[896,256]{1,0:T(8,128)(2,1)S(1)} collective-permute-done((bf16[896,256]{1,0:T(8,128)(2,1)S(1)}, bf16[896,256]{1,0:T(8,128)(2,1)S(1)}, u32[]{:S(2)}, u32[]{:S(2)}) %collective-permute-start.9) | collective-permute-done | bytes 458784 | tf_op jit(solution)/shard_map/x/ppermute | solution.py:37
  60.5 1.8 collective-permute-start.13
  63.1 1.8 collective-permute-start.12
  65.0 3.8 %hidden_kernel.5 = (bf16[608,512]{1,0:T(8,128)(2,1)S(1)}, bf16[608,512]{1,0:T(8,128)(2,1)S(1)}, bf16[608,512]{1,0:T(8,128)(2,1)S(1)}, bf16[896,256]{1,0:T(8,128)(2,1)S(1)}, bf16[896,256]{1,0:T(8,128)(2,1)S(1)}) custom-call(bf16[256,896]{1,0:T(8,128)(2,1)S(1)} %collective-permute-done.1.refs_0_.refs_6_, ...), custom_call_target="tpu_custom_call" | custom-call | tf_op jit(solution)/shard_map/hidden_kernel/pallas_call | solution.py:96
  70.9 2.7 collective-permute-done.11.refs_2_
  73.5 1.5 collective-permute-done.12.refs_3_
  75.1 3.8 %hidden_kernel.6 = (bf16[608,512]{1,0:T(8,128)(2,1)S(1)}, bf16[608,512]{1,0:T(8,128)(2,1)S(1)}, bf16[608,512]{1,0:T(8,128)(2,1)S(1)}, bf16[896,256]{1,0:T(8,128)(2,1)S(1)}, bf16[896,256]{1,0:T(8,128)(2,1)S(1)}) custom-call(bf16[256,896]{1,0:T(8,128)(2,1)S(1)} %collective-permute-done.20.refs_0_.refs_8_, ...), custom_call_target="tpu_custom_call" | custom-call | tf_op jit(solution)/shard_map/hidden_kernel/pallas_call | solution.py:96
  82.4 4.0 %hidden_kernel.7 = (bf16[608,512]{1,0:T(8,128)(2,1)S(1)}, bf16[608,512]{1,0:T(8,128)(2,1)S(1)}, bf16[608,512]{1,0:T(8,128)(2,1)S(1)}, bf16[896,256]{1,0:T(8,128)(2,1)S(1)}, bf16[896,256]{1,0:T(8,128)(2,1)S(1)}) custom-call(bf16[128,896]{1,0:T(8,128)(2,1)S(1)} %collective-permute-done.15.refs_0_.refs_10_, ...), custom_call_target="tpu_custom_call" | custom-call | tf_op jit(solution)/shard_map/hidden_kernel/pallas_call | solution.py:96
  90.1 2.1 collective-permute-start.27
  94.5 3.0 project_kernel.1
  98.3 6.8 %collective-permute-done.25.refs_4_.refs_7_ = bf16[896,256]{1,0:T(8,128)(2,1)S(1)} collective-permute-done((bf16[896,256]{1,0:T(8,128)(2,1)S(1)}, bf16[896,256]{1,0:T(8,128)(2,1)S(1)}, u32[]{:S(2)}, u32[]{:S(2)}) %collective-permute-start.25) | collective-permute-done | bytes 458784 | tf_op jit(solution)/shard_map/back/ppermute | solution.py:37
  107.7 1.6 collective-permute-start.29
  109.3 2.8 weight_kernel.6
  112.2 2.8 weight_kernel.7
  115.0 6.3 %collective-permute-done.29.refs_9_.refs_6_ = bf16[896,256]{1,0:T(8,128)(2,1)S(1)} collective-permute-done((bf16[896,256]{1,0:T(8,128)(2,1)S(1)}, bf16[896,256]{1,0:T(8,128)(2,1)S(1)}, u32[]{:S(2)}, u32[]{:S(2)}) %collective-permute-start.29) | collective-permute-done | bytes 458784 | tf_op jit(solution)/shard_map/back/ppermute | solution.py:37
  126.4 4.8 %collective-permute-start.32 = (bf16[1824,128]{1,0:T(8,128)(2,1)S(1)}, bf16[1824,128]{1,0:T(8,128)(2,1)S(1)}, u32[]{:S(2)}, u32[]{:S(2)}) collective-permute-start(bf16[1824,128]{1,0:T(8,128)(2,1)S(1)} %get-tuple-element.215), channel_id=1, source_target_pairs={{0,8},{8,0},{16,24},{24,16},{1,9},{9,1},{17,25},{25,17},{2,10},{10... | collective-permute-start | bytes 1400840 | tf_op jit(solution)/shard_map/swap_d1_g1/ppermute | solution.py:78
  131.2 1.7 collective-permute-start.35
  136.1 6.4 %attend_back_kernel.1 = (bf16[448,512]{1,0:T(8,128)(2,1)S(1)}, bf16[512,128]{1,0:T(8,128)(2,1)S(1)}, bf16[512,128]{1,0:T(8,128)(2,1)S(1)}, bf16[512,128]{1,0:T(8,128)(2,1)S(1)}, bf16[512,128]{1,0:T(8,128)(2,1)S(1)}) custom-call(s32[1,3]{1,0:T(1,128)S(1)} %copy-done.80, s32[3]{0:T(128)S(1)} %pad_add_fusion.refs_1_.refs_0_, ...), custom_call_target="tpu_custom_call" | custom-call | tf_op jit(solution)/shard_map/attend_back_kernel/pallas_call | solution.py:96
  142.4 2.2 collective-permute-done.35.refs_10_.refs_2_
  144.6 10.1 %collective-permute-done.36.refs_11_.refs_3_ = bf16[896,256]{1,0:T(8,128)(2,1)S(1)} collective-permute-done((bf16[896,256]{1,0:T(8,128)(2,1)S(1)}, bf16[896,256]{1,0:T(8,128)(2,1)S(1)}, u32[]{:S(2)}, u32[]{:S(2)}) %collective-permute-start.36) | collective-permute-done | bytes 458784 | tf_op jit(solution)/shard_map/layer/ppermute | solution.py:37
  157.0 5.5 %collective-permute-start.41 = (bf16[2336,128]{1,0:T(8,128)(2,1)S(1)}, bf16[2336,128]{1,0:T(8,128)(2,1)S(1)}, u32[]{:S(2)}, u32[]{:S(2)}) collective-permute-start(bf16[2336,128]{1,0:T(8,128)(2,1)S(1)} %get-tuple-element.237), channel_id=1, source_target_pairs={{0,2},{2,0},{4,6},{6,4},{1,3},{3,1},{5,7},{7,5},{8,10},{10,8},{12,... | collective-permute-start | bytes 1794056 | tf_op jit(solution)/shard_map/d1_x/ppermute | solution.py:37
  163.3 2.3 query_kernel.1
  166.8 10.7 %collective-permute-done.42.refs_11_.refs_15_ = bf16[512,128]{1,0:T(8,128)(2,1)S(1)} collective-permute-done((bf16[512,128]{1,0:T(8,128)(2,1)S(1)}, bf16[512,128]{1,0:T(8,128)(2,1)S(1)}, u32[]{:S(2)}, u32[]{:S(2)}) %collective-permute-start.42) | collective-permute-done | bytes 131104 | tf_op jit(solution)/shard_map/grad_kv/ppermute | solution.py:37
  179.0 1.7 collective-permute-start.46
  180.7 1.7 collective-permute-start.47
  183.4 4.5 %collective-permute-start.44 = (bf16[1824,128]{1,0:T(8,128)(2,1)S(1)}, bf16[1824,128]{1,0:T(8,128)(2,1)S(1)}, u32[]{:S(2)}, u32[]{:S(2)}) collective-permute-start(bf16[1824,128]{1,0:T(8,128)(2,1)S(1)} %get-tuple-element.243), channel_id=1, source_target_pairs={{0,8},{8,0},{16,24},{24,16},{1,9},{9,1},{17,25},{25,17},{2,10},{10... | collective-permute-start | bytes 1400840 | tf_op jit(solution)/shard_map/swap_g1_u1/ppermute | solution.py:78
  187.9 3.0 key_kernel.1
  191.8 3.3 collective-permute-done.44.refs_1_
  195.1 2.9 collective-permute-done.46.refs_7_.refs_13_.refs_4_.refs_5_.refs_3_
  199.1 2.8 tick_kernel.13
  207.5 2.9 place_kernel.6.refs_6_.refs_9_
  210.3 3.5 %copy-done = f32[2432,896]{1,0:T(8,128)S(1)} copy-done((f32[2432,896]{1,0:T(8,128)S(1)}, f32[2432,896]{1,0:T(8,128)}, u32[]{:S(2)}) %copy-start) | copy-done | bytes 8716312
  213.8 2.1 leave_kernel.1.refs_4_.refs_9_
  215.9 24.1 %collective-permute-done.52.refs_3_ = bf16[1904,128]{1,0:T(8,128)(2,1)S(1)} collective-permute-done((bf16[1904,128]{1,0:T(8,128)(2,1)}, bf16[1904,128]{1,0:T(8,128)(2,1)S(1)}, u32[]{:S(2)}, u32[]{:S(2)}) %collective-permute-start.52) | collective-permute-done | bytes 487456 | tf_op jit(solution)/shard_map/shares/ppermute | solution.py:37
  244.5 3.9 %collective-permute-start.57 = (bf16[1904,128]{1,0:T(8,128)(2,1)S(1)}, bf16[1904,128]{1,0:T(8,128)(2,1)S(1)}, u32[]{:S(2)}, u32[]{:S(2)}) collective-permute-start(bf16[1904,128]{1,0:T(8,128)(2,1)S(1)} %get-tuple-element.272.refs_5_), channel_id=1, source_target_pairs={{0,8},{8,0},{16,24},{24,16},{1,9},{9,1},{17,25},{25,17},{2,10},{10... | collective-permute-start | bytes 1462280 | tf_op jit(solution)/shard_map/swap_share/ppermute | solution.py:78
  248.5 3.2 place_kernel.7.refs_9_
  251.8 13.1 %collective-permute-done.55.refs_1_ = bf16[1824,128]{1,0:T(8,128)(2,1)S(1)} collective-permute-done((bf16[1824,128]{1,0:T(8,128)(2,1)S(1)}, bf16[1824,128]{1,0:T(8,128)(2,1)S(1)}, u32[]{:S(2)}, u32[]{:S(2)}) %collective-permute-start.55) | collective-permute-done | bytes 466976 | tf_op jit(solution)/shard_map/swap_u1/ppermute | solution.py:78
  266.3 7.2 %collective-permute-start.63 = (bf16[3040,128]{1,0:T(8,128)(2,1)S(1)}, bf16[3040,128]{1,0:T(8,128)(2,1)S(1)}, u32[]{:S(2)}, u32[]{:S(2)}) collective-permute-start(bf16[3040,128]{1,0:T(8,128)(2,1)S(1)} %get-tuple-element.278), channel_id=1, source_target_pairs={{0,2},{2,0},{4,6},{6,4},{1,3},{3,1},{5,7},{7,5},{8,10},{10,8},{12,... | collective-permute-start | bytes 2334728 | tf_op jit(solution)/shard_map/u1_x/ppermute | solution.py:37
  273.4 1.9 collective-permute-start.61
  275.3 3.6 %place_kernel.8.refs_7_.refs_9_ = f32[896,2432]{1,0:T(8,128)} custom-call(s32[3]{0:T(128)S(1)} %pad_add_fusion.refs_1_.refs_0_, bf16[1824,128]{1,0:T(8,128)(2,1)S(1)} %get-tuple-element.268.refs_8_.refs_1_, bf16[4944,128]{1,0:T(8,128)(2,1)S(1)} %collective-permute-done.51.refs_1_.refs_7_.refs_6_.refs_8_.refs_2_, ...), custom_call_target="tpu_custom_call" | custom-call | tf_op jit(solution)/shard_map/place_kernel/pallas_call | solution.py:607
  279.0 7.9 %collective-permute-done.61.refs_4_ = bf16[1904,128]{1,0:T(8,128)(2,1)S(1)} collective-permute-done((bf16[1904,128]{1,0:T(8,128)(2,1)S(1)}, bf16[1904,128]{1,0:T(8,128)(2,1)S(1)}, u32[]{:S(2)}, u32[]{:S(2)}) %collective-permute-start.61) | collective-permute-done | bytes 487456 | tf_op jit(solution)/shard_map/share_far/ppermute | solution.py:37
  286.9 2.0 collective-permute-done.60.refs_1_
  290.2 3.7 %collective-permute-start.65 = (bf16[5248,128]{1,0:T(8,128)(2,1)S(1)}, bf16[5248,128]{1,0:T(8,128)(2,1)S(1)}, u32[]{:S(2)}, u32[]{:S(2)}) collective-permute-start(bf16[5248,128]{1,0:T(8,128)(2,1)S(1)} %get-tuple-element.282), channel_id=1, source_target_pairs={{0,4},{2,6},{4,0},{6,2},{1,5},{3,7},{5,1},{7,3},{8,12},{10,14},{12... | collective-permute-start | bytes 4030472 | tf_op jit(solution)/shard_map/u2_y/ppermute | solution.py:37
  294.5 4.2 %place_kernel.9.refs_3_ = f32[896,2432]{1,0:T(8,128)} custom-call(s32[3]{0:T(128)S(1)} %pad_add_fusion.refs_1_.refs_0_, bf16[2432,128]{1,0:T(8,128)(2,1)S(1)} %get-tuple-element.283.refs_1_, bf16[3344,128]{1,0:T(8,128)(2,1)S(1)} %collective-permute-done.59.refs_8_.refs_10_.refs_6_.refs_7_.refs_2_, ...), custom_call_target="tpu_custom_call", output_to_operand_aliasing={{}: (9, {})} | custom-call | tf_op jit(solution)/shard_map/place_kernel/pallas_call | solution.py:607
  298.7 13.6 %collective-permute-done.64.refs_2_.refs_6_.refs_7_ = bf16[5248,128]{1,0:T(8,128)(2,1)S(1)} collective-permute-done((bf16[5248,128]{1,0:T(8,128)(2,1)S(1)}, bf16[5248,128]{1,0:T(8,128)(2,1)S(1)}, u32[]{:S(2)}, u32[]{:S(2)}) %collective-permute-start.64) | collective-permute-done | bytes 1343520 | tf_op jit(solution)/shard_map/u2_x/ppermute | solution.py:37
  312.3 3.5 %copy-done.1 = f32[896,2432]{1,0:T(8,128)S(1)} copy-done((f32[896,2432]{1,0:T(8,128)S(1)}, f32[896,2432]{1,0:T(8,128)}, u32[]{:S(2)}) %copy-start.1) | copy-done | bytes 8716312
  315.8 1.6 tick_kernel.17
  317.4 2.3 collective-permute-start.67
  319.7 3.7 %collective-permute-start.66 = (bf16[2160,128]{1,0:T(8,128)(2,1)}, bf16[2160,128]{1,0:T(8,128)(2,1)}, u32[]{:S(2)}, u32[]{:S(2)}) collective-permute-start(bf16[2160,128]{1,0:T(8,128)(2,1)} %get-tuple-element.284), channel_id=1, source_target_pairs={{0,4},{2,6},{4,0},{6,2},{1,5},{3,7},{5,1},{7,3},{8,12},{10,14},{12... | collective-permute-start | bytes 1658888 | tf_op jit(solution)/shard_map/far_y/ppermute | solution.py:37
  323.4 2.6 maximum_select_fusion
  326.0 2.9 fusion
  329.0 3.7 %place_kernel.10.refs_8_ = f32[896,2432]{1,0:T(8,128)} custom-call(s32[3]{0:T(128)S(1)} %pad_add_fusion.refs_1_.refs_0_, bf16[1824,128]{1,0:T(8,128)(2,1)S(1)} %copy-done.26, bf16[3040,128]{1,0:T(8,128)(2,1)S(1)} %collective-permute-done.63.refs_6_.refs_8_.refs_7_.refs_2_, bf16[3040,128]{1,0:T(8,128)(2,1)S(1)} %copy-done.3, ...), custom_call_target="tpu_custom_call" | custom-call | tf_op jit(solution)/shard_map/place_kernel/pallas_call | solution.py:607
  332.7 3.5 %unpack_kernel.1 = (f32[448,896]{1,0:T(8,128)}, f32[64,896]{1,0:T(8,128)}, f32[64,896]{1,0:T(8,128)}, f32[448,896]{1,0:T(8,128)}, f32[64,896]{1,0:T(8,128)S(1)}) custom-call(s32[3]{0:T(128)S(1)} %pad_add_fusion.refs_1_.refs_0_, bf16[1904,128]{1,0:T(8,128)(2,1)S(1)} %copy-done.62, bf16[5248,128]{1,0:T(8,128)(2,1)S(1)} %collective-permute-done.64.refs_2_.refs_6_.refs_7_, ...), custom_call_target="tpu_custom_call" | custom-call | tf_op jit(solution)/shard_map/unpack_kernel/pallas_call | solution.py:96
  337.3 5.0 %place_kernel.11 = f32[896,2432]{1,0:T(8,128)} custom-call(s32[3]{0:T(128)S(1)} %pad_add_fusion.refs_1_.refs_0_, bf16[2432,128]{1,0:T(8,128)(2,1)S(1)} %copy-done.52, bf16[5248,128]{1,0:T(8,128)(2,1)S(1)} %collective-permute-done.64.refs_2_.refs_6_.refs_7_, ...), custom_call_target="tpu_custom_call", output_to_operand_aliasing={{}: (8, {})} | custom-call | tf_op jit(solution)/shard_map/place_kernel/pallas_call | solution.py:607
  (302 shorter events, 65.2 us)
Async XLA Ops:
  12.1 16.2 %collective-permute-start.2 = (bf16[512,128]{1,0:T(8,128)(2,1)S(1)}, bf16[512,128]{1,0:T(8,128)(2,1)S(1)}, u32[]{:S(2)}, u32[]{:S(2)}) collective-permute-start(bf16[512,128]{1,0:T(8,128)(2,1)S(1)} %get-tuple-element.157.refs_4_.refs_8_), channel_id=1, source_target_pairs={{0,2},{2,0},{4,6},{6,4},{1,3},{3,1},{5,7},{7,5},{8,10},{10,8},{12,... | collective-permute-start | bytes 393224 | tf_op jit(solution)/shard_map/kv/ppermute | solution.py:37
  15.0 13.3 %collective-permute-start.3 = (bf16[512,128]{1,0:T(8,128)(2,1)S(1)}, bf16[512,128]{1,0:T(8,128)(2,1)S(1)}, u32[]{:S(2)}, u32[]{:S(2)}) collective-permute-start(bf16[512,128]{1,0:T(8,128)(2,1)S(1)} %get-tuple-element.157.refs_4_.refs_8_), channel_id=1, source_target_pairs={{0,4},{2,6},{4,0},{6,2},{1,5},{3,7},{5,1},{7,3},{8,12},{10,14},{12... | collective-permute-start | bytes 393224 | tf_op jit(solution)/shard_map/kv/ppermute | solution.py:37
  16.5 11.8 %collective-permute-start.4 = (bf16[512,128]{1,0:T(8,128)(2,1)S(1)}, bf16[512,128]{1,0:T(8,128)(2,1)S(1)}, u32[]{:S(2)}, u32[]{:S(2)}) collective-permute-start(bf16[512,128]{1,0:T(8,128)(2,1)S(1)} %get-tuple-element.157.refs_4_.refs_8_), channel_id=1, source_target_pairs={{0,6},{2,4},{4,2},{6,0},{1,7},{3,5},{5,3},{7,1},{8,14},{10,12},{12... | collective-permute-start | bytes 393224 | tf_op jit(solution)/shard_map/kv/ppermute | solution.py:37
  24.8 11.8 %collective-permute-start = (bf16[256,896]{1,0:T(8,128)(2,1)S(1)}, bf16[256,896]{1,0:T(8,128)(2,1)S(1)}, u32[]{:S(2)}, u32[]{:S(2)}) collective-permute-start(bf16[256,896]{1,0:T(8,128)(2,1)S(1)} %get-tuple-element.154.refs_1_.refs_5_.refs_2_), channel_id=1, source_target_pairs={{0,2},{2,0},{4,6},{6,4},{1,3},{3,1},{5,7},{7,5},{8,10},{10,8},{12,... | collective-permute-start | bytes 1376264 | tf_op jit(solution)/shard_map/gy/ppermute | solution.py:37
  26.8 11.1 %collective-permute-start.6 = (bf16[256,896]{1,0:T(8,128)(2,1)S(1)}, bf16[256,896]{1,0:T(8,128)(2,1)S(1)}, u32[]{:S(2)}, u32[]{:S(2)}) collective-permute-start(bf16[256,896]{1,0:T(8,128)(2,1)S(1)} %get-tuple-element.154.refs_1_.refs_5_.refs_2_), channel_id=1, source_target_pairs={{0,4},{2,6},{4,0},{6,2},{1,5},{3,7},{5,1},{7,3},{8,12},{10,14},{12... | collective-permute-start | bytes 1376264 | tf_op jit(solution)/shard_map/gy/ppermute | solution.py:37
  34.7 3.2 collective-permute-start.5
  39.9 9.9 %collective-permute-start.7 = (bf16[896,256]{1,0:T(8,128)(2,1)S(1)}, bf16[896,256]{1,0:T(8,128)(2,1)S(1)}, u32[]{:S(2)}, u32[]{:S(2)}) collective-permute-start(bf16[896,256]{1,0:T(8,128)(2,1)S(1)} %get-tuple-element.161.refs_3_.refs_9_.refs_5_), channel_id=1, source_target_pairs={{0,1},{1,0},{2,3},{3,2},{4,5},{5,4},{6,7},{7,6},{8,9},{9,8},{10,11... | collective-permute-start | bytes 1376264 | tf_op jit(solution)/shard_map/x_core/ppermute | solution.py:37
  39.9 13.8 %collective-permute-start.8 = (bf16[896,256]{1,0:T(8,128)(2,1)S(1)}, bf16[896,256]{1,0:T(8,128)(2,1)S(1)}, u32[]{:S(2)}, u32[]{:S(2)}) collective-permute-start(bf16[896,256]{1,0:T(8,128)(2,1)S(1)} %get-tuple-element.161.refs_3_.refs_9_.refs_5_), channel_id=1, source_target_pairs={{0,2},{2,0},{4,6},{6,4},{1,3},{3,1},{5,7},{7,5},{8,10},{10,8},{12,... | collective-permute-start | bytes 1376264 | tf_op jit(solution)/shard_map/x/ppermute | solution.py:37
  42.7 17.8 %collective-permute-start.9 = (bf16[896,256]{1,0:T(8,128)(2,1)S(1)}, bf16[896,256]{1,0:T(8,128)(2,1)S(1)}, u32[]{:S(2)}, u32[]{:S(2)}) collective-permute-start(bf16[896,256]{1,0:T(8,128)(2,1)S(1)} %get-tuple-element.161.refs_3_.refs_9_.refs_5_), channel_id=1, source_target_pairs={{0,4},{2,6},{4,0},{6,2},{1,5},{3,7},{5,1},{7,3},{8,12},{10,14},{12... | collective-permute-start | bytes 1376264 | tf_op jit(solution)/shard_map/x/ppermute | solution.py:37
  49.8 13.4 %collective-permute-start.1 = (bf16[256,896]{1,0:T(8,128)(2,1)S(1)}, bf16[256,896]{1,0:T(8,128)(2,1)S(1)}, u32[]{:S(2)}, u32[]{:S(2)}) collective-permute-start(bf16[256,896]{1,0:T(8,128)(2,1)S(1)} %collective-permute-done.refs_5_.refs_1_.refs_7_), channel_id=1, source_target_pairs={{0,1},{1,0},{2,3},{3,2},{4,5},{5,4},{6,7},{7,6},{8,9},{9,8},{10,11... | collective-permute-start | bytes 1376264 | tf_op jit(solution)/shard_map/gy_core/ppermute | solution.py:37
  60.5 4.4 %collective-permute-start.10 = (bf16[896,256]{1,0:T(8,128)(2,1)S(1)}, bf16[896,256]{1,0:T(8,128)(2,1)S(1)}, u32[]{:S(2)}, u32[]{:S(2)}) collective-permute-start(bf16[896,256]{1,0:T(8,128)(2,1)S(1)} %get-tuple-element.167.refs_3_.refs_7_), channel_id=1, source_target_pairs={{0,1},{1,0},{2,3},{3,2},{4,5},{5,4},{6,7},{7,6},{8,9},{9,8},{10,11... | collective-permute-start | bytes 1376264 | tf_op jit(solution)/shard_map/x_core/ppermute | solution.py:37
  60.5 8.5 %collective-permute-start.13 = (bf16[128,896]{1,0:T(8,128)(2,1)S(1)}, bf16[128,896]{1,0:T(8,128)(2,1)S(1)}, u32[]{:S(2)}, u32[]{:S(2)}) collective-permute-start(bf16[128,896]{1,0:T(8,128)(2,1)S(1)} %slice.56), channel_id=1, source_target_pairs={{0,4},{2,6},{4,0},{6,2},{1,5},{3,7},{5,1},{7,3},{8,12},{10,14},{12... | collective-permute-start | bytes 688136 | tf_op jit(solution)/shard_map/gy_relay/ppermute | solution.py:37
  62.4 8.5 %collective-permute-start.14 = (bf16[128,896]{1,0:T(8,128)(2,1)S(1)}, bf16[128,896]{1,0:T(8,128)(2,1)S(1)}, u32[]{:S(2)}, u32[]{:S(2)}) collective-permute-start(bf16[128,896]{1,0:T(8,128)(2,1)S(1)} %slice.57), channel_id=1, source_target_pairs={{0,2},{2,0},{4,6},{6,4},{1,3},{3,1},{5,7},{7,5},{8,10},{10,8},{12,... | collective-permute-start | bytes 688136 | tf_op jit(solution)/shard_map/gy_relay/ppermute | solution.py:37
  62.8 10.8 %collective-permute-start.11 = (bf16[448,256]{1,0:T(8,128)(2,1)S(1)}, bf16[448,256]{1,0:T(8,128)(2,1)S(1)}, u32[]{:S(2)}, u32[]{:S(2)}) collective-permute-start(bf16[448,256]{1,0:T(8,128)(2,1)S(1)} %slice.43), channel_id=1, source_target_pairs={{0,4},{2,6},{4,0},{6,2},{1,5},{3,7},{5,1},{7,3},{8,12},{10,14},{12... | collective-permute-start | bytes 688136 | tf_op jit(solution)/shard_map/x_relay/ppermute | solution.py:37
  63.1 11.9 %collective-permute-start.12 = (bf16[448,256]{1,0:T(8,128)(2,1)S(1)}, bf16[448,256]{1,0:T(8,128)(2,1)S(1)}, u32[]{:S(2)}, u32[]{:S(2)}) collective-permute-start(bf16[448,256]{1,0:T(8,128)(2,1)S(1)} %slice.44), channel_id=1, source_target_pairs={{0,2},{2,0},{4,6},{6,4},{1,3},{3,1},{5,7},{7,5},{8,10},{10,8},{12,... | collective-permute-start | bytes 688136 | tf_op jit(solution)/shard_map/x_relay/ppermute | solution.py:37
  65.0 10.1 %collective-permute-start.20 = (bf16[256,896]{1,0:T(8,128)(2,1)S(1)}, bf16[256,896]{1,0:T(8,128)(2,1)S(1)}, u32[]{:S(2)}, u32[]{:S(2)}) collective-permute-start(bf16[256,896]{1,0:T(8,128)(2,1)S(1)} %collective-permute-done.6.refs_6_.refs_1_.refs_9_), channel_id=1, source_target_pairs={{0,1},{1,0},{2,3},{3,2},{4,5},{5,4},{6,7},{7,6},{8,9},{9,8},{10,11... | collective-permute-start | bytes 1376264 | tf_op jit(solution)/shard_map/gy_core/ppermute | solution.py:37
  69.0 6.1 %collective-permute-start.21 = (bf16[896,256]{1,0:T(8,128)(2,1)S(1)}, bf16[896,256]{1,0:T(8,128)(2,1)S(1)}, u32[]{:S(2)}, u32[]{:S(2)}) collective-permute-start(bf16[896,256]{1,0:T(8,128)(2,1)S(1)} %get-tuple-element.171.refs_3_.refs_9_), channel_id=1, source_target_pairs={{0,1},{1,0},{2,3},{3,2},{4,5},{5,4},{6,7},{7,6},{8,9},{9,8},{10,11... | collective-permute-start | bytes 1376264 | tf_op jit(solution)/shard_map/x_core/ppermute | solution.py:37
  75.1 3.9 %collective-permute-start.19 = (bf16[896,256]{1,0:T(8,128)(2,1)S(1)}, bf16[896,256]{1,0:T(8,128)(2,1)S(1)}, u32[]{:S(2)}, u32[]{:S(2)}) collective-permute-start(bf16[896,256]{1,0:T(8,128)(2,1)S(1)} %get-tuple-element.177.refs_9_), channel_id=1, source_target_pairs={{0,1},{1,0},{2,3},{3,2},{4,5},{5,4},{6,7},{7,6},{8,9},{9,8},{10,11... | collective-permute-start | bytes 1376264 | tf_op jit(solution)/shard_map/back_core/ppermute | solution.py:37
  79.1 8.2 %collective-permute-start.22 = (bf16[896,256]{1,0:T(8,128)(2,1)S(1)}, bf16[896,256]{1,0:T(8,128)(2,1)S(1)}, u32[]{:S(2)}, u32[]{:S(2)}) collective-permute-start(bf16[896,256]{1,0:T(8,128)(2,1)S(1)} %get-tuple-element.183), channel_id=1, source_target_pairs={{0,1},{1,0},{2,3},{3,2},{4,5},{5,4},{6,7},{7,6},{8,9},{9,8},{10,11... | collective-permute-start | bytes 1376264 | tf_op jit(solution)/shard_map/back_core/ppermute | solution.py:37
  90.1 15.4 %collective-permute-start.27 = (bf16[1824,128]{1,0:T(8,128)(2,1)S(1)}, bf16[1824,128]{1,0:T(8,128)(2,1)S(1)}, u32[]{:S(2)}, u32[]{:S(2)}) collective-permute-start(bf16[1824,128]{1,0:T(8,128)(2,1)S(1)} %weight_kernel.4.refs_14_.refs_1_), channel_id=1, source_target_pairs={{0,8},{8,0},{16,24},{24,16},{1,9},{9,1},{17,25},{25,17},{2,10},{10... | collective-permute-start | bytes 1400840 | tf_op jit(solution)/shard_map/swap_d1/ppermute | solution.py:78
  92.2 6.1 %collective-permute-start.24 = (bf16[896,256]{1,0:T(8,128)(2,1)S(1)}, bf16[896,256]{1,0:T(8,128)(2,1)S(1)}, u32[]{:S(2)}, u32[]{:S(2)}) collective-permute-start(bf16[896,256]{1,0:T(8,128)(2,1)S(1)} %get-tuple-element.168.refs_9_), channel_id=1, source_target_pairs={{0,1},{1,0},{2,3},{3,2},{4,5},{5,4},{6,7},{7,6},{8,9},{9,8},{10,11... | collective-permute-start | bytes 1376264 | tf_op jit(solution)/shard_map/back_core/ppermute | solution.py:37
  92.3 12.9 %collective-permute-start.25 = (bf16[896,256]{1,0:T(8,128)(2,1)S(1)}, bf16[896,256]{1,0:T(8,128)(2,1)S(1)}, u32[]{:S(2)}, u32[]{:S(2)}) collective-permute-start(bf16[896,256]{1,0:T(8,128)(2,1)S(1)} %get-tuple-element.180.refs_13_), channel_id=1, source_target_pairs={{0,2},{2,0},{4,6},{6,4},{1,3},{3,1},{5,7},{7,5},{8,10},{10,8},{12,... | collective-permute-start | bytes 1376264 | tf_op jit(solution)/shard_map/back/ppermute | solution.py:37
  92.6 12.6 %collective-permute-start.23 = (bf16[896,256]{1,0:T(8,128)(2,1)S(1)}, bf16[896,256]{1,0:T(8,128)(2,1)S(1)}, u32[]{:S(2)}, u32[]{:S(2)}) collective-permute-start(bf16[896,256]{1,0:T(8,128)(2,1)S(1)} %get-tuple-element.186), channel_id=1, source_target_pairs={{0,1},{1,0},{2,3},{3,2},{4,5},{5,4},{6,7},{7,6},{8,9},{9,8},{10,11... | collective-permute-start | bytes 1376264 | tf_op jit(solution)/shard_map/back_core/ppermute | solution.py:37
  92.7 12.8 %collective-permute-start.26 = (bf16[896,256]{1,0:T(8,128)(2,1)S(1)}, bf16[896,256]{1,0:T(8,128)(2,1)S(1)}, u32[]{:S(2)}, u32[]{:S(2)}) collective-permute-start(bf16[896,256]{1,0:T(8,128)(2,1)S(1)} %get-tuple-element.188.refs_14_), channel_id=1, source_target_pairs={{0,4},{2,6},{4,0},{6,2},{1,5},{3,7},{5,1},{7,3},{8,12},{10,14},{12... | collective-permute-start | bytes 1376264 | tf_op jit(solution)/shard_map/back/ppermute | solution.py:37
  105.8 18.8 %collective-permute-start.28 = (bf16[4,896,256]{2,1,0:T(8,128)(2,1)S(1)}, bf16[4,896,256]{2,1,0:T(8,128)(2,1)S(1)}, u32[]{:S(2)}, u32[]{:S(2)}) collective-permute-start(bf16[4,896,256]{2,1,0:T(8,128)(2,1)S(1)} %get-tuple-element.191), channel_id=1, source_target_pairs={{0,1},{1,0},{2,3},{3,2},{4,5},{5,4},{6,7},{7,6},{8,9},{9,8},{10,11... | collective-permute-start | bytes 5505032 | tf_op jit(solution)/shard_map/layer_core/ppermute | solution.py:37
  105.9 16.4 %collective-permute-start.31 = (bf16[2432,128]{1,0:T(8,128)(2,1)S(1)}, bf16[2432,128]{1,0:T(8,128)(2,1)S(1)}, u32[]{:S(2)}, u32[]{:S(2)}) collective-permute-start(bf16[2432,128]{1,0:T(8,128)(2,1)S(1)} %get-tuple-element.199.refs_3_), channel_id=1, source_target_pairs={{0,8},{8,0},{16,24},{24,16},{1,9},{9,1},{17,25},{25,17},{2,10},{10... | collective-permute-start | bytes 1867784 | tf_op jit(solution)/shard_map/swap_d2/ppermute | solution.py:78
  107.0 14.3 %collective-permute-start.30 = (bf16[1824,128]{1,0:T(8,128)(2,1)S(1)}, bf16[1824,128]{1,0:T(8,128)(2,1)S(1)}, u32[]{:S(2)}, u32[]{:S(2)}) collective-permute-start(bf16[1824,128]{1,0:T(8,128)(2,1)S(1)} %tick_kernel.9.refs_14_.refs_1_), channel_id=1, source_target_pairs={{8,16},{16,8},{9,17},{17,9},{10,18},{18,10},{11,19},{19,11},{12,20... | collective-permute-start | bytes 1400840 | tf_op jit(solution)/shard_map/cross_d1/ppermute | solution.py:83
  107.7 13.6 %collective-permute-start.29 = (bf16[896,256]{1,0:T(8,128)(2,1)S(1)}, bf16[896,256]{1,0:T(8,128)(2,1)S(1)}, u32[]{:S(2)}, u32[]{:S(2)}) collective-permute-start(bf16[896,256]{1,0:T(8,128)(2,1)S(1)} %get-tuple-element.198.refs_3_), channel_id=1, source_target_pairs={{0,6},{2,4},{4,2},{6,0},{1,7},{3,5},{5,3},{7,1},{8,14},{10,12},{12... | collective-permute-start | bytes 1376264 | tf_op jit(solution)/shard_map/back/ppermute | solution.py:37
  125.3 8.0 %collective-permute-start.34 = (bf16[896,256]{1,0:T(8,128)(2,1)S(1)}, bf16[896,256]{1,0:T(8,128)(2,1)S(1)}, u32[]{:S(2)}, u32[]{:S(2)}) collective-permute-start(bf16[896,256]{1,0:T(8,128)(2,1)S(1)} %get-tuple-element.218.refs_1_.refs_4_), channel_id=1, source_target_pairs={{0,1},{1,0},{2,3},{3,2},{4,5},{5,4},{6,7},{7,6},{8,9},{9,8},{10,11... | collective-permute-start | bytes 1376264 | tf_op jit(solution)/shard_map/mid_core/ppermute | solution.py:37
  125.4 29.4 %collective-permute-start.33 = (bf16[2432,128]{1,0:T(8,128)(2,1)S(1)}, bf16[2432,128]{1,0:T(8,128)(2,1)S(1)}, u32[]{:S(2)}, u32[]{:S(2)}) collective-permute-start(bf16[2432,128]{1,0:T(8,128)(2,1)S(1)} %get-tuple-element.216.refs_4_), channel_id=1, source_target_pairs={{8,16},{16,8},{9,17},{17,9},{10,18},{18,10},{11,19},{19,11},{12,20... | collective-permute-start | bytes 1867784 | tf_op jit(solution)/shard_map/cross_d2/ppermute | solution.py:83
  126.4 28.3 %collective-permute-start.32 = (bf16[1824,128]{1,0:T(8,128)(2,1)S(1)}, bf16[1824,128]{1,0:T(8,128)(2,1)S(1)}, u32[]{:S(2)}, u32[]{:S(2)}) collective-permute-start(bf16[1824,128]{1,0:T(8,128)(2,1)S(1)} %get-tuple-element.215), channel_id=1, source_target_pairs={{0,8},{8,0},{16,24},{24,16},{1,9},{9,1},{17,25},{25,17},{2,10},{10... | collective-permute-start | bytes 1400840 | tf_op jit(solution)/shard_map/swap_d1_g1/ppermute | solution.py:78
  131.2 13.4 %collective-permute-start.35 = (bf16[896,256]{1,0:T(8,128)(2,1)S(1)}, bf16[896,256]{1,0:T(8,128)(2,1)S(1)}, u32[]{:S(2)}, u32[]{:S(2)}) collective-permute-start(bf16[896,256]{1,0:T(8,128)(2,1)S(1)} %get-tuple-element.229), channel_id=1, source_target_pairs={{0,2},{2,0},{4,6},{6,4},{1,3},{3,1},{5,7},{7,5},{8,10},{10,8},{12,... | collective-permute-start | bytes 1376264 | tf_op jit(solution)/shard_map/layer/ppermute | solution.py:37
  133.0 21.8 %collective-permute-start.36 = (bf16[896,256]{1,0:T(8,128)(2,1)S(1)}, bf16[896,256]{1,0:T(8,128)(2,1)S(1)}, u32[]{:S(2)}, u32[]{:S(2)}) collective-permute-start(bf16[896,256]{1,0:T(8,128)(2,1)S(1)} %get-tuple-element.230), channel_id=1, source_target_pairs={{0,4},{2,6},{4,0},{6,2},{1,5},{3,7},{5,1},{7,3},{8,12},{10,14},{12... | collective-permute-start | bytes 1376264 | tf_op jit(solution)/shard_map/layer/ppermute | solution.py:37
  133.3 21.5 %collective-permute-start.37 = (bf16[896,256]{1,0:T(8,128)(2,1)S(1)}, bf16[896,256]{1,0:T(8,128)(2,1)S(1)}, u32[]{:S(2)}, u32[]{:S(2)}) collective-permute-start(bf16[896,256]{1,0:T(8,128)(2,1)S(1)} %get-tuple-element.231), channel_id=1, source_target_pairs={{0,6},{2,4},{4,2},{6,0},{1,7},{3,5},{5,3},{7,1},{8,14},{10,12},{12... | collective-permute-start | bytes 1376264 | tf_op jit(solution)/shard_map/layer/ppermute | solution.py:37
  156.2 21.2 %collective-permute-start.38 = (bf16[2432,128]{1,0:T(8,128)(2,1)S(1)}, bf16[2432,128]{1,0:T(8,128)(2,1)S(1)}, u32[]{:S(2)}, u32[]{:S(2)}) collective-permute-start(bf16[2432,128]{1,0:T(8,128)(2,1)S(1)} %get-tuple-element.233), channel_id=1, source_target_pairs={{0,8},{8,0},{16,24},{24,16},{1,9},{9,1},{17,25},{25,17},{2,10},{10... | collective-permute-start | bytes 1867784 | tf_op jit(solution)/shard_map/swap_d2_g2/ppermute | solution.py:78
  156.7 20.8 %collective-permute-start.40 = (bf16[2336,128]{1,0:T(8,128)(2,1)S(1)}, bf16[2336,128]{1,0:T(8,128)(2,1)S(1)}, u32[]{:S(2)}, u32[]{:S(2)}) collective-permute-start(bf16[2336,128]{1,0:T(8,128)(2,1)S(1)} %get-tuple-element.236), channel_id=1, source_target_pairs={{0,4},{2,6},{4,0},{6,2},{1,5},{3,7},{5,1},{7,3},{8,12},{10,14},{12... | collective-permute-start | bytes 1794056 | tf_op jit(solution)/shard_map/d1_y/ppermute | solution.py:37
  157.0 20.5 %collective-permute-start.41 = (bf16[2336,128]{1,0:T(8,128)(2,1)S(1)}, bf16[2336,128]{1,0:T(8,128)(2,1)S(1)}, u32[]{:S(2)}, u32[]{:S(2)}) collective-permute-start(bf16[2336,128]{1,0:T(8,128)(2,1)S(1)} %get-tuple-element.237), channel_id=1, source_target_pairs={{0,2},{2,0},{4,6},{6,4},{1,3},{3,1},{5,7},{7,5},{8,10},{10,8},{12,... | collective-permute-start | bytes 1794056 | tf_op jit(solution)/shard_map/d1_x/ppermute | solution.py:37
  162.5 14.9 %collective-permute-start.39 = (bf16[1824,128]{1,0:T(8,128)(2,1)S(1)}, bf16[1824,128]{1,0:T(8,128)(2,1)S(1)}, u32[]{:S(2)}, u32[]{:S(2)}) collective-permute-start(bf16[1824,128]{1,0:T(8,128)(2,1)S(1)} %get-tuple-element.235.refs_4_), channel_id=1, source_target_pairs={{8,16},{16,8},{9,17},{17,9},{10,18},{18,10},{11,19},{19,11},{12,20... | collective-permute-start | bytes 1400840 | tf_op jit(solution)/shard_map/cross_g1/ppermute | solution.py:83
  163.2 14.3 %collective-permute-start.42 = (bf16[512,128]{1,0:T(8,128)(2,1)S(1)}, bf16[512,128]{1,0:T(8,128)(2,1)S(1)}, u32[]{:S(2)}, u32[]{:S(2)}) collective-permute-start(bf16[512,128]{1,0:T(8,128)(2,1)S(1)} %get-tuple-element.238), channel_id=1, source_target_pairs={{0,6},{2,4},{4,2},{6,0},{1,7},{3,5},{5,3},{7,1},{8,14},{10,12},{12... | collective-permute-start | bytes 393224 | tf_op jit(solution)/shard_map/grad_kv/ppermute | solution.py:37
  179.0 19.0 %collective-permute-start.46 = (bf16[3344,128]{1,0:T(8,128)(2,1)S(1)}, bf16[3344,128]{1,0:T(8,128)(2,1)S(1)}, u32[]{:S(2)}, u32[]{:S(2)}) collective-permute-start(bf16[3344,128]{1,0:T(8,128)(2,1)S(1)} %get-tuple-element.247), channel_id=1, source_target_pairs={{0,4},{2,6},{4,0},{6,2},{1,5},{3,7},{5,1},{7,3},{8,12},{10,14},{12... | collective-permute-start | bytes 2568200 | tf_op jit(solution)/shard_map/d2_y/ppermute | solution.py:37
  180.7 18.4 %collective-permute-start.47 = (bf16[3344,128]{1,0:T(8,128)(2,1)S(1)}, bf16[3344,128]{1,0:T(8,128)(2,1)S(1)}, u32[]{:S(2)}, u32[]{:S(2)}) collective-permute-start(bf16[3344,128]{1,0:T(8,128)(2,1)S(1)} %get-tuple-element.255), channel_id=1, source_target_pairs={{0,2},{2,0},{4,6},{6,4},{1,3},{3,1},{5,7},{7,5},{8,10},{10,8},{12,... | collective-permute-start | bytes 2568200 | tf_op jit(solution)/shard_map/d2_x/ppermute | solution.py:37
  182.4 12.7 %collective-permute-start.45 = (bf16[2432,128]{1,0:T(8,128)(2,1)S(1)}, bf16[2432,128]{1,0:T(8,128)(2,1)S(1)}, u32[]{:S(2)}, u32[]{:S(2)}) collective-permute-start(bf16[2432,128]{1,0:T(8,128)(2,1)S(1)} %get-tuple-element.245.refs_4_), channel_id=1, source_target_pairs={{8,16},{16,8},{9,17},{17,9},{10,18},{18,10},{11,19},{19,11},{12,20... | collective-permute-start | bytes 1867784 | tf_op jit(solution)/shard_map/cross_g2/ppermute | solution.py:83
  183.4 11.7 %collective-permute-start.44 = (bf16[1824,128]{1,0:T(8,128)(2,1)S(1)}, bf16[1824,128]{1,0:T(8,128)(2,1)S(1)}, u32[]{:S(2)}, u32[]{:S(2)}) collective-permute-start(bf16[1824,128]{1,0:T(8,128)(2,1)S(1)} %get-tuple-element.243), channel_id=1, source_target_pairs={{0,8},{8,0},{16,24},{24,16},{1,9},{9,1},{17,25},{25,17},{2,10},{10... | collective-permute-start | bytes 1400840 | tf_op jit(solution)/shard_map/swap_g1_u1/ppermute | solution.py:78
  201.9 38.1 %collective-permute-start.50 = (bf16[4944,128]{1,0:T(8,128)(2,1)}, bf16[4944,128]{1,0:T(8,128)(2,1)S(1)}, u32[]{:S(2)}, u32[]{:S(2)}) collective-permute-start(bf16[4944,128]{1,0:T(8,128)(2,1)} %get-tuple-element.263), channel_id=1, source_target_pairs={{0,4},{2,6},{4,0},{6,2},{1,5},{3,7},{5,1},{7,3},{8,12},{10,14},{12... | collective-permute-start | bytes 3797000 | tf_op jit(solution)/shard_map/g1_y/ppermute | solution.py:37
  202.5 37.5 %collective-permute-start.51 = (bf16[4944,128]{1,0:T(8,128)(2,1)}, bf16[4944,128]{1,0:T(8,128)(2,1)S(1)}, u32[]{:S(2)}, u32[]{:S(2)}) collective-permute-start(bf16[4944,128]{1,0:T(8,128)(2,1)} %get-tuple-element.264), channel_id=1, source_target_pairs={{0,2},{2,0},{4,6},{6,4},{1,3},{3,1},{5,7},{7,5},{8,10},{10,8},{12,... | collective-permute-start | bytes 3797000 | tf_op jit(solution)/shard_map/g1_x/ppermute | solution.py:37
  204.0 36.3 %collective-permute-start.48 = (bf16[2432,128]{1,0:T(8,128)(2,1)}, bf16[2432,128]{1,0:T(8,128)(2,1)S(1)}, u32[]{:S(2)}, u32[]{:S(2)}) collective-permute-start(bf16[2432,128]{1,0:T(8,128)(2,1)} %get-tuple-element.260), channel_id=1, source_target_pairs={{0,8},{8,0},{16,24},{24,16},{1,9},{9,1},{17,25},{25,17},{2,10},{10... | collective-permute-start | bytes 1867784 | tf_op jit(solution)/shard_map/swap_g2_u2/ppermute | solution.py:78
  205.3 34.7 %collective-permute-start.52 = (bf16[1904,128]{1,0:T(8,128)(2,1)}, bf16[1904,128]{1,0:T(8,128)(2,1)S(1)}, u32[]{:S(2)}, u32[]{:S(2)}) collective-permute-start(bf16[1904,128]{1,0:T(8,128)(2,1)} %get-tuple-element.265), channel_id=1, source_target_pairs={{0,6},{2,4},{4,2},{6,0},{1,7},{3,5},{5,3},{7,1},{8,14},{10,12},{12... | collective-permute-start | bytes 1462280 | tf_op jit(solution)/shard_map/shares/ppermute | solution.py:37
  206.8 33.5 %collective-permute-start.49 = (bf16[1824,128]{1,0:T(8,128)(2,1)S(1)}, bf16[1824,128]{1,0:T(8,128)(2,1)S(1)}, u32[]{:S(2)}, u32[]{:S(2)}) collective-permute-start(bf16[1824,128]{1,0:T(8,128)(2,1)S(1)} %get-tuple-element.262.refs_4_), channel_id=1, source_target_pairs={{8,16},{16,8},{9,17},{17,9},{10,18},{18,10},{11,19},{19,11},{12,20... | collective-permute-start | bytes 1400840 | tf_op jit(solution)/shard_map/cross_u1/ppermute | solution.py:83
  241.7 23.2 %collective-permute-start.58 = (bf16[3344,128]{1,0:T(8,128)(2,1)S(1)}, bf16[3344,128]{1,0:T(8,128)(2,1)S(1)}, u32[]{:S(2)}, u32[]{:S(2)}) collective-permute-start(bf16[3344,128]{1,0:T(8,128)(2,1)S(1)} %get-tuple-element.273), channel_id=1, source_target_pairs={{0,4},{2,6},{4,0},{6,2},{1,5},{3,7},{5,1},{7,3},{8,12},{10,14},{12... | collective-permute-start | bytes 2568200 | tf_op jit(solution)/shard_map/g2_y/ppermute | solution.py:37
  242.6 22.2 %collective-permute-start.59 = (bf16[3344,128]{1,0:T(8,128)(2,1)S(1)}, bf16[3344,128]{1,0:T(8,128)(2,1)S(1)}, u32[]{:S(2)}, u32[]{:S(2)}) collective-permute-start(bf16[3344,128]{1,0:T(8,128)(2,1)S(1)} %get-tuple-element.274), channel_id=1, source_target_pairs={{0,2},{2,0},{4,6},{6,4},{1,3},{3,1},{5,7},{7,5},{8,10},{10,8},{12,... | collective-permute-start | bytes 2568200 | tf_op jit(solution)/shard_map/g2_x/ppermute | solution.py:37
  243.8 21.0 %collective-permute-start.56 = (bf16[2432,128]{1,0:T(8,128)(2,1)S(1)}, bf16[2432,128]{1,0:T(8,128)(2,1)S(1)}, u32[]{:S(2)}, u32[]{:S(2)}) collective-permute-start(bf16[2432,128]{1,0:T(8,128)(2,1)S(1)} %get-tuple-element.271.refs_3_), channel_id=1, source_target_pairs={{8,16},{16,8},{9,17},{17,9},{10,18},{18,10},{11,19},{19,11},{12,20... | collective-permute-start | bytes 1867784 | tf_op jit(solution)/shard_map/cross_u2/ppermute | solution.py:83
  244.5 20.3 %collective-permute-start.57 = (bf16[1904,128]{1,0:T(8,128)(2,1)S(1)}, bf16[1904,128]{1,0:T(8,128)(2,1)S(1)}, u32[]{:S(2)}, u32[]{:S(2)}) collective-permute-start(bf16[1904,128]{1,0:T(8,128)(2,1)S(1)} %get-tuple-element.272.refs_5_), channel_id=1, source_target_pairs={{0,8},{8,0},{16,24},{24,16},{1,9},{9,1},{17,25},{25,17},{2,10},{10... | collective-permute-start | bytes 1462280 | tf_op jit(solution)/shard_map/swap_share/ppermute | solution.py:78
  248.4 16.4 %collective-permute-start.55 = (bf16[1824,128]{1,0:T(8,128)(2,1)S(1)}, bf16[1824,128]{1,0:T(8,128)(2,1)S(1)}, u32[]{:S(2)}, u32[]{:S(2)}) collective-permute-start(bf16[1824,128]{1,0:T(8,128)(2,1)S(1)} %get-tuple-element.270.refs_2_), channel_id=1, source_target_pairs={{0,8},{8,0},{16,24},{24,16},{1,9},{9,1},{17,25},{25,17},{2,10},{10... | collective-permute-start | bytes 1400840 | tf_op jit(solution)/shard_map/swap_u1/ppermute | solution.py:78
  266.2 22.7 %collective-permute-start.62 = (bf16[3040,128]{1,0:T(8,128)(2,1)S(1)}, bf16[3040,128]{1,0:T(8,128)(2,1)S(1)}, u32[]{:S(2)}, u32[]{:S(2)}) collective-permute-start(bf16[3040,128]{1,0:T(8,128)(2,1)S(1)} %get-tuple-element.277), channel_id=1, source_target_pairs={{0,4},{2,6},{4,0},{6,2},{1,5},{3,7},{5,1},{7,3},{8,12},{10,14},{12... | collective-permute-start | bytes 2334728 | tf_op jit(solution)/shard_map/u1_y/ppermute | solution.py:37
  266.3 22.6 %collective-permute-start.63 = (bf16[3040,128]{1,0:T(8,128)(2,1)S(1)}, bf16[3040,128]{1,0:T(8,128)(2,1)S(1)}, u32[]{:S(2)}, u32[]{:S(2)}) collective-permute-start(bf16[3040,128]{1,0:T(8,128)(2,1)S(1)} %get-tuple-element.278), channel_id=1, source_target_pairs={{0,2},{2,0},{4,6},{6,4},{1,3},{3,1},{5,7},{7,5},{8,10},{10,8},{12,... | collective-permute-start | bytes 2334728 | tf_op jit(solution)/shard_map/u1_x/ppermute | solution.py:37
  273.4 15.5 %collective-permute-start.60 = (bf16[2432,128]{1,0:T(8,128)(2,1)S(1)}, bf16[2432,128]{1,0:T(8,128)(2,1)S(1)}, u32[]{:S(2)}, u32[]{:S(2)}) collective-permute-start(bf16[2432,128]{1,0:T(8,128)(2,1)S(1)} %get-tuple-element.275.refs_2_), channel_id=1, source_target_pairs={{0,8},{8,0},{16,24},{24,16},{1,9},{9,1},{17,25},{25,17},{2,10},{10... | collective-permute-start | bytes 1867784 | tf_op jit(solution)/shard_map/swap_u2/ppermute | solution.py:78
  273.4 13.5 %collective-permute-start.61 = (bf16[1904,128]{1,0:T(8,128)(2,1)S(1)}, bf16[1904,128]{1,0:T(8,128)(2,1)S(1)}, u32[]{:S(2)}, u32[]{:S(2)}) collective-permute-start(bf16[1904,128]{1,0:T(8,128)(2,1)S(1)} %get-tuple-element.276.refs_3_), channel_id=1, source_target_pairs={{0,16},{8,24},{16,0},{24,8},{1,17},{9,25},{17,1},{25,9},{2,18},{10... | collective-permute-start | bytes 1462280 | tf_op jit(solution)/shard_map/share_far/ppermute | solution.py:37
  290.0 22.3 %collective-permute-start.64 = (bf16[5248,128]{1,0:T(8,128)(2,1)S(1)}, bf16[5248,128]{1,0:T(8,128)(2,1)S(1)}, u32[]{:S(2)}, u32[]{:S(2)}) collective-permute-start(bf16[5248,128]{1,0:T(8,128)(2,1)S(1)} %get-tuple-element.281), channel_id=1, source_target_pairs={{0,2},{2,0},{4,6},{6,4},{1,3},{3,1},{5,7},{7,5},{8,10},{10,8},{12,... | collective-permute-start | bytes 4030472 | tf_op jit(solution)/shard_map/u2_x/ppermute | solution.py:37
  290.2 22.0 %collective-permute-start.65 = (bf16[5248,128]{1,0:T(8,128)(2,1)S(1)}, bf16[5248,128]{1,0:T(8,128)(2,1)S(1)}, u32[]{:S(2)}, u32[]{:S(2)}) collective-permute-start(bf16[5248,128]{1,0:T(8,128)(2,1)S(1)} %get-tuple-element.282), channel_id=1, source_target_pairs={{0,4},{2,6},{4,0},{6,2},{1,5},{3,7},{5,1},{7,3},{8,12},{10,14},{12... | collective-permute-start | bytes 4030472 | tf_op jit(solution)/shard_map/u2_y/ppermute | solution.py:37
  294.0 29.4 %collective-permute-start.43 = (bf16[256,896]{1,0:T(8,128)(2,1)}, bf16[256,896]{1,0:T(8,128)(2,1)}, u32[]{:S(2)}, u32[]{:S(2)}) collective-permute-start(bf16[256,896]{1,0:T(8,128)(2,1)} %get-tuple-element.242), channel_id=1, source_target_pairs={{0,1},{1,0},{2,3},{3,2},{4,5},{5,4},{6,7},{7,6},{8,9},{9,8},{10,11... | collective-permute-start | bytes 1376264 | tf_op jit(solution)/shard_map/rows_core/ppermute | solution.py:37
  294.0 32.1 %collective-permute-start.54 = (bf16[256,896]{1,0:T(8,128)(2,1)}, bf16[256,896]{1,0:T(8,128)(2,1)}, u32[]{:S(2)}, u32[]{:S(2)}) collective-permute-start(bf16[256,896]{1,0:T(8,128)(2,1)} %get-tuple-element.269), channel_id=1, source_target_pairs={{0,1},{1,0},{2,3},{3,2},{4,5},{5,4},{6,7},{7,6},{8,9},{9,8},{10,11... | collective-permute-start | bytes 1376264 | tf_op jit(solution)/shard_map/rows_core/ppermute | solution.py:37
  317.4 15.3 %collective-permute-start.67 = (bf16[2176,128]{1,0:T(8,128)(2,1)}, bf16[2176,128]{1,0:T(8,128)(2,1)}, u32[]{:S(2)}, u32[]{:S(2)}) collective-permute-start(bf16[2176,128]{1,0:T(8,128)(2,1)} %get-tuple-element.285.refs_8_), channel_id=1, source_target_pairs={{0,2},{2,0},{4,6},{6,4},{1,3},{3,1},{5,7},{7,5},{8,10},{10,8},{12,... | collective-permute-start | bytes 1671176 | tf_op jit(solution)/shard_map/far_x/ppermute | solution.py:37
  319.7 13.0 %collective-permute-start.66 = (bf16[2160,128]{1,0:T(8,128)(2,1)}, bf16[2160,128]{1,0:T(8,128)(2,1)}, u32[]{:S(2)}, u32[]{:S(2)}) collective-permute-start(bf16[2160,128]{1,0:T(8,128)(2,1)} %get-tuple-element.284), channel_id=1, source_target_pairs={{0,4},{2,6},{4,0},{6,2},{1,5},{3,7},{5,1},{7,3},{8,12},{10,14},{12... | collective-permute-start | bytes 1658888 | tf_op jit(solution)/shard_map/far_y/ppermute | solution.py:37
  336.2 6.2 %collective-permute-start.68 = (f32[2,896]{1,0:T(2,128)S(1)}, f32[2,896]{1,0:T(2,128)S(1)}, u32[]{:S(2)}, u32[]{:S(2)}) collective-permute-start(f32[2,896]{1,0:T(2,128)S(1)} %slice.47), channel_id=1, source_target_pairs={{0,1},{1,0},{2,3},{3,2},{4,5},{5,4},{6,7},{7,6},{8,9},{9,8},{10,11... | collective-permute-start | bytes 21512 | tf_op jit(solution)/shard_map/gains_core/ppermute | solution.py:37
  (89 other events, 587.9 us)

commit v4 on v3

--- a/solution.py
+++ b/solution.py
@@ -212,7 +212,7 @@
 
 def attend_kernel(blocks, lengths_ref, place_ref, q_ref, w_out_ref, *refs):
     kv_refs = refs[:blocks]
-    out_ref, log_ref, mine_ref, other_ref, kv_ref, acc_ref, max_ref, bias_ref, part_ref = refs[blocks:]
+    out_ref, log_ref, mine_ref, other_ref, kv_ref, acc_ref, max_ref, bias_ref, part_ref, score_ref = refs[blocks:]
     rows = q_ref.shape[1]
     heads = q_ref.shape[0] // HEAD_DIM
     own, core = place_ref[0], place_ref[1]
@@ -229,13 +229,27 @@
         values = pair.astype(wide).T[HEAD_DIM:].astype(low)
         values = jnp.concatenate([values, jnp.ones((16, rows), low)], axis=0)
         bias_ref[...] = mask_bias(block * rows, rows, q_index, q_start)
+
+        def scores(h):
+            score_ref[h % 2] = dot_nn(keys, q_ref[h * HEAD_DIM : (h + 1) * HEAD_DIM, :])
+
+        def gather(h, weight, shrink):
+            acc_ref[h] = acc_ref[h] * shrink + dot_nn(values, weight)
+
+        scores(0)
+        waiting = None
         for h in range(heads):
-            scores = dot_nn(keys, q_ref[h * HEAD_DIM : (h + 1) * HEAD_DIM, :]) + bias_ref[...]
+            if h + 1 < heads:
+                scores(h + 1)
+            masked = score_ref[h % 2] + bias_ref[...]
             old = max_ref[h : h + 1, :]
-            new = jnp.maximum(old, jnp.max(scores, axis=0, keepdims=True))
-            weight = jnp.exp(scores - new).astype(low)
-            acc_ref[h] = acc_ref[h] * jnp.exp(old - new) + dot_nn(values, weight)
+            new = jnp.maximum(old, jnp.max(masked, axis=0, keepdims=True))
+            weight = jnp.exp(masked - new).astype(low)
             max_ref[h : h + 1, :] = new
+            if waiting is not None:
+                gather(*waiting)
+            waiting = (h, weight, jnp.exp(old - new))
+        gather(*waiting)
         return carry
 
     lax.fori_loop(first_row(lengths_ref, own * rows) // rows, own + 1, visit, 0)
@@ -342,6 +356,13 @@
         refs[2 * count + i][...] = (refs[2 * i][...].astype(wide) + refs[2 * i + 1][...].astype(wide)).astype(low)
 
 
+def join_kernel(place_ref, mine_ref, other_ref, out_ref):
+    half = mine_ref.shape[0]
+    core = place_ref[1]
+    out_ref[pl.ds(pl.multiple_of(core * half, half), half), :] = mine_ref[...].astype(out_ref.dtype)
+    out_ref[pl.ds(pl.multiple_of((1 - core) * half, half), half), :] = other_ref[...].astype(out_ref.dtype)
+
+
 def wait_kernel(*refs):
     pass
 
@@ -410,13 +431,23 @@
 ):
     kv_refs, refs = refs[:blocks], refs[blocks:]
     (grad_q_ref, *grad_kv_refs), refs = refs[: blocks + 1], refs[blocks + 1 :]
-    kv_ref, bias_ref, dq_ref, dk_ref, dv_ref, grad_kv_ref = refs
+    kv_ref, bias_ref, dq_ref, q_all_ref, go_all_ref, weight_ref, grad_ref, grad_kv_ref, score_ref, grad_weight_ref = refs
     rows = q_ref.shape[1]
     heads = grad_q_ref.shape[0] // HEAD_DIM
     own = place_ref[0]
+
+    def lanes(h):
+        return slice(h * rows, (h + 1) * rows)
+
+    def span(h):
+        return slice(h * HEAD_DIM, (h + 1) * HEAD_DIM)
+
     for r in range(blocks):
         kv_ref[r] = kv_refs[r][...]
         grad_kv_ref[r] = jnp.zeros_like(grad_kv_ref[r])
+    for h in range(heads):
+        q_all_ref[:, lanes(h)] = q_ref[span(h), :]
+        go_all_ref[:, lanes(h)] = go_ref[span(h), :]
     dq_ref[...] = jnp.zeros_like(dq_ref)
     q_index = own * rows + lax.broadcasted_iota(jnp.int32, (1, rows), 1)
     q_start = segment_start(lengths_ref, q_index)
@@ -427,31 +458,31 @@
         values = pair[:, HEAD_DIM:]
         keys_t = pair.astype(wide).T[:HEAD_DIM].astype(low)
         bias_ref[...] = mask_bias(block * rows, rows, q_index, q_start)
+
+        def products(h):
+            score_ref[h % 2] = dot_nn(keys, q_all_ref[:, lanes(h)])
+            grad_weight_ref[h % 2] = dot_nn(values, go_all_ref[:, lanes(h)])
+
+        products(0)
         for h in range(heads):
-            span = slice(h * HEAD_DIM, (h + 1) * HEAD_DIM)
-            scores = dot_nn(keys, q_ref[span, :]) + bias_ref[...]
-            weight = jnp.exp(scores - log_ref[h : h + 1, :])
-            grad_weight = dot_nn(values, go_ref[span, :])
-            grad_scores = (weight * (grad_weight - delta_ref[h : h + 1, :])).astype(low)
-            dq_ref[span, :] += dot_nn(keys_t, grad_scores)
-            dk = dot_nt(grad_scores, q_ref[span, :])
-            dv = dot_nt(weight.astype(low), go_ref[span, :])
-            if h == 0:
-                dk_ref[...] = dk
-                dv_ref[...] = dv
-            else:
-                dk_ref[...] += dk
-                dv_ref[...] += dv
-        grad_kv_ref[block ^ own] = jnp.concatenate([dk_ref[...], dv_ref[...]], axis=1).astype(low)
+            if h + 1 < heads:
+                products(h + 1)
+            weight = jnp.exp(score_ref[h % 2] + bias_ref[...] - log_ref[h : h + 1, :])
+            grad = (weight * (grad_weight_ref[h % 2] - delta_ref[h : h + 1, :])).astype(low)
+            weight_ref[:, lanes(h)] = weight.astype(low)
+            grad_ref[:, lanes(h)] = grad
+            dq_ref[span(h), :] += dot_nn(keys_t, grad)
+        grad_keys = dot_nt(grad_ref[...], q_all_ref[...])
+        grad_values = dot_nt(weight_ref[...], go_all_ref[...])
+        grad_kv_ref[block ^ own] = jnp.concatenate([grad_keys, grad_values], axis=1).astype(low)
         return carry
 
     lax.fori_loop(first_row(lengths_ref, own * rows) // rows, own + 1, visit, 0)
     for r in range(blocks):
         grad_kv_refs[r][...] = grad_kv_ref[r]
     for h in range(heads):
-        span = slice(h * HEAD_DIM, (h + 1) * HEAD_DIM)
-        turned = rotate(dq_ref[span, :] * HEAD_DIM**-0.5, cos_ref[...], -sin_ref[...])
-        grad_q_ref[span, :] = turned.astype(low)
+        turned = rotate(dq_ref[span(h), :] * HEAD_DIM**-0.5, cos_ref[...], -sin_ref[...])
+        grad_q_ref[span(h), :] = turned.astype(low)
 
 
 def query_kernel(
@@ -539,11 +570,9 @@
     out_ref[...] = grad.T.astype(low)
 
 
-def place_kernel(transposed, tiles, place_ref, *refs):
-    own_ref, near_x_ref, near_y_ref, *far_refs = refs[:7]
-    out_ref = refs[-2] if transposed else refs[-1]
-    all_ref = refs[-1]
-    step = pl.program_id(0)
+def place_kernel(transposed, tiles, place_ref, refs, out_ref, all_ref):
+    own_ref, near_x_ref, near_y_ref, *far_refs = refs
+    step, tiles = tiles
     units = own_ref.shape[0]
     half = units // 2
     for r, ref in enumerate((own_ref, near_x_ref, near_y_ref)):
@@ -565,28 +594,30 @@
         out_ref[...] = all_ref[...].T
 
 
-def place_share(place, own, near_x, near_y, far_y, far_x, units, transposed, width, at, whole, last):
+def place_shares(place, shares, units, transposed, width, at, whole, last):
     tile, half = 128, units // 2
-    tiles = own.shape[0] // units
+    counts = [share[0].shape[0] // units for share in shares]
+    begins = [sum(counts[:i]) for i in range(len(counts))]
     first = at // tile
-    piece = pl.BlockSpec((units, tile), lambda i: (i, 0))
-
-    def halves(start, k, later):
-        base = start // half
-
-        def index(i):
-            part = 2 * i + k - (tiles if later else 0)
-            return (base + jnp.clip(part, 0, tiles - 1), 0)
-
-        return pl.BlockSpec((half, tile), index)
-
-    ins = [place, own, near_x, near_y, far_y[0], far_y[0], far_x[0], far_x[0]] + last
-    specs = (
-        [in_smem, piece, piece, piece]
-        + [halves(far_y[1], k, False) for k in range(2)]
-        + [halves(far_x[1], k, True) for k in range(2)]
-        + [pl.BlockSpec(memory_space=pl.ANY)] * len(last)
-    )
+    ins, specs = [place], [in_smem]
+    for (own, near_x, near_y, far_y, far_x), tiles, begin in zip(shares, counts, begins):
+
+        def step_of(i, tiles=tiles, begin=begin):
+            return jnp.clip(i - begin, 0, tiles - 1)
+
+        def halves(start, k, later, tiles=tiles, step_of=step_of):
+            def index(i):
+                part = 2 * step_of(i) + k - (tiles if later else 0)
+                return (start // half + jnp.clip(part, 0, tiles - 1), 0)
+
+            return pl.BlockSpec((half, tile), index)
+
+        ins += [own, near_x, near_y, far_y[0], far_y[0], far_x[0], far_x[0]]
+        specs += [pl.BlockSpec((units, tile), lambda i, step_of=step_of: (step_of(i), 0))] * 3
+        specs += [halves(far_y[1], k, False) for k in range(2)]
+        specs += [halves(far_x[1], k, True) for k in range(2)]
+    ins += last
+    specs += [pl.BlockSpec(memory_space=pl.ANY)] * len(last)
     aliases = {}
     if whole is not None:
         aliases = {len(ins): 0}
@@ -594,7 +625,15 @@
         specs.append(pl.BlockSpec(memory_space=pl.ANY))
 
     def body(*refs):
-        place_kernel(transposed, tiles, *refs[:8], *refs[len(ins) :])
+        out_ref, token_ref = refs[len(ins) : len(ins) + 2]
+        all_ref = refs[-1] if transposed else out_ref
+        token_ref[...] = jnp.zeros_like(token_ref)
+        for n, (tiles, begin) in enumerate(zip(counts, begins)):
+            step = pl.program_id(0) - begin
+
+            @pl.when((step >= 0) & (step < tiles))
+            def _(n=n, step=step, tiles=tiles):
+                place_kernel(transposed, (step, tiles), refs[0], refs[1 + 7 * n : 8 + 7 * n], out_ref, all_ref)
 
     if transposed:
         dims = (width, 4 * units)
@@ -607,10 +646,10 @@
     return pl.pallas_call(
         body,
         name="place_kernel",
-        out_shape=shape(dims, wide),
-        grid=(tiles,),
+        out_shape=(shape(dims, wide), shape((8, 128), wide)),
+        grid=(sum(counts),),
         in_specs=specs,
-        out_specs=out_spec,
+        out_specs=(out_spec, pl.BlockSpec((8, 128), lambda i: (0, 0))),
         scratch_shapes=scratch,
         input_output_aliases=aliases,
         cost_estimate=pl.CostEstimate(flops=0, bytes_accessed=0, transcendentals=0),
@@ -646,14 +685,6 @@
     place = jnp.stack([own_block, own_core, lax.axis_index("dp")]).astype(jnp.int32)
     gain_two = norm2_gain.reshape(1, width)
 
-    def whole_rows(mine):
-        other = partner(mine, "tensor", 1, "rows_core")
-        return jnp.where(
-            own_core == 0,
-            jnp.concatenate([mine, other], axis=0),
-            jnp.concatenate([other, mine], axis=0),
-        )
-
     half_dim = HEAD_DIM // 2
     turn = (rope_base ** (-2.0 * jnp.arange(half_dim, dtype=wide) / HEAD_DIM)).reshape(half_dim, 1)
     q_t, key_value, normed_t, tokens_t, cosine, sine = call(
@@ -709,6 +740,7 @@
             pltpu.VMEM((heads + 1, rows), wide),
             pltpu.VMEM((rows, rows), wide),
             pltpu.VMEM((width, rows), wide),
+            pltpu.VMEM((2, rows, rows), wide),
         ],
         in_specs=[in_smem] * 2 + [in_vmem] * (2 + blocks),
         after=[gate_t],
@@ -889,9 +921,13 @@
             pltpu.VMEM((blocks, rows, 2 * HEAD_DIM), low),
             pltpu.VMEM((rows, rows), wide),
             pltpu.VMEM((q_width, rows), wide),
-            pltpu.VMEM((rows, HEAD_DIM), wide),
-            pltpu.VMEM((rows, HEAD_DIM), wide),
+            pltpu.VMEM((HEAD_DIM, heads * rows), low),
+            pltpu.VMEM((HEAD_DIM, heads * rows), low),
+            pltpu.VMEM((rows, heads * rows), low),
+            pltpu.VMEM((rows, heads * rows), low),
             pltpu.VMEM((blocks, rows, 2 * HEAD_DIM), low),
+            pltpu.VMEM((2, rows, rows), wide),
+            pltpu.VMEM((2, rows, rows), wide),
         ],
         in_specs=[in_smem] * 2 + [in_vmem] * (6 + blocks),
     )
@@ -939,6 +975,15 @@
             in_specs=[in_smem] + [in_vmem] * 5,
         )
         return grad_half
+
+    def join(mine, other, kind):
+        (whole,) = ordered(
+            join_kernel,
+            [shape((rows, width), kind)],
+            [place, mine.astype(kind), other.astype(kind)],
+            in_specs=[in_smem] + [in_vmem] * 2,
+        )
+        return whole
 
     def layer_leave():
         (layer_half,) = ordered(layer_kernel, [shape((half, width), low)], [hidden] + layer_pieces)
@@ -963,8 +1008,10 @@
         kv_pieces = scatter_blocks(grad_kv, "grad_kv")
         grad_w_query, normed_part, grad_b_query, grad_w_out = query_back()
         *shares, normed_mine, normed_other = key_back(kv_pieces, [0] * blocks)
-        layer_out = whole_rows(layer_leave())
+        layer_half = layer_leave()
+        layer_out = join(layer_half, partner(layer_half, "tensor", 1, "rows_core"), low)
         grad_half = leave(normed_mine, partner(normed_other, "tensor", 1, "normed_core"))
+        grad_tokens = join(grad_half, partner(grad_half, "tensor", 1, "rows_core"), wide)
         own_share = sum_share(scatter_blocks(shares, "shares"), [0] * blocks)
         own_share = lax.psum(own_share, "dp")
         pieces = gather_blocks(own_share, "all_share")
@@ -1020,7 +1067,7 @@
         )
         x2, y2 = both_ways(x2, y2, "d2")
         g1_u1_swap, g2_cross = swap(g1_u1, "swap_g1_u1"), cross(g2_sum, "cross_g2")
-        layer_out = whole_rows(layer_half)
+        layer_passed = partner(layer_half, "tensor", 1, "rows_core")
         *shares, normed_mine, normed_other = key_back([grad_kv[0], x1, y1, kv_far], [0, r1, r1, 0])
         g1_all, u1_sum, g2_sum, g2_u2, x3, y3, share_far, normed_other = tick(
             [
@@ -1038,10 +1085,7 @@
         share_far = partner(share_far, "blk", 3, "shares")
         g2_u2_swap, u1_cross = swap(g2_u2, "swap_g2_u2"), cross(u1_sum, "cross_u1")
         normed_passed = partner(normed_other, "tensor", 1, "normed_core")
-        grad_w_down = place_share(
-            place, d1_all, x1, y1, (y2, r2), (x2, r2), units, False, width, 0, None, last
-        )
-        last = [grad_w_down]
+        layer_out = join(layer_half, layer_passed, low)
         grad_half = leave(normed_mine, normed_passed)
         own_share = sum_share([shares[0], x3, y3, share_far], [0, r1 + h2, r1 + h2, 0])
         g2_all, u2_sum, u1_sum, x4, y4, own_share, grad_half = tick(
@@ -1057,11 +1101,9 @@
         x4, y4 = both_ways(x4, y4, "g2")
         share_swap = swap(own_share, "swap_share")
         u1_swap, u2_cross = swap(u1_sum, "swap_u1"), cross(u2_sum, "cross_u2")
-        grad_tokens = whole_rows(grad_half).astype(wide)
-        grad_w_down = place_share(
-            place, d2_all, x2, y2, (y3, r1), (x3, r1), units, False, width, cut_at, grad_w_down, [x3]
-        )
-        last = [grad_w_down]
+        grad_passed = partner(grad_half, "tensor", 1, "rows_core")
+        d_shares = [(d1_all, x1, y1, (y2, r2), (x2, r2)), (d2_all, x2, y2, (y3, r1), (x3, r1))]
+        grad_w_down, *last = place_shares(place, d_shares, units, False, width, 0, None, last)
         u1_all, u2_sum, own_share, x5, y5 = tick(
             [
                 ("pick", u1_swap, u1_sum),
@@ -1074,10 +1116,6 @@
         )
         x5, y5 = both_ways(x5, y5, "u1")
         u2_swap, share_swap = swap(u2_sum, "swap_u2"), partner(own_share, "dp", 2, "share_far")
-        grad_w_gate = place_share(
-            place, g1_all, x3, y3, (y4, r2), (x4, r2), units, True, width, 0, None, last
-        )
-        last = [grad_w_gate]
         u2_all, own_share, x6, y6 = tick(
             [
                 ("pick", u2_swap, u2_sum),
@@ -1088,39 +1126,36 @@
             needs=[x5, y5],
         )
         x6, y6 = both_ways(x6, y6, "u2")
-        grad_w_gate = place_share(
-            place, g2_all, x4, y4, (y5, r1), (x5, r1), units, True, width, cut_at, grad_w_gate, [x5]
-        )
-        last = [grad_w_gate]
+        grad_tokens = join(grad_half, grad_passed, wide)
+        g_shares = [(g1_all, x3, y3, (y4, r2), (x4, r2)), (g2_all, x4, y4, (y5, r1), (x5, r1))]
+        grad_w_gate, *last = place_shares(place, g_shares, units, True, width, 0, None, last)
         first_half = stack_rows // 32 * 16
         share_at = r2 + h1
-        x7, y7 = tick(
+        far = tick(
             [
-                ("cat", (y6, h2, h2), (y6, share_at + first_half, stack_rows - first_half)),
-                ("cat", (x6, 0, h2), (x6, share_at, first_half)),
+                ("cat", (y6, share_at + first_half, stack_rows - first_half)),
+                ("cat", (x6, share_at, first_half)),
+                ("cat", (y6, h2, h2)),
+                ("cat", (x6, 0, h2)),
             ],
         )
-        x7, y7 = both_ways(x7, y7, "far")
-        grad_w_up = place_share(
-            place, u1_all, x5, y5, (y6, r2), (x6, r2), units, True, width, 0, None, last
-        )
-        last = [grad_w_up]
-        grad_w_up = place_share(
-            place, u2_all, x6, y6, (y7, 0), (x7, 0), units, True, width, cut_at, grad_w_up, []
-        )
-        last = [y7]
+        share_x, share_y = both_ways(far[0], far[1], "far_share")
+        x7, y7 = both_ways(far[2], far[3], "far_u2")
+        u_shares = [(u1_all, x5, y5, (y6, r2), (x6, r2)), (u2_all, x6, y6, (y7, 0), (x7, 0))]
+        grad_w_up, *last = place_shares(place, u_shares[:1], units, True, width, 0, None, last)
         grad_w_query, grad_w_key, grad_w_value, grad_w_out, small = unpack(
-            [own_share, x6, y6, y7, x7],
+            [own_share, x6, y6, share_y, share_x],
             [
                 (0, 0, stack_rows, 0),
                 (1, 0, stack_rows, share_at),
                 (2, 0, stack_rows, share_at),
-                (3, 0, first_half, h2),
-                (3, first_half, stack_rows - first_half, h2),
+                (3, 0, first_half, 0),
+                (3, first_half, stack_rows - first_half, 0),
             ],
         )
-    if blocks != 4:
-        grad_tokens = whole_rows(grad_half).astype(wide)
+        grad_w_up, _ = place_shares(
+            place, u_shares[1:], units, True, width, cut_at, grad_w_up, [small]
+        )
     gains = small[:2]
     gains = gains + partner(gains, "tensor", 1, "gains_core")
     grad_b = small[2]

time: 350 us -> 338 us (0.966)
  other arithmetic: 5.65 us -> 0.22 us
  starting transfers between devices: 87.3 us -> 82.4 us
    ppermute x54 -> x56, starting transfers between devices: 65 us -> 60.4 us  [partner(): return lax.ppermute(value, axis, [(i, i ^ step) for i in range(count)])]
    ppermute x54 -> x56, waiting for transfers between devices: 104 us -> 108 us  [partner(): return lax.ppermute(value, axis, [(i, i ^ step) for i in range(count)])]
    pallas_call x6 -> x4, Pallas kernels: 22.7 us -> 20 us  [place_shares(): pl.pallas_call(body, name='place_kernel', out_shape=(shape(dims, wide), s...]
    unnamed x168 -> x148, local copies, waits for them, and re-layouts: 22.9 us -> 21.8 us
    pallas_call x37 -> x39, Pallas kernels: 75 us -> 74.7 us  [call(): pl.pallas_call(run, name=getattr(body, 'func', body).__name__, out_shape=...]
  transfers between devices with their start and end apart: 69 -> 71, of which waited for: 27 -> 29; matrix products, arithmetic and copies ran while one was open for 2% -> 1% of each run, Pallas kernels for 23% -> 23%
where the time goes in v4:
time: 338 us; the launch traced here: 332 us
  waiting for transfers between devices  126 us (37%)
  Pallas kernels  94.7 us (28%)
  starting transfers between devices  82.4 us (24%)
  local copies, waits for them, and re-layouts  26.4 us (8%)
    ppermute x56, waiting for transfers between devices, partner(): return lax.ppermute(value, axis, [(i, i ^ step) for i in range(count)])  108 us
    pallas_call x39, Pallas kernels, call(): pl.pallas_call(run, name=getattr(body, 'func', body).__name__, out_shape=...  74.7 us
    ppermute x56, starting transfers between devices, partner(): return lax.ppermute(value, axis, [(i, i ^ step) for i in range(count)])  60.4 us
    unnamed x148, local copies, waits for them, and re-layouts  21.8 us
    pallas_call x4, Pallas kernels, place_shares(): pl.pallas_call(body, name='place_kernel', out_shape=(shape(dims, wide), s...  20 us
    ppermute x9, waiting for transfers between devices, swap(): return lax.ppermute(value, 'dp', [(0, 1), (1, 0), (2, 3), (3, 2)])  17.6 us
    ppermute x9, starting transfers between devices, swap(): return lax.ppermute(value, 'dp', [(0, 1), (1, 0), (2, 3), (3, 2)])  17.5 us
  transfers between devices with their start and end apart: 71, of which 29 were waited for; matrix products, arithmetic and copies ran while one was open for 1% of the time, Pallas kernels for 23%

profile of v4, /device:TPU:0, one launch (start us, length us, event | category | flops | bytes accessed | tf_op | source)
XLA Modules:
  0.0 331.8 jit_solution(18041435400647907727)
XLA Ops:
  8.2 2.3 enter_kernel.1
  12.1 3.9 %collective-permute-start.4 = (bf16[512,128]{1,0:T(8,128)(2,1)S(1)}, bf16[512,128]{1,0:T(8,128)(2,1)S(1)}, u32[]{:S(2)}, u32[]{:S(2)}) collective-permute-start(bf16[512,128]{1,0:T(8,128)(2,1)S(1)} %get-tuple-element.166.refs_4_.refs_8_), channel_id=1, source_target_pairs={{0,6},{2,4},{4,2},{6,0},{1,7},{3,5},{5,3},{7,1},{8,14},{10,12},{12... | collective-permute-start | bytes 393224 | tf_op jit(solution)/shard_map/kv/ppermute | solution.py:37
  17.9 2.2 copy-done.1
  20.1 4.6 %weights_kernel.1 = (bf16[608,896]{1,0:T(8,128)(2,1)S(1)}, bf16[896,608]{1,0:T(8,128)(2,1)S(1)}, bf16[608,896]{1,0:T(8,128)(2,1)S(1)}, bf16[896,608]{1,0:T(8,128...) custom-call(s32[1,3]{1,0:T(1,128)S(1)} %copy-done.70, ...), custom_call_target="tpu_custom_call" | custom-call | tf_op jit(solution)/shard_map/weights_kernel/pallas_call | solution.py:96
  24.8 2.1 collective-permute-start.6
  26.9 1.5 collective-permute-start
  28.4 4.5 %attend_kernel.1 = (f32[448,512]{1,0:T(8,128)S(1)}, f32[8,512]{1,0:T(8,128)S(1)}, f32[896,256]{1,0:T(8,128)S(1)}, bf16[896,256]{1,0:T(8,128)(2,1)S(1)}) custom-call(s32[1,3]{1,0:T(1,128)S(1)} %copy-done.70, s32[3]{0:T(128)S(1)} %pad_add_fusion.refs_1_.refs_0_, bf16[448,512]{1,0:T(8,128)(2,1)S(1)} %get-tuple-element.162.refs_6_.refs_2_.refs_5_, ...), custom_call_target="tpu_custom_call" | custom-call | tf_op jit(solution)/shard_map/attend_kernel/pallas_call | solution.py:96
  33.9 2.7 collective-permute-done.6.refs_6_.refs_1_.refs_9_
  40.0 3.5 %collective-permute-start.9 = (bf16[896,256]{1,0:T(8,128)(2,1)S(1)}, bf16[896,256]{1,0:T(8,128)(2,1)S(1)}, u32[]{:S(2)}, u32[]{:S(2)}) collective-permute-start(bf16[896,256]{1,0:T(8,128)(2,1)S(1)} %get-tuple-element.170.refs_3_.refs_9_.refs_5_), channel_id=1, source_target_pairs={{0,4},{2,6},{4,0},{6,2},{1,5},{3,7},{5,1},{7,3},{8,12},{10,14},{12... | collective-permute-start | bytes 1376264 | tf_op jit(solution)/shard_map/x/ppermute | solution.py:37
  43.5 2.7 collective-permute-start.8
  46.2 3.9 %hidden_kernel.4 = (bf16[608,512]{1,0:T(8,128)(2,1)S(1)}, bf16[608,512]{1,0:T(8,128)(2,1)S(1)}, bf16[608,512]{1,0:T(8,128)(2,1)S(1)}, bf16[896,256]{1,0:T(8,128)(2,1)S(1)}, bf16[896,256]{1,0:T(8,128)(2,1)S(1)}) custom-call(bf16[256,896]{1,0:T(8,128)(2,1)S(1)} %get-tuple-element.164.refs_0_.refs_4_, ...), custom_call_target="tpu_custom_call" | custom-call | tf_op jit(solution)/shard_map/hidden_kernel/pallas_call | solution.py:96
  50.2 4.4 %collective-permute-done.9.refs_3_ = bf16[896,256]{1,0:T(8,128)(2,1)S(1)} collective-permute-done((bf16[896,256]{1,0:T(8,128)(2,1)S(1)}, bf16[896,256]{1,0:T(8,128)(2,1)S(1)}, u32[]{:S(2)}, u32[]{:S(2)}) %collective-permute-start.9) | collective-permute-done | bytes 458784 | tf_op jit(solution)/shard_map/x/ppermute | solution.py:37
  54.6 2.5 collective-permute-done.8.refs_2_
  57.1 1.8 collective-permute-start.14
  59.6 1.8 collective-permute-start.11
  61.4 3.9 %hidden_kernel.5 = (bf16[608,512]{1,0:T(8,128)(2,1)S(1)}, bf16[608,512]{1,0:T(8,128)(2,1)S(1)}, bf16[608,512]{1,0:T(8,128)(2,1)S(1)}, bf16[896,256]{1,0:T(8,128)(2,1)S(1)}, bf16[896,256]{1,0:T(8,128)(2,1)S(1)}) custom-call(bf16[256,896]{1,0:T(8,128)(2,1)S(1)} %collective-permute-done.1.refs_0_.refs_6_, ...), custom_call_target="tpu_custom_call" | custom-call | tf_op jit(solution)/shard_map/hidden_kernel/pallas_call | solution.py:96
  67.4 2.7 collective-permute-done.12.refs_3_
  70.1 1.5 collective-permute-done.11.refs_2_
  71.7 3.9 %hidden_kernel.6 = (bf16[608,512]{1,0:T(8,128)(2,1)S(1)}, bf16[608,512]{1,0:T(8,128)(2,1)S(1)}, bf16[608,512]{1,0:T(8,128)(2,1)S(1)}, bf16[896,256]{1,0:T(8,128)(2,1)S(1)}, bf16[896,256]{1,0:T(8,128)(2,1)S(1)}) custom-call(bf16[256,896]{1,0:T(8,128)(2,1)S(1)} %collective-permute-done.20.refs_0_.refs_8_, ...), custom_call_target="tpu_custom_call" | custom-call | tf_op jit(solution)/shard_map/hidden_kernel/pallas_call | solution.py:96
  79.9 4.1 %hidden_kernel.7 = (bf16[608,512]{1,0:T(8,128)(2,1)S(1)}, bf16[608,512]{1,0:T(8,128)(2,1)S(1)}, bf16[608,512]{1,0:T(8,128)(2,1)S(1)}, bf16[896,256]{1,0:T(8,128)(2,1)S(1)}, bf16[896,256]{1,0:T(8,128)(2,1)S(1)}) custom-call(bf16[128,896]{1,0:T(8,128)(2,1)S(1)} %collective-permute-done.15.refs_0_.refs_10_, ...), custom_call_target="tpu_custom_call" | custom-call | tf_op jit(solution)/shard_map/hidden_kernel/pallas_call | solution.py:96
  86.9 1.5 weight_kernel.4.refs_14_.refs_1_
  88.5 2.1 collective-permute-start.27
  92.9 4.2 %project_kernel.1 = (bf16[4,896,256]{2,1,0:T(8,128)(2,1)}, bf16[896,256]{1,0:T(8,128)(2,1)S(1)}, bf16[896,256]{1,0:T(8,128)(2,1)S(1)}, bf16[896,256]{1,0:T(8,128)(2,1)S(1)}, bf16[896,256]{1,0:T(8,128)(2,1)S(1)}) custom-call(bf16[896,608]{1,0:T(8,128)(2,1)S(1)} %copy-done.28, bf16[608,512]{1,0:T(8,128)(2,1)S(1)} %get-tuple-element.174.refs_0_.refs_1_, ...), custom_call_target="tpu_custom_call" | custom-call | tf_op jit(solution)/shard_map/project_kernel/pallas_call | solution.py:96
  98.7 5.0 %collective-permute-done.25.refs_4_.refs_7_ = bf16[896,256]{1,0:T(8,128)(2,1)S(1)} collective-permute-done((bf16[896,256]{1,0:T(8,128)(2,1)}, bf16[896,256]{1,0:T(8,128)(2,1)S(1)}, u32[]{:S(2)}, u32[]{:S(2)}) %collective-permute-start.25) | collective-permute-done | bytes 458784 | tf_op jit(solution)/shard_map/back/ppermute | solution.py:37
  106.0 1.5 collective-permute-start.29
  107.6 2.8 weight_kernel.6
  110.5 2.8 weight_kernel.7
  113.3 6.3 %collective-permute-done.29.refs_9_.refs_6_ = bf16[896,256]{1,0:T(8,128)(2,1)S(1)} collective-permute-done((bf16[896,256]{1,0:T(8,128)(2,1)S(1)}, bf16[896,256]{1,0:T(8,128)(2,1)S(1)}, u32[]{:S(2)}, u32[]{:S(2)}) %collective-permute-start.29) | collective-permute-done | bytes 458784 | tf_op jit(solution)/shard_map/back/ppermute | solution.py:37
  124.8 4.8 %collective-permute-start.32 = (bf16[1824,128]{1,0:T(8,128)(2,1)S(1)}, bf16[1824,128]{1,0:T(8,128)(2,1)S(1)}, u32[]{:S(2)}, u32[]{:S(2)}) collective-permute-start(bf16[1824,128]{1,0:T(8,128)(2,1)S(1)} %get-tuple-element.224), channel_id=1, source_target_pairs={{0,8},{8,0},{16,24},{24,16},{1,9},{9,1},{17,25},{25,17},{2,10},{10... | collective-permute-start | bytes 1400840 | tf_op jit(solution)/shard_map/swap_d1_g1/ppermute | solution.py:78
  129.6 1.7 collective-permute-start.35
  134.5 6.3 %attend_back_kernel.1 = (bf16[448,512]{1,0:T(8,128)(2,1)S(1)}, bf16[512,128]{1,0:T(8,128)(2,1)S(1)}, bf16[512,128]{1,0:T(8,128)(2,1)S(1)}, bf16[512,128]{1,0:T(8,128)(2,1)S(1)}, bf16[512,128]{1,0:T(8,128)(2,1)S(1)}) custom-call(s32[1,3]{1,0:T(1,128)S(1)} %copy-done.70, s32[3]{0:T(128)S(1)} %pad_add_fusion.refs_1_.refs_0_, ...), custom_call_target="tpu_custom_call" | custom-call | tf_op jit(solution)/shard_map/attend_back_kernel/pallas_call | solution.py:96
  140.8 2.3 collective-permute-done.35.refs_10_.refs_2_
  143.1 10.1 %collective-permute-done.36.refs_11_.refs_3_ = bf16[896,256]{1,0:T(8,128)(2,1)S(1)} collective-permute-done((bf16[896,256]{1,0:T(8,128)(2,1)S(1)}, bf16[896,256]{1,0:T(8,128)(2,1)S(1)}, u32[]{:S(2)}, u32[]{:S(2)}) %collective-permute-start.36) | collective-permute-done | bytes 458784 | tf_op jit(solution)/shard_map/layer/ppermute | solution.py:37
  155.3 4.3 %collective-permute-start.41 = (bf16[2336,128]{1,0:T(8,128)(2,1)S(1)}, bf16[2336,128]{1,0:T(8,128)(2,1)S(1)}, u32[]{:S(2)}, u32[]{:S(2)}) collective-permute-start(bf16[2336,128]{1,0:T(8,128)(2,1)S(1)} %get-tuple-element.246), channel_id=1, source_target_pairs={{0,2},{2,0},{4,6},{6,4},{1,3},{3,1},{5,7},{7,5},{8,10},{10,8},{12,... | collective-permute-start | bytes 1794056 | tf_op jit(solution)/shard_map/d1_x/ppermute | solution.py:37
  160.4 2.3 query_kernel.1
  164.0 10.6 %collective-permute-done.42.refs_11_.refs_15_ = bf16[512,128]{1,0:T(8,128)(2,1)S(1)} collective-permute-done((bf16[512,128]{1,0:T(8,128)(2,1)S(1)}, bf16[512,128]{1,0:T(8,128)(2,1)S(1)}, u32[]{:S(2)}, u32[]{:S(2)}) %collective-permute-start.42) | collective-permute-done | bytes 131104 | tf_op jit(solution)/shard_map/grad_kv/ppermute | solution.py:37
  176.1 1.7 collective-permute-start.46
  177.9 1.7 collective-permute-start.47
  180.3 4.5 %collective-permute-start.44 = (bf16[1824,128]{1,0:T(8,128)(2,1)S(1)}, bf16[1824,128]{1,0:T(8,128)(2,1)S(1)}, u32[]{:S(2)}, u32[]{:S(2)}) collective-permute-start(bf16[1824,128]{1,0:T(8,128)(2,1)S(1)} %get-tuple-element.252), channel_id=1, source_target_pairs={{0,8},{8,0},{16,24},{24,16},{1,9},{9,1},{17,25},{25,17},{2,10},{10... | collective-permute-start | bytes 1400840 | tf_op jit(solution)/shard_map/swap_g1_u1/ppermute | solution.py:78
  184.8 1.5 copy-done.26
  186.3 2.2 key_kernel.1
  188.6 3.4 %collective-permute-done.44.refs_1_ = bf16[1824,128]{1,0:T(8,128)(2,1)S(1)} collective-permute-done((bf16[1824,128]{1,0:T(8,128)(2,1)S(1)}, bf16[1824,128]{1,0:T(8,128)(2,1)S(1)}, u32[]{:S(2)}, u32[]{:S(2)}) %collective-permute-start.44) | collective-permute-done | bytes 466976 | tf_op jit(solution)/shard_map/swap_g1_u1/ppermute | solution.py:78
  192.0 3.1 collective-permute-done.46.refs_7_.refs_13_.refs_4_.refs_5_.refs_10_
  196.3 1.5 tick_kernel.13
  204.2 1.5 join_kernel.2.refs_6_
  208.3 27.5 %collective-permute-done.52.refs_3_ = bf16[1904,128]{1,0:T(8,128)(2,1)S(1)} collective-permute-done((bf16[1904,128]{1,0:T(8,128)(2,1)S(1)}, bf16[1904,128]{1,0:T(8,128)(2,1)S(1)}, u32[]{:S(2)}, u32[]{:S(2)}) %collective-permute-start.52) | collective-permute-done | bytes 487456 | tf_op jit(solution)/shard_map/shares/ppermute | solution.py:37
  240.3 3.9 %collective-permute-start.57 = (bf16[1904,128]{1,0:T(8,128)(2,1)S(1)}, bf16[1904,128]{1,0:T(8,128)(2,1)S(1)}, u32[]{:S(2)}, u32[]{:S(2)}) collective-permute-start(bf16[1904,128]{1,0:T(8,128)(2,1)S(1)} %get-tuple-element.281.refs_5_), channel_id=1, source_target_pairs={{0,8},{8,0},{16,24},{24,16},{1,9},{9,1},{17,25},{25,17},{2,10},{10... | collective-permute-start | bytes 1462280 | tf_op jit(solution)/shard_map/swap_share/ppermute | solution.py:78
  244.3 5.3 %place_kernel.4 = (f32[2432,896]{1,0:T(8,128)}, f32[8,128]{1,0:T(8,128)S(1)}) custom-call(s32[3]{0:T(128)S(1)} %pad_add_fusion.refs_1_.refs_0_, bf16[1824,128]{1,0:T(8,128)(2,1)S(1)} %get-tuple-element.249.refs_7_.refs_1_, bf16[2336,128]{1,0:T(8,128)(2,1)S(1)} %collective-permute-done.41.refs_8_.refs_9_.refs_13_.refs_2_, ...), custom_call_target="tpu_custom_call" | custom-call | tf_op jit(solution)/shard_map/place_kernel/pallas_call | solution.py:646
  249.5 11.1 %collective-permute-done.55.refs_1_ = bf16[1824,128]{1,0:T(8,128)(2,1)S(1)} collective-permute-done((bf16[1824,128]{1,0:T(8,128)(2,1)S(1)}, bf16[1824,128]{1,0:T(8,128)(2,1)S(1)}, u32[]{:S(2)}, u32[]{:S(2)}) %collective-permute-start.55) | collective-permute-done | bytes 466976 | tf_op jit(solution)/shard_map/swap_u1/ppermute | solution.py:78
  262.0 7.2 %collective-permute-start.63 = (bf16[3040,128]{1,0:T(8,128)(2,1)S(1)}, bf16[3040,128]{1,0:T(8,128)(2,1)S(1)}, u32[]{:S(2)}, u32[]{:S(2)}) collective-permute-start(bf16[3040,128]{1,0:T(8,128)(2,1)S(1)} %get-tuple-element.289), channel_id=1, source_target_pairs={{0,2},{2,0},{4,6},{6,4},{1,3},{3,1},{5,7},{7,5},{8,10},{10,8},{12,... | collective-permute-start | bytes 2334728 | tf_op jit(solution)/shard_map/u1_x/ppermute | solution.py:37
  269.2 1.9 collective-permute-start.61
  271.1 11.6 %collective-permute-done.61.refs_4_ = bf16[1904,128]{1,0:T(8,128)(2,1)S(1)} collective-permute-done((bf16[1904,128]{1,0:T(8,128)(2,1)S(1)}, bf16[1904,128]{1,0:T(8,128)(2,1)S(1)}, u32[]{:S(2)}, u32[]{:S(2)}) %collective-permute-start.61) | collective-permute-done | bytes 487456 | tf_op jit(solution)/shard_map/share_far/ppermute | solution.py:37
  282.7 2.0 collective-permute-done.60.refs_1_
  286.0 3.7 %collective-permute-start.65 = (bf16[5248,128]{1,0:T(8,128)(2,1)S(1)}, bf16[5248,128]{1,0:T(8,128)(2,1)S(1)}, u32[]{:S(2)}, u32[]{:S(2)}) collective-permute-start(bf16[5248,128]{1,0:T(8,128)(2,1)S(1)} %get-tuple-element.294), channel_id=1, source_target_pairs={{0,4},{2,6},{4,0},{6,2},{1,5},{3,7},{5,1},{7,3},{8,12},{10,14},{12... | collective-permute-start | bytes 4030472 | tf_op jit(solution)/shard_map/u2_y/ppermute | solution.py:37
  289.8 1.7 collective-permute-done.54
  291.6 1.9 join_kernel.3.refs_15_
  293.5 1.5 copy-done
  295.0 6.9 %place_kernel.5 = (f32[896,2432]{1,0:T(8,128)}, f32[8,128]{1,0:T(8,128)S(1)}) custom-call(s32[3]{0:T(128)S(1)} %pad_add_fusion.refs_1_.refs_0_, bf16[1824,128]{1,0:T(8,128)(2,1)S(1)} %get-tuple-element.269.refs_3_.refs_1_, bf16[4944,128]{1,0:T(8,128)(2,1)S(1)} %collective-permute-done.51.refs_1_.refs_7_.refs_13_.refs_14_.refs_2_, ...), custom_call_target="tpu_custom_call" | custom-call | tf_op jit(solution)/shard_map/place_kernel/pallas_call | solution.py:646
  301.9 9.7 %collective-permute-done.64.refs_2_.refs_6_.refs_7_ = bf16[5248,128]{1,0:T(8,128)(2,1)S(1)} collective-permute-done((bf16[5248,128]{1,0:T(8,128)(2,1)S(1)}, bf16[5248,128]{1,0:T(8,128)(2,1)S(1)}, u32[]{:S(2)}, u32[]{:S(2)}) %collective-permute-start.64) | collective-permute-done | bytes 1343520 | tf_op jit(solution)/shard_map/u2_x/ppermute | solution.py:37
  312.2 2.5 collective-permute-start.67
  314.8 3.7 %collective-permute-start.66 = (bf16[944,128]{1,0:T(8,128)(2,1)S(1)}, bf16[944,128]{1,0:T(8,128)(2,1)S(1)}, u32[]{:S(2)}, u32[]{:S(2)}) collective-permute-start(bf16[944,128]{1,0:T(8,128)(2,1)S(1)} %get-tuple-element.296), channel_id=1, source_target_pairs={{0,4},{2,6},{4,0},{6,2},{1,5},{3,7},{5,1},{7,3},{8,12},{10,14},{12... | collective-permute-start | bytes 725000 | tf_op jit(solution)/shard_map/far_share_y/ppermute | solution.py:37
  318.6 3.7 %place_kernel.6 = (f32[896,2432]{1,0:T(8,128)}, f32[8,128]{1,0:T(8,128)S(1)}) custom-call(s32[3]{0:T(128)S(1)} %pad_add_fusion.refs_1_.refs_0_, bf16[1824,128]{1,0:T(8,128)(2,1)S(1)} %get-tuple-element.290.refs_7_.refs_1_, bf16[3040,128]{1,0:T(8,128)(2,1)S(1)} %collective-permute-done.63.refs_6_.refs_8_.refs_13_.refs_14_.refs_2_, ...), custom_call_target="tpu_custom_call" | custom-call | tf_op jit(solution)/shard_map/place_kernel/pallas_call | solution.py:646
  322.6 2.7 unpack_kernel.1
  327.1 4.2 %place_kernel.7 = (f32[896,2432]{1,0:T(8,128)}, f32[8,128]{1,0:T(8,128)}) custom-call(s32[3]{0:T(128)S(1)} %pad_add_fusion.refs_1_.refs_0_, bf16[2432,128]{1,0:T(8,128)(2,1)S(1)} %get-tuple-element.291.refs_3_.refs_1_, bf16[5248,128]{1,0:T(8,128)(2,1)S(1)} %collective-permute-done.64.refs_2_.refs_6_.refs_7_, ...), custom_call_target="tpu_custom_call", output_to_operand_aliasing={{0}: (9, {})} | custom-call | tf_op jit(solution)/shard_map/place_kernel/pallas_call | solution.py:646
  (286 shorter events, 66.3 us)
Async XLA Ops:
  12.1 16.3 %collective-permute-start.4 = (bf16[512,128]{1,0:T(8,128)(2,1)S(1)}, bf16[512,128]{1,0:T(8,128)(2,1)S(1)}, u32[]{:S(2)}, u32[]{:S(2)}) collective-permute-start(bf16[512,128]{1,0:T(8,128)(2,1)S(1)} %get-tuple-element.166.refs_4_.refs_8_), channel_id=1, source_target_pairs={{0,6},{2,4},{4,2},{6,0},{1,7},{3,5},{5,3},{7,1},{8,14},{10,12},{12... | collective-permute-start | bytes 393224 | tf_op jit(solution)/shard_map/kv/ppermute | solution.py:37
  16.0 12.4 %collective-permute-start.3 = (bf16[512,128]{1,0:T(8,128)(2,1)S(1)}, bf16[512,128]{1,0:T(8,128)(2,1)S(1)}, u32[]{:S(2)}, u32[]{:S(2)}) collective-permute-start(bf16[512,128]{1,0:T(8,128)(2,1)S(1)} %get-tuple-element.166.refs_4_.refs_8_), channel_id=1, source_target_pairs={{0,4},{2,6},{4,0},{6,2},{1,5},{3,7},{5,1},{7,3},{8,12},{10,14},{12... | collective-permute-start | bytes 393224 | tf_op jit(solution)/shard_map/kv/ppermute | solution.py:37
  16.5 11.9 %collective-permute-start.2 = (bf16[512,128]{1,0:T(8,128)(2,1)S(1)}, bf16[512,128]{1,0:T(8,128)(2,1)S(1)}, u32[]{:S(2)}, u32[]{:S(2)}) collective-permute-start(bf16[512,128]{1,0:T(8,128)(2,1)S(1)} %get-tuple-element.166.refs_4_.refs_8_), channel_id=1, source_target_pairs={{0,2},{2,0},{4,6},{6,4},{1,3},{3,1},{5,7},{7,5},{8,10},{10,8},{12,... | collective-permute-start | bytes 393224 | tf_op jit(solution)/shard_map/kv/ppermute | solution.py:37
  24.8 11.8 %collective-permute-start.6 = (bf16[256,896]{1,0:T(8,128)(2,1)S(1)}, bf16[256,896]{1,0:T(8,128)(2,1)S(1)}, u32[]{:S(2)}, u32[]{:S(2)}) collective-permute-start(bf16[256,896]{1,0:T(8,128)(2,1)S(1)} %get-tuple-element.163.refs_1_.refs_5_.refs_2_), channel_id=1, source_target_pairs={{0,4},{2,6},{4,0},{6,2},{1,5},{3,7},{5,1},{7,3},{8,12},{10,14},{12... | collective-permute-start | bytes 1376264 | tf_op jit(solution)/shard_map/gy/ppermute | solution.py:37
  26.9 11.1 %collective-permute-start = (bf16[256,896]{1,0:T(8,128)(2,1)S(1)}, bf16[256,896]{1,0:T(8,128)(2,1)S(1)}, u32[]{:S(2)}, u32[]{:S(2)}) collective-permute-start(bf16[256,896]{1,0:T(8,128)(2,1)S(1)} %get-tuple-element.163.refs_1_.refs_5_.refs_2_), channel_id=1, source_target_pairs={{0,2},{2,0},{4,6},{6,4},{1,3},{3,1},{5,7},{7,5},{8,10},{10,8},{12,... | collective-permute-start | bytes 1376264 | tf_op jit(solution)/shard_map/gy/ppermute | solution.py:37
  33.9 4.1 %collective-permute-start.5 = (bf16[896,256]{1,0:T(8,128)(2,1)S(1)}, bf16[896,256]{1,0:T(8,128)(2,1)S(1)}, u32[]{:S(2)}, u32[]{:S(2)}) collective-permute-start(bf16[896,256]{1,0:T(8,128)(2,1)S(1)} %get-tuple-element.169), channel_id=1, source_target_pairs={{0,1},{1,0},{2,3},{3,2},{4,5},{5,4},{6,7},{7,6},{8,9},{9,8},{10,11... | collective-permute-start | bytes 1376264 | tf_op jit(solution)/shard_map/part_core/ppermute | solution.py:37
  40.0 6.2 %collective-permute-start.7 = (bf16[896,256]{1,0:T(8,128)(2,1)S(1)}, bf16[896,256]{1,0:T(8,128)(2,1)S(1)}, u32[]{:S(2)}, u32[]{:S(2)}) collective-permute-start(bf16[896,256]{1,0:T(8,128)(2,1)S(1)} %get-tuple-element.170.refs_3_.refs_9_.refs_5_), channel_id=1, source_target_pairs={{0,1},{1,0},{2,3},{3,2},{4,5},{5,4},{6,7},{7,6},{8,9},{9,8},{10,11... | collective-permute-start | bytes 1376264 | tf_op jit(solution)/shard_map/x_core/ppermute | solution.py:37
  40.0 14.6 %collective-permute-start.9 = (bf16[896,256]{1,0:T(8,128)(2,1)S(1)}, bf16[896,256]{1,0:T(8,128)(2,1)S(1)}, u32[]{:S(2)}, u32[]{:S(2)}) collective-permute-start(bf16[896,256]{1,0:T(8,128)(2,1)S(1)} %get-tuple-element.170.refs_3_.refs_9_.refs_5_), channel_id=1, source_target_pairs={{0,4},{2,6},{4,0},{6,2},{1,5},{3,7},{5,1},{7,3},{8,12},{10,14},{12... | collective-permute-start | bytes 1376264 | tf_op jit(solution)/shard_map/x/ppermute | solution.py:37
  43.5 13.6 %collective-permute-start.8 = (bf16[896,256]{1,0:T(8,128)(2,1)S(1)}, bf16[896,256]{1,0:T(8,128)(2,1)S(1)}, u32[]{:S(2)}, u32[]{:S(2)}) collective-permute-start(bf16[896,256]{1,0:T(8,128)(2,1)S(1)} %get-tuple-element.170.refs_3_.refs_9_.refs_5_), channel_id=1, source_target_pairs={{0,2},{2,0},{4,6},{6,4},{1,3},{3,1},{5,7},{7,5},{8,10},{10,8},{12,... | collective-permute-start | bytes 1376264 | tf_op jit(solution)/shard_map/x/ppermute | solution.py:37
  46.2 13.4 %collective-permute-start.1 = (bf16[256,896]{1,0:T(8,128)(2,1)S(1)}, bf16[256,896]{1,0:T(8,128)(2,1)S(1)}, u32[]{:S(2)}, u32[]{:S(2)}) collective-permute-start(bf16[256,896]{1,0:T(8,128)(2,1)S(1)} %collective-permute-done.refs_5_.refs_1_.refs_7_), channel_id=1, source_target_pairs={{0,1},{1,0},{2,3},{3,2},{4,5},{5,4},{6,7},{7,6},{8,9},{9,8},{10,11... | collective-permute-start | bytes 1376264 | tf_op jit(solution)/shard_map/gy_core/ppermute | solution.py:37
  57.1 4.4 %collective-permute-start.10 = (bf16[896,256]{1,0:T(8,128)(2,1)S(1)}, bf16[896,256]{1,0:T(8,128)(2,1)S(1)}, u32[]{:S(2)}, u32[]{:S(2)}) collective-permute-start(bf16[896,256]{1,0:T(8,128)(2,1)S(1)} %get-tuple-element.176.refs_3_.refs_7_), channel_id=1, source_target_pairs={{0,1},{1,0},{2,3},{3,2},{4,5},{5,4},{6,7},{7,6},{8,9},{9,8},{10,11... | collective-permute-start | bytes 1376264 | tf_op jit(solution)/shard_map/x_core/ppermute | solution.py:37
  57.1 8.5 %collective-permute-start.14 = (bf16[128,896]{1,0:T(8,128)(2,1)S(1)}, bf16[128,896]{1,0:T(8,128)(2,1)S(1)}, u32[]{:S(2)}, u32[]{:S(2)}) collective-permute-start(bf16[128,896]{1,0:T(8,128)(2,1)S(1)} %slice.57), channel_id=1, source_target_pairs={{0,2},{2,0},{4,6},{6,4},{1,3},{3,1},{5,7},{7,5},{8,10},{10,8},{12,... | collective-permute-start | bytes 688136 | tf_op jit(solution)/shard_map/gy_relay/ppermute | solution.py:37
  58.9 8.5 %collective-permute-start.13 = (bf16[128,896]{1,0:T(8,128)(2,1)S(1)}, bf16[128,896]{1,0:T(8,128)(2,1)S(1)}, u32[]{:S(2)}, u32[]{:S(2)}) collective-permute-start(bf16[128,896]{1,0:T(8,128)(2,1)S(1)} %slice.56), channel_id=1, source_target_pairs={{0,4},{2,6},{4,0},{6,2},{1,5},{3,7},{5,1},{7,3},{8,12},{10,14},{12... | collective-permute-start | bytes 688136 | tf_op jit(solution)/shard_map/gy_relay/ppermute | solution.py:37
  59.3 10.8 %collective-permute-start.12 = (bf16[448,256]{1,0:T(8,128)(2,1)S(1)}, bf16[448,256]{1,0:T(8,128)(2,1)S(1)}, u32[]{:S(2)}, u32[]{:S(2)}) collective-permute-start(bf16[448,256]{1,0:T(8,128)(2,1)S(1)} %slice.44), channel_id=1, source_target_pairs={{0,2},{2,0},{4,6},{6,4},{1,3},{3,1},{5,7},{7,5},{8,10},{10,8},{12,... | collective-permute-start | bytes 688136 | tf_op jit(solution)/shard_map/x_relay/ppermute | solution.py:37
  59.6 12.0 %collective-permute-start.11 = (bf16[448,256]{1,0:T(8,128)(2,1)S(1)}, bf16[448,256]{1,0:T(8,128)(2,1)S(1)}, u32[]{:S(2)}, u32[]{:S(2)}) collective-permute-start(bf16[448,256]{1,0:T(8,128)(2,1)S(1)} %slice.43), channel_id=1, source_target_pairs={{0,4},{2,6},{4,0},{6,2},{1,5},{3,7},{5,1},{7,3},{8,12},{10,14},{12... | collective-permute-start | bytes 688136 | tf_op jit(solution)/shard_map/x_relay/ppermute | solution.py:37
  61.4 10.2 %collective-permute-start.20 = (bf16[256,896]{1,0:T(8,128)(2,1)S(1)}, bf16[256,896]{1,0:T(8,128)(2,1)S(1)}, u32[]{:S(2)}, u32[]{:S(2)}) collective-permute-start(bf16[256,896]{1,0:T(8,128)(2,1)S(1)} %collective-permute-done.6.refs_6_.refs_1_.refs_9_), channel_id=1, source_target_pairs={{0,1},{1,0},{2,3},{3,2},{4,5},{5,4},{6,7},{7,6},{8,9},{9,8},{10,11... | collective-permute-start | bytes 1376264 | tf_op jit(solution)/shard_map/gy_core/ppermute | solution.py:37
  65.5 6.1 %collective-permute-start.21 = (bf16[896,256]{1,0:T(8,128)(2,1)S(1)}, bf16[896,256]{1,0:T(8,128)(2,1)S(1)}, u32[]{:S(2)}, u32[]{:S(2)}) collective-permute-start(bf16[896,256]{1,0:T(8,128)(2,1)S(1)} %get-tuple-element.180.refs_3_.refs_9_), channel_id=1, source_target_pairs={{0,1},{1,0},{2,3},{3,2},{4,5},{5,4},{6,7},{7,6},{8,9},{9,8},{10,11... | collective-permute-start | bytes 1376264 | tf_op jit(solution)/shard_map/x_core/ppermute | solution.py:37
  71.6 4.0 %collective-permute-start.19 = (bf16[896,256]{1,0:T(8,128)(2,1)S(1)}, bf16[896,256]{1,0:T(8,128)(2,1)S(1)}, u32[]{:S(2)}, u32[]{:S(2)}) collective-permute-start(bf16[896,256]{1,0:T(8,128)(2,1)S(1)} %get-tuple-element.186.refs_9_), channel_id=1, source_target_pairs={{0,1},{1,0},{2,3},{3,2},{4,5},{5,4},{6,7},{7,6},{8,9},{9,8},{10,11... | collective-permute-start | bytes 1376264 | tf_op jit(solution)/shard_map/back_core/ppermute | solution.py:37
  76.7 9.0 %collective-permute-start.22 = (bf16[896,256]{1,0:T(8,128)(2,1)S(1)}, bf16[896,256]{1,0:T(8,128)(2,1)S(1)}, u32[]{:S(2)}, u32[]{:S(2)}) collective-permute-start(bf16[896,256]{1,0:T(8,128)(2,1)S(1)} %get-tuple-element.192), channel_id=1, source_target_pairs={{0,1},{1,0},{2,3},{3,2},{4,5},{5,4},{6,7},{7,6},{8,9},{9,8},{10,11... | collective-permute-start | bytes 1376264 | tf_op jit(solution)/shard_map/back_core/ppermute | solution.py:37
  88.5 15.4 %collective-permute-start.27 = (bf16[1824,128]{1,0:T(8,128)(2,1)S(1)}, bf16[1824,128]{1,0:T(8,128)(2,1)S(1)}, u32[]{:S(2)}, u32[]{:S(2)}) collective-permute-start(bf16[1824,128]{1,0:T(8,128)(2,1)S(1)} %weight_kernel.4.refs_14_.refs_1_), channel_id=1, source_target_pairs={{0,8},{8,0},{16,24},{24,16},{1,9},{9,1},{17,25},{25,17},{2,10},{10... | collective-permute-start | bytes 1400840 | tf_op jit(solution)/shard_map/swap_d1/ppermute | solution.py:78
  90.6 8.1 %collective-permute-start.24 = (bf16[896,256]{1,0:T(8,128)(2,1)S(1)}, bf16[896,256]{1,0:T(8,128)(2,1)S(1)}, u32[]{:S(2)}, u32[]{:S(2)}) collective-permute-start(bf16[896,256]{1,0:T(8,128)(2,1)S(1)} %get-tuple-element.177.refs_9_), channel_id=1, source_target_pairs={{0,1},{1,0},{2,3},{3,2},{4,5},{5,4},{6,7},{7,6},{8,9},{9,8},{10,11... | collective-permute-start | bytes 1376264 | tf_op jit(solution)/shard_map/back_core/ppermute | solution.py:37
  90.6 13.1 %collective-permute-start.25 = (bf16[896,256]{1,0:T(8,128)(2,1)}, bf16[896,256]{1,0:T(8,128)(2,1)S(1)}, u32[]{:S(2)}, u32[]{:S(2)}) collective-permute-start(bf16[896,256]{1,0:T(8,128)(2,1)} %get-tuple-element.189.refs_13_), channel_id=1, source_target_pairs={{0,2},{2,0},{4,6},{6,4},{1,3},{3,1},{5,7},{7,5},{8,10},{10,8},{12,... | collective-permute-start | bytes 1376264 | tf_op jit(solution)/shard_map/back/ppermute | solution.py:37
  90.9 12.8 %collective-permute-start.23 = (bf16[896,256]{1,0:T(8,128)(2,1)S(1)}, bf16[896,256]{1,0:T(8,128)(2,1)S(1)}, u32[]{:S(2)}, u32[]{:S(2)}) collective-permute-start(bf16[896,256]{1,0:T(8,128)(2,1)S(1)} %get-tuple-element.195), channel_id=1, source_target_pairs={{0,1},{1,0},{2,3},{3,2},{4,5},{5,4},{6,7},{7,6},{8,9},{9,8},{10,11... | collective-permute-start | bytes 1376264 | tf_op jit(solution)/shard_map/back_core/ppermute | solution.py:37
  91.1 12.8 %collective-permute-start.26 = (bf16[896,256]{1,0:T(8,128)(2,1)S(1)}, bf16[896,256]{1,0:T(8,128)(2,1)S(1)}, u32[]{:S(2)}, u32[]{:S(2)}) collective-permute-start(bf16[896,256]{1,0:T(8,128)(2,1)S(1)} %get-tuple-element.197.refs_14_), channel_id=1, source_target_pairs={{0,4},{2,6},{4,0},{6,2},{1,5},{3,7},{5,1},{7,3},{8,12},{10,14},{12... | collective-permute-start | bytes 1376264 | tf_op jit(solution)/shard_map/back/ppermute | solution.py:37
  104.2 18.8 %collective-permute-start.28 = (bf16[4,896,256]{2,1,0:T(8,128)(2,1)}, bf16[4,896,256]{2,1,0:T(8,128)(2,1)S(1)}, u32[]{:S(2)}, u32[]{:S(2)}) collective-permute-start(bf16[4,896,256]{2,1,0:T(8,128)(2,1)} %get-tuple-element.200), channel_id=1, source_target_pairs={{0,1},{1,0},{2,3},{3,2},{4,5},{5,4},{6,7},{7,6},{8,9},{9,8},{10,11... | collective-permute-start | bytes 5505032 | tf_op jit(solution)/shard_map/layer_core/ppermute | solution.py:37
  104.3 16.4 %collective-permute-start.31 = (bf16[2432,128]{1,0:T(8,128)(2,1)S(1)}, bf16[2432,128]{1,0:T(8,128)(2,1)S(1)}, u32[]{:S(2)}, u32[]{:S(2)}) collective-permute-start(bf16[2432,128]{1,0:T(8,128)(2,1)S(1)} %get-tuple-element.208.refs_3_), channel_id=1, source_target_pairs={{0,8},{8,0},{16,24},{24,16},{1,9},{9,1},{17,25},{25,17},{2,10},{10... | collective-permute-start | bytes 1867784 | tf_op jit(solution)/shard_map/swap_d2/ppermute | solution.py:78
  105.3 14.3 %collective-permute-start.30 = (bf16[1824,128]{1,0:T(8,128)(2,1)S(1)}, bf16[1824,128]{1,0:T(8,128)(2,1)S(1)}, u32[]{:S(2)}, u32[]{:S(2)}) collective-permute-start(bf16[1824,128]{1,0:T(8,128)(2,1)S(1)} %tick_kernel.9.refs_14_.refs_1_), channel_id=1, source_target_pairs={{8,16},{16,8},{9,17},{17,9},{10,18},{18,10},{11,19},{19,11},{12,20... | collective-permute-start | bytes 1400840 | tf_op jit(solution)/shard_map/cross_d1/ppermute | solution.py:83
  106.0 13.6 %collective-permute-start.29 = (bf16[896,256]{1,0:T(8,128)(2,1)S(1)}, bf16[896,256]{1,0:T(8,128)(2,1)S(1)}, u32[]{:S(2)}, u32[]{:S(2)}) collective-permute-start(bf16[896,256]{1,0:T(8,128)(2,1)S(1)} %get-tuple-element.207.refs_3_), channel_id=1, source_target_pairs={{0,6},{2,4},{4,2},{6,0},{1,7},{3,5},{5,3},{7,1},{8,14},{10,12},{12... | collective-permute-start | bytes 1376264 | tf_op jit(solution)/shard_map/back/ppermute | solution.py:37
  123.9 7.7 %collective-permute-start.34 = (bf16[896,256]{1,0:T(8,128)(2,1)S(1)}, bf16[896,256]{1,0:T(8,128)(2,1)S(1)}, u32[]{:S(2)}, u32[]{:S(2)}) collective-permute-start(bf16[896,256]{1,0:T(8,128)(2,1)S(1)} %get-tuple-element.227.refs_1_.refs_4_), channel_id=1, source_target_pairs={{0,1},{1,0},{2,3},{3,2},{4,5},{5,4},{6,7},{7,6},{8,9},{9,8},{10,11... | collective-permute-start | bytes 1376264 | tf_op jit(solution)/shard_map/mid_core/ppermute | solution.py:37
  124.0 29.1 %collective-permute-start.33 = (bf16[2432,128]{1,0:T(8,128)(2,1)S(1)}, bf16[2432,128]{1,0:T(8,128)(2,1)S(1)}, u32[]{:S(2)}, u32[]{:S(2)}) collective-permute-start(bf16[2432,128]{1,0:T(8,128)(2,1)S(1)} %get-tuple-element.225.refs_4_), channel_id=1, source_target_pairs={{8,16},{16,8},{9,17},{17,9},{10,18},{18,10},{11,19},{19,11},{12,20... | collective-permute-start | bytes 1867784 | tf_op jit(solution)/shard_map/cross_d2/ppermute | solution.py:83
  124.8 28.3 %collective-permute-start.32 = (bf16[1824,128]{1,0:T(8,128)(2,1)S(1)}, bf16[1824,128]{1,0:T(8,128)(2,1)S(1)}, u32[]{:S(2)}, u32[]{:S(2)}) collective-permute-start(bf16[1824,128]{1,0:T(8,128)(2,1)S(1)} %get-tuple-element.224), channel_id=1, source_target_pairs={{0,8},{8,0},{16,24},{24,16},{1,9},{9,1},{17,25},{25,17},{2,10},{10... | collective-permute-start | bytes 1400840 | tf_op jit(solution)/shard_map/swap_d1_g1/ppermute | solution.py:78
  129.6 13.4 %collective-permute-start.35 = (bf16[896,256]{1,0:T(8,128)(2,1)S(1)}, bf16[896,256]{1,0:T(8,128)(2,1)S(1)}, u32[]{:S(2)}, u32[]{:S(2)}) collective-permute-start(bf16[896,256]{1,0:T(8,128)(2,1)S(1)} %get-tuple-element.238), channel_id=1, source_target_pairs={{0,2},{2,0},{4,6},{6,4},{1,3},{3,1},{5,7},{7,5},{8,10},{10,8},{12,... | collective-permute-start | bytes 1376264 | tf_op jit(solution)/shard_map/layer/ppermute | solution.py:37
  131.4 21.8 %collective-permute-start.36 = (bf16[896,256]{1,0:T(8,128)(2,1)S(1)}, bf16[896,256]{1,0:T(8,128)(2,1)S(1)}, u32[]{:S(2)}, u32[]{:S(2)}) collective-permute-start(bf16[896,256]{1,0:T(8,128)(2,1)S(1)} %get-tuple-element.239), channel_id=1, source_target_pairs={{0,4},{2,6},{4,0},{6,2},{1,5},{3,7},{5,1},{7,3},{8,12},{10,14},{12... | collective-permute-start | bytes 1376264 | tf_op jit(solution)/shard_map/layer/ppermute | solution.py:37
  131.7 21.5 %collective-permute-start.37 = (bf16[896,256]{1,0:T(8,128)(2,1)S(1)}, bf16[896,256]{1,0:T(8,128)(2,1)S(1)}, u32[]{:S(2)}, u32[]{:S(2)}) collective-permute-start(bf16[896,256]{1,0:T(8,128)(2,1)S(1)} %get-tuple-element.240), channel_id=1, source_target_pairs={{0,6},{2,4},{4,2},{6,0},{1,7},{3,5},{5,3},{7,1},{8,14},{10,12},{12... | collective-permute-start | bytes 1376264 | tf_op jit(solution)/shard_map/layer/ppermute | solution.py:37
  154.6 20.0 %collective-permute-start.38 = (bf16[2432,128]{1,0:T(8,128)(2,1)S(1)}, bf16[2432,128]{1,0:T(8,128)(2,1)S(1)}, u32[]{:S(2)}, u32[]{:S(2)}) collective-permute-start(bf16[2432,128]{1,0:T(8,128)(2,1)S(1)} %get-tuple-element.242), channel_id=1, source_target_pairs={{0,8},{8,0},{16,24},{24,16},{1,9},{9,1},{17,25},{25,17},{2,10},{10... | collective-permute-start | bytes 1867784 | tf_op jit(solution)/shard_map/swap_d2_g2/ppermute | solution.py:78
  155.0 19.6 %collective-permute-start.40 = (bf16[2336,128]{1,0:T(8,128)(2,1)S(1)}, bf16[2336,128]{1,0:T(8,128)(2,1)S(1)}, u32[]{:S(2)}, u32[]{:S(2)}) collective-permute-start(bf16[2336,128]{1,0:T(8,128)(2,1)S(1)} %get-tuple-element.245), channel_id=1, source_target_pairs={{0,4},{2,6},{4,0},{6,2},{1,5},{3,7},{5,1},{7,3},{8,12},{10,14},{12... | collective-permute-start | bytes 1794056 | tf_op jit(solution)/shard_map/d1_y/ppermute | solution.py:37
  155.3 19.3 %collective-permute-start.41 = (bf16[2336,128]{1,0:T(8,128)(2,1)S(1)}, bf16[2336,128]{1,0:T(8,128)(2,1)S(1)}, u32[]{:S(2)}, u32[]{:S(2)}) collective-permute-start(bf16[2336,128]{1,0:T(8,128)(2,1)S(1)} %get-tuple-element.246), channel_id=1, source_target_pairs={{0,2},{2,0},{4,6},{6,4},{1,3},{3,1},{5,7},{7,5},{8,10},{10,8},{12,... | collective-permute-start | bytes 1794056 | tf_op jit(solution)/shard_map/d1_x/ppermute | solution.py:37
  159.7 14.9 %collective-permute-start.39 = (bf16[1824,128]{1,0:T(8,128)(2,1)S(1)}, bf16[1824,128]{1,0:T(8,128)(2,1)S(1)}, u32[]{:S(2)}, u32[]{:S(2)}) collective-permute-start(bf16[1824,128]{1,0:T(8,128)(2,1)S(1)} %get-tuple-element.244.refs_4_), channel_id=1, source_target_pairs={{8,16},{16,8},{9,17},{17,9},{10,18},{18,10},{11,19},{19,11},{12,20... | collective-permute-start | bytes 1400840 | tf_op jit(solution)/shard_map/cross_g1/ppermute | solution.py:83
  160.3 14.3 %collective-permute-start.42 = (bf16[512,128]{1,0:T(8,128)(2,1)S(1)}, bf16[512,128]{1,0:T(8,128)(2,1)S(1)}, u32[]{:S(2)}, u32[]{:S(2)}) collective-permute-start(bf16[512,128]{1,0:T(8,128)(2,1)S(1)} %get-tuple-element.247), channel_id=1, source_target_pairs={{0,6},{2,4},{4,2},{6,0},{1,7},{3,5},{5,3},{7,1},{8,14},{10,12},{12... | collective-permute-start | bytes 393224 | tf_op jit(solution)/shard_map/grad_kv/ppermute | solution.py:37
  176.1 19.0 %collective-permute-start.46 = (bf16[3344,128]{1,0:T(8,128)(2,1)S(1)}, bf16[3344,128]{1,0:T(8,128)(2,1)S(1)}, u32[]{:S(2)}, u32[]{:S(2)}) collective-permute-start(bf16[3344,128]{1,0:T(8,128)(2,1)S(1)} %get-tuple-element.256), channel_id=1, source_target_pairs={{0,4},{2,6},{4,0},{6,2},{1,5},{3,7},{5,1},{7,3},{8,12},{10,14},{12... | collective-permute-start | bytes 2568200 | tf_op jit(solution)/shard_map/d2_y/ppermute | solution.py:37
  177.9 18.4 %collective-permute-start.47 = (bf16[3344,128]{1,0:T(8,128)(2,1)S(1)}, bf16[3344,128]{1,0:T(8,128)(2,1)S(1)}, u32[]{:S(2)}, u32[]{:S(2)}) collective-permute-start(bf16[3344,128]{1,0:T(8,128)(2,1)S(1)} %get-tuple-element.264), channel_id=1, source_target_pairs={{0,2},{2,0},{4,6},{6,4},{1,3},{3,1},{5,7},{7,5},{8,10},{10,8},{12,... | collective-permute-start | bytes 2568200 | tf_op jit(solution)/shard_map/d2_x/ppermute | solution.py:37
  179.6 12.4 %collective-permute-start.45 = (bf16[2432,128]{1,0:T(8,128)(2,1)S(1)}, bf16[2432,128]{1,0:T(8,128)(2,1)S(1)}, u32[]{:S(2)}, u32[]{:S(2)}) collective-permute-start(bf16[2432,128]{1,0:T(8,128)(2,1)S(1)} %get-tuple-element.254.refs_4_), channel_id=1, source_target_pairs={{8,16},{16,8},{9,17},{17,9},{10,18},{18,10},{11,19},{19,11},{12,20... | collective-permute-start | bytes 1867784 | tf_op jit(solution)/shard_map/cross_g2/ppermute | solution.py:83
  180.3 11.7 %collective-permute-start.44 = (bf16[1824,128]{1,0:T(8,128)(2,1)S(1)}, bf16[1824,128]{1,0:T(8,128)(2,1)S(1)}, u32[]{:S(2)}, u32[]{:S(2)}) collective-permute-start(bf16[1824,128]{1,0:T(8,128)(2,1)S(1)} %get-tuple-element.252), channel_id=1, source_target_pairs={{0,8},{8,0},{16,24},{24,16},{1,9},{9,1},{17,25},{25,17},{2,10},{10... | collective-permute-start | bytes 1400840 | tf_op jit(solution)/shard_map/swap_g1_u1/ppermute | solution.py:78
  197.8 38.0 %collective-permute-start.50 = (bf16[4944,128]{1,0:T(8,128)(2,1)S(1)}, bf16[4944,128]{1,0:T(8,128)(2,1)S(1)}, u32[]{:S(2)}, u32[]{:S(2)}) collective-permute-start(bf16[4944,128]{1,0:T(8,128)(2,1)S(1)} %get-tuple-element.273), channel_id=1, source_target_pairs={{0,4},{2,6},{4,0},{6,2},{1,5},{3,7},{5,1},{7,3},{8,12},{10,14},{12... | collective-permute-start | bytes 3797000 | tf_op jit(solution)/shard_map/g1_y/ppermute | solution.py:37
  198.5 37.3 %collective-permute-start.51 = (bf16[4944,128]{1,0:T(8,128)(2,1)S(1)}, bf16[4944,128]{1,0:T(8,128)(2,1)S(1)}, u32[]{:S(2)}, u32[]{:S(2)}) collective-permute-start(bf16[4944,128]{1,0:T(8,128)(2,1)S(1)} %get-tuple-element.274), channel_id=1, source_target_pairs={{0,2},{2,0},{4,6},{6,4},{1,3},{3,1},{5,7},{7,5},{8,10},{10,8},{12,... | collective-permute-start | bytes 3797000 | tf_op jit(solution)/shard_map/g1_x/ppermute | solution.py:37
  200.0 3.3 collective-permute-start.53
  200.5 35.6 %collective-permute-start.48 = (bf16[2432,128]{1,0:T(8,128)(2,1)S(1)}, bf16[2432,128]{1,0:T(8,128)(2,1)S(1)}, u32[]{:S(2)}, u32[]{:S(2)}) collective-permute-start(bf16[2432,128]{1,0:T(8,128)(2,1)S(1)} %get-tuple-element.270), channel_id=1, source_target_pairs={{0,8},{8,0},{16,24},{24,16},{1,9},{9,1},{17,25},{25,17},{2,10},{10... | collective-permute-start | bytes 1867784 | tf_op jit(solution)/shard_map/swap_g2_u2/ppermute | solution.py:78
  201.8 34.0 %collective-permute-start.52 = (bf16[1904,128]{1,0:T(8,128)(2,1)S(1)}, bf16[1904,128]{1,0:T(8,128)(2,1)S(1)}, u32[]{:S(2)}, u32[]{:S(2)}) collective-permute-start(bf16[1904,128]{1,0:T(8,128)(2,1)S(1)} %get-tuple-element.275), channel_id=1, source_target_pairs={{0,6},{2,4},{4,2},{6,0},{1,7},{3,5},{5,3},{7,1},{8,14},{10,12},{12... | collective-permute-start | bytes 1462280 | tf_op jit(solution)/shard_map/shares/ppermute | solution.py:37
  203.3 32.8 %collective-permute-start.49 = (bf16[1824,128]{1,0:T(8,128)(2,1)S(1)}, bf16[1824,128]{1,0:T(8,128)(2,1)S(1)}, u32[]{:S(2)}, u32[]{:S(2)}) collective-permute-start(bf16[1824,128]{1,0:T(8,128)(2,1)S(1)} %get-tuple-element.272.refs_4_), channel_id=1, source_target_pairs={{8,16},{16,8},{9,17},{17,9},{10,18},{18,10},{11,19},{19,11},{12,20... | collective-permute-start | bytes 1400840 | tf_op jit(solution)/shard_map/cross_u1/ppermute | solution.py:83
  237.4 23.2 %collective-permute-start.58 = (bf16[3344,128]{1,0:T(8,128)(2,1)S(1)}, bf16[3344,128]{1,0:T(8,128)(2,1)S(1)}, u32[]{:S(2)}, u32[]{:S(2)}) collective-permute-start(bf16[3344,128]{1,0:T(8,128)(2,1)S(1)} %get-tuple-element.282), channel_id=1, source_target_pairs={{0,4},{2,6},{4,0},{6,2},{1,5},{3,7},{5,1},{7,3},{8,12},{10,14},{12... | collective-permute-start | bytes 2568200 | tf_op jit(solution)/shard_map/g2_y/ppermute | solution.py:37
  238.4 22.3 %collective-permute-start.59 = (bf16[3344,128]{1,0:T(8,128)(2,1)S(1)}, bf16[3344,128]{1,0:T(8,128)(2,1)S(1)}, u32[]{:S(2)}, u32[]{:S(2)}) collective-permute-start(bf16[3344,128]{1,0:T(8,128)(2,1)S(1)} %get-tuple-element.283), channel_id=1, source_target_pairs={{0,2},{2,0},{4,6},{6,4},{1,3},{3,1},{5,7},{7,5},{8,10},{10,8},{12,... | collective-permute-start | bytes 2568200 | tf_op jit(solution)/shard_map/g2_x/ppermute | solution.py:37
  239.6 21.1 %collective-permute-start.56 = (bf16[2432,128]{1,0:T(8,128)(2,1)S(1)}, bf16[2432,128]{1,0:T(8,128)(2,1)S(1)}, u32[]{:S(2)}, u32[]{:S(2)}) collective-permute-start(bf16[2432,128]{1,0:T(8,128)(2,1)S(1)} %get-tuple-element.280.refs_3_), channel_id=1, source_target_pairs={{8,16},{16,8},{9,17},{17,9},{10,18},{18,10},{11,19},{19,11},{12,20... | collective-permute-start | bytes 1867784 | tf_op jit(solution)/shard_map/cross_u2/ppermute | solution.py:83
  240.3 20.4 %collective-permute-start.57 = (bf16[1904,128]{1,0:T(8,128)(2,1)S(1)}, bf16[1904,128]{1,0:T(8,128)(2,1)S(1)}, u32[]{:S(2)}, u32[]{:S(2)}) collective-permute-start(bf16[1904,128]{1,0:T(8,128)(2,1)S(1)} %get-tuple-element.281.refs_5_), channel_id=1, source_target_pairs={{0,8},{8,0},{16,24},{24,16},{1,9},{9,1},{17,25},{25,17},{2,10},{10... | collective-permute-start | bytes 1462280 | tf_op jit(solution)/shard_map/swap_share/ppermute | solution.py:78
  244.2 16.4 %collective-permute-start.55 = (bf16[1824,128]{1,0:T(8,128)(2,1)S(1)}, bf16[1824,128]{1,0:T(8,128)(2,1)S(1)}, u32[]{:S(2)}, u32[]{:S(2)}) collective-permute-start(bf16[1824,128]{1,0:T(8,128)(2,1)S(1)} %get-tuple-element.279.refs_2_), channel_id=1, source_target_pairs={{0,8},{8,0},{16,24},{24,16},{1,9},{9,1},{17,25},{25,17},{2,10},{10... | collective-permute-start | bytes 1400840 | tf_op jit(solution)/shard_map/swap_u1/ppermute | solution.py:78
  261.9 22.7 %collective-permute-start.62 = (bf16[3040,128]{1,0:T(8,128)(2,1)S(1)}, bf16[3040,128]{1,0:T(8,128)(2,1)S(1)}, u32[]{:S(2)}, u32[]{:S(2)}) collective-permute-start(bf16[3040,128]{1,0:T(8,128)(2,1)S(1)} %get-tuple-element.288), channel_id=1, source_target_pairs={{0,4},{2,6},{4,0},{6,2},{1,5},{3,7},{5,1},{7,3},{8,12},{10,14},{12... | collective-permute-start | bytes 2334728 | tf_op jit(solution)/shard_map/u1_y/ppermute | solution.py:37
  262.0 22.6 %collective-permute-start.63 = (bf16[3040,128]{1,0:T(8,128)(2,1)S(1)}, bf16[3040,128]{1,0:T(8,128)(2,1)S(1)}, u32[]{:S(2)}, u32[]{:S(2)}) collective-permute-start(bf16[3040,128]{1,0:T(8,128)(2,1)S(1)} %get-tuple-element.289), channel_id=1, source_target_pairs={{0,2},{2,0},{4,6},{6,4},{1,3},{3,1},{5,7},{7,5},{8,10},{10,8},{12,... | collective-permute-start | bytes 2334728 | tf_op jit(solution)/shard_map/u1_x/ppermute | solution.py:37
  269.2 15.5 %collective-permute-start.60 = (bf16[2432,128]{1,0:T(8,128)(2,1)S(1)}, bf16[2432,128]{1,0:T(8,128)(2,1)S(1)}, u32[]{:S(2)}, u32[]{:S(2)}) collective-permute-start(bf16[2432,128]{1,0:T(8,128)(2,1)S(1)} %get-tuple-element.286.refs_2_), channel_id=1, source_target_pairs={{0,8},{8,0},{16,24},{24,16},{1,9},{9,1},{17,25},{25,17},{2,10},{10... | collective-permute-start | bytes 1867784 | tf_op jit(solution)/shard_map/swap_u2/ppermute | solution.py:78
  269.2 13.5 %collective-permute-start.61 = (bf16[1904,128]{1,0:T(8,128)(2,1)S(1)}, bf16[1904,128]{1,0:T(8,128)(2,1)S(1)}, u32[]{:S(2)}, u32[]{:S(2)}) collective-permute-start(bf16[1904,128]{1,0:T(8,128)(2,1)S(1)} %get-tuple-element.287.refs_3_), channel_id=1, source_target_pairs={{0,16},{8,24},{16,0},{24,8},{1,17},{9,25},{17,1},{25,9},{2,18},{10... | collective-permute-start | bytes 1462280 | tf_op jit(solution)/shard_map/share_far/ppermute | solution.py:37
  285.7 25.9 %collective-permute-start.64 = (bf16[5248,128]{1,0:T(8,128)(2,1)S(1)}, bf16[5248,128]{1,0:T(8,128)(2,1)S(1)}, u32[]{:S(2)}, u32[]{:S(2)}) collective-permute-start(bf16[5248,128]{1,0:T(8,128)(2,1)S(1)} %get-tuple-element.293), channel_id=1, source_target_pairs={{0,2},{2,0},{4,6},{6,4},{1,3},{3,1},{5,7},{7,5},{8,10},{10,8},{12,... | collective-permute-start | bytes 4030472 | tf_op jit(solution)/shard_map/u2_x/ppermute | solution.py:37
  286.0 25.6 %collective-permute-start.65 = (bf16[5248,128]{1,0:T(8,128)(2,1)S(1)}, bf16[5248,128]{1,0:T(8,128)(2,1)S(1)}, u32[]{:S(2)}, u32[]{:S(2)}) collective-permute-start(bf16[5248,128]{1,0:T(8,128)(2,1)S(1)} %get-tuple-element.294), channel_id=1, source_target_pairs={{0,4},{2,6},{4,0},{6,2},{1,5},{3,7},{5,1},{7,3},{8,12},{10,14},{12... | collective-permute-start | bytes 4030472 | tf_op jit(solution)/shard_map/u2_y/ppermute | solution.py:37
  312.2 10.4 %collective-permute-start.67 = (bf16[960,128]{1,0:T(8,128)(2,1)S(1)}, bf16[960,128]{1,0:T(8,128)(2,1)S(1)}, u32[]{:S(2)}, u32[]{:S(2)}) collective-permute-start(bf16[960,128]{1,0:T(8,128)(2,1)S(1)} %get-tuple-element.297.refs_8_), channel_id=1, source_target_pairs={{0,2},{2,0},{4,6},{6,4},{1,3},{3,1},{5,7},{7,5},{8,10},{10,8},{12,... | collective-permute-start | bytes 737288 | tf_op jit(solution)/shard_map/far_share_x/ppermute | solution.py:37
  314.8 7.8 %collective-permute-start.66 = (bf16[944,128]{1,0:T(8,128)(2,1)S(1)}, bf16[944,128]{1,0:T(8,128)(2,1)S(1)}, u32[]{:S(2)}, u32[]{:S(2)}) collective-permute-start(bf16[944,128]{1,0:T(8,128)(2,1)S(1)} %get-tuple-element.296), channel_id=1, source_target_pairs={{0,4},{2,6},{4,0},{6,2},{1,5},{3,7},{5,1},{7,3},{8,12},{10,14},{12... | collective-permute-start | bytes 725000 | tf_op jit(solution)/shard_map/far_share_y/ppermute | solution.py:37
  318.5 8.7 %collective-permute-start.69 = (bf16[1216,128]{1,0:T(8,128)(2,1)S(1)}, bf16[1216,128]{1,0:T(8,128)(2,1)S(1)}, u32[]{:S(2)}, u32[]{:S(2)}) collective-permute-start(bf16[1216,128]{1,0:T(8,128)(2,1)S(1)} %get-tuple-element.305), channel_id=1, source_target_pairs={{0,4},{2,6},{4,0},{6,2},{1,5},{3,7},{5,1},{7,3},{8,12},{10,14},{12... | collective-permute-start | bytes 933896 | tf_op jit(solution)/shard_map/far_u2_y/ppermute | solution.py:37
  318.5 8.6 %collective-permute-start.70 = (bf16[1216,128]{1,0:T(8,128)(2,1)S(1)}, bf16[1216,128]{1,0:T(8,128)(2,1)S(1)}, u32[]{:S(2)}, u32[]{:S(2)}) collective-permute-start(bf16[1216,128]{1,0:T(8,128)(2,1)S(1)} %get-tuple-element.306), channel_id=1, source_target_pairs={{0,2},{2,0},{4,6},{6,4},{1,3},{3,1},{5,7},{7,5},{8,10},{10,8},{12,... | collective-permute-start | bytes 933896 | tf_op jit(solution)/shard_map/far_u2_x/ppermute | solution.py:37
  (81 other events, 506.4 us)

commit v5 on v4

--- a/solution.py
+++ b/solution.py
@@ -112,6 +112,15 @@
 
 in_smem = pl.BlockSpec(memory_space=pltpu.SMEM)
 in_vmem = pl.BlockSpec(memory_space=pltpu.VMEM)
+in_hbm = pl.BlockSpec(memory_space=pltpu.HBM)
+
+
+def arriving(pairs, sems):
+    copies = []
+    for i, (source, target) in enumerate(pairs):
+        copies.append(pltpu.make_async_copy(source, target, sems.at[i]))
+        copies[-1].start()
+    return copies
 
 
 def as_row(column):
@@ -145,13 +154,20 @@
 
 
 def enter_kernel(
-    lengths_ref, place_ref, tokens_ref, gain_ref, wq_ref, wk_ref, wv_ref, bq_ref, bk_ref, bv_ref,
-    turn_ref, q_ref, kv_ref, normed_ref, tokens_t_ref, cos_ref, sin_ref,
+    lengths_ref, place_ref, small_ref, turn_ref, tokens_in, wq_in, wk_in, wv_in,
+    q_ref, kv_ref, normed_ref, tokens_t_ref, cos_ref, sin_ref, tokens_ref, wq_ref, wk_ref, wv_ref, sems,
 ):
-    rows = tokens_ref.shape[0]
+    ins = (tokens_in, wq_in, wk_in, wv_in)
+    copies = arriving(zip(ins, (tokens_ref, wq_ref, wk_ref, wv_ref)), sems)
+    rows, width = tokens_ref.shape
+    q_width = wq_ref.shape[0]
+    small = small_ref[...].astype(wide)
+    gain = small[:, :width]
+    bias = as_column(small[:, width:])
+    copies[0].wait()
     hidden = tokens_ref[...].astype(wide)
     inverse = lax.rsqrt(jnp.mean(hidden * hidden, axis=1, keepdims=True) + epsilon)
-    normed = (hidden * inverse * gain_ref[...].astype(wide)).astype(low)
+    normed = (hidden * inverse * gain).astype(low)
     tokens_t_ref[...] = hidden.T.astype(low)
     normed_ref[...] = normed.astype(wide).T.astype(low)
     index = place_ref[0] * rows + lax.broadcasted_iota(jnp.int32, (1, rows), 1)
@@ -160,30 +176,47 @@
     cosine, sine = jnp.cos(angles), jnp.sin(angles)
     cos_ref[...] = cosine
     sin_ref[...] = sine
-    q_lin = dot_nt(wq_ref[...], normed) + as_column(bq_ref[...])
+    for copy in copies[1:]:
+        copy.wait()
+    q_lin = dot_nt(wq_ref[...], normed) + bias[:q_width]
     for h in range(q_lin.shape[0] // HEAD_DIM):
         head = rotate(q_lin[h * HEAD_DIM : (h + 1) * HEAD_DIM], cosine, sine)
         q_ref[h * HEAD_DIM : (h + 1) * HEAD_DIM, :] = head.astype(low) * low(HEAD_DIM**-0.5)
-    k_lin = dot_nt(wk_ref[...], normed) + as_column(bk_ref[...])
-    v_lin = dot_nt(wv_ref[...], normed) + as_column(bv_ref[...])
+    k_lin = dot_nt(wk_ref[...], normed) + bias[q_width : q_width + HEAD_DIM]
+    v_lin = dot_nt(wv_ref[...], normed) + bias[q_width + HEAD_DIM :]
     kv_ref[...] = jnp.concatenate([rotate(k_lin, cosine, sine), v_lin], axis=0).T.astype(low)
 
 
 def weights_kernel(
-    lengths_ref, place_ref, gate_ref, up_ref, down_ref, cotangent_ref,
-    gate_t_ref, gate_own_ref, up_t_ref, up_own_ref, down_t_ref, mine_ref, other_ref, turned_ref, grad_ref,
+    whole_down, lengths_ref, place_ref, gate_in, up_in, down_in, cotangent_in,
+    gate_t_ref, gate_own_ref, up_t_ref, up_own_ref, down_t_ref, down_ref, mine_ref, other_ref,
+    gate_ref, up_ref, cotangent_ref, turned_ref, grad_ref, sems,
 ):
     units = gate_t_ref.shape[0]
-    width, hidden = gate_ref.shape
+    hidden = gate_in.shape[1]
     window = turned_ref.shape[0]
     first = place_ref[0] * units
     base = pl.multiple_of(jnp.minimum(first // 128 * 128, hidden - window), 128)
-    for ref, turned, own in ((gate_ref, gate_t_ref, gate_own_ref), (up_ref, up_t_ref, up_own_ref)):
-        turned_ref[...] = ref[:, pl.ds(base, window)].astype(wide).T
+    down_rows = down_in.at[pl.ds(pl.multiple_of(first, 16), units), :] if whole_down else down_in
+    copies = arriving(
+        [
+            (gate_in.at[:, pl.ds(base, window)], gate_ref),
+            (up_in.at[:, pl.ds(base, window)], up_ref),
+            (cotangent_in, cotangent_ref),
+            (down_rows, down_ref),
+        ],
+        sems,
+    )
+    for copy, ref, turned, own in (
+        (copies[0], gate_ref, gate_t_ref, gate_own_ref),
+        (copies[1], up_ref, up_t_ref, up_own_ref),
+    ):
+        copy.wait()
+        turned_ref[...] = ref[...].astype(wide).T
         part = turned_ref[pl.ds(pl.multiple_of(first - base, 8), units), :]
         turned[...] = part.astype(low)
         own[...] = part.T.astype(low)
-    down_t_ref[...] = down_ref[...].astype(wide).T.astype(low)
+    copies[2].wait()
     rows = cotangent_ref.shape[0]
     half = rows // 2
     row = place_ref[0] * rows + lax.broadcasted_iota(jnp.int32, (rows, 1), 0)
@@ -194,6 +227,8 @@
     core = place_ref[1]
     mine_ref[...] = grad_ref[pl.ds(pl.multiple_of(core * half, half), half), :].astype(low)
     other_ref[...] = grad_ref[pl.ds(pl.multiple_of((1 - core) * half, half), half), :].astype(low)
+    copies[3].wait()
+    down_t_ref[...] = down_ref[...].astype(wide).T.astype(low)
 
 
 def mask_bias(key_base, key_rows, q_index, q_start):
@@ -427,7 +462,7 @@
 
 
 def attend_back_kernel(
-    blocks, lengths_ref, place_ref, go_ref, delta_ref, log_ref, q_ref, cos_ref, sin_ref, *refs,
+    blocks, tile, lengths_ref, place_ref, go_ref, delta_ref, log_ref, q_ref, cos_ref, sin_ref, *refs,
 ):
     kv_refs, refs = refs[:blocks], refs[blocks:]
     (grad_q_ref, *grad_kv_refs), refs = refs[: blocks + 1], refs[blocks + 1 :]
@@ -435,6 +470,7 @@
     rows = q_ref.shape[1]
     heads = grad_q_ref.shape[0] // HEAD_DIM
     own = place_ref[0]
+    parts = rows // tile
 
     def lanes(h):
         return slice(h * rows, (h + 1) * rows)
@@ -453,11 +489,13 @@
     q_start = segment_start(lengths_ref, q_index)
 
     def visit(block, carry):
-        pair = kv_ref[block ^ own]
+        part = pl.multiple_of(block % parts * tile, tile)
+        at = ((block // parts) ^ own, pl.ds(part, tile), slice(None))
+        pair = kv_ref[at]
         keys = pair[:, :HEAD_DIM]
         values = pair[:, HEAD_DIM:]
         keys_t = pair.astype(wide).T[:HEAD_DIM].astype(low)
-        bias_ref[...] = mask_bias(block * rows, rows, q_index, q_start)
+        bias_ref[...] = mask_bias(block * tile, tile, q_index, q_start)
 
         def products(h):
             score_ref[h % 2] = dot_nn(keys, q_all_ref[:, lanes(h)])
@@ -474,10 +512,10 @@
             dq_ref[span(h), :] += dot_nn(keys_t, grad)
         grad_keys = dot_nt(grad_ref[...], q_all_ref[...])
         grad_values = dot_nt(weight_ref[...], go_all_ref[...])
-        grad_kv_ref[block ^ own] = jnp.concatenate([grad_keys, grad_values], axis=1).astype(low)
+        grad_kv_ref[at] = jnp.concatenate([grad_keys, grad_values], axis=1).astype(low)
         return carry
 
-    lax.fori_loop(first_row(lengths_ref, own * rows) // rows, own + 1, visit, 0)
+    lax.fori_loop(first_row(lengths_ref, own * rows) // tile, (own + 1) * parts, visit, 0)
     for r in range(blocks):
         grad_kv_refs[r][...] = grad_kv_ref[r]
     for h in range(heads):
@@ -684,9 +722,11 @@
     units = w_gate.shape[1] // blocks
     place = jnp.stack([own_block, own_core, lax.axis_index("dp")]).astype(jnp.int32)
     gain_two = norm2_gain.reshape(1, width)
+    key_tile = rows // 2
 
     half_dim = HEAD_DIM // 2
     turn = (rope_base ** (-2.0 * jnp.arange(half_dim, dtype=wide) / HEAD_DIM)).reshape(half_dim, 1)
+    small = jnp.concatenate([norm1_gain, b_query, b_key, b_value]).reshape(1, -1)
     q_t, key_value, normed_t, tokens_t, cosine, sine = call(
         enter_kernel,
         [
@@ -697,30 +737,43 @@
             shape((half_dim, rows), wide),
             shape((half_dim, rows), wide),
         ],
+        [lengths, place, small, turn, tokens, w_query.T, w_key.T, w_value.T],
         [
-            lengths, place, tokens, norm1_gain.reshape(1, width), w_query.T, w_key.T, w_value.T,
-            b_query.reshape(1, -1), b_key.reshape(1, -1), b_value.reshape(1, -1), turn,
+            pltpu.VMEM((rows, width), low),
+            pltpu.VMEM((q_width, width), low),
+            pltpu.VMEM((HEAD_DIM, width), low),
+            pltpu.VMEM((HEAD_DIM, width), low),
+            pltpu.SemaphoreType.DMA((4,)),
         ],
-        in_specs=[in_smem] * 2 + [in_vmem] * 9,
+        in_specs=[in_smem] * 2 + [in_vmem] * 2 + [in_hbm] * 4,
     )
     kv_blocks = gather_blocks(key_value, "kv")
 
-    down_own = lax.dynamic_slice_in_dim(w_down, own_block * units, units, 0)
     window = -(-(units + 127) // 128) * 128
-    gate_t, gate_own, up_t, up_own, down_t, grad_y_mine, grad_y_other = call(
-        weights_kernel,
+    whole_down = units % 16 == 0
+    down = w_down if whole_down else lax.dynamic_slice_in_dim(w_down, own_block * units, units, 0)
+    gate_t, gate_own, up_t, up_own, down_t, down_own, grad_y_mine, grad_y_other = call(
+        functools.partial(weights_kernel, whole_down),
         [
             shape((units, width), low),
             shape((width, units), low),
             shape((units, width), low),
             shape((width, units), low),
             shape((width, units), low),
+            shape((units, width), low),
             shape((half, width), low),
             shape((half, width), low),
         ],
-        [lengths, place, w_gate, w_up, down_own, cotangent],
-        [pltpu.VMEM((window, width), wide), pltpu.VMEM((rows, width), wide)],
-        in_specs=[in_smem] * 2 + [in_vmem] * 4,
+        [lengths, place, w_gate, w_up, down, cotangent],
+        [
+            pltpu.VMEM((width, window), low),
+            pltpu.VMEM((width, window), low),
+            pltpu.VMEM((rows, width), low),
+            pltpu.VMEM((window, width), wide),
+            pltpu.VMEM((rows, width), wide),
+            pltpu.SemaphoreType.DMA((4,)),
+        ],
+        in_specs=[in_smem] * 2 + [in_hbm] * 4,
         after=[q_t],
     )
     gy_near = {r: partner(grad_y_mine, "blk", r, "gy") for r in range(1, blocks) if r & (r - 1) == 0}
@@ -856,23 +909,21 @@
     gy_mine = relay_far(gy_near, grad_y_mine, "gy")
     x_other = {r: cores(parts, "x_core") for r, parts in x_mine.items() if r in x_near}
     gy_other = {r: cores(parts, "gy_core") for r, parts in gy_mine.items() if r in x_near}
-    waiting, out_of = [], list(range(1, blocks))
-    for i, r in enumerate(out_of):
-        other = hidden_units(r, x_mine[r], x_other[r], gy_mine[r], gy_other[r])
-        ready = [k for k in out_of if k not in x_near] if i == 0 else []
-        fars = [part for k in ready for part in x_mine[k] + gy_mine[k]]
-        if i == 0:
-            other, *fars = wait([other] + fars)
-        else:
-            other, *fars = add_back([out_of[i - 1]], [other])
+    others = [hidden_units(r, x_mine[r], x_other[r], gy_mine[r], gy_other[r]) for r in x_near]
+    fars = [r for r in x_mine if r not in x_near]
+    parts = [part for r in fars for part in x_mine[r] + gy_mine[r]]
+    results = wait(others + parts)
+    for r in x_near:
+        passed[r] = partner(results.pop(0), "tensor", 1, "back_core")
+    for r in fars:
+        x_mine[r] = [results.pop(0) for _ in x_mine[r]]
+        gy_mine[r] = [results.pop(0) for _ in gy_mine[r]]
+        x_other[r], gy_other[r] = cores(x_mine[r], "x_core"), cores(gy_mine[r], "gy_core")
+    others = [hidden_units(r, x_mine[r], x_other[r], gy_mine[r], gy_other[r]) for r in fars]
+    for r, other in zip(fars, add_back(list(x_near), others)):
         passed[r] = partner(other, "tensor", 1, "back_core")
-        for k in ready:
-            count = len(x_mine[k])
-            x_mine[k], fars = fars[:count], fars[count:]
-            count = len(gy_mine[k])
-            gy_mine[k], fars = fars[:count], fars[count:]
-            x_other[k] = cores(x_mine[k], "x_core")
-            gy_other[k] = cores(gy_mine[k], "gy_core")
+    if len(fars) > 1:
+        add_back(fars[:-1], [])
     cut_at = width // 2 // 128 * 128
     (d1,) = hidden_weight(False, 0, gy_parts, 0, [cut_at])
     d1_swap = swap(d1, "swap_d1")
@@ -914,20 +965,20 @@
     )
 
     grad_q, *grad_kv = ordered(
-        functools.partial(attend_back_kernel, blocks),
+        functools.partial(attend_back_kernel, blocks, key_tile),
         [shape((q_width, rows), low)] + [shape((rows, 2 * HEAD_DIM), low)] * blocks,
         [lengths, place, grad_out, delta, log_total, q_t, cosine, sine] + kv_blocks,
         scratch=[
             pltpu.VMEM((blocks, rows, 2 * HEAD_DIM), low),
-            pltpu.VMEM((rows, rows), wide),
+            pltpu.VMEM((key_tile, rows), wide),
             pltpu.VMEM((q_width, rows), wide),
             pltpu.VMEM((HEAD_DIM, heads * rows), low),
             pltpu.VMEM((HEAD_DIM, heads * rows), low),
-            pltpu.VMEM((rows, heads * rows), low),
-            pltpu.VMEM((rows, heads * rows), low),
+            pltpu.VMEM((key_tile, heads * rows), low),
+            pltpu.VMEM((key_tile, heads * rows), low),
             pltpu.VMEM((blocks, rows, 2 * HEAD_DIM), low),
-            pltpu.VMEM((2, rows, rows), wide),
-            pltpu.VMEM((2, rows, rows), wide),
+            pltpu.VMEM((2, key_tile, rows), wide),
+            pltpu.VMEM((2, key_tile, rows), wide),
         ],
         in_specs=[in_smem] * 2 + [in_vmem] * (6 + blocks),
     )

time: 338 us -> 332 us (0.982)
  waiting for transfers between devices: 126 us -> 136 us
  starting transfers between devices: 82.4 us -> 74.4 us
  local copies, waits for them, and re-layouts: 26.4 us -> 21.6 us
    ppermute x56, waiting for transfers between devices: 108 us -> 117 us  [partner(): return lax.ppermute(value, axis, [(i, i ^ step) for i in range(count)])]
    ppermute x56, starting transfers between devices: 60.4 us -> 52.2 us  [partner(): return lax.ppermute(value, axis, [(i, i ^ step) for i in range(count)])]
    unnamed x148 -> x154, local copies, waits for them, and re-layouts: 21.8 us -> 16.9 us
    pallas_call x39 -> x38, Pallas kernels: 74.7 us -> 72.2 us  [call(): pl.pallas_call(run, name=getattr(body, 'func', body).__name__, out_shape=...]
  transfers between devices with their start and end apart: 71 -> 71, of which waited for: 29 -> 27; matrix products, arithmetic and copies ran while one was open for 1% -> 1% of each run, Pallas kernels for 23% -> 22%
where the time goes in v5:
time: 332 us; the launch traced here: 327 us
  waiting for transfers between devices  136 us (41%)
  Pallas kernels  92.2 us (28%)
  starting transfers between devices  74.4 us (22%)
  local copies, waits for them, and re-layouts  21.6 us (7%)
    ppermute x56, waiting for transfers between devices, partner(): return lax.ppermute(value, axis, [(i, i ^ step) for i in range(count)])  117 us
    pallas_call x38, Pallas kernels, call(): pl.pallas_call(run, name=getattr(body, 'func', body).__name__, out_shape=...  72.2 us
    ppermute x56, starting transfers between devices, partner(): return lax.ppermute(value, axis, [(i, i ^ step) for i in range(count)])  52.2 us
    pallas_call x4, Pallas kernels, place_shares(): pl.pallas_call(body, name='place_kernel', out_shape=(shape(dims, wide), s...  20 us
    ppermute x9, waiting for transfers between devices, swap(): return lax.ppermute(value, 'dp', [(0, 1), (1, 0), (2, 3), (3, 2)])  18.8 us
    ppermute x9, starting transfers between devices, swap(): return lax.ppermute(value, 'dp', [(0, 1), (1, 0), (2, 3), (3, 2)])  17.5 us
    unnamed x154, local copies, waits for them, and re-layouts  16.9 us
  transfers between devices with their start and end apart: 71, of which 27 were waited for; matrix products, arithmetic and copies ran while one was open for 1% of the time, Pallas kernels for 22%

profile of v5, /device:TPU:0, one launch (start us, length us, event | category | flops | bytes accessed | tf_op | source)
XLA Modules:
  0.0 326.8 jit_solution(6791651663875625308)
XLA Ops:
  0.7 2.8 concatenate.3
  8.3 3.6 %enter_kernel.1 = (bf16[448,512]{1,0:T(8,128)(2,1)S(1)}, bf16[512,128]{1,0:T(8,128)(2,1)S(1)}, bf16[896,512]{1,0:T(8,128)(2,1)S(1)}, bf16[896,512]{1,0:T(8,128)(...) custom-call(s32[1,3]{1,0:T(1,128)S(1)} %copy-done.73, s32[3]{0:T(128)S(1)} %pad_add_fusion.refs_1_.refs_0_, ...), custom_call_target="tpu_custom_call" | custom-call | tf_op jit(solution)/shard_map/enter_kernel/pallas_call | solution.py:96
  14.2 3.9 %collective-permute-start.4 = (bf16[512,128]{1,0:T(8,128)(2,1)S(1)}, bf16[512,128]{1,0:T(8,128)(2,1)S(1)}, u32[]{:S(2)}, u32[]{:S(2)}) collective-permute-start(bf16[512,128]{1,0:T(8,128)(2,1)S(1)} %get-tuple-element.167.refs_4_.refs_8_), channel_id=1, source_target_pairs={{0,6},{2,4},{4,2},{6,0},{1,7},{3,5},{5,3},{7,1},{8,14},{10,12},{12... | collective-permute-start | bytes 393224 | tf_op jit(solution)/shard_map/kv/ppermute | solution.py:37
  18.6 2.2 copy-done.1
  20.8 3.7 %weights_kernel.1 = (bf16[608,896]{1,0:T(8,128)(2,1)S(1)}, bf16[896,608]{1,0:T(8,128)(2,1)S(1)}, bf16[608,896]{1,0:T(8,128)(2,1)S(1)}, bf16[896,608]{1,0:T(8,128...) custom-call(s32[1,3]{1,0:T(1,128)S(1)} %copy-done.73, ...), custom_call_target="tpu_custom_call" | custom-call | tf_op jit(solution)/shard_map/weights_kernel/pallas_call | solution.py:96
  24.6 2.0 collective-permute-start.6
  26.6 1.5 collective-permute-start
  28.2 4.5 %attend_kernel.1 = (f32[448,512]{1,0:T(8,128)S(1)}, f32[8,512]{1,0:T(8,128)S(1)}, f32[896,256]{1,0:T(8,128)S(1)}, bf16[896,256]{1,0:T(8,128)(2,1)S(1)}) custom-call(s32[1,3]{1,0:T(1,128)S(1)} %copy-done.73, s32[3]{0:T(128)S(1)} %pad_add_fusion.refs_1_.refs_0_, bf16[448,512]{1,0:T(8,128)(2,1)S(1)} %get-tuple-element.163.refs_6_.refs_2_.refs_5_, ...), custom_call_target="tpu_custom_call" | custom-call | tf_op jit(solution)/shard_map/attend_kernel/pallas_call | solution.py:96
  33.6 2.7 collective-permute-done.6.refs_5_.refs_1_.refs_7_
  38.9 3.5 %collective-permute-start.9 = (bf16[896,256]{1,0:T(8,128)(2,1)S(1)}, bf16[896,256]{1,0:T(8,128)(2,1)S(1)}, u32[]{:S(2)}, u32[]{:S(2)}) collective-permute-start(bf16[896,256]{1,0:T(8,128)(2,1)S(1)} %get-tuple-element.171.refs_3_.refs_9_.refs_5_), channel_id=1, source_target_pairs={{0,4},{2,6},{4,0},{6,2},{1,5},{3,7},{5,1},{7,3},{8,12},{10,14},{12... | collective-permute-start | bytes 1376264 | tf_op jit(solution)/shard_map/x/ppermute | solution.py:37
  42.4 2.7 collective-permute-start.8
  45.6 3.9 %hidden_kernel.4 = (bf16[608,512]{1,0:T(8,128)(2,1)S(1)}, bf16[608,512]{1,0:T(8,128)(2,1)S(1)}, bf16[608,512]{1,0:T(8,128)(2,1)S(1)}, bf16[896,256]{1,0:T(8,128)(2,1)S(1)}, bf16[896,256]{1,0:T(8,128)(2,1)S(1)}) custom-call(bf16[256,896]{1,0:T(8,128)(2,1)S(1)} %get-tuple-element.165.refs_0_.refs_4_, ...), custom_call_target="tpu_custom_call" | custom-call | tf_op jit(solution)/shard_map/hidden_kernel/pallas_call | solution.py:96
  49.5 4.0 %collective-permute-done.9.refs_3_ = bf16[896,256]{1,0:T(8,128)(2,1)S(1)} collective-permute-done((bf16[896,256]{1,0:T(8,128)(2,1)S(1)}, bf16[896,256]{1,0:T(8,128)(2,1)S(1)}, u32[]{:S(2)}, u32[]{:S(2)}) %collective-permute-start.9) | collective-permute-done | bytes 458784 | tf_op jit(solution)/shard_map/x/ppermute | solution.py:37
  53.4 2.4 collective-permute-done.8.refs_2_
  56.8 1.8 collective-permute-start.16
  58.6 1.7 collective-permute-start.13
  60.7 3.9 %hidden_kernel.5 = (bf16[608,512]{1,0:T(8,128)(2,1)S(1)}, bf16[608,512]{1,0:T(8,128)(2,1)S(1)}, bf16[608,512]{1,0:T(8,128)(2,1)S(1)}, bf16[896,256]{1,0:T(8,128)(2,1)S(1)}, bf16[896,256]{1,0:T(8,128)(2,1)S(1)}) custom-call(bf16[256,896]{1,0:T(8,128)(2,1)S(1)} %collective-permute-done.11.refs_0_.refs_6_, ...), custom_call_target="tpu_custom_call" | custom-call | tf_op jit(solution)/shard_map/hidden_kernel/pallas_call | solution.py:96
  66.2 3.9 %hidden_kernel.6 = (bf16[608,512]{1,0:T(8,128)(2,1)S(1)}, bf16[608,512]{1,0:T(8,128)(2,1)S(1)}, bf16[608,512]{1,0:T(8,128)(2,1)S(1)}, bf16[896,256]{1,0:T(8,128)(2,1)S(1)}, bf16[896,256]{1,0:T(8,128)(2,1)S(1)}) custom-call(bf16[256,896]{1,0:T(8,128)(2,1)S(1)} %collective-permute-done.1.refs_0_.refs_8_, ...), custom_call_target="tpu_custom_call" | custom-call | tf_op jit(solution)/shard_map/hidden_kernel/pallas_call | solution.py:96
  71.8 1.5 collective-permute-done.18.refs_1_.refs_11_
  74.0 4.0 %hidden_kernel.7 = (bf16[608,512]{1,0:T(8,128)(2,1)S(1)}, bf16[608,512]{1,0:T(8,128)(2,1)S(1)}, bf16[608,512]{1,0:T(8,128)(2,1)S(1)}, bf16[896,256]{1,0:T(8,128)(2,1)S(1)}, bf16[896,256]{1,0:T(8,128)(2,1)S(1)}) custom-call(bf16[128,896]{1,0:T(8,128)(2,1)S(1)} %collective-permute-done.17.refs_0_.refs_10_, ...), custom_call_target="tpu_custom_call" | custom-call | tf_op jit(solution)/shard_map/hidden_kernel/pallas_call | solution.py:96
  78.9 1.5 weight_kernel.4.refs_14_.refs_1_
  80.4 2.1 collective-permute-start.27
  83.7 1.7 collective-permute-start.25
  86.9 3.0 project_kernel.1
  90.7 4.8 %collective-permute-done.26.refs_5_.refs_8_ = bf16[896,256]{1,0:T(8,128)(2,1)S(1)} collective-permute-done((bf16[896,256]{1,0:T(8,128)(2,1)S(1)}, bf16[896,256]{1,0:T(8,128)(2,1)S(1)}, u32[]{:S(2)}, u32[]{:S(2)}) %collective-permute-start.26) | collective-permute-done | bytes 458784 | tf_op jit(solution)/shard_map/back/ppermute | solution.py:37
  97.9 2.7 collective-permute-start.29
  100.7 2.8 weight_kernel.6
  103.5 2.8 weight_kernel.7
  106.3 5.2 %collective-permute-done.29.refs_9_.refs_6_ = bf16[896,256]{1,0:T(8,128)(2,1)S(1)} collective-permute-done((bf16[896,256]{1,0:T(8,128)(2,1)S(1)}, bf16[896,256]{1,0:T(8,128)(2,1)S(1)}, u32[]{:S(2)}, u32[]{:S(2)}) %collective-permute-start.29) | collective-permute-done | bytes 458784 | tf_op jit(solution)/shard_map/back/ppermute | solution.py:37
  116.9 4.8 %collective-permute-start.32 = (bf16[1824,128]{1,0:T(8,128)(2,1)S(1)}, bf16[1824,128]{1,0:T(8,128)(2,1)S(1)}, u32[]{:S(2)}, u32[]{:S(2)}) collective-permute-start(bf16[1824,128]{1,0:T(8,128)(2,1)S(1)} %get-tuple-element.226), channel_id=1, source_target_pairs={{0,8},{8,0},{16,24},{24,16},{1,9},{9,1},{17,25},{25,17},{2,10},{10... | collective-permute-start | bytes 1400840 | tf_op jit(solution)/shard_map/swap_d1_g1/ppermute | solution.py:78
  121.7 1.7 collective-permute-start.35
  126.5 5.9 %attend_back_kernel.1 = (bf16[448,512]{1,0:T(8,128)(2,1)S(1)}, bf16[512,128]{1,0:T(8,128)(2,1)S(1)}, bf16[512,128]{1,0:T(8,128)(2,1)S(1)}, bf16[512,128]{1,0:T(8,128)(2,1)S(1)}, bf16[512,128]{1,0:T(8,128)(2,1)S(1)}) custom-call(s32[1,3]{1,0:T(1,128)S(1)} %copy-done.74, s32[3]{0:T(128)S(1)} %pad_add_fusion.refs_1_.refs_0_, ...), custom_call_target="tpu_custom_call" | custom-call | tf_op jit(solution)/shard_map/attend_back_kernel/pallas_call | solution.py:96
  132.5 2.6 collective-permute-done.35.refs_10_.refs_2_
  135.1 10.1 %collective-permute-done.36.refs_11_.refs_3_ = bf16[896,256]{1,0:T(8,128)(2,1)S(1)} collective-permute-done((bf16[896,256]{1,0:T(8,128)(2,1)S(1)}, bf16[896,256]{1,0:T(8,128)(2,1)S(1)}, u32[]{:S(2)}, u32[]{:S(2)}) %collective-permute-start.36) | collective-permute-done | bytes 458784 | tf_op jit(solution)/shard_map/layer/ppermute | solution.py:37
  148.5 3.6 %collective-permute-start.41 = (bf16[2336,128]{1,0:T(8,128)(2,1)S(1)}, bf16[2336,128]{1,0:T(8,128)(2,1)S(1)}, u32[]{:S(2)}, u32[]{:S(2)}) collective-permute-start(bf16[2336,128]{1,0:T(8,128)(2,1)S(1)} %get-tuple-element.248), channel_id=1, source_target_pairs={{0,2},{2,0},{4,6},{6,4},{1,3},{3,1},{5,7},{7,5},{8,10},{10,8},{12,... | collective-permute-start | bytes 1794056 | tf_op jit(solution)/shard_map/d1_x/ppermute | solution.py:37
  152.9 2.3 query_kernel.1
  156.1 10.9 %collective-permute-done.42.refs_11_.refs_15_ = bf16[512,128]{1,0:T(8,128)(2,1)S(1)} collective-permute-done((bf16[512,128]{1,0:T(8,128)(2,1)S(1)}, bf16[512,128]{1,0:T(8,128)(2,1)S(1)}, u32[]{:S(2)}, u32[]{:S(2)}) %collective-permute-start.42) | collective-permute-done | bytes 131104 | tf_op jit(solution)/shard_map/grad_kv/ppermute | solution.py:37
  167.1 1.5 tick_kernel.12
  168.5 1.8 collective-permute-start.46
  170.3 1.7 collective-permute-start.47
  172.8 3.2 collective-permute-start.44
  176.0 2.2 key_kernel.1
  178.2 5.5 %collective-permute-done.44.refs_1_ = bf16[1824,128]{1,0:T(8,128)(2,1)S(1)} collective-permute-done((bf16[1824,128]{1,0:T(8,128)(2,1)S(1)}, bf16[1824,128]{1,0:T(8,128)(2,1)S(1)}, u32[]{:S(2)}, u32[]{:S(2)}) %collective-permute-start.44) | collective-permute-done | bytes 466976 | tf_op jit(solution)/shard_map/swap_g1_u1/ppermute | solution.py:78
  183.7 3.8 %collective-permute-done.46.refs_7_.refs_13_.refs_4_.refs_5_.refs_10_ = bf16[3344,128]{1,0:T(8,128)(2,1)S(1)} collective-permute-done((bf16[3344,128]{1,0:T(8,128)(2,1)S(1)}, bf16[3344,128]{1,0:T(8,128)(2,1)S(1)}, u32[]{:S(2)}, u32[]{:S(2)}) %collective-permute-start.46) | collective-permute-done | bytes 856096 | tf_op jit(solution)/shard_map/d2_y/ppermute | solution.py:37
  188.7 1.5 tick_kernel.13
  190.9 1.5 collective-permute-start.51
  194.2 1.5 collective-permute-start.52
  196.6 1.5 join_kernel.2.refs_6_
  200.7 27.6 %collective-permute-done.52.refs_3_ = bf16[1904,128]{1,0:T(8,128)(2,1)S(1)} collective-permute-done((bf16[1904,128]{1,0:T(8,128)(2,1)S(1)}, bf16[1904,128]{1,0:T(8,128)(2,1)S(1)}, u32[]{:S(2)}, u32[]{:S(2)}) %collective-permute-start.52) | collective-permute-done | bytes 487456 | tf_op jit(solution)/shard_map/shares/ppermute | solution.py:37
  232.7 3.8 %collective-permute-start.57 = (bf16[1904,128]{1,0:T(8,128)(2,1)S(1)}, bf16[1904,128]{1,0:T(8,128)(2,1)S(1)}, u32[]{:S(2)}, u32[]{:S(2)}) collective-permute-start(bf16[1904,128]{1,0:T(8,128)(2,1)S(1)} %get-tuple-element.283.refs_5_), channel_id=1, source_target_pairs={{0,8},{8,0},{16,24},{24,16},{1,9},{9,1},{17,25},{25,17},{2,10},{10... | collective-permute-start | bytes 1462280 | tf_op jit(solution)/shard_map/swap_share/ppermute | solution.py:78
  236.6 5.3 %place_kernel.4 = (f32[2432,896]{1,0:T(8,128)}, f32[8,128]{1,0:T(8,128)S(1)}) custom-call(s32[3]{0:T(128)S(1)} %pad_add_fusion.refs_1_.refs_0_, bf16[1824,128]{1,0:T(8,128)(2,1)S(1)} %copy-done.22, bf16[2336,128]{1,0:T(8,128)(2,1)S(1)} %collective-permute-done.41.refs_8_.refs_9_.refs_13_.refs_2_, ...), custom_call_target="tpu_custom_call" | custom-call | tf_op jit(solution)/shard_map/place_kernel/pallas_call | solution.py:684
  241.8 11.3 %collective-permute-done.55.refs_1_ = bf16[1824,128]{1,0:T(8,128)(2,1)S(1)} collective-permute-done((bf16[1824,128]{1,0:T(8,128)(2,1)S(1)}, bf16[1824,128]{1,0:T(8,128)(2,1)S(1)}, u32[]{:S(2)}, u32[]{:S(2)}) %collective-permute-start.55) | collective-permute-done | bytes 466976 | tf_op jit(solution)/shard_map/swap_u1/ppermute | solution.py:78
  255.9 2.0 collective-permute-start.60
  258.0 17.6 %collective-permute-done.61.refs_4_ = bf16[1904,128]{1,0:T(8,128)(2,1)S(1)} collective-permute-done((bf16[1904,128]{1,0:T(8,128)(2,1)S(1)}, bf16[1904,128]{1,0:T(8,128)(2,1)S(1)}, u32[]{:S(2)}, u32[]{:S(2)}) %collective-permute-start.61) | collective-permute-done | bytes 487456 | tf_op jit(solution)/shard_map/share_far/ppermute | solution.py:37
  279.4 1.7 collective-permute-done.54
  281.2 1.9 join_kernel.3.refs_15_
  283.1 1.5 copy-done
  284.6 6.9 %place_kernel.5 = (f32[896,2432]{1,0:T(8,128)}, f32[8,128]{1,0:T(8,128)S(1)}) custom-call(s32[3]{0:T(128)S(1)} %pad_add_fusion.refs_1_.refs_0_, bf16[1824,128]{1,0:T(8,128)(2,1)S(1)} %get-tuple-element.271.refs_3_.refs_1_, bf16[4944,128]{1,0:T(8,128)(2,1)S(1)} %collective-permute-done.51.refs_1_.refs_7_.refs_13_.refs_14_.refs_2_, ...), custom_call_target="tpu_custom_call" | custom-call | tf_op jit(solution)/shard_map/place_kernel/pallas_call | solution.py:684
  291.5 15.7 %collective-permute-done.64.refs_2_.refs_6_.refs_7_ = bf16[5248,128]{1,0:T(8,128)(2,1)S(1)} collective-permute-done((bf16[5248,128]{1,0:T(8,128)(2,1)S(1)}, bf16[5248,128]{1,0:T(8,128)(2,1)S(1)}, u32[]{:S(2)}, u32[]{:S(2)}) %collective-permute-start.64) | collective-permute-done | bytes 1343520 | tf_op jit(solution)/shard_map/u2_x/ppermute | solution.py:37
  307.9 1.7 collective-permute-start.67
  312.0 3.7 %place_kernel.6 = (f32[896,2432]{1,0:T(8,128)}, f32[8,128]{1,0:T(8,128)S(1)}) custom-call(s32[3]{0:T(128)S(1)} %pad_add_fusion.refs_1_.refs_0_, bf16[1824,128]{1,0:T(8,128)(2,1)S(1)} %get-tuple-element.292.refs_7_.refs_1_, bf16[3040,128]{1,0:T(8,128)(2,1)S(1)} %collective-permute-done.63.refs_6_.refs_8_.refs_13_.refs_14_.refs_2_, ...), custom_call_target="tpu_custom_call" | custom-call | tf_op jit(solution)/shard_map/place_kernel/pallas_call | solution.py:684
  315.7 1.9 collective-permute-done.66.refs_4_
  317.6 2.7 unpack_kernel.1
  322.1 4.2 %place_kernel.7 = (f32[896,2432]{1,0:T(8,128)}, f32[8,128]{1,0:T(8,128)}) custom-call(s32[3]{0:T(128)S(1)} %pad_add_fusion.refs_1_.refs_0_, bf16[2432,128]{1,0:T(8,128)(2,1)S(1)} %get-tuple-element.293.refs_3_.refs_1_, bf16[5248,128]{1,0:T(8,128)(2,1)S(1)} %collective-permute-done.64.refs_2_.refs_6_.refs_7_, ...), custom_call_target="tpu_custom_call", output_to_operand_aliasing={{0}: (9, {})} | custom-call | tf_op jit(solution)/shard_map/place_kernel/pallas_call | solution.py:684
  (291 shorter events, 60.3 us)
Async XLA Ops:
  14.2 14.0 %collective-permute-start.4 = (bf16[512,128]{1,0:T(8,128)(2,1)S(1)}, bf16[512,128]{1,0:T(8,128)(2,1)S(1)}, u32[]{:S(2)}, u32[]{:S(2)}) collective-permute-start(bf16[512,128]{1,0:T(8,128)(2,1)S(1)} %get-tuple-element.167.refs_4_.refs_8_), channel_id=1, source_target_pairs={{0,6},{2,4},{4,2},{6,0},{1,7},{3,5},{5,3},{7,1},{8,14},{10,12},{12... | collective-permute-start | bytes 393224 | tf_op jit(solution)/shard_map/kv/ppermute | solution.py:37
  18.0 10.1 %collective-permute-start.3 = (bf16[512,128]{1,0:T(8,128)(2,1)S(1)}, bf16[512,128]{1,0:T(8,128)(2,1)S(1)}, u32[]{:S(2)}, u32[]{:S(2)}) collective-permute-start(bf16[512,128]{1,0:T(8,128)(2,1)S(1)} %get-tuple-element.167.refs_4_.refs_8_), channel_id=1, source_target_pairs={{0,4},{2,6},{4,0},{6,2},{1,5},{3,7},{5,1},{7,3},{8,12},{10,14},{12... | collective-permute-start | bytes 393224 | tf_op jit(solution)/shard_map/kv/ppermute | solution.py:37
  18.5 9.6 %collective-permute-start.2 = (bf16[512,128]{1,0:T(8,128)(2,1)S(1)}, bf16[512,128]{1,0:T(8,128)(2,1)S(1)}, u32[]{:S(2)}, u32[]{:S(2)}) collective-permute-start(bf16[512,128]{1,0:T(8,128)(2,1)S(1)} %get-tuple-element.167.refs_4_.refs_8_), channel_id=1, source_target_pairs={{0,2},{2,0},{4,6},{6,4},{1,3},{3,1},{5,7},{7,5},{8,10},{10,8},{12,... | collective-permute-start | bytes 393224 | tf_op jit(solution)/shard_map/kv/ppermute | solution.py:37
  24.6 11.8 %collective-permute-start.6 = (bf16[256,896]{1,0:T(8,128)(2,1)S(1)}, bf16[256,896]{1,0:T(8,128)(2,1)S(1)}, u32[]{:S(2)}, u32[]{:S(2)}) collective-permute-start(bf16[256,896]{1,0:T(8,128)(2,1)S(1)} %get-tuple-element.164.refs_1_.refs_5_.refs_2_), channel_id=1, source_target_pairs={{0,2},{2,0},{4,6},{6,4},{1,3},{3,1},{5,7},{7,5},{8,10},{10,8},{12,... | collective-permute-start | bytes 1376264 | tf_op jit(solution)/shard_map/gy/ppermute | solution.py:37
  26.6 11.1 %collective-permute-start = (bf16[256,896]{1,0:T(8,128)(2,1)S(1)}, bf16[256,896]{1,0:T(8,128)(2,1)S(1)}, u32[]{:S(2)}, u32[]{:S(2)}) collective-permute-start(bf16[256,896]{1,0:T(8,128)(2,1)S(1)} %get-tuple-element.164.refs_1_.refs_5_.refs_2_), channel_id=1, source_target_pairs={{0,4},{2,6},{4,0},{6,2},{1,5},{3,7},{5,1},{7,3},{8,12},{10,14},{12... | collective-permute-start | bytes 1376264 | tf_op jit(solution)/shard_map/gy/ppermute | solution.py:37
  33.6 4.1 %collective-permute-start.5 = (bf16[896,256]{1,0:T(8,128)(2,1)S(1)}, bf16[896,256]{1,0:T(8,128)(2,1)S(1)}, u32[]{:S(2)}, u32[]{:S(2)}) collective-permute-start(bf16[896,256]{1,0:T(8,128)(2,1)S(1)} %get-tuple-element.170), channel_id=1, source_target_pairs={{0,1},{1,0},{2,3},{3,2},{4,5},{5,4},{6,7},{7,6},{8,9},{9,8},{10,11... | collective-permute-start | bytes 1376264 | tf_op jit(solution)/shard_map/part_core/ppermute | solution.py:37
  38.8 6.8 %collective-permute-start.7 = (bf16[896,256]{1,0:T(8,128)(2,1)S(1)}, bf16[896,256]{1,0:T(8,128)(2,1)S(1)}, u32[]{:S(2)}, u32[]{:S(2)}) collective-permute-start(bf16[896,256]{1,0:T(8,128)(2,1)S(1)} %get-tuple-element.171.refs_3_.refs_9_.refs_5_), channel_id=1, source_target_pairs={{0,1},{1,0},{2,3},{3,2},{4,5},{5,4},{6,7},{7,6},{8,9},{9,8},{10,11... | collective-permute-start | bytes 1376264 | tf_op jit(solution)/shard_map/x_core/ppermute | solution.py:37
  38.9 14.6 %collective-permute-start.9 = (bf16[896,256]{1,0:T(8,128)(2,1)S(1)}, bf16[896,256]{1,0:T(8,128)(2,1)S(1)}, u32[]{:S(2)}, u32[]{:S(2)}) collective-permute-start(bf16[896,256]{1,0:T(8,128)(2,1)S(1)} %get-tuple-element.171.refs_3_.refs_9_.refs_5_), channel_id=1, source_target_pairs={{0,4},{2,6},{4,0},{6,2},{1,5},{3,7},{5,1},{7,3},{8,12},{10,14},{12... | collective-permute-start | bytes 1376264 | tf_op jit(solution)/shard_map/x/ppermute | solution.py:37
  42.4 13.4 %collective-permute-start.8 = (bf16[896,256]{1,0:T(8,128)(2,1)S(1)}, bf16[896,256]{1,0:T(8,128)(2,1)S(1)}, u32[]{:S(2)}, u32[]{:S(2)}) collective-permute-start(bf16[896,256]{1,0:T(8,128)(2,1)S(1)} %get-tuple-element.171.refs_3_.refs_9_.refs_5_), channel_id=1, source_target_pairs={{0,2},{2,0},{4,6},{6,4},{1,3},{3,1},{5,7},{7,5},{8,10},{10,8},{12,... | collective-permute-start | bytes 1376264 | tf_op jit(solution)/shard_map/x/ppermute | solution.py:37
  45.1 11.7 %collective-permute-start.11 = (bf16[256,896]{1,0:T(8,128)(2,1)S(1)}, bf16[256,896]{1,0:T(8,128)(2,1)S(1)}, u32[]{:S(2)}, u32[]{:S(2)}) collective-permute-start(bf16[256,896]{1,0:T(8,128)(2,1)S(1)} %collective-permute-done.6.refs_5_.refs_1_.refs_7_), channel_id=1, source_target_pairs={{0,1},{1,0},{2,3},{3,2},{4,5},{5,4},{6,7},{7,6},{8,9},{9,8},{10,11... | collective-permute-start | bytes 1376264 | tf_op jit(solution)/shard_map/gy_core/ppermute | solution.py:37
  45.1 13.6 %collective-permute-start.1 = (bf16[256,896]{1,0:T(8,128)(2,1)S(1)}, bf16[256,896]{1,0:T(8,128)(2,1)S(1)}, u32[]{:S(2)}, u32[]{:S(2)}) collective-permute-start(bf16[256,896]{1,0:T(8,128)(2,1)S(1)} %collective-permute-done.refs_6_.refs_1_.refs_9_), channel_id=1, source_target_pairs={{0,1},{1,0},{2,3},{3,2},{4,5},{5,4},{6,7},{7,6},{8,9},{9,8},{10,11... | collective-permute-start | bytes 1376264 | tf_op jit(solution)/shard_map/gy_core/ppermute | solution.py:37
  55.8 4.5 %collective-permute-start.12 = (bf16[896,256]{1,0:T(8,128)(2,1)S(1)}, bf16[896,256]{1,0:T(8,128)(2,1)S(1)}, u32[]{:S(2)}, u32[]{:S(2)}) collective-permute-start(bf16[896,256]{1,0:T(8,128)(2,1)S(1)} %get-tuple-element.179.refs_3_.refs_7_), channel_id=1, source_target_pairs={{0,1},{1,0},{2,3},{3,2},{4,5},{5,4},{6,7},{7,6},{8,9},{9,8},{10,11... | collective-permute-start | bytes 1376264 | tf_op jit(solution)/shard_map/x_core/ppermute | solution.py:37
  55.8 10.3 %collective-permute-start.10 = (bf16[896,256]{1,0:T(8,128)(2,1)S(1)}, bf16[896,256]{1,0:T(8,128)(2,1)S(1)}, u32[]{:S(2)}, u32[]{:S(2)}) collective-permute-start(bf16[896,256]{1,0:T(8,128)(2,1)S(1)} %get-tuple-element.178.refs_3_.refs_9_), channel_id=1, source_target_pairs={{0,1},{1,0},{2,3},{3,2},{4,5},{5,4},{6,7},{7,6},{8,9},{9,8},{10,11... | collective-permute-start | bytes 1376264 | tf_op jit(solution)/shard_map/x_core/ppermute | solution.py:37
  56.4 13.7 %collective-permute-start.15 = (bf16[128,896]{1,0:T(8,128)(2,1)S(1)}, bf16[128,896]{1,0:T(8,128)(2,1)S(1)}, u32[]{:S(2)}, u32[]{:S(2)}) collective-permute-start(bf16[128,896]{1,0:T(8,128)(2,1)S(1)} %slice.56), channel_id=1, source_target_pairs={{0,4},{2,6},{4,0},{6,2},{1,5},{3,7},{5,1},{7,3},{8,12},{10,14},{12... | collective-permute-start | bytes 688136 | tf_op jit(solution)/shard_map/gy_relay/ppermute | solution.py:37
  56.8 13.2 %collective-permute-start.16 = (bf16[128,896]{1,0:T(8,128)(2,1)S(1)}, bf16[128,896]{1,0:T(8,128)(2,1)S(1)}, u32[]{:S(2)}, u32[]{:S(2)}) collective-permute-start(bf16[128,896]{1,0:T(8,128)(2,1)S(1)} %slice.57), channel_id=1, source_target_pairs={{0,2},{2,0},{4,6},{6,4},{1,3},{3,1},{5,7},{7,5},{8,10},{10,8},{12,... | collective-permute-start | bytes 688136 | tf_op jit(solution)/shard_map/gy_relay/ppermute | solution.py:37
  58.6 11.4 %collective-permute-start.13 = (bf16[448,256]{1,0:T(8,128)(2,1)S(1)}, bf16[448,256]{1,0:T(8,128)(2,1)S(1)}, u32[]{:S(2)}, u32[]{:S(2)}) collective-permute-start(bf16[448,256]{1,0:T(8,128)(2,1)S(1)} %slice.43), channel_id=1, source_target_pairs={{0,4},{2,6},{4,0},{6,2},{1,5},{3,7},{5,1},{7,3},{8,12},{10,14},{12... | collective-permute-start | bytes 688136 | tf_op jit(solution)/shard_map/x_relay/ppermute | solution.py:37
  60.4 9.7 %collective-permute-start.14 = (bf16[448,256]{1,0:T(8,128)(2,1)S(1)}, bf16[448,256]{1,0:T(8,128)(2,1)S(1)}, u32[]{:S(2)}, u32[]{:S(2)}) collective-permute-start(bf16[448,256]{1,0:T(8,128)(2,1)S(1)} %slice.44), channel_id=1, source_target_pairs={{0,2},{2,0},{4,6},{6,4},{1,3},{3,1},{5,7},{7,5},{8,10},{10,8},{12,... | collective-permute-start | bytes 688136 | tf_op jit(solution)/shard_map/x_relay/ppermute | solution.py:37
  70.2 7.9 %collective-permute-start.22 = (bf16[896,256]{1,0:T(8,128)(2,1)S(1)}, bf16[896,256]{1,0:T(8,128)(2,1)S(1)}, u32[]{:S(2)}, u32[]{:S(2)}) collective-permute-start(bf16[896,256]{1,0:T(8,128)(2,1)S(1)} %get-tuple-element.193), channel_id=1, source_target_pairs={{0,1},{1,0},{2,3},{3,2},{4,5},{5,4},{6,7},{7,6},{8,9},{9,8},{10,11... | collective-permute-start | bytes 1376264 | tf_op jit(solution)/shard_map/back_core/ppermute | solution.py:37
  70.7 7.4 %collective-permute-start.21 = (bf16[896,256]{1,0:T(8,128)(2,1)S(1)}, bf16[896,256]{1,0:T(8,128)(2,1)S(1)}, u32[]{:S(2)}, u32[]{:S(2)}) collective-permute-start(bf16[896,256]{1,0:T(8,128)(2,1)S(1)} %get-tuple-element.189.refs_13_), channel_id=1, source_target_pairs={{0,1},{1,0},{2,3},{3,2},{4,5},{5,4},{6,7},{7,6},{8,9},{9,8},{10,11... | collective-permute-start | bytes 1376264 | tf_op jit(solution)/shard_map/back_core/ppermute | solution.py:37
  80.4 15.4 %collective-permute-start.27 = (bf16[1824,128]{1,0:T(8,128)(2,1)S(1)}, bf16[1824,128]{1,0:T(8,128)(2,1)S(1)}, u32[]{:S(2)}, u32[]{:S(2)}) collective-permute-start(bf16[1824,128]{1,0:T(8,128)(2,1)S(1)} %weight_kernel.4.refs_14_.refs_1_), channel_id=1, source_target_pairs={{0,8},{8,0},{16,24},{24,16},{1,9},{9,1},{17,25},{25,17},{2,10},{10... | collective-permute-start | bytes 1400840 | tf_op jit(solution)/shard_map/swap_d1/ppermute | solution.py:78
  82.5 8.1 %collective-permute-start.24 = (bf16[896,256]{1,0:T(8,128)(2,1)S(1)}, bf16[896,256]{1,0:T(8,128)(2,1)S(1)}, u32[]{:S(2)}, u32[]{:S(2)}) collective-permute-start(bf16[896,256]{1,0:T(8,128)(2,1)S(1)} %get-tuple-element.180.refs_9_), channel_id=1, source_target_pairs={{0,1},{1,0},{2,3},{3,2},{4,5},{5,4},{6,7},{7,6},{8,9},{9,8},{10,11... | collective-permute-start | bytes 1376264 | tf_op jit(solution)/shard_map/back_core/ppermute | solution.py:37
  82.6 8.1 %collective-permute-start.23 = (bf16[896,256]{1,0:T(8,128)(2,1)S(1)}, bf16[896,256]{1,0:T(8,128)(2,1)S(1)}, u32[]{:S(2)}, u32[]{:S(2)}) collective-permute-start(bf16[896,256]{1,0:T(8,128)(2,1)S(1)} %get-tuple-element.196), channel_id=1, source_target_pairs={{0,1},{1,0},{2,3},{3,2},{4,5},{5,4},{6,7},{7,6},{8,9},{9,8},{10,11... | collective-permute-start | bytes 1376264 | tf_op jit(solution)/shard_map/back_core/ppermute | solution.py:37
  83.1 12.4 %collective-permute-start.26 = (bf16[896,256]{1,0:T(8,128)(2,1)S(1)}, bf16[896,256]{1,0:T(8,128)(2,1)S(1)}, u32[]{:S(2)}, u32[]{:S(2)}) collective-permute-start(bf16[896,256]{1,0:T(8,128)(2,1)S(1)} %get-tuple-element.199), channel_id=1, source_target_pairs={{0,4},{2,6},{4,0},{6,2},{1,5},{3,7},{5,1},{7,3},{8,12},{10,14},{12... | collective-permute-start | bytes 1376264 | tf_op jit(solution)/shard_map/back/ppermute | solution.py:37
  83.7 12.1 %collective-permute-start.25 = (bf16[896,256]{1,0:T(8,128)(2,1)S(1)}, bf16[896,256]{1,0:T(8,128)(2,1)S(1)}, u32[]{:S(2)}, u32[]{:S(2)}) collective-permute-start(bf16[896,256]{1,0:T(8,128)(2,1)S(1)} %get-tuple-element.198.refs_14_), channel_id=1, source_target_pairs={{0,2},{2,0},{4,6},{6,4},{1,3},{3,1},{5,7},{7,5},{8,10},{10,8},{12,... | collective-permute-start | bytes 1376264 | tf_op jit(solution)/shard_map/back/ppermute | solution.py:37
  96.1 18.7 %collective-permute-start.28 = (bf16[4,896,256]{2,1,0:T(8,128)(2,1)S(1)}, bf16[4,896,256]{2,1,0:T(8,128)(2,1)S(1)}, u32[]{:S(2)}, u32[]{:S(2)}) collective-permute-start(bf16[4,896,256]{2,1,0:T(8,128)(2,1)S(1)} %get-tuple-element.202), channel_id=1, source_target_pairs={{0,1},{1,0},{2,3},{3,2},{4,5},{5,4},{6,7},{7,6},{8,9},{9,8},{10,11... | collective-permute-start | bytes 5505032 | tf_op jit(solution)/shard_map/layer_core/ppermute | solution.py:37
  96.2 16.4 %collective-permute-start.31 = (bf16[2432,128]{1,0:T(8,128)(2,1)S(1)}, bf16[2432,128]{1,0:T(8,128)(2,1)S(1)}, u32[]{:S(2)}, u32[]{:S(2)}) collective-permute-start(bf16[2432,128]{1,0:T(8,128)(2,1)S(1)} %get-tuple-element.210.refs_3_), channel_id=1, source_target_pairs={{0,8},{8,0},{16,24},{24,16},{1,9},{9,1},{17,25},{25,17},{2,10},{10... | collective-permute-start | bytes 1867784 | tf_op jit(solution)/shard_map/swap_d2/ppermute | solution.py:78
  97.2 14.3 %collective-permute-start.30 = (bf16[1824,128]{1,0:T(8,128)(2,1)S(1)}, bf16[1824,128]{1,0:T(8,128)(2,1)S(1)}, u32[]{:S(2)}, u32[]{:S(2)}) collective-permute-start(bf16[1824,128]{1,0:T(8,128)(2,1)S(1)} %tick_kernel.9.refs_14_.refs_1_), channel_id=1, source_target_pairs={{8,16},{16,8},{9,17},{17,9},{10,18},{18,10},{11,19},{19,11},{12,20... | collective-permute-start | bytes 1400840 | tf_op jit(solution)/shard_map/cross_d1/ppermute | solution.py:83
  97.9 13.6 %collective-permute-start.29 = (bf16[896,256]{1,0:T(8,128)(2,1)S(1)}, bf16[896,256]{1,0:T(8,128)(2,1)S(1)}, u32[]{:S(2)}, u32[]{:S(2)}) collective-permute-start(bf16[896,256]{1,0:T(8,128)(2,1)S(1)} %get-tuple-element.209.refs_3_), channel_id=1, source_target_pairs={{0,6},{2,4},{4,2},{6,0},{1,7},{3,5},{5,3},{7,1},{8,14},{10,12},{12... | collective-permute-start | bytes 1376264 | tf_op jit(solution)/shard_map/back/ppermute | solution.py:37
  115.8 9.1 %collective-permute-start.34 = (bf16[896,256]{1,0:T(8,128)(2,1)S(1)}, bf16[896,256]{1,0:T(8,128)(2,1)S(1)}, u32[]{:S(2)}, u32[]{:S(2)}) collective-permute-start(bf16[896,256]{1,0:T(8,128)(2,1)S(1)} %get-tuple-element.229.refs_1_.refs_4_), channel_id=1, source_target_pairs={{0,1},{1,0},{2,3},{3,2},{4,5},{5,4},{6,7},{7,6},{8,9},{9,8},{10,11... | collective-permute-start | bytes 1376264 | tf_op jit(solution)/shard_map/mid_core/ppermute | solution.py:37
  115.8 29.4 %collective-permute-start.33 = (bf16[2432,128]{1,0:T(8,128)(2,1)S(1)}, bf16[2432,128]{1,0:T(8,128)(2,1)S(1)}, u32[]{:S(2)}, u32[]{:S(2)}) collective-permute-start(bf16[2432,128]{1,0:T(8,128)(2,1)S(1)} %get-tuple-element.227.refs_4_), channel_id=1, source_target_pairs={{8,16},{16,8},{9,17},{17,9},{10,18},{18,10},{11,19},{19,11},{12,20... | collective-permute-start | bytes 1867784 | tf_op jit(solution)/shard_map/cross_d2/ppermute | solution.py:83
  116.9 28.3 %collective-permute-start.32 = (bf16[1824,128]{1,0:T(8,128)(2,1)S(1)}, bf16[1824,128]{1,0:T(8,128)(2,1)S(1)}, u32[]{:S(2)}, u32[]{:S(2)}) collective-permute-start(bf16[1824,128]{1,0:T(8,128)(2,1)S(1)} %get-tuple-element.226), channel_id=1, source_target_pairs={{0,8},{8,0},{16,24},{24,16},{1,9},{9,1},{17,25},{25,17},{2,10},{10... | collective-permute-start | bytes 1400840 | tf_op jit(solution)/shard_map/swap_d1_g1/ppermute | solution.py:78
  121.7 13.4 %collective-permute-start.35 = (bf16[896,256]{1,0:T(8,128)(2,1)S(1)}, bf16[896,256]{1,0:T(8,128)(2,1)S(1)}, u32[]{:S(2)}, u32[]{:S(2)}) collective-permute-start(bf16[896,256]{1,0:T(8,128)(2,1)S(1)} %get-tuple-element.240), channel_id=1, source_target_pairs={{0,2},{2,0},{4,6},{6,4},{1,3},{3,1},{5,7},{7,5},{8,10},{10,8},{12,... | collective-permute-start | bytes 1376264 | tf_op jit(solution)/shard_map/layer/ppermute | solution.py:37
  123.4 21.8 %collective-permute-start.36 = (bf16[896,256]{1,0:T(8,128)(2,1)S(1)}, bf16[896,256]{1,0:T(8,128)(2,1)S(1)}, u32[]{:S(2)}, u32[]{:S(2)}) collective-permute-start(bf16[896,256]{1,0:T(8,128)(2,1)S(1)} %get-tuple-element.241), channel_id=1, source_target_pairs={{0,4},{2,6},{4,0},{6,2},{1,5},{3,7},{5,1},{7,3},{8,12},{10,14},{12... | collective-permute-start | bytes 1376264 | tf_op jit(solution)/shard_map/layer/ppermute | solution.py:37
  124.9 20.3 %collective-permute-start.37 = (bf16[896,256]{1,0:T(8,128)(2,1)S(1)}, bf16[896,256]{1,0:T(8,128)(2,1)S(1)}, u32[]{:S(2)}, u32[]{:S(2)}) collective-permute-start(bf16[896,256]{1,0:T(8,128)(2,1)S(1)} %get-tuple-element.242), channel_id=1, source_target_pairs={{0,6},{2,4},{4,2},{6,0},{1,7},{3,5},{5,3},{7,1},{8,14},{10,12},{12... | collective-permute-start | bytes 1376264 | tf_op jit(solution)/shard_map/layer/ppermute | solution.py:37
  146.7 20.3 %collective-permute-start.38 = (bf16[2432,128]{1,0:T(8,128)(2,1)S(1)}, bf16[2432,128]{1,0:T(8,128)(2,1)S(1)}, u32[]{:S(2)}, u32[]{:S(2)}) collective-permute-start(bf16[2432,128]{1,0:T(8,128)(2,1)S(1)} %get-tuple-element.244), channel_id=1, source_target_pairs={{0,8},{8,0},{16,24},{24,16},{1,9},{9,1},{17,25},{25,17},{2,10},{10... | collective-permute-start | bytes 1867784 | tf_op jit(solution)/shard_map/swap_d2_g2/ppermute | solution.py:78
  147.1 19.9 %collective-permute-start.40 = (bf16[2336,128]{1,0:T(8,128)(2,1)S(1)}, bf16[2336,128]{1,0:T(8,128)(2,1)S(1)}, u32[]{:S(2)}, u32[]{:S(2)}) collective-permute-start(bf16[2336,128]{1,0:T(8,128)(2,1)S(1)} %get-tuple-element.247), channel_id=1, source_target_pairs={{0,4},{2,6},{4,0},{6,2},{1,5},{3,7},{5,1},{7,3},{8,12},{10,14},{12... | collective-permute-start | bytes 1794056 | tf_op jit(solution)/shard_map/d1_y/ppermute | solution.py:37
  148.5 18.5 %collective-permute-start.41 = (bf16[2336,128]{1,0:T(8,128)(2,1)S(1)}, bf16[2336,128]{1,0:T(8,128)(2,1)S(1)}, u32[]{:S(2)}, u32[]{:S(2)}) collective-permute-start(bf16[2336,128]{1,0:T(8,128)(2,1)S(1)} %get-tuple-element.248), channel_id=1, source_target_pairs={{0,2},{2,0},{4,6},{6,4},{1,3},{3,1},{5,7},{7,5},{8,10},{10,8},{12,... | collective-permute-start | bytes 1794056 | tf_op jit(solution)/shard_map/d1_x/ppermute | solution.py:37
  152.1 14.9 %collective-permute-start.39 = (bf16[1824,128]{1,0:T(8,128)(2,1)S(1)}, bf16[1824,128]{1,0:T(8,128)(2,1)S(1)}, u32[]{:S(2)}, u32[]{:S(2)}) collective-permute-start(bf16[1824,128]{1,0:T(8,128)(2,1)S(1)} %get-tuple-element.246.refs_4_), channel_id=1, source_target_pairs={{8,16},{16,8},{9,17},{17,9},{10,18},{18,10},{11,19},{19,11},{12,20... | collective-permute-start | bytes 1400840 | tf_op jit(solution)/shard_map/cross_g1/ppermute | solution.py:83
  152.8 14.2 %collective-permute-start.42 = (bf16[512,128]{1,0:T(8,128)(2,1)S(1)}, bf16[512,128]{1,0:T(8,128)(2,1)S(1)}, u32[]{:S(2)}, u32[]{:S(2)}) collective-permute-start(bf16[512,128]{1,0:T(8,128)(2,1)S(1)} %get-tuple-element.249), channel_id=1, source_target_pairs={{0,6},{2,4},{4,2},{6,0},{1,7},{3,5},{5,3},{7,1},{8,14},{10,12},{12... | collective-permute-start | bytes 393224 | tf_op jit(solution)/shard_map/grad_kv/ppermute | solution.py:37
  168.5 19.0 %collective-permute-start.46 = (bf16[3344,128]{1,0:T(8,128)(2,1)S(1)}, bf16[3344,128]{1,0:T(8,128)(2,1)S(1)}, u32[]{:S(2)}, u32[]{:S(2)}) collective-permute-start(bf16[3344,128]{1,0:T(8,128)(2,1)S(1)} %get-tuple-element.258), channel_id=1, source_target_pairs={{0,4},{2,6},{4,0},{6,2},{1,5},{3,7},{5,1},{7,3},{8,12},{10,14},{12... | collective-permute-start | bytes 2568200 | tf_op jit(solution)/shard_map/d2_y/ppermute | solution.py:37
  170.3 18.4 %collective-permute-start.47 = (bf16[3344,128]{1,0:T(8,128)(2,1)S(1)}, bf16[3344,128]{1,0:T(8,128)(2,1)S(1)}, u32[]{:S(2)}, u32[]{:S(2)}) collective-permute-start(bf16[3344,128]{1,0:T(8,128)(2,1)S(1)} %get-tuple-element.266), channel_id=1, source_target_pairs={{0,2},{2,0},{4,6},{6,4},{1,3},{3,1},{5,7},{7,5},{8,10},{10,8},{12,... | collective-permute-start | bytes 2568200 | tf_op jit(solution)/shard_map/d2_x/ppermute | solution.py:37
  172.1 11.7 %collective-permute-start.45 = (bf16[2432,128]{1,0:T(8,128)(2,1)S(1)}, bf16[2432,128]{1,0:T(8,128)(2,1)S(1)}, u32[]{:S(2)}, u32[]{:S(2)}) collective-permute-start(bf16[2432,128]{1,0:T(8,128)(2,1)S(1)} %get-tuple-element.256.refs_4_), channel_id=1, source_target_pairs={{8,16},{16,8},{9,17},{17,9},{10,18},{18,10},{11,19},{19,11},{12,20... | collective-permute-start | bytes 1867784 | tf_op jit(solution)/shard_map/cross_g2/ppermute | solution.py:83
  172.8 11.0 %collective-permute-start.44 = (bf16[1824,128]{1,0:T(8,128)(2,1)S(1)}, bf16[1824,128]{1,0:T(8,128)(2,1)S(1)}, u32[]{:S(2)}, u32[]{:S(2)}) collective-permute-start(bf16[1824,128]{1,0:T(8,128)(2,1)S(1)} %get-tuple-element.254), channel_id=1, source_target_pairs={{0,8},{8,0},{16,24},{24,16},{1,9},{9,1},{17,25},{25,17},{2,10},{10... | collective-permute-start | bytes 1400840 | tf_op jit(solution)/shard_map/swap_g1_u1/ppermute | solution.py:78
  190.3 38.0 %collective-permute-start.50 = (bf16[4944,128]{1,0:T(8,128)(2,1)S(1)}, bf16[4944,128]{1,0:T(8,128)(2,1)S(1)}, u32[]{:S(2)}, u32[]{:S(2)}) collective-permute-start(bf16[4944,128]{1,0:T(8,128)(2,1)S(1)} %get-tuple-element.275), channel_id=1, source_target_pairs={{0,4},{2,6},{4,0},{6,2},{1,5},{3,7},{5,1},{7,3},{8,12},{10,14},{12... | collective-permute-start | bytes 3797000 | tf_op jit(solution)/shard_map/g1_y/ppermute | solution.py:37
  190.9 37.4 %collective-permute-start.51 = (bf16[4944,128]{1,0:T(8,128)(2,1)S(1)}, bf16[4944,128]{1,0:T(8,128)(2,1)S(1)}, u32[]{:S(2)}, u32[]{:S(2)}) collective-permute-start(bf16[4944,128]{1,0:T(8,128)(2,1)S(1)} %get-tuple-element.276), channel_id=1, source_target_pairs={{0,2},{2,0},{4,6},{6,4},{1,3},{3,1},{5,7},{7,5},{8,10},{10,8},{12,... | collective-permute-start | bytes 3797000 | tf_op jit(solution)/shard_map/g1_x/ppermute | solution.py:37
  192.4 3.3 %collective-permute-start.53 = (bf16[896,256]{1,0:T(8,128)(2,1)S(1)}, bf16[896,256]{1,0:T(8,128)(2,1)S(1)}, u32[]{:S(2)}, u32[]{:S(2)}) collective-permute-start(bf16[896,256]{1,0:T(8,128)(2,1)S(1)} %get-tuple-element.279), channel_id=1, source_target_pairs={{0,1},{1,0},{2,3},{3,2},{4,5},{5,4},{6,7},{7,6},{8,9},{9,8},{10,11... | collective-permute-start | bytes 1376264 | tf_op jit(solution)/shard_map/normed_core/ppermute | solution.py:37
  192.9 35.7 %collective-permute-start.48 = (bf16[2432,128]{1,0:T(8,128)(2,1)S(1)}, bf16[2432,128]{1,0:T(8,128)(2,1)S(1)}, u32[]{:S(2)}, u32[]{:S(2)}) collective-permute-start(bf16[2432,128]{1,0:T(8,128)(2,1)S(1)} %get-tuple-element.272), channel_id=1, source_target_pairs={{0,8},{8,0},{16,24},{24,16},{1,9},{9,1},{17,25},{25,17},{2,10},{10... | collective-permute-start | bytes 1867784 | tf_op jit(solution)/shard_map/swap_g2_u2/ppermute | solution.py:78
  194.2 34.1 %collective-permute-start.52 = (bf16[1904,128]{1,0:T(8,128)(2,1)S(1)}, bf16[1904,128]{1,0:T(8,128)(2,1)S(1)}, u32[]{:S(2)}, u32[]{:S(2)}) collective-permute-start(bf16[1904,128]{1,0:T(8,128)(2,1)S(1)} %get-tuple-element.277), channel_id=1, source_target_pairs={{0,6},{2,4},{4,2},{6,0},{1,7},{3,5},{5,3},{7,1},{8,14},{10,12},{12... | collective-permute-start | bytes 1462280 | tf_op jit(solution)/shard_map/shares/ppermute | solution.py:37
  195.6 32.9 %collective-permute-start.49 = (bf16[1824,128]{1,0:T(8,128)(2,1)S(1)}, bf16[1824,128]{1,0:T(8,128)(2,1)S(1)}, u32[]{:S(2)}, u32[]{:S(2)}) collective-permute-start(bf16[1824,128]{1,0:T(8,128)(2,1)S(1)} %get-tuple-element.274.refs_4_), channel_id=1, source_target_pairs={{8,16},{16,8},{9,17},{17,9},{10,18},{18,10},{11,19},{19,11},{12,20... | collective-permute-start | bytes 1400840 | tf_op jit(solution)/shard_map/cross_u1/ppermute | solution.py:83
  229.9 23.3 %collective-permute-start.58 = (bf16[3344,128]{1,0:T(8,128)(2,1)S(1)}, bf16[3344,128]{1,0:T(8,128)(2,1)S(1)}, u32[]{:S(2)}, u32[]{:S(2)}) collective-permute-start(bf16[3344,128]{1,0:T(8,128)(2,1)S(1)} %get-tuple-element.284), channel_id=1, source_target_pairs={{0,4},{2,6},{4,0},{6,2},{1,5},{3,7},{5,1},{7,3},{8,12},{10,14},{12... | collective-permute-start | bytes 2568200 | tf_op jit(solution)/shard_map/g2_y/ppermute | solution.py:37
  230.8 22.4 %collective-permute-start.59 = (bf16[3344,128]{1,0:T(8,128)(2,1)S(1)}, bf16[3344,128]{1,0:T(8,128)(2,1)S(1)}, u32[]{:S(2)}, u32[]{:S(2)}) collective-permute-start(bf16[3344,128]{1,0:T(8,128)(2,1)S(1)} %get-tuple-element.285), channel_id=1, source_target_pairs={{0,2},{2,0},{4,6},{6,4},{1,3},{3,1},{5,7},{7,5},{8,10},{10,8},{12,... | collective-permute-start | bytes 2568200 | tf_op jit(solution)/shard_map/g2_x/ppermute | solution.py:37
  232.0 21.2 %collective-permute-start.56 = (bf16[2432,128]{1,0:T(8,128)(2,1)S(1)}, bf16[2432,128]{1,0:T(8,128)(2,1)S(1)}, u32[]{:S(2)}, u32[]{:S(2)}) collective-permute-start(bf16[2432,128]{1,0:T(8,128)(2,1)S(1)} %get-tuple-element.282.refs_3_), channel_id=1, source_target_pairs={{8,16},{16,8},{9,17},{17,9},{10,18},{18,10},{11,19},{19,11},{12,20... | collective-permute-start | bytes 1867784 | tf_op jit(solution)/shard_map/cross_u2/ppermute | solution.py:83
  232.7 20.5 %collective-permute-start.57 = (bf16[1904,128]{1,0:T(8,128)(2,1)S(1)}, bf16[1904,128]{1,0:T(8,128)(2,1)S(1)}, u32[]{:S(2)}, u32[]{:S(2)}) collective-permute-start(bf16[1904,128]{1,0:T(8,128)(2,1)S(1)} %get-tuple-element.283.refs_5_), channel_id=1, source_target_pairs={{0,8},{8,0},{16,24},{24,16},{1,9},{9,1},{17,25},{25,17},{2,10},{10... | collective-permute-start | bytes 1462280 | tf_op jit(solution)/shard_map/swap_share/ppermute | solution.py:78
  236.5 16.7 %collective-permute-start.55 = (bf16[1824,128]{1,0:T(8,128)(2,1)S(1)}, bf16[1824,128]{1,0:T(8,128)(2,1)S(1)}, u32[]{:S(2)}, u32[]{:S(2)}) collective-permute-start(bf16[1824,128]{1,0:T(8,128)(2,1)S(1)} %get-tuple-element.281.refs_2_), channel_id=1, source_target_pairs={{0,8},{8,0},{16,24},{24,16},{1,9},{9,1},{17,25},{25,17},{2,10},{10... | collective-permute-start | bytes 1400840 | tf_op jit(solution)/shard_map/swap_u1/ppermute | solution.py:78
  254.5 21.9 %collective-permute-start.62 = (bf16[3040,128]{1,0:T(8,128)(2,1)S(1)}, bf16[3040,128]{1,0:T(8,128)(2,1)S(1)}, u32[]{:S(2)}, u32[]{:S(2)}) collective-permute-start(bf16[3040,128]{1,0:T(8,128)(2,1)S(1)} %get-tuple-element.290), channel_id=1, source_target_pairs={{0,4},{2,6},{4,0},{6,2},{1,5},{3,7},{5,1},{7,3},{8,12},{10,14},{12... | collective-permute-start | bytes 2334728 | tf_op jit(solution)/shard_map/u1_y/ppermute | solution.py:37
  255.3 21.1 %collective-permute-start.63 = (bf16[3040,128]{1,0:T(8,128)(2,1)S(1)}, bf16[3040,128]{1,0:T(8,128)(2,1)S(1)}, u32[]{:S(2)}, u32[]{:S(2)}) collective-permute-start(bf16[3040,128]{1,0:T(8,128)(2,1)S(1)} %get-tuple-element.291), channel_id=1, source_target_pairs={{0,2},{2,0},{4,6},{6,4},{1,3},{3,1},{5,7},{7,5},{8,10},{10,8},{12,... | collective-permute-start | bytes 2334728 | tf_op jit(solution)/shard_map/u1_x/ppermute | solution.py:37
  255.9 20.4 %collective-permute-start.60 = (bf16[2432,128]{1,0:T(8,128)(2,1)S(1)}, bf16[2432,128]{1,0:T(8,128)(2,1)S(1)}, u32[]{:S(2)}, u32[]{:S(2)}) collective-permute-start(bf16[2432,128]{1,0:T(8,128)(2,1)S(1)} %get-tuple-element.288.refs_2_), channel_id=1, source_target_pairs={{0,8},{8,0},{16,24},{24,16},{1,9},{9,1},{17,25},{25,17},{2,10},{10... | collective-permute-start | bytes 1867784 | tf_op jit(solution)/shard_map/swap_u2/ppermute | solution.py:78
  258.0 17.6 %collective-permute-start.61 = (bf16[1904,128]{1,0:T(8,128)(2,1)S(1)}, bf16[1904,128]{1,0:T(8,128)(2,1)S(1)}, u32[]{:S(2)}, u32[]{:S(2)}) collective-permute-start(bf16[1904,128]{1,0:T(8,128)(2,1)S(1)} %get-tuple-element.289.refs_3_), channel_id=1, source_target_pairs={{0,16},{8,24},{16,0},{24,8},{1,17},{9,25},{17,1},{25,9},{2,18},{10... | collective-permute-start | bytes 1462280 | tf_op jit(solution)/shard_map/share_far/ppermute | solution.py:37
  277.4 29.8 %collective-permute-start.64 = (bf16[5248,128]{1,0:T(8,128)(2,1)S(1)}, bf16[5248,128]{1,0:T(8,128)(2,1)S(1)}, u32[]{:S(2)}, u32[]{:S(2)}) collective-permute-start(bf16[5248,128]{1,0:T(8,128)(2,1)S(1)} %get-tuple-element.295), channel_id=1, source_target_pairs={{0,2},{2,0},{4,6},{6,4},{1,3},{3,1},{5,7},{7,5},{8,10},{10,8},{12,... | collective-permute-start | bytes 4030472 | tf_op jit(solution)/shard_map/u2_x/ppermute | solution.py:37
  278.0 29.3 %collective-permute-start.65 = (bf16[5248,128]{1,0:T(8,128)(2,1)S(1)}, bf16[5248,128]{1,0:T(8,128)(2,1)S(1)}, u32[]{:S(2)}, u32[]{:S(2)}) collective-permute-start(bf16[5248,128]{1,0:T(8,128)(2,1)S(1)} %get-tuple-element.296), channel_id=1, source_target_pairs={{0,4},{2,6},{4,0},{6,2},{1,5},{3,7},{5,1},{7,3},{8,12},{10,14},{12... | collective-permute-start | bytes 4030472 | tf_op jit(solution)/shard_map/u2_y/ppermute | solution.py:37
  307.9 9.7 %collective-permute-start.67 = (bf16[960,128]{1,0:T(8,128)(2,1)S(1)}, bf16[960,128]{1,0:T(8,128)(2,1)S(1)}, u32[]{:S(2)}, u32[]{:S(2)}) collective-permute-start(bf16[960,128]{1,0:T(8,128)(2,1)S(1)} %get-tuple-element.299.refs_8_), channel_id=1, source_target_pairs={{0,2},{2,0},{4,6},{6,4},{1,3},{3,1},{5,7},{7,5},{8,10},{10,8},{12,... | collective-permute-start | bytes 737288 | tf_op jit(solution)/shard_map/far_share_x/ppermute | solution.py:37
  309.6 8.0 %collective-permute-start.66 = (bf16[944,128]{1,0:T(8,128)(2,1)S(1)}, bf16[944,128]{1,0:T(8,128)(2,1)S(1)}, u32[]{:S(2)}, u32[]{:S(2)}) collective-permute-start(bf16[944,128]{1,0:T(8,128)(2,1)S(1)} %get-tuple-element.298), channel_id=1, source_target_pairs={{0,4},{2,6},{4,0},{6,2},{1,5},{3,7},{5,1},{7,3},{8,12},{10,14},{12... | collective-permute-start | bytes 725000 | tf_op jit(solution)/shard_map/far_share_y/ppermute | solution.py:37
  310.4 11.8 %collective-permute-start.69 = (bf16[1216,128]{1,0:T(8,128)(2,1)S(1)}, bf16[1216,128]{1,0:T(8,128)(2,1)S(1)}, u32[]{:S(2)}, u32[]{:S(2)}) collective-permute-start(bf16[1216,128]{1,0:T(8,128)(2,1)S(1)} %get-tuple-element.307), channel_id=1, source_target_pairs={{0,4},{2,6},{4,0},{6,2},{1,5},{3,7},{5,1},{7,3},{8,12},{10,14},{12... | collective-permute-start | bytes 933896 | tf_op jit(solution)/shard_map/far_u2_y/ppermute | solution.py:37
  311.7 10.5 %collective-permute-start.70 = (bf16[1216,128]{1,0:T(8,128)(2,1)S(1)}, bf16[1216,128]{1,0:T(8,128)(2,1)S(1)}, u32[]{:S(2)}, u32[]{:S(2)}) collective-permute-start(bf16[1216,128]{1,0:T(8,128)(2,1)S(1)} %get-tuple-element.308), channel_id=1, source_target_pairs={{0,2},{2,0},{4,6},{6,4},{1,3},{3,1},{5,7},{7,5},{8,10},{10,8},{12,... | collective-permute-start | bytes 933896 | tf_op jit(solution)/shard_map/far_u2_x/ppermute | solution.py:37
  (84 other events, 433.2 us)

commit v6 on v5

--- a/solution.py
+++ b/solution.py
@@ -16,7 +16,7 @@
 
 low = jnp.bfloat16
 wide = jnp.float32
-vmem_limit = 40 * 1024 * 1024
+vmem_limit = 34 * 1024 * 1024
 
 
 def dot_nn(left, right):

time: 332 us -> 327 us (0.985)
  waiting for transfers between devices: 136 us -> 124 us
  starting transfers between devices: 74.4 us -> 85 us
  local copies, waits for them, and re-layouts: 21.6 us -> 17.6 us
    ppermute x56, waiting for transfers between devices: 117 us -> 105 us  [partner(): return lax.ppermute(value, axis, [(i, i ^ step) for i in range(count)])]
    ppermute x56, starting transfers between devices: 52.2 us -> 62.9 us  [partner(): return lax.ppermute(value, axis, [(i, i ^ step) for i in range(count)])]
    unnamed x154 -> x90, local copies, waits for them, and re-layouts: 16.9 us -> 13 us
  transfers between devices with their start and end apart: 71 -> 71, of which waited for: 27 -> 25; matrix products, arithmetic and copies ran while one was open for 1% -> 1% of each run, Pallas kernels for 22% -> 22%
where the time goes in v6:
time: 327 us; the launch traced here: 322 us
  waiting for transfers between devices  124 us (38%)
  Pallas kernels  92.2 us (28%)
  starting transfers between devices  85 us (26%)
  local copies, waits for them, and re-layouts  17.6 us (5%)
    ppermute x56, waiting for transfers between devices, partner(): return lax.ppermute(value, axis, [(i, i ^ step) for i in range(count)])  105 us
    pallas_call x38, Pallas kernels, call(): pl.pallas_call(run, name=getattr(body, 'func', body).__name__, out_shape=...  72.2 us
    ppermute x56, starting transfers between devices, partner(): return lax.ppermute(value, axis, [(i, i ^ step) for i in range(count)])  62.9 us
    pallas_call x4, Pallas kernels, place_shares(): pl.pallas_call(body, name='place_kernel', out_shape=(shape(dims, wide), s...  20 us
    ppermute x9, waiting for transfers between devices, swap(): return lax.ppermute(value, 'dp', [(0, 1), (1, 0), (2, 3), (3, 2)])  19.2 us
    ppermute x9, starting transfers between devices, swap(): return lax.ppermute(value, 'dp', [(0, 1), (1, 0), (2, 3), (3, 2)])  17.4 us
    unnamed x90, local copies, waits for them, and re-layouts  13 us
  transfers between devices with their start and end apart: 71, of which 25 were waited for; matrix products, arithmetic and copies ran while one was open for 1% of the time, Pallas kernels for 22%

profile of v6, /device:TPU:0, one launch (start us, length us, event | category | flops | bytes accessed | tf_op | source)
XLA Modules:
  0.0 321.6 jit_solution(11172667818234096713)
XLA Ops:
  0.7 2.8 concatenate.3
  8.3 3.6 %enter_kernel.1 = (bf16[448,512]{1,0:T(8,128)(2,1)S(1)}, bf16[512,128]{1,0:T(8,128)(2,1)S(1)}, bf16[896,512]{1,0:T(8,128)(2,1)S(1)}, bf16[896,512]{1,0:T(8,128)(...) custom-call(s32[1,3]{1,0:T(1,128)S(1)} %copy-done.41, s32[3]{0:T(128)S(1)} %pad_add_fusion.refs_1_.refs_0_, ...), custom_call_target="tpu_custom_call" | custom-call | tf_op jit(solution)/shard_map/enter_kernel/pallas_call | solution.py:96
  12.0 3.9 %collective-permute-start.4 = (bf16[512,128]{1,0:T(8,128)(2,1)S(1)}, bf16[512,128]{1,0:T(8,128)(2,1)S(1)}, u32[]{:S(2)}, u32[]{:S(2)}) collective-permute-start(bf16[512,128]{1,0:T(8,128)(2,1)S(1)} %get-tuple-element.167.refs_4_.refs_8_), channel_id=1, source_target_pairs={{0,6},{2,4},{4,2},{6,0},{1,7},{3,5},{5,3},{7,1},{8,14},{10,12},{12... | collective-permute-start | bytes 393224 | tf_op jit(solution)/shard_map/kv/ppermute | solution.py:37
  16.6 2.2 copy-done.1
  18.8 2.2 copy-done.2
  21.1 3.6 %weights_kernel.1 = (bf16[608,896]{1,0:T(8,128)(2,1)S(1)}, bf16[896,608]{1,0:T(8,128)(2,1)S(1)}, bf16[608,896]{1,0:T(8,128)(2,1)S(1)}, bf16[896,608]{1,0:T(8,128...) custom-call(s32[1,3]{1,0:T(1,128)S(1)} %copy-done.41, ...), custom_call_target="tpu_custom_call" | custom-call | tf_op jit(solution)/shard_map/weights_kernel/pallas_call | solution.py:96
  24.7 2.0 collective-permute-start.6
  26.6 1.5 collective-permute-start
  28.2 4.5 %attend_kernel.1 = (f32[448,512]{1,0:T(8,128)S(1)}, f32[8,512]{1,0:T(8,128)S(1)}, f32[896,256]{1,0:T(8,128)S(1)}, bf16[896,256]{1,0:T(8,128)(2,1)S(1)}) custom-call(s32[1,3]{1,0:T(1,128)S(1)} %copy-done.41, s32[3]{0:T(128)S(1)} %pad_add_fusion.refs_1_.refs_0_, bf16[448,512]{1,0:T(8,128)(2,1)S(1)} %get-tuple-element.163.refs_6_.refs_2_.refs_5_, ...), custom_call_target="tpu_custom_call" | custom-call | tf_op jit(solution)/shard_map/attend_kernel/pallas_call | solution.py:96
  32.9 3.6 %collective-permute-done.6.refs_5_.refs_1_.refs_7_ = bf16[256,896]{1,0:T(8,128)(2,1)S(1)} collective-permute-done((bf16[256,896]{1,0:T(8,128)(2,1)S(1)}, bf16[256,896]{1,0:T(8,128)(2,1)S(1)}, u32[]{:S(2)}, u32[]{:S(2)}) %collective-permute-start.6) | collective-permute-done | bytes 458784 | tf_op jit(solution)/shard_map/gy/ppermute | solution.py:37
  38.9 2.7 collective-permute-start.9
  41.6 2.7 collective-permute-start.8
  44.8 3.9 %hidden_kernel.4 = (bf16[608,512]{1,0:T(8,128)(2,1)S(1)}, bf16[608,512]{1,0:T(8,128)(2,1)S(1)}, bf16[608,512]{1,0:T(8,128)(2,1)S(1)}, bf16[896,256]{1,0:T(8,128)(2,1)S(1)}, bf16[896,256]{1,0:T(8,128)(2,1)S(1)}) custom-call(bf16[256,896]{1,0:T(8,128)(2,1)S(1)} %get-tuple-element.165.refs_0_.refs_4_, ...), custom_call_target="tpu_custom_call" | custom-call | tf_op jit(solution)/shard_map/hidden_kernel/pallas_call | solution.py:96
  48.8 3.9 %collective-permute-done.9.refs_3_ = bf16[896,256]{1,0:T(8,128)(2,1)S(1)} collective-permute-done((bf16[896,256]{1,0:T(8,128)(2,1)S(1)}, bf16[896,256]{1,0:T(8,128)(2,1)S(1)}, u32[]{:S(2)}, u32[]{:S(2)}) %collective-permute-start.9) | collective-permute-done | bytes 458784 | tf_op jit(solution)/shard_map/x/ppermute | solution.py:37
  52.6 2.4 collective-permute-done.8.refs_2_
  56.1 1.8 collective-permute-start.16
  57.9 1.7 collective-permute-start.13
  59.9 3.9 %hidden_kernel.5 = (bf16[608,512]{1,0:T(8,128)(2,1)S(1)}, bf16[608,512]{1,0:T(8,128)(2,1)S(1)}, bf16[608,512]{1,0:T(8,128)(2,1)S(1)}, bf16[896,256]{1,0:T(8,128)(2,1)S(1)}, bf16[896,256]{1,0:T(8,128)(2,1)S(1)}) custom-call(bf16[256,896]{1,0:T(8,128)(2,1)S(1)} %collective-permute-done.11.refs_0_.refs_6_, ...), custom_call_target="tpu_custom_call" | custom-call | tf_op jit(solution)/shard_map/hidden_kernel/pallas_call | solution.py:96
  64.6 3.9 %hidden_kernel.6 = (bf16[608,512]{1,0:T(8,128)(2,1)S(1)}, bf16[608,512]{1,0:T(8,128)(2,1)S(1)}, bf16[608,512]{1,0:T(8,128)(2,1)S(1)}, bf16[896,256]{1,0:T(8,128)(2,1)S(1)}, bf16[896,256]{1,0:T(8,128)(2,1)S(1)}) custom-call(bf16[256,896]{1,0:T(8,128)(2,1)S(1)} %collective-permute-done.1.refs_0_.refs_8_, ...), custom_call_target="tpu_custom_call" | custom-call | tf_op jit(solution)/shard_map/hidden_kernel/pallas_call | solution.py:96
  72.5 4.0 %hidden_kernel.7 = (bf16[608,512]{1,0:T(8,128)(2,1)S(1)}, bf16[608,512]{1,0:T(8,128)(2,1)S(1)}, bf16[608,512]{1,0:T(8,128)(2,1)S(1)}, bf16[896,256]{1,0:T(8,128)(2,1)S(1)}, bf16[896,256]{1,0:T(8,128)(2,1)S(1)}) custom-call(bf16[128,896]{1,0:T(8,128)(2,1)S(1)} %collective-permute-done.17.refs_0_.refs_10_, ...), custom_call_target="tpu_custom_call" | custom-call | tf_op jit(solution)/shard_map/hidden_kernel/pallas_call | solution.py:96
  76.7 1.5 weight_kernel.4.refs_14_.refs_1_
  78.3 2.1 collective-permute-start.27
  82.2 1.7 collective-permute-start.25
  85.4 3.0 project_kernel.1
  88.5 4.8 %collective-permute-done.26.refs_5_.refs_8_ = bf16[896,256]{1,0:T(8,128)(2,1)S(1)} collective-permute-done((bf16[896,256]{1,0:T(8,128)(2,1)S(1)}, bf16[896,256]{1,0:T(8,128)(2,1)S(1)}, u32[]{:S(2)}, u32[]{:S(2)}) %collective-permute-start.26) | collective-permute-done | bytes 458784 | tf_op jit(solution)/shard_map/back/ppermute | solution.py:37
  96.4 1.9 collective-permute-start.29
  98.4 2.8 weight_kernel.6
  101.2 2.8 weight_kernel.7
  104.0 6.0 %collective-permute-done.29.refs_9_.refs_6_ = bf16[896,256]{1,0:T(8,128)(2,1)S(1)} collective-permute-done((bf16[896,256]{1,0:T(8,128)(2,1)S(1)}, bf16[896,256]{1,0:T(8,128)(2,1)S(1)}, u32[]{:S(2)}, u32[]{:S(2)}) %collective-permute-start.29) | collective-permute-done | bytes 458784 | tf_op jit(solution)/shard_map/back/ppermute | solution.py:37
  115.0 4.8 %collective-permute-start.32 = (bf16[1824,128]{1,0:T(8,128)(2,1)S(1)}, bf16[1824,128]{1,0:T(8,128)(2,1)S(1)}, u32[]{:S(2)}, u32[]{:S(2)}) collective-permute-start(bf16[1824,128]{1,0:T(8,128)(2,1)S(1)} %get-tuple-element.226), channel_id=1, source_target_pairs={{0,8},{8,0},{16,24},{24,16},{1,9},{9,1},{17,25},{25,17},{2,10},{10... | collective-permute-start | bytes 1400840 | tf_op jit(solution)/shard_map/swap_d1_g1/ppermute | solution.py:78
  119.8 1.7 collective-permute-start.35
  124.7 5.9 %attend_back_kernel.1 = (bf16[448,512]{1,0:T(8,128)(2,1)S(1)}, bf16[512,128]{1,0:T(8,128)(2,1)S(1)}, bf16[512,128]{1,0:T(8,128)(2,1)S(1)}, bf16[512,128]{1,0:T(8,128)(2,1)S(1)}, bf16[512,128]{1,0:T(8,128)(2,1)S(1)}) custom-call(s32[1,3]{1,0:T(1,128)S(1)} %copy-done.42, s32[3]{0:T(128)S(1)} %pad_add_fusion.refs_1_.refs_0_, ...), custom_call_target="tpu_custom_call" | custom-call | tf_op jit(solution)/shard_map/attend_back_kernel/pallas_call | solution.py:96
  130.6 2.7 collective-permute-done.35.refs_10_.refs_2_
  133.2 10.1 %collective-permute-done.36.refs_11_.refs_3_ = bf16[896,256]{1,0:T(8,128)(2,1)S(1)} collective-permute-done((bf16[896,256]{1,0:T(8,128)(2,1)S(1)}, bf16[896,256]{1,0:T(8,128)(2,1)S(1)}, u32[]{:S(2)}, u32[]{:S(2)}) %collective-permute-start.36) | collective-permute-done | bytes 458784 | tf_op jit(solution)/shard_map/layer/ppermute | solution.py:37
  145.9 3.5 %collective-permute-start.41 = (bf16[2336,128]{1,0:T(8,128)(2,1)S(1)}, bf16[2336,128]{1,0:T(8,128)(2,1)S(1)}, u32[]{:S(2)}, u32[]{:S(2)}) collective-permute-start(bf16[2336,128]{1,0:T(8,128)(2,1)S(1)} %get-tuple-element.248), channel_id=1, source_target_pairs={{0,2},{2,0},{4,6},{6,4},{1,3},{3,1},{5,7},{7,5},{8,10},{10,8},{12,... | collective-permute-start | bytes 1794056 | tf_op jit(solution)/shard_map/d1_x/ppermute | solution.py:37
  150.2 2.3 query_kernel.1
  152.9 11.5 %collective-permute-done.42.refs_11_.refs_15_ = bf16[512,128]{1,0:T(8,128)(2,1)S(1)} collective-permute-done((bf16[512,128]{1,0:T(8,128)(2,1)S(1)}, bf16[512,128]{1,0:T(8,128)(2,1)S(1)}, u32[]{:S(2)}, u32[]{:S(2)}) %collective-permute-start.42) | collective-permute-done | bytes 131104 | tf_op jit(solution)/shard_map/grad_kv/ppermute | solution.py:37
  164.4 1.5 tick_kernel.12
  165.9 1.7 collective-permute-start.46
  167.6 1.7 collective-permute-start.47
  170.1 4.5 %collective-permute-start.44 = (bf16[1824,128]{1,0:T(8,128)(2,1)S(1)}, bf16[1824,128]{1,0:T(8,128)(2,1)S(1)}, u32[]{:S(2)}, u32[]{:S(2)}) collective-permute-start(bf16[1824,128]{1,0:T(8,128)(2,1)S(1)} %get-tuple-element.254), channel_id=1, source_target_pairs={{0,8},{8,0},{16,24},{24,16},{1,9},{9,1},{17,25},{25,17},{2,10},{10... | collective-permute-start | bytes 1400840 | tf_op jit(solution)/shard_map/swap_g1_u1/ppermute | solution.py:78
  174.6 2.2 key_kernel.1
  176.8 5.0 %collective-permute-done.44.refs_1_ = bf16[1824,128]{1,0:T(8,128)(2,1)S(1)} collective-permute-done((bf16[1824,128]{1,0:T(8,128)(2,1)S(1)}, bf16[1824,128]{1,0:T(8,128)(2,1)S(1)}, u32[]{:S(2)}, u32[]{:S(2)}) %collective-permute-start.44) | collective-permute-done | bytes 466976 | tf_op jit(solution)/shard_map/swap_g1_u1/ppermute | solution.py:78
  181.8 3.1 collective-permute-done.46.refs_7_.refs_13_.refs_4_.refs_5_.refs_10_
  186.0 1.5 tick_kernel.13
  194.0 1.5 join_kernel.2.refs_6_
  198.0 27.5 %collective-permute-done.52.refs_3_ = bf16[1904,128]{1,0:T(8,128)(2,1)S(1)} collective-permute-done((bf16[1904,128]{1,0:T(8,128)(2,1)S(1)}, bf16[1904,128]{1,0:T(8,128)(2,1)S(1)}, u32[]{:S(2)}, u32[]{:S(2)}) %collective-permute-start.52) | collective-permute-done | bytes 487456 | tf_op jit(solution)/shard_map/shares/ppermute | solution.py:37
  230.0 3.9 %collective-permute-start.57 = (bf16[1904,128]{1,0:T(8,128)(2,1)S(1)}, bf16[1904,128]{1,0:T(8,128)(2,1)S(1)}, u32[]{:S(2)}, u32[]{:S(2)}) collective-permute-start(bf16[1904,128]{1,0:T(8,128)(2,1)S(1)} %get-tuple-element.283.refs_5_), channel_id=1, source_target_pairs={{0,8},{8,0},{16,24},{24,16},{1,9},{9,1},{17,25},{25,17},{2,10},{10... | collective-permute-start | bytes 1462280 | tf_op jit(solution)/shard_map/swap_share/ppermute | solution.py:78
  234.0 5.3 %place_kernel.4 = (f32[2432,896]{1,0:T(8,128)}, f32[8,128]{1,0:T(8,128)S(1)}) custom-call(s32[3]{0:T(128)S(1)} %pad_add_fusion.refs_1_.refs_0_, bf16[1824,128]{1,0:T(8,128)(2,1)S(1)} %get-tuple-element.251.refs_7_.refs_1_, bf16[2336,128]{1,0:T(8,128)(2,1)S(1)} %collective-permute-done.41.refs_8_.refs_9_.refs_13_.refs_2_, ...), custom_call_target="tpu_custom_call" | custom-call | tf_op jit(solution)/shard_map/place_kernel/pallas_call | solution.py:684
  239.3 11.1 %collective-permute-done.55.refs_1_ = bf16[1824,128]{1,0:T(8,128)(2,1)S(1)} collective-permute-done((bf16[1824,128]{1,0:T(8,128)(2,1)S(1)}, bf16[1824,128]{1,0:T(8,128)(2,1)S(1)}, u32[]{:S(2)}, u32[]{:S(2)}) %collective-permute-start.55) | collective-permute-done | bytes 466976 | tf_op jit(solution)/shard_map/swap_u1/ppermute | solution.py:78
  251.8 7.2 %collective-permute-start.63 = (bf16[3040,128]{1,0:T(8,128)(2,1)S(1)}, bf16[3040,128]{1,0:T(8,128)(2,1)S(1)}, u32[]{:S(2)}, u32[]{:S(2)}) collective-permute-start(bf16[3040,128]{1,0:T(8,128)(2,1)S(1)} %get-tuple-element.291), channel_id=1, source_target_pairs={{0,2},{2,0},{4,6},{6,4},{1,3},{3,1},{5,7},{7,5},{8,10},{10,8},{12,... | collective-permute-start | bytes 2334728 | tf_op jit(solution)/shard_map/u1_x/ppermute | solution.py:37
  258.9 1.9 collective-permute-start.61
  260.9 11.6 %collective-permute-done.61.refs_4_ = bf16[1904,128]{1,0:T(8,128)(2,1)S(1)} collective-permute-done((bf16[1904,128]{1,0:T(8,128)(2,1)S(1)}, bf16[1904,128]{1,0:T(8,128)(2,1)S(1)}, u32[]{:S(2)}, u32[]{:S(2)}) %collective-permute-start.61) | collective-permute-done | bytes 487456 | tf_op jit(solution)/shard_map/share_far/ppermute | solution.py:37
  272.4 2.0 collective-permute-done.60.refs_1_
  275.8 3.7 %collective-permute-start.65 = (bf16[5248,128]{1,0:T(8,128)(2,1)S(1)}, bf16[5248,128]{1,0:T(8,128)(2,1)S(1)}, u32[]{:S(2)}, u32[]{:S(2)}) collective-permute-start(bf16[5248,128]{1,0:T(8,128)(2,1)S(1)} %get-tuple-element.296), channel_id=1, source_target_pairs={{0,4},{2,6},{4,0},{6,2},{1,5},{3,7},{5,1},{7,3},{8,12},{10,14},{12... | collective-permute-start | bytes 4030472 | tf_op jit(solution)/shard_map/u2_y/ppermute | solution.py:37
  279.6 1.7 collective-permute-done.54
  281.4 1.9 join_kernel.3.refs_15_
  284.8 6.9 %place_kernel.5 = (f32[896,2432]{1,0:T(8,128)}, f32[8,128]{1,0:T(8,128)S(1)}) custom-call(s32[3]{0:T(128)S(1)} %pad_add_fusion.refs_1_.refs_0_, bf16[1824,128]{1,0:T(8,128)(2,1)S(1)} %get-tuple-element.271.refs_3_.refs_1_, bf16[4944,128]{1,0:T(8,128)(2,1)S(1)} %collective-permute-done.51.refs_1_.refs_7_.refs_13_.refs_14_.refs_2_, ...), custom_call_target="tpu_custom_call" | custom-call | tf_op jit(solution)/shard_map/place_kernel/pallas_call | solution.py:684
  291.6 9.7 %collective-permute-done.64.refs_2_.refs_6_.refs_7_ = bf16[5248,128]{1,0:T(8,128)(2,1)S(1)} collective-permute-done((bf16[5248,128]{1,0:T(8,128)(2,1)S(1)}, bf16[5248,128]{1,0:T(8,128)(2,1)S(1)}, u32[]{:S(2)}, u32[]{:S(2)}) %collective-permute-start.64) | collective-permute-done | bytes 1343520 | tf_op jit(solution)/shard_map/u2_x/ppermute | solution.py:37
  302.0 2.5 collective-permute-start.67
  304.5 3.7 %collective-permute-start.66 = (bf16[944,128]{1,0:T(8,128)(2,1)S(1)}, bf16[944,128]{1,0:T(8,128)(2,1)S(1)}, u32[]{:S(2)}, u32[]{:S(2)}) collective-permute-start(bf16[944,128]{1,0:T(8,128)(2,1)S(1)} %get-tuple-element.298), channel_id=1, source_target_pairs={{0,4},{2,6},{4,0},{6,2},{1,5},{3,7},{5,1},{7,3},{8,12},{10,14},{12... | collective-permute-start | bytes 725000 | tf_op jit(solution)/shard_map/far_share_y/ppermute | solution.py:37
  308.4 3.7 %place_kernel.6 = (f32[896,2432]{1,0:T(8,128)}, f32[8,128]{1,0:T(8,128)S(1)}) custom-call(s32[3]{0:T(128)S(1)} %pad_add_fusion.refs_1_.refs_0_, bf16[1824,128]{1,0:T(8,128)(2,1)S(1)} %get-tuple-element.292.refs_7_.refs_1_, bf16[3040,128]{1,0:T(8,128)(2,1)S(1)} %collective-permute-done.63.refs_6_.refs_8_.refs_13_.refs_14_.refs_2_, ...), custom_call_target="tpu_custom_call" | custom-call | tf_op jit(solution)/shard_map/place_kernel/pallas_call | solution.py:684
  312.4 2.7 unpack_kernel.1
  316.9 4.2 %place_kernel.7 = (f32[896,2432]{1,0:T(8,128)}, f32[8,128]{1,0:T(8,128)}) custom-call(s32[3]{0:T(128)S(1)} %pad_add_fusion.refs_1_.refs_0_, bf16[2432,128]{1,0:T(8,128)(2,1)S(1)} %get-tuple-element.293.refs_3_.refs_1_, bf16[5248,128]{1,0:T(8,128)(2,1)S(1)} %collective-permute-done.64.refs_2_.refs_6_.refs_7_, ...), custom_call_target="tpu_custom_call", output_to_operand_aliasing={{0}: (9, {})} | custom-call | tf_op jit(solution)/shard_map/place_kernel/pallas_call | solution.py:684
  (227 shorter events, 55.3 us)
Async XLA Ops:
  12.0 16.2 %collective-permute-start.4 = (bf16[512,128]{1,0:T(8,128)(2,1)S(1)}, bf16[512,128]{1,0:T(8,128)(2,1)S(1)}, u32[]{:S(2)}, u32[]{:S(2)}) collective-permute-start(bf16[512,128]{1,0:T(8,128)(2,1)S(1)} %get-tuple-element.167.refs_4_.refs_8_), channel_id=1, source_target_pairs={{0,6},{2,4},{4,2},{6,0},{1,7},{3,5},{5,3},{7,1},{8,14},{10,12},{12... | collective-permute-start | bytes 393224 | tf_op jit(solution)/shard_map/kv/ppermute | solution.py:37
  15.9 12.2 %collective-permute-start.3 = (bf16[512,128]{1,0:T(8,128)(2,1)S(1)}, bf16[512,128]{1,0:T(8,128)(2,1)S(1)}, u32[]{:S(2)}, u32[]{:S(2)}) collective-permute-start(bf16[512,128]{1,0:T(8,128)(2,1)S(1)} %get-tuple-element.167.refs_4_.refs_8_), channel_id=1, source_target_pairs={{0,4},{2,6},{4,0},{6,2},{1,5},{3,7},{5,1},{7,3},{8,12},{10,14},{12... | collective-permute-start | bytes 393224 | tf_op jit(solution)/shard_map/kv/ppermute | solution.py:37
  16.4 11.8 %collective-permute-start.2 = (bf16[512,128]{1,0:T(8,128)(2,1)S(1)}, bf16[512,128]{1,0:T(8,128)(2,1)S(1)}, u32[]{:S(2)}, u32[]{:S(2)}) collective-permute-start(bf16[512,128]{1,0:T(8,128)(2,1)S(1)} %get-tuple-element.167.refs_4_.refs_8_), channel_id=1, source_target_pairs={{0,2},{2,0},{4,6},{6,4},{1,3},{3,1},{5,7},{7,5},{8,10},{10,8},{12,... | collective-permute-start | bytes 393224 | tf_op jit(solution)/shard_map/kv/ppermute | solution.py:37
  24.7 11.8 %collective-permute-start.6 = (bf16[256,896]{1,0:T(8,128)(2,1)S(1)}, bf16[256,896]{1,0:T(8,128)(2,1)S(1)}, u32[]{:S(2)}, u32[]{:S(2)}) collective-permute-start(bf16[256,896]{1,0:T(8,128)(2,1)S(1)} %get-tuple-element.164.refs_1_.refs_5_.refs_2_), channel_id=1, source_target_pairs={{0,2},{2,0},{4,6},{6,4},{1,3},{3,1},{5,7},{7,5},{8,10},{10,8},{12,... | collective-permute-start | bytes 1376264 | tf_op jit(solution)/shard_map/gy/ppermute | solution.py:37
  26.6 11.1 %collective-permute-start = (bf16[256,896]{1,0:T(8,128)(2,1)S(1)}, bf16[256,896]{1,0:T(8,128)(2,1)S(1)}, u32[]{:S(2)}, u32[]{:S(2)}) collective-permute-start(bf16[256,896]{1,0:T(8,128)(2,1)S(1)} %get-tuple-element.164.refs_1_.refs_5_.refs_2_), channel_id=1, source_target_pairs={{0,4},{2,6},{4,0},{6,2},{1,5},{3,7},{5,1},{7,3},{8,12},{10,14},{12... | collective-permute-start | bytes 1376264 | tf_op jit(solution)/shard_map/gy/ppermute | solution.py:37
  32.8 5.0 %collective-permute-start.5 = (bf16[896,256]{1,0:T(8,128)(2,1)S(1)}, bf16[896,256]{1,0:T(8,128)(2,1)S(1)}, u32[]{:S(2)}, u32[]{:S(2)}) collective-permute-start(bf16[896,256]{1,0:T(8,128)(2,1)S(1)} %get-tuple-element.170), channel_id=1, source_target_pairs={{0,1},{1,0},{2,3},{3,2},{4,5},{5,4},{6,7},{7,6},{8,9},{9,8},{10,11... | collective-permute-start | bytes 1376264 | tf_op jit(solution)/shard_map/part_core/ppermute | solution.py:37
  38.8 6.0 %collective-permute-start.7 = (bf16[896,256]{1,0:T(8,128)(2,1)S(1)}, bf16[896,256]{1,0:T(8,128)(2,1)S(1)}, u32[]{:S(2)}, u32[]{:S(2)}) collective-permute-start(bf16[896,256]{1,0:T(8,128)(2,1)S(1)} %get-tuple-element.171.refs_3_.refs_9_.refs_5_), channel_id=1, source_target_pairs={{0,1},{1,0},{2,3},{3,2},{4,5},{5,4},{6,7},{7,6},{8,9},{9,8},{10,11... | collective-permute-start | bytes 1376264 | tf_op jit(solution)/shard_map/x_core/ppermute | solution.py:37
  38.9 13.7 %collective-permute-start.9 = (bf16[896,256]{1,0:T(8,128)(2,1)S(1)}, bf16[896,256]{1,0:T(8,128)(2,1)S(1)}, u32[]{:S(2)}, u32[]{:S(2)}) collective-permute-start(bf16[896,256]{1,0:T(8,128)(2,1)S(1)} %get-tuple-element.171.refs_3_.refs_9_.refs_5_), channel_id=1, source_target_pairs={{0,4},{2,6},{4,0},{6,2},{1,5},{3,7},{5,1},{7,3},{8,12},{10,14},{12... | collective-permute-start | bytes 1376264 | tf_op jit(solution)/shard_map/x/ppermute | solution.py:37
  41.6 13.5 %collective-permute-start.8 = (bf16[896,256]{1,0:T(8,128)(2,1)S(1)}, bf16[896,256]{1,0:T(8,128)(2,1)S(1)}, u32[]{:S(2)}, u32[]{:S(2)}) collective-permute-start(bf16[896,256]{1,0:T(8,128)(2,1)S(1)} %get-tuple-element.171.refs_3_.refs_9_.refs_5_), channel_id=1, source_target_pairs={{0,2},{2,0},{4,6},{6,4},{1,3},{3,1},{5,7},{7,5},{8,10},{10,8},{12,... | collective-permute-start | bytes 1376264 | tf_op jit(solution)/shard_map/x/ppermute | solution.py:37
  44.3 11.7 %collective-permute-start.11 = (bf16[256,896]{1,0:T(8,128)(2,1)S(1)}, bf16[256,896]{1,0:T(8,128)(2,1)S(1)}, u32[]{:S(2)}, u32[]{:S(2)}) collective-permute-start(bf16[256,896]{1,0:T(8,128)(2,1)S(1)} %collective-permute-done.6.refs_5_.refs_1_.refs_7_), channel_id=1, source_target_pairs={{0,1},{1,0},{2,3},{3,2},{4,5},{5,4},{6,7},{7,6},{8,9},{9,8},{10,11... | collective-permute-start | bytes 1376264 | tf_op jit(solution)/shard_map/gy_core/ppermute | solution.py:37
  44.3 13.5 %collective-permute-start.1 = (bf16[256,896]{1,0:T(8,128)(2,1)S(1)}, bf16[256,896]{1,0:T(8,128)(2,1)S(1)}, u32[]{:S(2)}, u32[]{:S(2)}) collective-permute-start(bf16[256,896]{1,0:T(8,128)(2,1)S(1)} %collective-permute-done.refs_6_.refs_1_.refs_9_), channel_id=1, source_target_pairs={{0,1},{1,0},{2,3},{3,2},{4,5},{5,4},{6,7},{7,6},{8,9},{9,8},{10,11... | collective-permute-start | bytes 1376264 | tf_op jit(solution)/shard_map/gy_core/ppermute | solution.py:37
  55.1 4.5 %collective-permute-start.12 = (bf16[896,256]{1,0:T(8,128)(2,1)S(1)}, bf16[896,256]{1,0:T(8,128)(2,1)S(1)}, u32[]{:S(2)}, u32[]{:S(2)}) collective-permute-start(bf16[896,256]{1,0:T(8,128)(2,1)S(1)} %get-tuple-element.179.refs_3_.refs_7_), channel_id=1, source_target_pairs={{0,1},{1,0},{2,3},{3,2},{4,5},{5,4},{6,7},{7,6},{8,9},{9,8},{10,11... | collective-permute-start | bytes 1376264 | tf_op jit(solution)/shard_map/x_core/ppermute | solution.py:37
  55.1 9.5 %collective-permute-start.10 = (bf16[896,256]{1,0:T(8,128)(2,1)S(1)}, bf16[896,256]{1,0:T(8,128)(2,1)S(1)}, u32[]{:S(2)}, u32[]{:S(2)}) collective-permute-start(bf16[896,256]{1,0:T(8,128)(2,1)S(1)} %get-tuple-element.178.refs_3_.refs_9_), channel_id=1, source_target_pairs={{0,1},{1,0},{2,3},{3,2},{4,5},{5,4},{6,7},{7,6},{8,9},{9,8},{10,11... | collective-permute-start | bytes 1376264 | tf_op jit(solution)/shard_map/x_core/ppermute | solution.py:37
  55.6 12.9 %collective-permute-start.15 = (bf16[128,896]{1,0:T(8,128)(2,1)S(1)}, bf16[128,896]{1,0:T(8,128)(2,1)S(1)}, u32[]{:S(2)}, u32[]{:S(2)}) collective-permute-start(bf16[128,896]{1,0:T(8,128)(2,1)S(1)} %slice.56), channel_id=1, source_target_pairs={{0,4},{2,6},{4,0},{6,2},{1,5},{3,7},{5,1},{7,3},{8,12},{10,14},{12... | collective-permute-start | bytes 688136 | tf_op jit(solution)/shard_map/gy_relay/ppermute | solution.py:37
  56.1 12.5 %collective-permute-start.16 = (bf16[128,896]{1,0:T(8,128)(2,1)S(1)}, bf16[128,896]{1,0:T(8,128)(2,1)S(1)}, u32[]{:S(2)}, u32[]{:S(2)}) collective-permute-start(bf16[128,896]{1,0:T(8,128)(2,1)S(1)} %slice.57), channel_id=1, source_target_pairs={{0,2},{2,0},{4,6},{6,4},{1,3},{3,1},{5,7},{7,5},{8,10},{10,8},{12,... | collective-permute-start | bytes 688136 | tf_op jit(solution)/shard_map/gy_relay/ppermute | solution.py:37
  57.9 10.7 %collective-permute-start.13 = (bf16[448,256]{1,0:T(8,128)(2,1)S(1)}, bf16[448,256]{1,0:T(8,128)(2,1)S(1)}, u32[]{:S(2)}, u32[]{:S(2)}) collective-permute-start(bf16[448,256]{1,0:T(8,128)(2,1)S(1)} %slice.43), channel_id=1, source_target_pairs={{0,4},{2,6},{4,0},{6,2},{1,5},{3,7},{5,1},{7,3},{8,12},{10,14},{12... | collective-permute-start | bytes 688136 | tf_op jit(solution)/shard_map/x_relay/ppermute | solution.py:37
  59.6 9.0 %collective-permute-start.14 = (bf16[448,256]{1,0:T(8,128)(2,1)S(1)}, bf16[448,256]{1,0:T(8,128)(2,1)S(1)}, u32[]{:S(2)}, u32[]{:S(2)}) collective-permute-start(bf16[448,256]{1,0:T(8,128)(2,1)S(1)} %slice.44), channel_id=1, source_target_pairs={{0,2},{2,0},{4,6},{6,4},{1,3},{3,1},{5,7},{7,5},{8,10},{10,8},{12,... | collective-permute-start | bytes 688136 | tf_op jit(solution)/shard_map/x_relay/ppermute | solution.py:37
  68.7 7.8 %collective-permute-start.22 = (bf16[896,256]{1,0:T(8,128)(2,1)S(1)}, bf16[896,256]{1,0:T(8,128)(2,1)S(1)}, u32[]{:S(2)}, u32[]{:S(2)}) collective-permute-start(bf16[896,256]{1,0:T(8,128)(2,1)S(1)} %get-tuple-element.193), channel_id=1, source_target_pairs={{0,1},{1,0},{2,3},{3,2},{4,5},{5,4},{6,7},{7,6},{8,9},{9,8},{10,11... | collective-permute-start | bytes 1376264 | tf_op jit(solution)/shard_map/back_core/ppermute | solution.py:37
  69.2 7.3 %collective-permute-start.21 = (bf16[896,256]{1,0:T(8,128)(2,1)S(1)}, bf16[896,256]{1,0:T(8,128)(2,1)S(1)}, u32[]{:S(2)}, u32[]{:S(2)}) collective-permute-start(bf16[896,256]{1,0:T(8,128)(2,1)S(1)} %get-tuple-element.189.refs_13_), channel_id=1, source_target_pairs={{0,1},{1,0},{2,3},{3,2},{4,5},{5,4},{6,7},{7,6},{8,9},{9,8},{10,11... | collective-permute-start | bytes 1376264 | tf_op jit(solution)/shard_map/back_core/ppermute | solution.py:37
  78.3 16.1 %collective-permute-start.27 = (bf16[1824,128]{1,0:T(8,128)(2,1)S(1)}, bf16[1824,128]{1,0:T(8,128)(2,1)S(1)}, u32[]{:S(2)}, u32[]{:S(2)}) collective-permute-start(bf16[1824,128]{1,0:T(8,128)(2,1)S(1)} %weight_kernel.4.refs_14_.refs_1_), channel_id=1, source_target_pairs={{0,8},{8,0},{16,24},{24,16},{1,9},{9,1},{17,25},{25,17},{2,10},{10... | collective-permute-start | bytes 1400840 | tf_op jit(solution)/shard_map/swap_d1/ppermute | solution.py:78
  80.4 8.1 %collective-permute-start.24 = (bf16[896,256]{1,0:T(8,128)(2,1)S(1)}, bf16[896,256]{1,0:T(8,128)(2,1)S(1)}, u32[]{:S(2)}, u32[]{:S(2)}) collective-permute-start(bf16[896,256]{1,0:T(8,128)(2,1)S(1)} %get-tuple-element.180.refs_9_), channel_id=1, source_target_pairs={{0,1},{1,0},{2,3},{3,2},{4,5},{5,4},{6,7},{7,6},{8,9},{9,8},{10,11... | collective-permute-start | bytes 1376264 | tf_op jit(solution)/shard_map/back_core/ppermute | solution.py:37
  80.4 8.1 %collective-permute-start.23 = (bf16[896,256]{1,0:T(8,128)(2,1)S(1)}, bf16[896,256]{1,0:T(8,128)(2,1)S(1)}, u32[]{:S(2)}, u32[]{:S(2)}) collective-permute-start(bf16[896,256]{1,0:T(8,128)(2,1)S(1)} %get-tuple-element.196), channel_id=1, source_target_pairs={{0,1},{1,0},{2,3},{3,2},{4,5},{5,4},{6,7},{7,6},{8,9},{9,8},{10,11... | collective-permute-start | bytes 1376264 | tf_op jit(solution)/shard_map/back_core/ppermute | solution.py:37
  80.9 12.4 %collective-permute-start.26 = (bf16[896,256]{1,0:T(8,128)(2,1)S(1)}, bf16[896,256]{1,0:T(8,128)(2,1)S(1)}, u32[]{:S(2)}, u32[]{:S(2)}) collective-permute-start(bf16[896,256]{1,0:T(8,128)(2,1)S(1)} %get-tuple-element.199), channel_id=1, source_target_pairs={{0,4},{2,6},{4,0},{6,2},{1,5},{3,7},{5,1},{7,3},{8,12},{10,14},{12... | collective-permute-start | bytes 1376264 | tf_op jit(solution)/shard_map/back/ppermute | solution.py:37
  82.2 12.1 %collective-permute-start.25 = (bf16[896,256]{1,0:T(8,128)(2,1)S(1)}, bf16[896,256]{1,0:T(8,128)(2,1)S(1)}, u32[]{:S(2)}, u32[]{:S(2)}) collective-permute-start(bf16[896,256]{1,0:T(8,128)(2,1)S(1)} %get-tuple-element.198.refs_14_), channel_id=1, source_target_pairs={{0,2},{2,0},{4,6},{6,4},{1,3},{3,1},{5,7},{7,5},{8,10},{10,8},{12,... | collective-permute-start | bytes 1376264 | tf_op jit(solution)/shard_map/back/ppermute | solution.py:37
  94.6 18.7 %collective-permute-start.28 = (bf16[4,896,256]{2,1,0:T(8,128)(2,1)S(1)}, bf16[4,896,256]{2,1,0:T(8,128)(2,1)S(1)}, u32[]{:S(2)}, u32[]{:S(2)}) collective-permute-start(bf16[4,896,256]{2,1,0:T(8,128)(2,1)S(1)} %get-tuple-element.202), channel_id=1, source_target_pairs={{0,1},{1,0},{2,3},{3,2},{4,5},{5,4},{6,7},{7,6},{8,9},{9,8},{10,11... | collective-permute-start | bytes 5505032 | tf_op jit(solution)/shard_map/layer_core/ppermute | solution.py:37
  94.7 16.4 %collective-permute-start.31 = (bf16[2432,128]{1,0:T(8,128)(2,1)S(1)}, bf16[2432,128]{1,0:T(8,128)(2,1)S(1)}, u32[]{:S(2)}, u32[]{:S(2)}) collective-permute-start(bf16[2432,128]{1,0:T(8,128)(2,1)S(1)} %get-tuple-element.210.refs_3_), channel_id=1, source_target_pairs={{0,8},{8,0},{16,24},{24,16},{1,9},{9,1},{17,25},{25,17},{2,10},{10... | collective-permute-start | bytes 1867784 | tf_op jit(solution)/shard_map/swap_d2/ppermute | solution.py:78
  95.7 14.3 %collective-permute-start.30 = (bf16[1824,128]{1,0:T(8,128)(2,1)S(1)}, bf16[1824,128]{1,0:T(8,128)(2,1)S(1)}, u32[]{:S(2)}, u32[]{:S(2)}) collective-permute-start(bf16[1824,128]{1,0:T(8,128)(2,1)S(1)} %tick_kernel.9.refs_14_.refs_1_), channel_id=1, source_target_pairs={{8,16},{16,8},{9,17},{17,9},{10,18},{18,10},{11,19},{19,11},{12,20... | collective-permute-start | bytes 1400840 | tf_op jit(solution)/shard_map/cross_d1/ppermute | solution.py:83
  96.4 13.6 %collective-permute-start.29 = (bf16[896,256]{1,0:T(8,128)(2,1)S(1)}, bf16[896,256]{1,0:T(8,128)(2,1)S(1)}, u32[]{:S(2)}, u32[]{:S(2)}) collective-permute-start(bf16[896,256]{1,0:T(8,128)(2,1)S(1)} %get-tuple-element.209.refs_3_), channel_id=1, source_target_pairs={{0,6},{2,4},{4,2},{6,0},{1,7},{3,5},{5,3},{7,1},{8,14},{10,12},{12... | collective-permute-start | bytes 1376264 | tf_op jit(solution)/shard_map/back/ppermute | solution.py:37
  113.9 8.3 %collective-permute-start.34 = (bf16[896,256]{1,0:T(8,128)(2,1)S(1)}, bf16[896,256]{1,0:T(8,128)(2,1)S(1)}, u32[]{:S(2)}, u32[]{:S(2)}) collective-permute-start(bf16[896,256]{1,0:T(8,128)(2,1)S(1)} %get-tuple-element.229.refs_1_.refs_4_), channel_id=1, source_target_pairs={{0,1},{1,0},{2,3},{3,2},{4,5},{5,4},{6,7},{7,6},{8,9},{9,8},{10,11... | collective-permute-start | bytes 1376264 | tf_op jit(solution)/shard_map/mid_core/ppermute | solution.py:37
  114.0 29.4 %collective-permute-start.33 = (bf16[2432,128]{1,0:T(8,128)(2,1)S(1)}, bf16[2432,128]{1,0:T(8,128)(2,1)S(1)}, u32[]{:S(2)}, u32[]{:S(2)}) collective-permute-start(bf16[2432,128]{1,0:T(8,128)(2,1)S(1)} %get-tuple-element.227.refs_4_), channel_id=1, source_target_pairs={{8,16},{16,8},{9,17},{17,9},{10,18},{18,10},{11,19},{19,11},{12,20... | collective-permute-start | bytes 1867784 | tf_op jit(solution)/shard_map/cross_d2/ppermute | solution.py:83
  115.0 28.3 %collective-permute-start.32 = (bf16[1824,128]{1,0:T(8,128)(2,1)S(1)}, bf16[1824,128]{1,0:T(8,128)(2,1)S(1)}, u32[]{:S(2)}, u32[]{:S(2)}) collective-permute-start(bf16[1824,128]{1,0:T(8,128)(2,1)S(1)} %get-tuple-element.226), channel_id=1, source_target_pairs={{0,8},{8,0},{16,24},{24,16},{1,9},{9,1},{17,25},{25,17},{2,10},{10... | collective-permute-start | bytes 1400840 | tf_op jit(solution)/shard_map/swap_d1_g1/ppermute | solution.py:78
  119.8 13.4 %collective-permute-start.35 = (bf16[896,256]{1,0:T(8,128)(2,1)S(1)}, bf16[896,256]{1,0:T(8,128)(2,1)S(1)}, u32[]{:S(2)}, u32[]{:S(2)}) collective-permute-start(bf16[896,256]{1,0:T(8,128)(2,1)S(1)} %get-tuple-element.240), channel_id=1, source_target_pairs={{0,2},{2,0},{4,6},{6,4},{1,3},{3,1},{5,7},{7,5},{8,10},{10,8},{12,... | collective-permute-start | bytes 1376264 | tf_op jit(solution)/shard_map/layer/ppermute | solution.py:37
  121.6 21.8 %collective-permute-start.36 = (bf16[896,256]{1,0:T(8,128)(2,1)S(1)}, bf16[896,256]{1,0:T(8,128)(2,1)S(1)}, u32[]{:S(2)}, u32[]{:S(2)}) collective-permute-start(bf16[896,256]{1,0:T(8,128)(2,1)S(1)} %get-tuple-element.241), channel_id=1, source_target_pairs={{0,4},{2,6},{4,0},{6,2},{1,5},{3,7},{5,1},{7,3},{8,12},{10,14},{12... | collective-permute-start | bytes 1376264 | tf_op jit(solution)/shard_map/layer/ppermute | solution.py:37
  122.2 21.1 %collective-permute-start.37 = (bf16[896,256]{1,0:T(8,128)(2,1)S(1)}, bf16[896,256]{1,0:T(8,128)(2,1)S(1)}, u32[]{:S(2)}, u32[]{:S(2)}) collective-permute-start(bf16[896,256]{1,0:T(8,128)(2,1)S(1)} %get-tuple-element.242), channel_id=1, source_target_pairs={{0,6},{2,4},{4,2},{6,0},{1,7},{3,5},{5,3},{7,1},{8,14},{10,12},{12... | collective-permute-start | bytes 1376264 | tf_op jit(solution)/shard_map/layer/ppermute | solution.py:37
  144.8 19.6 %collective-permute-start.38 = (bf16[2432,128]{1,0:T(8,128)(2,1)S(1)}, bf16[2432,128]{1,0:T(8,128)(2,1)S(1)}, u32[]{:S(2)}, u32[]{:S(2)}) collective-permute-start(bf16[2432,128]{1,0:T(8,128)(2,1)S(1)} %get-tuple-element.244), channel_id=1, source_target_pairs={{0,8},{8,0},{16,24},{24,16},{1,9},{9,1},{17,25},{25,17},{2,10},{10... | collective-permute-start | bytes 1867784 | tf_op jit(solution)/shard_map/swap_d2_g2/ppermute | solution.py:78
  145.2 19.1 %collective-permute-start.40 = (bf16[2336,128]{1,0:T(8,128)(2,1)S(1)}, bf16[2336,128]{1,0:T(8,128)(2,1)S(1)}, u32[]{:S(2)}, u32[]{:S(2)}) collective-permute-start(bf16[2336,128]{1,0:T(8,128)(2,1)S(1)} %get-tuple-element.247), channel_id=1, source_target_pairs={{0,4},{2,6},{4,0},{6,2},{1,5},{3,7},{5,1},{7,3},{8,12},{10,14},{12... | collective-permute-start | bytes 1794056 | tf_op jit(solution)/shard_map/d1_y/ppermute | solution.py:37
  145.9 18.5 %collective-permute-start.41 = (bf16[2336,128]{1,0:T(8,128)(2,1)S(1)}, bf16[2336,128]{1,0:T(8,128)(2,1)S(1)}, u32[]{:S(2)}, u32[]{:S(2)}) collective-permute-start(bf16[2336,128]{1,0:T(8,128)(2,1)S(1)} %get-tuple-element.248), channel_id=1, source_target_pairs={{0,2},{2,0},{4,6},{6,4},{1,3},{3,1},{5,7},{7,5},{8,10},{10,8},{12,... | collective-permute-start | bytes 1794056 | tf_op jit(solution)/shard_map/d1_x/ppermute | solution.py:37
  149.4 15.0 %collective-permute-start.39 = (bf16[1824,128]{1,0:T(8,128)(2,1)S(1)}, bf16[1824,128]{1,0:T(8,128)(2,1)S(1)}, u32[]{:S(2)}, u32[]{:S(2)}) collective-permute-start(bf16[1824,128]{1,0:T(8,128)(2,1)S(1)} %get-tuple-element.246.refs_4_), channel_id=1, source_target_pairs={{8,16},{16,8},{9,17},{17,9},{10,18},{18,10},{11,19},{19,11},{12,20... | collective-permute-start | bytes 1400840 | tf_op jit(solution)/shard_map/cross_g1/ppermute | solution.py:83
  150.1 14.3 %collective-permute-start.42 = (bf16[512,128]{1,0:T(8,128)(2,1)S(1)}, bf16[512,128]{1,0:T(8,128)(2,1)S(1)}, u32[]{:S(2)}, u32[]{:S(2)}) collective-permute-start(bf16[512,128]{1,0:T(8,128)(2,1)S(1)} %get-tuple-element.249), channel_id=1, source_target_pairs={{0,6},{2,4},{4,2},{6,0},{1,7},{3,5},{5,3},{7,1},{8,14},{10,12},{12... | collective-permute-start | bytes 393224 | tf_op jit(solution)/shard_map/grad_kv/ppermute | solution.py:37
  165.9 19.0 %collective-permute-start.46 = (bf16[3344,128]{1,0:T(8,128)(2,1)S(1)}, bf16[3344,128]{1,0:T(8,128)(2,1)S(1)}, u32[]{:S(2)}, u32[]{:S(2)}) collective-permute-start(bf16[3344,128]{1,0:T(8,128)(2,1)S(1)} %get-tuple-element.258), channel_id=1, source_target_pairs={{0,4},{2,6},{4,0},{6,2},{1,5},{3,7},{5,1},{7,3},{8,12},{10,14},{12... | collective-permute-start | bytes 2568200 | tf_op jit(solution)/shard_map/d2_y/ppermute | solution.py:37
  167.6 18.4 %collective-permute-start.47 = (bf16[3344,128]{1,0:T(8,128)(2,1)S(1)}, bf16[3344,128]{1,0:T(8,128)(2,1)S(1)}, u32[]{:S(2)}, u32[]{:S(2)}) collective-permute-start(bf16[3344,128]{1,0:T(8,128)(2,1)S(1)} %get-tuple-element.266), channel_id=1, source_target_pairs={{0,2},{2,0},{4,6},{6,4},{1,3},{3,1},{5,7},{7,5},{8,10},{10,8},{12,... | collective-permute-start | bytes 2568200 | tf_op jit(solution)/shard_map/d2_x/ppermute | solution.py:37
  169.4 12.4 %collective-permute-start.45 = (bf16[2432,128]{1,0:T(8,128)(2,1)S(1)}, bf16[2432,128]{1,0:T(8,128)(2,1)S(1)}, u32[]{:S(2)}, u32[]{:S(2)}) collective-permute-start(bf16[2432,128]{1,0:T(8,128)(2,1)S(1)} %get-tuple-element.256.refs_4_), channel_id=1, source_target_pairs={{8,16},{16,8},{9,17},{17,9},{10,18},{18,10},{11,19},{19,11},{12,20... | collective-permute-start | bytes 1867784 | tf_op jit(solution)/shard_map/cross_g2/ppermute | solution.py:83
  170.1 11.7 %collective-permute-start.44 = (bf16[1824,128]{1,0:T(8,128)(2,1)S(1)}, bf16[1824,128]{1,0:T(8,128)(2,1)S(1)}, u32[]{:S(2)}, u32[]{:S(2)}) collective-permute-start(bf16[1824,128]{1,0:T(8,128)(2,1)S(1)} %get-tuple-element.254), channel_id=1, source_target_pairs={{0,8},{8,0},{16,24},{24,16},{1,9},{9,1},{17,25},{25,17},{2,10},{10... | collective-permute-start | bytes 1400840 | tf_op jit(solution)/shard_map/swap_g1_u1/ppermute | solution.py:78
  187.6 38.0 %collective-permute-start.50 = (bf16[4944,128]{1,0:T(8,128)(2,1)S(1)}, bf16[4944,128]{1,0:T(8,128)(2,1)S(1)}, u32[]{:S(2)}, u32[]{:S(2)}) collective-permute-start(bf16[4944,128]{1,0:T(8,128)(2,1)S(1)} %get-tuple-element.275), channel_id=1, source_target_pairs={{0,4},{2,6},{4,0},{6,2},{1,5},{3,7},{5,1},{7,3},{8,12},{10,14},{12... | collective-permute-start | bytes 3797000 | tf_op jit(solution)/shard_map/g1_y/ppermute | solution.py:37
  188.3 37.3 %collective-permute-start.51 = (bf16[4944,128]{1,0:T(8,128)(2,1)S(1)}, bf16[4944,128]{1,0:T(8,128)(2,1)S(1)}, u32[]{:S(2)}, u32[]{:S(2)}) collective-permute-start(bf16[4944,128]{1,0:T(8,128)(2,1)S(1)} %get-tuple-element.276), channel_id=1, source_target_pairs={{0,2},{2,0},{4,6},{6,4},{1,3},{3,1},{5,7},{7,5},{8,10},{10,8},{12,... | collective-permute-start | bytes 3797000 | tf_op jit(solution)/shard_map/g1_x/ppermute | solution.py:37
  189.8 3.3 %collective-permute-start.53 = (bf16[896,256]{1,0:T(8,128)(2,1)S(1)}, bf16[896,256]{1,0:T(8,128)(2,1)S(1)}, u32[]{:S(2)}, u32[]{:S(2)}) collective-permute-start(bf16[896,256]{1,0:T(8,128)(2,1)S(1)} %get-tuple-element.279), channel_id=1, source_target_pairs={{0,1},{1,0},{2,3},{3,2},{4,5},{5,4},{6,7},{7,6},{8,9},{9,8},{10,11... | collective-permute-start | bytes 1376264 | tf_op jit(solution)/shard_map/normed_core/ppermute | solution.py:37
  190.3 35.6 %collective-permute-start.48 = (bf16[2432,128]{1,0:T(8,128)(2,1)S(1)}, bf16[2432,128]{1,0:T(8,128)(2,1)S(1)}, u32[]{:S(2)}, u32[]{:S(2)}) collective-permute-start(bf16[2432,128]{1,0:T(8,128)(2,1)S(1)} %get-tuple-element.272), channel_id=1, source_target_pairs={{0,8},{8,0},{16,24},{24,16},{1,9},{9,1},{17,25},{25,17},{2,10},{10... | collective-permute-start | bytes 1867784 | tf_op jit(solution)/shard_map/swap_g2_u2/ppermute | solution.py:78
  191.6 34.0 %collective-permute-start.52 = (bf16[1904,128]{1,0:T(8,128)(2,1)S(1)}, bf16[1904,128]{1,0:T(8,128)(2,1)S(1)}, u32[]{:S(2)}, u32[]{:S(2)}) collective-permute-start(bf16[1904,128]{1,0:T(8,128)(2,1)S(1)} %get-tuple-element.277), channel_id=1, source_target_pairs={{0,6},{2,4},{4,2},{6,0},{1,7},{3,5},{5,3},{7,1},{8,14},{10,12},{12... | collective-permute-start | bytes 1462280 | tf_op jit(solution)/shard_map/shares/ppermute | solution.py:37
  193.0 32.8 %collective-permute-start.49 = (bf16[1824,128]{1,0:T(8,128)(2,1)S(1)}, bf16[1824,128]{1,0:T(8,128)(2,1)S(1)}, u32[]{:S(2)}, u32[]{:S(2)}) collective-permute-start(bf16[1824,128]{1,0:T(8,128)(2,1)S(1)} %get-tuple-element.274.refs_4_), channel_id=1, source_target_pairs={{8,16},{16,8},{9,17},{17,9},{10,18},{18,10},{11,19},{19,11},{12,20... | collective-permute-start | bytes 1400840 | tf_op jit(solution)/shard_map/cross_u1/ppermute | solution.py:83
  227.2 23.2 %collective-permute-start.58 = (bf16[3344,128]{1,0:T(8,128)(2,1)S(1)}, bf16[3344,128]{1,0:T(8,128)(2,1)S(1)}, u32[]{:S(2)}, u32[]{:S(2)}) collective-permute-start(bf16[3344,128]{1,0:T(8,128)(2,1)S(1)} %get-tuple-element.284), channel_id=1, source_target_pairs={{0,4},{2,6},{4,0},{6,2},{1,5},{3,7},{5,1},{7,3},{8,12},{10,14},{12... | collective-permute-start | bytes 2568200 | tf_op jit(solution)/shard_map/g2_y/ppermute | solution.py:37
  228.1 22.3 %collective-permute-start.59 = (bf16[3344,128]{1,0:T(8,128)(2,1)S(1)}, bf16[3344,128]{1,0:T(8,128)(2,1)S(1)}, u32[]{:S(2)}, u32[]{:S(2)}) collective-permute-start(bf16[3344,128]{1,0:T(8,128)(2,1)S(1)} %get-tuple-element.285), channel_id=1, source_target_pairs={{0,2},{2,0},{4,6},{6,4},{1,3},{3,1},{5,7},{7,5},{8,10},{10,8},{12,... | collective-permute-start | bytes 2568200 | tf_op jit(solution)/shard_map/g2_x/ppermute | solution.py:37
  229.3 21.0 %collective-permute-start.56 = (bf16[2432,128]{1,0:T(8,128)(2,1)S(1)}, bf16[2432,128]{1,0:T(8,128)(2,1)S(1)}, u32[]{:S(2)}, u32[]{:S(2)}) collective-permute-start(bf16[2432,128]{1,0:T(8,128)(2,1)S(1)} %get-tuple-element.282.refs_3_), channel_id=1, source_target_pairs={{8,16},{16,8},{9,17},{17,9},{10,18},{18,10},{11,19},{19,11},{12,20... | collective-permute-start | bytes 1867784 | tf_op jit(solution)/shard_map/cross_u2/ppermute | solution.py:83
  230.0 20.3 %collective-permute-start.57 = (bf16[1904,128]{1,0:T(8,128)(2,1)S(1)}, bf16[1904,128]{1,0:T(8,128)(2,1)S(1)}, u32[]{:S(2)}, u32[]{:S(2)}) collective-permute-start(bf16[1904,128]{1,0:T(8,128)(2,1)S(1)} %get-tuple-element.283.refs_5_), channel_id=1, source_target_pairs={{0,8},{8,0},{16,24},{24,16},{1,9},{9,1},{17,25},{25,17},{2,10},{10... | collective-permute-start | bytes 1462280 | tf_op jit(solution)/shard_map/swap_share/ppermute | solution.py:78
  233.9 16.4 %collective-permute-start.55 = (bf16[1824,128]{1,0:T(8,128)(2,1)S(1)}, bf16[1824,128]{1,0:T(8,128)(2,1)S(1)}, u32[]{:S(2)}, u32[]{:S(2)}) collective-permute-start(bf16[1824,128]{1,0:T(8,128)(2,1)S(1)} %get-tuple-element.281.refs_2_), channel_id=1, source_target_pairs={{0,8},{8,0},{16,24},{24,16},{1,9},{9,1},{17,25},{25,17},{2,10},{10... | collective-permute-start | bytes 1400840 | tf_op jit(solution)/shard_map/swap_u1/ppermute | solution.py:78
  251.7 22.7 %collective-permute-start.62 = (bf16[3040,128]{1,0:T(8,128)(2,1)S(1)}, bf16[3040,128]{1,0:T(8,128)(2,1)S(1)}, u32[]{:S(2)}, u32[]{:S(2)}) collective-permute-start(bf16[3040,128]{1,0:T(8,128)(2,1)S(1)} %get-tuple-element.290), channel_id=1, source_target_pairs={{0,4},{2,6},{4,0},{6,2},{1,5},{3,7},{5,1},{7,3},{8,12},{10,14},{12... | collective-permute-start | bytes 2334728 | tf_op jit(solution)/shard_map/u1_y/ppermute | solution.py:37
  251.8 22.6 %collective-permute-start.63 = (bf16[3040,128]{1,0:T(8,128)(2,1)S(1)}, bf16[3040,128]{1,0:T(8,128)(2,1)S(1)}, u32[]{:S(2)}, u32[]{:S(2)}) collective-permute-start(bf16[3040,128]{1,0:T(8,128)(2,1)S(1)} %get-tuple-element.291), channel_id=1, source_target_pairs={{0,2},{2,0},{4,6},{6,4},{1,3},{3,1},{5,7},{7,5},{8,10},{10,8},{12,... | collective-permute-start | bytes 2334728 | tf_op jit(solution)/shard_map/u1_x/ppermute | solution.py:37
  258.9 15.5 %collective-permute-start.60 = (bf16[2432,128]{1,0:T(8,128)(2,1)S(1)}, bf16[2432,128]{1,0:T(8,128)(2,1)S(1)}, u32[]{:S(2)}, u32[]{:S(2)}) collective-permute-start(bf16[2432,128]{1,0:T(8,128)(2,1)S(1)} %get-tuple-element.288.refs_2_), channel_id=1, source_target_pairs={{0,8},{8,0},{16,24},{24,16},{1,9},{9,1},{17,25},{25,17},{2,10},{10... | collective-permute-start | bytes 1867784 | tf_op jit(solution)/shard_map/swap_u2/ppermute | solution.py:78
  258.9 13.5 %collective-permute-start.61 = (bf16[1904,128]{1,0:T(8,128)(2,1)S(1)}, bf16[1904,128]{1,0:T(8,128)(2,1)S(1)}, u32[]{:S(2)}, u32[]{:S(2)}) collective-permute-start(bf16[1904,128]{1,0:T(8,128)(2,1)S(1)} %get-tuple-element.289.refs_3_), channel_id=1, source_target_pairs={{0,16},{8,24},{16,0},{24,8},{1,17},{9,25},{17,1},{25,9},{2,18},{10... | collective-permute-start | bytes 1462280 | tf_op jit(solution)/shard_map/share_far/ppermute | solution.py:37
  275.5 25.9 %collective-permute-start.64 = (bf16[5248,128]{1,0:T(8,128)(2,1)S(1)}, bf16[5248,128]{1,0:T(8,128)(2,1)S(1)}, u32[]{:S(2)}, u32[]{:S(2)}) collective-permute-start(bf16[5248,128]{1,0:T(8,128)(2,1)S(1)} %get-tuple-element.295), channel_id=1, source_target_pairs={{0,2},{2,0},{4,6},{6,4},{1,3},{3,1},{5,7},{7,5},{8,10},{10,8},{12,... | collective-permute-start | bytes 4030472 | tf_op jit(solution)/shard_map/u2_x/ppermute | solution.py:37
  275.8 25.6 %collective-permute-start.65 = (bf16[5248,128]{1,0:T(8,128)(2,1)S(1)}, bf16[5248,128]{1,0:T(8,128)(2,1)S(1)}, u32[]{:S(2)}, u32[]{:S(2)}) collective-permute-start(bf16[5248,128]{1,0:T(8,128)(2,1)S(1)} %get-tuple-element.296), channel_id=1, source_target_pairs={{0,4},{2,6},{4,0},{6,2},{1,5},{3,7},{5,1},{7,3},{8,12},{10,14},{12... | collective-permute-start | bytes 4030472 | tf_op jit(solution)/shard_map/u2_y/ppermute | solution.py:37
  302.0 10.4 %collective-permute-start.67 = (bf16[960,128]{1,0:T(8,128)(2,1)S(1)}, bf16[960,128]{1,0:T(8,128)(2,1)S(1)}, u32[]{:S(2)}, u32[]{:S(2)}) collective-permute-start(bf16[960,128]{1,0:T(8,128)(2,1)S(1)} %get-tuple-element.299.refs_8_), channel_id=1, source_target_pairs={{0,2},{2,0},{4,6},{6,4},{1,3},{3,1},{5,7},{7,5},{8,10},{10,8},{12,... | collective-permute-start | bytes 737288 | tf_op jit(solution)/shard_map/far_share_x/ppermute | solution.py:37
  304.5 7.8 %collective-permute-start.66 = (bf16[944,128]{1,0:T(8,128)(2,1)S(1)}, bf16[944,128]{1,0:T(8,128)(2,1)S(1)}, u32[]{:S(2)}, u32[]{:S(2)}) collective-permute-start(bf16[944,128]{1,0:T(8,128)(2,1)S(1)} %get-tuple-element.298), channel_id=1, source_target_pairs={{0,4},{2,6},{4,0},{6,2},{1,5},{3,7},{5,1},{7,3},{8,12},{10,14},{12... | collective-permute-start | bytes 725000 | tf_op jit(solution)/shard_map/far_share_y/ppermute | solution.py:37
  308.2 8.7 %collective-permute-start.69 = (bf16[1216,128]{1,0:T(8,128)(2,1)S(1)}, bf16[1216,128]{1,0:T(8,128)(2,1)S(1)}, u32[]{:S(2)}, u32[]{:S(2)}) collective-permute-start(bf16[1216,128]{1,0:T(8,128)(2,1)S(1)} %get-tuple-element.307), channel_id=1, source_target_pairs={{0,4},{2,6},{4,0},{6,2},{1,5},{3,7},{5,1},{7,3},{8,12},{10,14},{12... | collective-permute-start | bytes 933896 | tf_op jit(solution)/shard_map/far_u2_y/ppermute | solution.py:37
  308.3 8.6 %collective-permute-start.70 = (bf16[1216,128]{1,0:T(8,128)(2,1)S(1)}, bf16[1216,128]{1,0:T(8,128)(2,1)S(1)}, u32[]{:S(2)}, u32[]{:S(2)}) collective-permute-start(bf16[1216,128]{1,0:T(8,128)(2,1)S(1)} %get-tuple-element.308), channel_id=1, source_target_pairs={{0,2},{2,0},{4,6},{6,4},{1,3},{3,1},{5,7},{7,5},{8,10},{10,8},{12,... | collective-permute-start | bytes 933896 | tf_op jit(solution)/shard_map/far_u2_x/ppermute | solution.py:37
  (52 other events, 282.0 us)

commit v7 on v6

--- a/solution.py
+++ b/solution.py
@@ -593,9 +593,14 @@
         for t in range(stack_ref.shape[1] // share):
             pack_ref[at, t * 128 : (t + 1) * 128] = stack_ref[r, t * share : (t + 1) * share, :]
     at = 0
+    *outs, bias_q_ref, bias_k_ref, bias_v_ref = outs
     for out_ref in outs:
         out_ref[...] = pack_ref[at : at + out_ref.shape[0], :]
         at += out_ref.shape[0]
+    start = 0
+    for out_ref in (bias_q_ref, bias_k_ref, bias_v_ref):
+        out_ref[...] = pack_ref[at : at + 1, start : start + out_ref.shape[1]]
+        start += out_ref.shape[1]
 
 
 def leave_kernel(place_ref, tokens_ref, mine_ref, passed_ref, gain_ref, grad_mid_ref, out_ref):
@@ -1048,7 +1053,10 @@
                 shape((HEAD_DIM, width), wide),
                 shape((HEAD_DIM, width), wide),
                 shape((q_width, width), wide),
-                shape((pack_rows - 2 * q_width - 2 * HEAD_DIM, width), wide),
+                shape((2, width), wide),
+                shape((1, q_width), wide),
+                shape((1, HEAD_DIM), wide),
+                shape((1, HEAD_DIM), wide),
             ],
             [place] + pieces,
             scratch=[pltpu.VMEM((blocks, stack_rows, 128), wide), pltpu.VMEM((pack_rows, width), wide)],
@@ -1066,7 +1074,7 @@
         own_share = sum_share(scatter_blocks(shares, "shares"), [0] * blocks)
         own_share = lax.psum(own_share, "dp")
         pieces = gather_blocks(own_share, "all_share")
-        grad_w_query, grad_w_key, grad_w_value, grad_w_out, small = unpack(
+        grad_w_query, grad_w_key, grad_w_value, grad_w_out, gains, *biases = unpack(
             pieces, [(r, 0, stack_rows, 0) for r in range(blocks)]
         )
 
@@ -1194,7 +1202,7 @@
         x7, y7 = both_ways(far[2], far[3], "far_u2")
         u_shares = [(u1_all, x5, y5, (y6, r2), (x6, r2)), (u2_all, x6, y6, (y7, 0), (x7, 0))]
         grad_w_up, *last = place_shares(place, u_shares[:1], units, True, width, 0, None, last)
-        grad_w_query, grad_w_key, grad_w_value, grad_w_out, small = unpack(
+        grad_w_query, grad_w_key, grad_w_value, grad_w_out, gains, *biases = unpack(
             [own_share, x6, y6, share_y, share_x],
             [
                 (0, 0, stack_rows, 0),
@@ -1205,21 +1213,20 @@
             ],
         )
         grad_w_up, _ = place_shares(
-            place, u_shares[1:], units, True, width, cut_at, grad_w_up, [small]
-        )
-    gains = small[:2]
+            place, u_shares[1:], units, True, width, cut_at, grad_w_up, [gains]
+        )
     gains = gains + partner(gains, "tensor", 1, "gains_core")
-    grad_b = small[2]
+    grad_b_query, grad_b_key, grad_b_value = (bias.reshape(-1) for bias in biases)
     return (
         layer_out,
         grad_tokens,
         gains[0],
         grad_w_query.T,
-        grad_b[:q_width],
+        grad_b_query,
         grad_w_key.T,
-        grad_b[q_width : q_width + HEAD_DIM],
+        grad_b_key,
         grad_w_value.T,
-        grad_b[q_width + HEAD_DIM : q_width + 2 * HEAD_DIM],
+        grad_b_value,
         grad_w_out,
         gains[1],
         grad_w_gate,

time: 327 us -> 329 us (level)
  waiting for transfers between devices: 124 us -> 136 us
  starting transfers between devices: 85 us -> 77.9 us
    ppermute x56, waiting for transfers between devices: 105 us -> 116 us  [partner(): return lax.ppermute(value, axis, [(i, i ^ step) for i in range(count)])]
    ppermute x56, starting transfers between devices: 62.9 us -> 55.3 us  [partner(): return lax.ppermute(value, axis, [(i, i ^ step) for i in range(count)])]
  transfers between devices with their start and end apart: 71 -> 71, of which waited for: 25 -> 27; matrix products, arithmetic and copies ran while one was open for 1% -> 0% of each run, Pallas kernels for 22% -> 22%
where the time goes in v7:
time: 329 us; the launch traced here: 325 us
  waiting for transfers between devices  136 us (41%)
  Pallas kernels  92.3 us (28%)
  starting transfers between devices  77.9 us (24%)
  local copies, waits for them, and re-layouts  16.4 us (5%)
    ppermute x56, waiting for transfers between devices, partner(): return lax.ppermute(value, axis, [(i, i ^ step) for i in range(count)])  116 us
    pallas_call x38, Pallas kernels, call(): pl.pallas_call(run, name=getattr(body, 'func', body).__name__, out_shape=...  72.3 us
    ppermute x56, starting transfers between devices, partner(): return lax.ppermute(value, axis, [(i, i ^ step) for i in range(count)])  55.3 us
    pallas_call x4, Pallas kernels, place_shares(): pl.pallas_call(body, name='place_kernel', out_shape=(shape(dims, wide), s...  20 us
    ppermute x9, waiting for transfers between devices, swap(): return lax.ppermute(value, 'dp', [(0, 1), (1, 0), (2, 3), (3, 2)])  19.1 us
    ppermute x9, starting transfers between devices, swap(): return lax.ppermute(value, 'dp', [(0, 1), (1, 0), (2, 3), (3, 2)])  17.9 us
    unnamed x90, local copies, waits for them, and re-layouts  13 us
  transfers between devices with their start and end apart: 71, of which 27 were waited for; matrix products, arithmetic and copies ran while one was open for 0% of the time, Pallas kernels for 22%

profile of v7, /device:TPU:0, one launch (start us, length us, event | category | flops | bytes accessed | tf_op | source)
XLA Modules:
  0.0 324.6 jit_solution(16096329666532346339)
XLA Ops:
  0.7 2.8 concatenate.3
  8.3 3.6 %enter_kernel.1 = (bf16[448,512]{1,0:T(8,128)(2,1)S(1)}, bf16[512,128]{1,0:T(8,128)(2,1)S(1)}, bf16[896,512]{1,0:T(8,128)(2,1)S(1)}, bf16[896,512]{1,0:T(8,128)(...) custom-call(s32[1,3]{1,0:T(1,128)S(1)} %copy-done.41, s32[3]{0:T(128)S(1)} %pad_add_fusion.refs_1_.refs_0_, ...), custom_call_target="tpu_custom_call" | custom-call | tf_op jit(solution)/shard_map/enter_kernel/pallas_call | solution.py:96
  12.0 3.9 %collective-permute-start.4 = (bf16[512,128]{1,0:T(8,128)(2,1)S(1)}, bf16[512,128]{1,0:T(8,128)(2,1)S(1)}, u32[]{:S(2)}, u32[]{:S(2)}) collective-permute-start(bf16[512,128]{1,0:T(8,128)(2,1)S(1)} %get-tuple-element.170.refs_4_.refs_8_), channel_id=1, source_target_pairs={{0,6},{2,4},{4,2},{6,0},{1,7},{3,5},{5,3},{7,1},{8,14},{10,12},{12... | collective-permute-start | bytes 393224 | tf_op jit(solution)/shard_map/kv/ppermute | solution.py:37
  16.6 2.2 copy-done.1
  18.8 2.2 copy-done.2
  21.1 3.6 %weights_kernel.1 = (bf16[608,896]{1,0:T(8,128)(2,1)S(1)}, bf16[896,608]{1,0:T(8,128)(2,1)S(1)}, bf16[608,896]{1,0:T(8,128)(2,1)S(1)}, bf16[896,608]{1,0:T(8,128...) custom-call(s32[1,3]{1,0:T(1,128)S(1)} %copy-done.41, ...), custom_call_target="tpu_custom_call" | custom-call | tf_op jit(solution)/shard_map/weights_kernel/pallas_call | solution.py:96
  24.7 2.0 collective-permute-start.6
  26.6 1.5 collective-permute-start
  28.2 4.5 %attend_kernel.1 = (f32[448,512]{1,0:T(8,128)S(1)}, f32[8,512]{1,0:T(8,128)S(1)}, f32[896,256]{1,0:T(8,128)S(1)}, bf16[896,256]{1,0:T(8,128)(2,1)S(1)}) custom-call(s32[1,3]{1,0:T(1,128)S(1)} %copy-done.41, s32[3]{0:T(128)S(1)} %pad_add_fusion.refs_1_.refs_0_, bf16[448,512]{1,0:T(8,128)(2,1)S(1)} %get-tuple-element.166.refs_6_.refs_2_.refs_5_, ...), custom_call_target="tpu_custom_call" | custom-call | tf_op jit(solution)/shard_map/attend_kernel/pallas_call | solution.py:96
  32.9 3.6 %collective-permute-done.6.refs_5_.refs_1_.refs_7_ = bf16[256,896]{1,0:T(8,128)(2,1)S(1)} collective-permute-done((bf16[256,896]{1,0:T(8,128)(2,1)S(1)}, bf16[256,896]{1,0:T(8,128)(2,1)S(1)}, u32[]{:S(2)}, u32[]{:S(2)}) %collective-permute-start.6) | collective-permute-done | bytes 458784 | tf_op jit(solution)/shard_map/gy/ppermute | solution.py:37
  38.9 2.7 collective-permute-start.9
  41.6 2.7 collective-permute-start.8
  44.8 3.9 %hidden_kernel.4 = (bf16[608,512]{1,0:T(8,128)(2,1)S(1)}, bf16[608,512]{1,0:T(8,128)(2,1)S(1)}, bf16[608,512]{1,0:T(8,128)(2,1)S(1)}, bf16[896,256]{1,0:T(8,128)(2,1)S(1)}, bf16[896,256]{1,0:T(8,128)(2,1)S(1)}) custom-call(bf16[256,896]{1,0:T(8,128)(2,1)S(1)} %get-tuple-element.168.refs_0_.refs_4_, ...), custom_call_target="tpu_custom_call" | custom-call | tf_op jit(solution)/shard_map/hidden_kernel/pallas_call | solution.py:96
  48.8 3.9 %collective-permute-done.9.refs_3_ = bf16[896,256]{1,0:T(8,128)(2,1)S(1)} collective-permute-done((bf16[896,256]{1,0:T(8,128)(2,1)S(1)}, bf16[896,256]{1,0:T(8,128)(2,1)S(1)}, u32[]{:S(2)}, u32[]{:S(2)}) %collective-permute-start.9) | collective-permute-done | bytes 458784 | tf_op jit(solution)/shard_map/x/ppermute | solution.py:37
  52.6 2.4 collective-permute-done.8.refs_2_
  56.1 1.8 collective-permute-start.16
  57.9 1.7 collective-permute-start.13
  59.9 3.9 %hidden_kernel.5 = (bf16[608,512]{1,0:T(8,128)(2,1)S(1)}, bf16[608,512]{1,0:T(8,128)(2,1)S(1)}, bf16[608,512]{1,0:T(8,128)(2,1)S(1)}, bf16[896,256]{1,0:T(8,128)(2,1)S(1)}, bf16[896,256]{1,0:T(8,128)(2,1)S(1)}) custom-call(bf16[256,896]{1,0:T(8,128)(2,1)S(1)} %collective-permute-done.11.refs_0_.refs_6_, ...), custom_call_target="tpu_custom_call" | custom-call | tf_op jit(solution)/shard_map/hidden_kernel/pallas_call | solution.py:96
  64.6 3.9 %hidden_kernel.6 = (bf16[608,512]{1,0:T(8,128)(2,1)S(1)}, bf16[608,512]{1,0:T(8,128)(2,1)S(1)}, bf16[608,512]{1,0:T(8,128)(2,1)S(1)}, bf16[896,256]{1,0:T(8,128)(2,1)S(1)}, bf16[896,256]{1,0:T(8,128)(2,1)S(1)}) custom-call(bf16[256,896]{1,0:T(8,128)(2,1)S(1)} %collective-permute-done.1.refs_0_.refs_8_, ...), custom_call_target="tpu_custom_call" | custom-call | tf_op jit(solution)/shard_map/hidden_kernel/pallas_call | solution.py:96
  70.3 1.5 collective-permute-done.18.refs_1_.refs_11_
  72.5 4.0 %hidden_kernel.7 = (bf16[608,512]{1,0:T(8,128)(2,1)S(1)}, bf16[608,512]{1,0:T(8,128)(2,1)S(1)}, bf16[608,512]{1,0:T(8,128)(2,1)S(1)}, bf16[896,256]{1,0:T(8,128)(2,1)S(1)}, bf16[896,256]{1,0:T(8,128)(2,1)S(1)}) custom-call(bf16[128,896]{1,0:T(8,128)(2,1)S(1)} %collective-permute-done.17.refs_0_.refs_10_, ...), custom_call_target="tpu_custom_call" | custom-call | tf_op jit(solution)/shard_map/hidden_kernel/pallas_call | solution.py:96
  76.7 1.5 weight_kernel.4.refs_14_.refs_1_
  78.3 2.1 collective-permute-start.27
  82.2 1.7 collective-permute-start.25
  85.4 3.0 project_kernel.1
  88.5 4.8 %collective-permute-done.26.refs_5_.refs_8_ = bf16[896,256]{1,0:T(8,128)(2,1)S(1)} collective-permute-done((bf16[896,256]{1,0:T(8,128)(2,1)S(1)}, bf16[896,256]{1,0:T(8,128)(2,1)S(1)}, u32[]{:S(2)}, u32[]{:S(2)}) %collective-permute-start.26) | collective-permute-done | bytes 458784 | tf_op jit(solution)/shard_map/back/ppermute | solution.py:37
  96.4 1.9 collective-permute-start.29
  98.4 2.8 weight_kernel.6
  101.2 2.8 weight_kernel.7
  104.0 6.0 %collective-permute-done.29.refs_9_.refs_6_ = bf16[896,256]{1,0:T(8,128)(2,1)S(1)} collective-permute-done((bf16[896,256]{1,0:T(8,128)(2,1)S(1)}, bf16[896,256]{1,0:T(8,128)(2,1)S(1)}, u32[]{:S(2)}, u32[]{:S(2)}) %collective-permute-start.29) | collective-permute-done | bytes 458784 | tf_op jit(solution)/shard_map/back/ppermute | solution.py:37
  115.0 4.8 %collective-permute-start.32 = (bf16[1824,128]{1,0:T(8,128)(2,1)S(1)}, bf16[1824,128]{1,0:T(8,128)(2,1)S(1)}, u32[]{:S(2)}, u32[]{:S(2)}) collective-permute-start(bf16[1824,128]{1,0:T(8,128)(2,1)S(1)} %get-tuple-element.229), channel_id=1, source_target_pairs={{0,8},{8,0},{16,24},{24,16},{1,9},{9,1},{17,25},{25,17},{2,10},{10... | collective-permute-start | bytes 1400840 | tf_op jit(solution)/shard_map/swap_d1_g1/ppermute | solution.py:78
  119.8 1.7 collective-permute-start.35
  124.7 5.9 %attend_back_kernel.1 = (bf16[448,512]{1,0:T(8,128)(2,1)S(1)}, bf16[512,128]{1,0:T(8,128)(2,1)S(1)}, bf16[512,128]{1,0:T(8,128)(2,1)S(1)}, bf16[512,128]{1,0:T(8,128)(2,1)S(1)}, bf16[512,128]{1,0:T(8,128)(2,1)S(1)}) custom-call(s32[1,3]{1,0:T(1,128)S(1)} %copy-done.42, s32[3]{0:T(128)S(1)} %pad_add_fusion.refs_1_.refs_0_, ...), custom_call_target="tpu_custom_call" | custom-call | tf_op jit(solution)/shard_map/attend_back_kernel/pallas_call | solution.py:96
  130.6 2.7 collective-permute-done.35.refs_10_.refs_2_
  133.2 10.1 %collective-permute-done.36.refs_11_.refs_3_ = bf16[896,256]{1,0:T(8,128)(2,1)S(1)} collective-permute-done((bf16[896,256]{1,0:T(8,128)(2,1)S(1)}, bf16[896,256]{1,0:T(8,128)(2,1)S(1)}, u32[]{:S(2)}, u32[]{:S(2)}) %collective-permute-start.36) | collective-permute-done | bytes 458784 | tf_op jit(solution)/shard_map/layer/ppermute | solution.py:37
  145.9 3.5 %collective-permute-start.41 = (bf16[2336,128]{1,0:T(8,128)(2,1)S(1)}, bf16[2336,128]{1,0:T(8,128)(2,1)S(1)}, u32[]{:S(2)}, u32[]{:S(2)}) collective-permute-start(bf16[2336,128]{1,0:T(8,128)(2,1)S(1)} %get-tuple-element.251), channel_id=1, source_target_pairs={{0,2},{2,0},{4,6},{6,4},{1,3},{3,1},{5,7},{7,5},{8,10},{10,8},{12,... | collective-permute-start | bytes 1794056 | tf_op jit(solution)/shard_map/d1_x/ppermute | solution.py:37
  150.2 2.3 query_kernel.1
  152.9 11.5 %collective-permute-done.42.refs_11_.refs_15_ = bf16[512,128]{1,0:T(8,128)(2,1)S(1)} collective-permute-done((bf16[512,128]{1,0:T(8,128)(2,1)S(1)}, bf16[512,128]{1,0:T(8,128)(2,1)S(1)}, u32[]{:S(2)}, u32[]{:S(2)}) %collective-permute-start.42) | collective-permute-done | bytes 131104 | tf_op jit(solution)/shard_map/grad_kv/ppermute | solution.py:37
  164.4 1.5 tick_kernel.12
  165.9 1.7 collective-permute-start.46
  167.6 1.7 collective-permute-start.47
  170.1 3.2 collective-permute-start.44
  173.3 2.2 key_kernel.1
  175.5 5.5 %collective-permute-done.44.refs_1_ = bf16[1824,128]{1,0:T(8,128)(2,1)S(1)} collective-permute-done((bf16[1824,128]{1,0:T(8,128)(2,1)S(1)}, bf16[1824,128]{1,0:T(8,128)(2,1)S(1)}, u32[]{:S(2)}, u32[]{:S(2)}) %collective-permute-start.44) | collective-permute-done | bytes 466976 | tf_op jit(solution)/shard_map/swap_g1_u1/ppermute | solution.py:78
  181.0 3.9 %collective-permute-done.46.refs_7_.refs_13_.refs_4_.refs_5_.refs_10_ = bf16[3344,128]{1,0:T(8,128)(2,1)S(1)} collective-permute-done((bf16[3344,128]{1,0:T(8,128)(2,1)S(1)}, bf16[3344,128]{1,0:T(8,128)(2,1)S(1)}, u32[]{:S(2)}, u32[]{:S(2)}) %collective-permute-start.46) | collective-permute-done | bytes 856096 | tf_op jit(solution)/shard_map/d2_y/ppermute | solution.py:37
  186.0 1.5 tick_kernel.13
  194.0 1.5 join_kernel.2.refs_6_
  198.0 27.5 %collective-permute-done.52.refs_3_ = bf16[1904,128]{1,0:T(8,128)(2,1)S(1)} collective-permute-done((bf16[1904,128]{1,0:T(8,128)(2,1)S(1)}, bf16[1904,128]{1,0:T(8,128)(2,1)S(1)}, u32[]{:S(2)}, u32[]{:S(2)}) %collective-permute-start.52) | collective-permute-done | bytes 487456 | tf_op jit(solution)/shard_map/shares/ppermute | solution.py:37
  230.0 3.7 %collective-permute-start.57 = (bf16[1904,128]{1,0:T(8,128)(2,1)S(1)}, bf16[1904,128]{1,0:T(8,128)(2,1)S(1)}, u32[]{:S(2)}, u32[]{:S(2)}) collective-permute-start(bf16[1904,128]{1,0:T(8,128)(2,1)S(1)} %get-tuple-element.286.refs_5_), channel_id=1, source_target_pairs={{0,8},{8,0},{16,24},{24,16},{1,9},{9,1},{17,25},{25,17},{2,10},{10... | collective-permute-start | bytes 1462280 | tf_op jit(solution)/shard_map/swap_share/ppermute | solution.py:78
  233.8 5.3 %place_kernel.4 = (f32[2432,896]{1,0:T(8,128)}, f32[8,128]{1,0:T(8,128)S(1)}) custom-call(s32[3]{0:T(128)S(1)} %pad_add_fusion.refs_1_.refs_0_, bf16[1824,128]{1,0:T(8,128)(2,1)S(1)} %get-tuple-element.254.refs_7_.refs_1_, bf16[2336,128]{1,0:T(8,128)(2,1)S(1)} %collective-permute-done.41.refs_8_.refs_9_.refs_13_.refs_2_, ...), custom_call_target="tpu_custom_call" | custom-call | tf_op jit(solution)/shard_map/place_kernel/pallas_call | solution.py:689
  239.1 11.6 %collective-permute-done.55.refs_1_ = bf16[1824,128]{1,0:T(8,128)(2,1)S(1)} collective-permute-done((bf16[1824,128]{1,0:T(8,128)(2,1)S(1)}, bf16[1824,128]{1,0:T(8,128)(2,1)S(1)}, u32[]{:S(2)}, u32[]{:S(2)}) %collective-permute-start.55) | collective-permute-done | bytes 466976 | tf_op jit(solution)/shard_map/swap_u1/ppermute | solution.py:78
  252.9 2.0 collective-permute-start.60
  254.9 5.4 %collective-permute-start.61 = (bf16[1904,128]{1,0:T(8,128)(2,1)S(1)}, bf16[1904,128]{1,0:T(8,128)(2,1)S(1)}, u32[]{:S(2)}, u32[]{:S(2)}) collective-permute-start(bf16[1904,128]{1,0:T(8,128)(2,1)S(1)} %get-tuple-element.292.refs_3_), channel_id=1, source_target_pairs={{0,16},{8,24},{16,0},{24,8},{1,17},{9,25},{17,1},{25,9},{2,18},{10... | collective-permute-start | bytes 1462280 | tf_op jit(solution)/shard_map/share_far/ppermute | solution.py:37
  260.3 12.5 %collective-permute-done.61.refs_4_ = bf16[1904,128]{1,0:T(8,128)(2,1)S(1)} collective-permute-done((bf16[1904,128]{1,0:T(8,128)(2,1)S(1)}, bf16[1904,128]{1,0:T(8,128)(2,1)S(1)}, u32[]{:S(2)}, u32[]{:S(2)}) %collective-permute-start.61) | collective-permute-done | bytes 487456 | tf_op jit(solution)/shard_map/share_far/ppermute | solution.py:37
  276.4 1.7 collective-permute-done.54
  278.2 1.9 join_kernel.3.refs_15_
  281.6 6.9 %place_kernel.5 = (f32[896,2432]{1,0:T(8,128)}, f32[8,128]{1,0:T(8,128)S(1)}) custom-call(s32[3]{0:T(128)S(1)} %pad_add_fusion.refs_1_.refs_0_, bf16[1824,128]{1,0:T(8,128)(2,1)S(1)} %get-tuple-element.274.refs_3_.refs_1_, bf16[4944,128]{1,0:T(8,128)(2,1)S(1)} %collective-permute-done.51.refs_1_.refs_7_.refs_13_.refs_14_.refs_2_, ...), custom_call_target="tpu_custom_call" | custom-call | tf_op jit(solution)/shard_map/place_kernel/pallas_call | solution.py:689
  288.5 16.2 %collective-permute-done.64.refs_2_.refs_6_.refs_7_ = bf16[5248,128]{1,0:T(8,128)(2,1)S(1)} collective-permute-done((bf16[5248,128]{1,0:T(8,128)(2,1)S(1)}, bf16[5248,128]{1,0:T(8,128)(2,1)S(1)}, u32[]{:S(2)}, u32[]{:S(2)}) %collective-permute-start.64) | collective-permute-done | bytes 1343520 | tf_op jit(solution)/shard_map/u2_x/ppermute | solution.py:37
  305.4 1.7 collective-permute-start.67
  307.5 1.6 collective-permute-start.69
  309.5 3.7 %place_kernel.6 = (f32[896,2432]{1,0:T(8,128)}, f32[8,128]{1,0:T(8,128)S(1)}) custom-call(s32[3]{0:T(128)S(1)} %pad_add_fusion.refs_1_.refs_0_, bf16[1824,128]{1,0:T(8,128)(2,1)S(1)} %get-tuple-element.295.refs_7_.refs_1_, bf16[3040,128]{1,0:T(8,128)(2,1)S(1)} %collective-permute-done.63.refs_6_.refs_8_.refs_13_.refs_14_.refs_2_, ...), custom_call_target="tpu_custom_call" | custom-call | tf_op jit(solution)/shard_map/place_kernel/pallas_call | solution.py:689
  313.1 2.2 collective-permute-done.66.refs_4_
  315.3 2.8 unpack_kernel.1
  319.9 4.2 %place_kernel.7 = (f32[896,2432]{1,0:T(8,128)}, f32[8,128]{1,0:T(8,128)}) custom-call(s32[3]{0:T(128)S(1)} %pad_add_fusion.refs_1_.refs_0_, bf16[2432,128]{1,0:T(8,128)(2,1)S(1)} %get-tuple-element.296.refs_3_.refs_1_, bf16[5248,128]{1,0:T(8,128)(2,1)S(1)} %collective-permute-done.64.refs_2_.refs_6_.refs_7_, ...), custom_call_target="tpu_custom_call", output_to_operand_aliasing={{0}: (9, {})} | custom-call | tf_op jit(solution)/shard_map/place_kernel/pallas_call | solution.py:689
  (224 shorter events, 57.0 us)
Async XLA Ops:
  12.0 16.2 %collective-permute-start.4 = (bf16[512,128]{1,0:T(8,128)(2,1)S(1)}, bf16[512,128]{1,0:T(8,128)(2,1)S(1)}, u32[]{:S(2)}, u32[]{:S(2)}) collective-permute-start(bf16[512,128]{1,0:T(8,128)(2,1)S(1)} %get-tuple-element.170.refs_4_.refs_8_), channel_id=1, source_target_pairs={{0,6},{2,4},{4,2},{6,0},{1,7},{3,5},{5,3},{7,1},{8,14},{10,12},{12... | collective-permute-start | bytes 393224 | tf_op jit(solution)/shard_map/kv/ppermute | solution.py:37
  15.9 12.2 %collective-permute-start.3 = (bf16[512,128]{1,0:T(8,128)(2,1)S(1)}, bf16[512,128]{1,0:T(8,128)(2,1)S(1)}, u32[]{:S(2)}, u32[]{:S(2)}) collective-permute-start(bf16[512,128]{1,0:T(8,128)(2,1)S(1)} %get-tuple-element.170.refs_4_.refs_8_), channel_id=1, source_target_pairs={{0,4},{2,6},{4,0},{6,2},{1,5},{3,7},{5,1},{7,3},{8,12},{10,14},{12... | collective-permute-start | bytes 393224 | tf_op jit(solution)/shard_map/kv/ppermute | solution.py:37
  16.4 11.8 %collective-permute-start.2 = (bf16[512,128]{1,0:T(8,128)(2,1)S(1)}, bf16[512,128]{1,0:T(8,128)(2,1)S(1)}, u32[]{:S(2)}, u32[]{:S(2)}) collective-permute-start(bf16[512,128]{1,0:T(8,128)(2,1)S(1)} %get-tuple-element.170.refs_4_.refs_8_), channel_id=1, source_target_pairs={{0,2},{2,0},{4,6},{6,4},{1,3},{3,1},{5,7},{7,5},{8,10},{10,8},{12,... | collective-permute-start | bytes 393224 | tf_op jit(solution)/shard_map/kv/ppermute | solution.py:37
  24.7 11.8 %collective-permute-start.6 = (bf16[256,896]{1,0:T(8,128)(2,1)S(1)}, bf16[256,896]{1,0:T(8,128)(2,1)S(1)}, u32[]{:S(2)}, u32[]{:S(2)}) collective-permute-start(bf16[256,896]{1,0:T(8,128)(2,1)S(1)} %get-tuple-element.167.refs_1_.refs_5_.refs_2_), channel_id=1, source_target_pairs={{0,2},{2,0},{4,6},{6,4},{1,3},{3,1},{5,7},{7,5},{8,10},{10,8},{12,... | collective-permute-start | bytes 1376264 | tf_op jit(solution)/shard_map/gy/ppermute | solution.py:37
  26.6 11.1 %collective-permute-start = (bf16[256,896]{1,0:T(8,128)(2,1)S(1)}, bf16[256,896]{1,0:T(8,128)(2,1)S(1)}, u32[]{:S(2)}, u32[]{:S(2)}) collective-permute-start(bf16[256,896]{1,0:T(8,128)(2,1)S(1)} %get-tuple-element.167.refs_1_.refs_5_.refs_2_), channel_id=1, source_target_pairs={{0,4},{2,6},{4,0},{6,2},{1,5},{3,7},{5,1},{7,3},{8,12},{10,14},{12... | collective-permute-start | bytes 1376264 | tf_op jit(solution)/shard_map/gy/ppermute | solution.py:37
  32.8 5.0 %collective-permute-start.5 = (bf16[896,256]{1,0:T(8,128)(2,1)S(1)}, bf16[896,256]{1,0:T(8,128)(2,1)S(1)}, u32[]{:S(2)}, u32[]{:S(2)}) collective-permute-start(bf16[896,256]{1,0:T(8,128)(2,1)S(1)} %get-tuple-element.173), channel_id=1, source_target_pairs={{0,1},{1,0},{2,3},{3,2},{4,5},{5,4},{6,7},{7,6},{8,9},{9,8},{10,11... | collective-permute-start | bytes 1376264 | tf_op jit(solution)/shard_map/part_core/ppermute | solution.py:37
  38.8 6.0 %collective-permute-start.7 = (bf16[896,256]{1,0:T(8,128)(2,1)S(1)}, bf16[896,256]{1,0:T(8,128)(2,1)S(1)}, u32[]{:S(2)}, u32[]{:S(2)}) collective-permute-start(bf16[896,256]{1,0:T(8,128)(2,1)S(1)} %get-tuple-element.174.refs_3_.refs_9_.refs_5_), channel_id=1, source_target_pairs={{0,1},{1,0},{2,3},{3,2},{4,5},{5,4},{6,7},{7,6},{8,9},{9,8},{10,11... | collective-permute-start | bytes 1376264 | tf_op jit(solution)/shard_map/x_core/ppermute | solution.py:37
  38.9 13.7 %collective-permute-start.9 = (bf16[896,256]{1,0:T(8,128)(2,1)S(1)}, bf16[896,256]{1,0:T(8,128)(2,1)S(1)}, u32[]{:S(2)}, u32[]{:S(2)}) collective-permute-start(bf16[896,256]{1,0:T(8,128)(2,1)S(1)} %get-tuple-element.174.refs_3_.refs_9_.refs_5_), channel_id=1, source_target_pairs={{0,4},{2,6},{4,0},{6,2},{1,5},{3,7},{5,1},{7,3},{8,12},{10,14},{12... | collective-permute-start | bytes 1376264 | tf_op jit(solution)/shard_map/x/ppermute | solution.py:37
  41.6 13.5 %collective-permute-start.8 = (bf16[896,256]{1,0:T(8,128)(2,1)S(1)}, bf16[896,256]{1,0:T(8,128)(2,1)S(1)}, u32[]{:S(2)}, u32[]{:S(2)}) collective-permute-start(bf16[896,256]{1,0:T(8,128)(2,1)S(1)} %get-tuple-element.174.refs_3_.refs_9_.refs_5_), channel_id=1, source_target_pairs={{0,2},{2,0},{4,6},{6,4},{1,3},{3,1},{5,7},{7,5},{8,10},{10,8},{12,... | collective-permute-start | bytes 1376264 | tf_op jit(solution)/shard_map/x/ppermute | solution.py:37
  44.3 11.7 %collective-permute-start.11 = (bf16[256,896]{1,0:T(8,128)(2,1)S(1)}, bf16[256,896]{1,0:T(8,128)(2,1)S(1)}, u32[]{:S(2)}, u32[]{:S(2)}) collective-permute-start(bf16[256,896]{1,0:T(8,128)(2,1)S(1)} %collective-permute-done.6.refs_5_.refs_1_.refs_7_), channel_id=1, source_target_pairs={{0,1},{1,0},{2,3},{3,2},{4,5},{5,4},{6,7},{7,6},{8,9},{9,8},{10,11... | collective-permute-start | bytes 1376264 | tf_op jit(solution)/shard_map/gy_core/ppermute | solution.py:37
  44.3 13.5 %collective-permute-start.1 = (bf16[256,896]{1,0:T(8,128)(2,1)S(1)}, bf16[256,896]{1,0:T(8,128)(2,1)S(1)}, u32[]{:S(2)}, u32[]{:S(2)}) collective-permute-start(bf16[256,896]{1,0:T(8,128)(2,1)S(1)} %collective-permute-done.refs_6_.refs_1_.refs_9_), channel_id=1, source_target_pairs={{0,1},{1,0},{2,3},{3,2},{4,5},{5,4},{6,7},{7,6},{8,9},{9,8},{10,11... | collective-permute-start | bytes 1376264 | tf_op jit(solution)/shard_map/gy_core/ppermute | solution.py:37
  55.1 4.5 %collective-permute-start.12 = (bf16[896,256]{1,0:T(8,128)(2,1)S(1)}, bf16[896,256]{1,0:T(8,128)(2,1)S(1)}, u32[]{:S(2)}, u32[]{:S(2)}) collective-permute-start(bf16[896,256]{1,0:T(8,128)(2,1)S(1)} %get-tuple-element.182.refs_3_.refs_7_), channel_id=1, source_target_pairs={{0,1},{1,0},{2,3},{3,2},{4,5},{5,4},{6,7},{7,6},{8,9},{9,8},{10,11... | collective-permute-start | bytes 1376264 | tf_op jit(solution)/shard_map/x_core/ppermute | solution.py:37
  55.1 9.5 %collective-permute-start.10 = (bf16[896,256]{1,0:T(8,128)(2,1)S(1)}, bf16[896,256]{1,0:T(8,128)(2,1)S(1)}, u32[]{:S(2)}, u32[]{:S(2)}) collective-permute-start(bf16[896,256]{1,0:T(8,128)(2,1)S(1)} %get-tuple-element.181.refs_3_.refs_9_), channel_id=1, source_target_pairs={{0,1},{1,0},{2,3},{3,2},{4,5},{5,4},{6,7},{7,6},{8,9},{9,8},{10,11... | collective-permute-start | bytes 1376264 | tf_op jit(solution)/shard_map/x_core/ppermute | solution.py:37
  55.6 12.9 %collective-permute-start.15 = (bf16[128,896]{1,0:T(8,128)(2,1)S(1)}, bf16[128,896]{1,0:T(8,128)(2,1)S(1)}, u32[]{:S(2)}, u32[]{:S(2)}) collective-permute-start(bf16[128,896]{1,0:T(8,128)(2,1)S(1)} %slice.24), channel_id=1, source_target_pairs={{0,4},{2,6},{4,0},{6,2},{1,5},{3,7},{5,1},{7,3},{8,12},{10,14},{12... | collective-permute-start | bytes 688136 | tf_op jit(solution)/shard_map/gy_relay/ppermute | solution.py:37
  56.1 12.5 %collective-permute-start.16 = (bf16[128,896]{1,0:T(8,128)(2,1)S(1)}, bf16[128,896]{1,0:T(8,128)(2,1)S(1)}, u32[]{:S(2)}, u32[]{:S(2)}) collective-permute-start(bf16[128,896]{1,0:T(8,128)(2,1)S(1)} %slice.25), channel_id=1, source_target_pairs={{0,2},{2,0},{4,6},{6,4},{1,3},{3,1},{5,7},{7,5},{8,10},{10,8},{12,... | collective-permute-start | bytes 688136 | tf_op jit(solution)/shard_map/gy_relay/ppermute | solution.py:37
  57.9 10.7 %collective-permute-start.13 = (bf16[448,256]{1,0:T(8,128)(2,1)S(1)}, bf16[448,256]{1,0:T(8,128)(2,1)S(1)}, u32[]{:S(2)}, u32[]{:S(2)}) collective-permute-start(bf16[448,256]{1,0:T(8,128)(2,1)S(1)} %slice.18), channel_id=1, source_target_pairs={{0,4},{2,6},{4,0},{6,2},{1,5},{3,7},{5,1},{7,3},{8,12},{10,14},{12... | collective-permute-start | bytes 688136 | tf_op jit(solution)/shard_map/x_relay/ppermute | solution.py:37
  59.6 9.0 %collective-permute-start.14 = (bf16[448,256]{1,0:T(8,128)(2,1)S(1)}, bf16[448,256]{1,0:T(8,128)(2,1)S(1)}, u32[]{:S(2)}, u32[]{:S(2)}) collective-permute-start(bf16[448,256]{1,0:T(8,128)(2,1)S(1)} %slice.19), channel_id=1, source_target_pairs={{0,2},{2,0},{4,6},{6,4},{1,3},{3,1},{5,7},{7,5},{8,10},{10,8},{12,... | collective-permute-start | bytes 688136 | tf_op jit(solution)/shard_map/x_relay/ppermute | solution.py:37
  68.7 7.8 %collective-permute-start.22 = (bf16[896,256]{1,0:T(8,128)(2,1)S(1)}, bf16[896,256]{1,0:T(8,128)(2,1)S(1)}, u32[]{:S(2)}, u32[]{:S(2)}) collective-permute-start(bf16[896,256]{1,0:T(8,128)(2,1)S(1)} %get-tuple-element.196), channel_id=1, source_target_pairs={{0,1},{1,0},{2,3},{3,2},{4,5},{5,4},{6,7},{7,6},{8,9},{9,8},{10,11... | collective-permute-start | bytes 1376264 | tf_op jit(solution)/shard_map/back_core/ppermute | solution.py:37
  69.2 7.3 %collective-permute-start.21 = (bf16[896,256]{1,0:T(8,128)(2,1)S(1)}, bf16[896,256]{1,0:T(8,128)(2,1)S(1)}, u32[]{:S(2)}, u32[]{:S(2)}) collective-permute-start(bf16[896,256]{1,0:T(8,128)(2,1)S(1)} %get-tuple-element.192.refs_13_), channel_id=1, source_target_pairs={{0,1},{1,0},{2,3},{3,2},{4,5},{5,4},{6,7},{7,6},{8,9},{9,8},{10,11... | collective-permute-start | bytes 1376264 | tf_op jit(solution)/shard_map/back_core/ppermute | solution.py:37
  78.3 16.1 %collective-permute-start.27 = (bf16[1824,128]{1,0:T(8,128)(2,1)S(1)}, bf16[1824,128]{1,0:T(8,128)(2,1)S(1)}, u32[]{:S(2)}, u32[]{:S(2)}) collective-permute-start(bf16[1824,128]{1,0:T(8,128)(2,1)S(1)} %weight_kernel.4.refs_14_.refs_1_), channel_id=1, source_target_pairs={{0,8},{8,0},{16,24},{24,16},{1,9},{9,1},{17,25},{25,17},{2,10},{10... | collective-permute-start | bytes 1400840 | tf_op jit(solution)/shard_map/swap_d1/ppermute | solution.py:78
  80.4 8.1 %collective-permute-start.24 = (bf16[896,256]{1,0:T(8,128)(2,1)S(1)}, bf16[896,256]{1,0:T(8,128)(2,1)S(1)}, u32[]{:S(2)}, u32[]{:S(2)}) collective-permute-start(bf16[896,256]{1,0:T(8,128)(2,1)S(1)} %get-tuple-element.183.refs_9_), channel_id=1, source_target_pairs={{0,1},{1,0},{2,3},{3,2},{4,5},{5,4},{6,7},{7,6},{8,9},{9,8},{10,11... | collective-permute-start | bytes 1376264 | tf_op jit(solution)/shard_map/back_core/ppermute | solution.py:37
  80.4 8.1 %collective-permute-start.23 = (bf16[896,256]{1,0:T(8,128)(2,1)S(1)}, bf16[896,256]{1,0:T(8,128)(2,1)S(1)}, u32[]{:S(2)}, u32[]{:S(2)}) collective-permute-start(bf16[896,256]{1,0:T(8,128)(2,1)S(1)} %get-tuple-element.199), channel_id=1, source_target_pairs={{0,1},{1,0},{2,3},{3,2},{4,5},{5,4},{6,7},{7,6},{8,9},{9,8},{10,11... | collective-permute-start | bytes 1376264 | tf_op jit(solution)/shard_map/back_core/ppermute | solution.py:37
  80.9 12.4 %collective-permute-start.26 = (bf16[896,256]{1,0:T(8,128)(2,1)S(1)}, bf16[896,256]{1,0:T(8,128)(2,1)S(1)}, u32[]{:S(2)}, u32[]{:S(2)}) collective-permute-start(bf16[896,256]{1,0:T(8,128)(2,1)S(1)} %get-tuple-element.202), channel_id=1, source_target_pairs={{0,4},{2,6},{4,0},{6,2},{1,5},{3,7},{5,1},{7,3},{8,12},{10,14},{12... | collective-permute-start | bytes 1376264 | tf_op jit(solution)/shard_map/back/ppermute | solution.py:37
  82.2 12.1 %collective-permute-start.25 = (bf16[896,256]{1,0:T(8,128)(2,1)S(1)}, bf16[896,256]{1,0:T(8,128)(2,1)S(1)}, u32[]{:S(2)}, u32[]{:S(2)}) collective-permute-start(bf16[896,256]{1,0:T(8,128)(2,1)S(1)} %get-tuple-element.201.refs_14_), channel_id=1, source_target_pairs={{0,2},{2,0},{4,6},{6,4},{1,3},{3,1},{5,7},{7,5},{8,10},{10,8},{12,... | collective-permute-start | bytes 1376264 | tf_op jit(solution)/shard_map/back/ppermute | solution.py:37
  94.6 18.7 %collective-permute-start.28 = (bf16[4,896,256]{2,1,0:T(8,128)(2,1)S(1)}, bf16[4,896,256]{2,1,0:T(8,128)(2,1)S(1)}, u32[]{:S(2)}, u32[]{:S(2)}) collective-permute-start(bf16[4,896,256]{2,1,0:T(8,128)(2,1)S(1)} %get-tuple-element.205), channel_id=1, source_target_pairs={{0,1},{1,0},{2,3},{3,2},{4,5},{5,4},{6,7},{7,6},{8,9},{9,8},{10,11... | collective-permute-start | bytes 5505032 | tf_op jit(solution)/shard_map/layer_core/ppermute | solution.py:37
  94.7 16.4 %collective-permute-start.31 = (bf16[2432,128]{1,0:T(8,128)(2,1)S(1)}, bf16[2432,128]{1,0:T(8,128)(2,1)S(1)}, u32[]{:S(2)}, u32[]{:S(2)}) collective-permute-start(bf16[2432,128]{1,0:T(8,128)(2,1)S(1)} %get-tuple-element.213.refs_3_), channel_id=1, source_target_pairs={{0,8},{8,0},{16,24},{24,16},{1,9},{9,1},{17,25},{25,17},{2,10},{10... | collective-permute-start | bytes 1867784 | tf_op jit(solution)/shard_map/swap_d2/ppermute | solution.py:78
  95.7 14.3 %collective-permute-start.30 = (bf16[1824,128]{1,0:T(8,128)(2,1)S(1)}, bf16[1824,128]{1,0:T(8,128)(2,1)S(1)}, u32[]{:S(2)}, u32[]{:S(2)}) collective-permute-start(bf16[1824,128]{1,0:T(8,128)(2,1)S(1)} %tick_kernel.9.refs_14_.refs_1_), channel_id=1, source_target_pairs={{8,16},{16,8},{9,17},{17,9},{10,18},{18,10},{11,19},{19,11},{12,20... | collective-permute-start | bytes 1400840 | tf_op jit(solution)/shard_map/cross_d1/ppermute | solution.py:83
  96.4 13.6 %collective-permute-start.29 = (bf16[896,256]{1,0:T(8,128)(2,1)S(1)}, bf16[896,256]{1,0:T(8,128)(2,1)S(1)}, u32[]{:S(2)}, u32[]{:S(2)}) collective-permute-start(bf16[896,256]{1,0:T(8,128)(2,1)S(1)} %get-tuple-element.212.refs_3_), channel_id=1, source_target_pairs={{0,6},{2,4},{4,2},{6,0},{1,7},{3,5},{5,3},{7,1},{8,14},{10,12},{12... | collective-permute-start | bytes 1376264 | tf_op jit(solution)/shard_map/back/ppermute | solution.py:37
  113.9 8.3 %collective-permute-start.34 = (bf16[896,256]{1,0:T(8,128)(2,1)S(1)}, bf16[896,256]{1,0:T(8,128)(2,1)S(1)}, u32[]{:S(2)}, u32[]{:S(2)}) collective-permute-start(bf16[896,256]{1,0:T(8,128)(2,1)S(1)} %get-tuple-element.232.refs_1_.refs_4_), channel_id=1, source_target_pairs={{0,1},{1,0},{2,3},{3,2},{4,5},{5,4},{6,7},{7,6},{8,9},{9,8},{10,11... | collective-permute-start | bytes 1376264 | tf_op jit(solution)/shard_map/mid_core/ppermute | solution.py:37
  114.0 29.4 %collective-permute-start.33 = (bf16[2432,128]{1,0:T(8,128)(2,1)S(1)}, bf16[2432,128]{1,0:T(8,128)(2,1)S(1)}, u32[]{:S(2)}, u32[]{:S(2)}) collective-permute-start(bf16[2432,128]{1,0:T(8,128)(2,1)S(1)} %get-tuple-element.230.refs_4_), channel_id=1, source_target_pairs={{8,16},{16,8},{9,17},{17,9},{10,18},{18,10},{11,19},{19,11},{12,20... | collective-permute-start | bytes 1867784 | tf_op jit(solution)/shard_map/cross_d2/ppermute | solution.py:83
  115.0 28.3 %collective-permute-start.32 = (bf16[1824,128]{1,0:T(8,128)(2,1)S(1)}, bf16[1824,128]{1,0:T(8,128)(2,1)S(1)}, u32[]{:S(2)}, u32[]{:S(2)}) collective-permute-start(bf16[1824,128]{1,0:T(8,128)(2,1)S(1)} %get-tuple-element.229), channel_id=1, source_target_pairs={{0,8},{8,0},{16,24},{24,16},{1,9},{9,1},{17,25},{25,17},{2,10},{10... | collective-permute-start | bytes 1400840 | tf_op jit(solution)/shard_map/swap_d1_g1/ppermute | solution.py:78
  119.8 13.4 %collective-permute-start.35 = (bf16[896,256]{1,0:T(8,128)(2,1)S(1)}, bf16[896,256]{1,0:T(8,128)(2,1)S(1)}, u32[]{:S(2)}, u32[]{:S(2)}) collective-permute-start(bf16[896,256]{1,0:T(8,128)(2,1)S(1)} %get-tuple-element.243), channel_id=1, source_target_pairs={{0,2},{2,0},{4,6},{6,4},{1,3},{3,1},{5,7},{7,5},{8,10},{10,8},{12,... | collective-permute-start | bytes 1376264 | tf_op jit(solution)/shard_map/layer/ppermute | solution.py:37
  121.6 21.8 %collective-permute-start.36 = (bf16[896,256]{1,0:T(8,128)(2,1)S(1)}, bf16[896,256]{1,0:T(8,128)(2,1)S(1)}, u32[]{:S(2)}, u32[]{:S(2)}) collective-permute-start(bf16[896,256]{1,0:T(8,128)(2,1)S(1)} %get-tuple-element.244), channel_id=1, source_target_pairs={{0,4},{2,6},{4,0},{6,2},{1,5},{3,7},{5,1},{7,3},{8,12},{10,14},{12... | collective-permute-start | bytes 1376264 | tf_op jit(solution)/shard_map/layer/ppermute | solution.py:37
  122.2 21.1 %collective-permute-start.37 = (bf16[896,256]{1,0:T(8,128)(2,1)S(1)}, bf16[896,256]{1,0:T(8,128)(2,1)S(1)}, u32[]{:S(2)}, u32[]{:S(2)}) collective-permute-start(bf16[896,256]{1,0:T(8,128)(2,1)S(1)} %get-tuple-element.245), channel_id=1, source_target_pairs={{0,6},{2,4},{4,2},{6,0},{1,7},{3,5},{5,3},{7,1},{8,14},{10,12},{12... | collective-permute-start | bytes 1376264 | tf_op jit(solution)/shard_map/layer/ppermute | solution.py:37
  144.8 19.6 %collective-permute-start.38 = (bf16[2432,128]{1,0:T(8,128)(2,1)S(1)}, bf16[2432,128]{1,0:T(8,128)(2,1)S(1)}, u32[]{:S(2)}, u32[]{:S(2)}) collective-permute-start(bf16[2432,128]{1,0:T(8,128)(2,1)S(1)} %get-tuple-element.247), channel_id=1, source_target_pairs={{0,8},{8,0},{16,24},{24,16},{1,9},{9,1},{17,25},{25,17},{2,10},{10... | collective-permute-start | bytes 1867784 | tf_op jit(solution)/shard_map/swap_d2_g2/ppermute | solution.py:78
  145.2 19.1 %collective-permute-start.40 = (bf16[2336,128]{1,0:T(8,128)(2,1)S(1)}, bf16[2336,128]{1,0:T(8,128)(2,1)S(1)}, u32[]{:S(2)}, u32[]{:S(2)}) collective-permute-start(bf16[2336,128]{1,0:T(8,128)(2,1)S(1)} %get-tuple-element.250), channel_id=1, source_target_pairs={{0,4},{2,6},{4,0},{6,2},{1,5},{3,7},{5,1},{7,3},{8,12},{10,14},{12... | collective-permute-start | bytes 1794056 | tf_op jit(solution)/shard_map/d1_y/ppermute | solution.py:37
  145.9 18.5 %collective-permute-start.41 = (bf16[2336,128]{1,0:T(8,128)(2,1)S(1)}, bf16[2336,128]{1,0:T(8,128)(2,1)S(1)}, u32[]{:S(2)}, u32[]{:S(2)}) collective-permute-start(bf16[2336,128]{1,0:T(8,128)(2,1)S(1)} %get-tuple-element.251), channel_id=1, source_target_pairs={{0,2},{2,0},{4,6},{6,4},{1,3},{3,1},{5,7},{7,5},{8,10},{10,8},{12,... | collective-permute-start | bytes 1794056 | tf_op jit(solution)/shard_map/d1_x/ppermute | solution.py:37
  149.4 15.0 %collective-permute-start.39 = (bf16[1824,128]{1,0:T(8,128)(2,1)S(1)}, bf16[1824,128]{1,0:T(8,128)(2,1)S(1)}, u32[]{:S(2)}, u32[]{:S(2)}) collective-permute-start(bf16[1824,128]{1,0:T(8,128)(2,1)S(1)} %get-tuple-element.249.refs_4_), channel_id=1, source_target_pairs={{8,16},{16,8},{9,17},{17,9},{10,18},{18,10},{11,19},{19,11},{12,20... | collective-permute-start | bytes 1400840 | tf_op jit(solution)/shard_map/cross_g1/ppermute | solution.py:83
  150.1 14.3 %collective-permute-start.42 = (bf16[512,128]{1,0:T(8,128)(2,1)S(1)}, bf16[512,128]{1,0:T(8,128)(2,1)S(1)}, u32[]{:S(2)}, u32[]{:S(2)}) collective-permute-start(bf16[512,128]{1,0:T(8,128)(2,1)S(1)} %get-tuple-element.252), channel_id=1, source_target_pairs={{0,6},{2,4},{4,2},{6,0},{1,7},{3,5},{5,3},{7,1},{8,14},{10,12},{12... | collective-permute-start | bytes 393224 | tf_op jit(solution)/shard_map/grad_kv/ppermute | solution.py:37
  165.9 19.0 %collective-permute-start.46 = (bf16[3344,128]{1,0:T(8,128)(2,1)S(1)}, bf16[3344,128]{1,0:T(8,128)(2,1)S(1)}, u32[]{:S(2)}, u32[]{:S(2)}) collective-permute-start(bf16[3344,128]{1,0:T(8,128)(2,1)S(1)} %get-tuple-element.261), channel_id=1, source_target_pairs={{0,4},{2,6},{4,0},{6,2},{1,5},{3,7},{5,1},{7,3},{8,12},{10,14},{12... | collective-permute-start | bytes 2568200 | tf_op jit(solution)/shard_map/d2_y/ppermute | solution.py:37
  167.6 18.4 %collective-permute-start.47 = (bf16[3344,128]{1,0:T(8,128)(2,1)S(1)}, bf16[3344,128]{1,0:T(8,128)(2,1)S(1)}, u32[]{:S(2)}, u32[]{:S(2)}) collective-permute-start(bf16[3344,128]{1,0:T(8,128)(2,1)S(1)} %get-tuple-element.269), channel_id=1, source_target_pairs={{0,2},{2,0},{4,6},{6,4},{1,3},{3,1},{5,7},{7,5},{8,10},{10,8},{12,... | collective-permute-start | bytes 2568200 | tf_op jit(solution)/shard_map/d2_x/ppermute | solution.py:37
  169.4 11.6 %collective-permute-start.45 = (bf16[2432,128]{1,0:T(8,128)(2,1)S(1)}, bf16[2432,128]{1,0:T(8,128)(2,1)S(1)}, u32[]{:S(2)}, u32[]{:S(2)}) collective-permute-start(bf16[2432,128]{1,0:T(8,128)(2,1)S(1)} %get-tuple-element.259.refs_4_), channel_id=1, source_target_pairs={{8,16},{16,8},{9,17},{17,9},{10,18},{18,10},{11,19},{19,11},{12,20... | collective-permute-start | bytes 1867784 | tf_op jit(solution)/shard_map/cross_g2/ppermute | solution.py:83
  170.1 10.9 %collective-permute-start.44 = (bf16[1824,128]{1,0:T(8,128)(2,1)S(1)}, bf16[1824,128]{1,0:T(8,128)(2,1)S(1)}, u32[]{:S(2)}, u32[]{:S(2)}) collective-permute-start(bf16[1824,128]{1,0:T(8,128)(2,1)S(1)} %get-tuple-element.257), channel_id=1, source_target_pairs={{0,8},{8,0},{16,24},{24,16},{1,9},{9,1},{17,25},{25,17},{2,10},{10... | collective-permute-start | bytes 1400840 | tf_op jit(solution)/shard_map/swap_g1_u1/ppermute | solution.py:78
  187.6 38.0 %collective-permute-start.50 = (bf16[4944,128]{1,0:T(8,128)(2,1)S(1)}, bf16[4944,128]{1,0:T(8,128)(2,1)S(1)}, u32[]{:S(2)}, u32[]{:S(2)}) collective-permute-start(bf16[4944,128]{1,0:T(8,128)(2,1)S(1)} %get-tuple-element.278), channel_id=1, source_target_pairs={{0,4},{2,6},{4,0},{6,2},{1,5},{3,7},{5,1},{7,3},{8,12},{10,14},{12... | collective-permute-start | bytes 3797000 | tf_op jit(solution)/shard_map/g1_y/ppermute | solution.py:37
  188.3 37.3 %collective-permute-start.51 = (bf16[4944,128]{1,0:T(8,128)(2,1)S(1)}, bf16[4944,128]{1,0:T(8,128)(2,1)S(1)}, u32[]{:S(2)}, u32[]{:S(2)}) collective-permute-start(bf16[4944,128]{1,0:T(8,128)(2,1)S(1)} %get-tuple-element.279), channel_id=1, source_target_pairs={{0,2},{2,0},{4,6},{6,4},{1,3},{3,1},{5,7},{7,5},{8,10},{10,8},{12,... | collective-permute-start | bytes 3797000 | tf_op jit(solution)/shard_map/g1_x/ppermute | solution.py:37
  189.8 3.3 %collective-permute-start.53 = (bf16[896,256]{1,0:T(8,128)(2,1)S(1)}, bf16[896,256]{1,0:T(8,128)(2,1)S(1)}, u32[]{:S(2)}, u32[]{:S(2)}) collective-permute-start(bf16[896,256]{1,0:T(8,128)(2,1)S(1)} %get-tuple-element.282), channel_id=1, source_target_pairs={{0,1},{1,0},{2,3},{3,2},{4,5},{5,4},{6,7},{7,6},{8,9},{9,8},{10,11... | collective-permute-start | bytes 1376264 | tf_op jit(solution)/shard_map/normed_core/ppermute | solution.py:37
  190.3 35.6 %collective-permute-start.48 = (bf16[2432,128]{1,0:T(8,128)(2,1)S(1)}, bf16[2432,128]{1,0:T(8,128)(2,1)S(1)}, u32[]{:S(2)}, u32[]{:S(2)}) collective-permute-start(bf16[2432,128]{1,0:T(8,128)(2,1)S(1)} %get-tuple-element.275), channel_id=1, source_target_pairs={{0,8},{8,0},{16,24},{24,16},{1,9},{9,1},{17,25},{25,17},{2,10},{10... | collective-permute-start | bytes 1867784 | tf_op jit(solution)/shard_map/swap_g2_u2/ppermute | solution.py:78
  191.6 34.0 %collective-permute-start.52 = (bf16[1904,128]{1,0:T(8,128)(2,1)S(1)}, bf16[1904,128]{1,0:T(8,128)(2,1)S(1)}, u32[]{:S(2)}, u32[]{:S(2)}) collective-permute-start(bf16[1904,128]{1,0:T(8,128)(2,1)S(1)} %get-tuple-element.280), channel_id=1, source_target_pairs={{0,6},{2,4},{4,2},{6,0},{1,7},{3,5},{5,3},{7,1},{8,14},{10,12},{12... | collective-permute-start | bytes 1462280 | tf_op jit(solution)/shard_map/shares/ppermute | solution.py:37
  193.0 32.8 %collective-permute-start.49 = (bf16[1824,128]{1,0:T(8,128)(2,1)S(1)}, bf16[1824,128]{1,0:T(8,128)(2,1)S(1)}, u32[]{:S(2)}, u32[]{:S(2)}) collective-permute-start(bf16[1824,128]{1,0:T(8,128)(2,1)S(1)} %get-tuple-element.277.refs_4_), channel_id=1, source_target_pairs={{8,16},{16,8},{9,17},{17,9},{10,18},{18,10},{11,19},{19,11},{12,20... | collective-permute-start | bytes 1400840 | tf_op jit(solution)/shard_map/cross_u1/ppermute | solution.py:83
  227.2 23.6 %collective-permute-start.58 = (bf16[3344,128]{1,0:T(8,128)(2,1)S(1)}, bf16[3344,128]{1,0:T(8,128)(2,1)S(1)}, u32[]{:S(2)}, u32[]{:S(2)}) collective-permute-start(bf16[3344,128]{1,0:T(8,128)(2,1)S(1)} %get-tuple-element.287), channel_id=1, source_target_pairs={{0,4},{2,6},{4,0},{6,2},{1,5},{3,7},{5,1},{7,3},{8,12},{10,14},{12... | collective-permute-start | bytes 2568200 | tf_op jit(solution)/shard_map/g2_y/ppermute | solution.py:37
  228.1 22.6 %collective-permute-start.59 = (bf16[3344,128]{1,0:T(8,128)(2,1)S(1)}, bf16[3344,128]{1,0:T(8,128)(2,1)S(1)}, u32[]{:S(2)}, u32[]{:S(2)}) collective-permute-start(bf16[3344,128]{1,0:T(8,128)(2,1)S(1)} %get-tuple-element.288), channel_id=1, source_target_pairs={{0,2},{2,0},{4,6},{6,4},{1,3},{3,1},{5,7},{7,5},{8,10},{10,8},{12,... | collective-permute-start | bytes 2568200 | tf_op jit(solution)/shard_map/g2_x/ppermute | solution.py:37
  229.3 21.4 %collective-permute-start.56 = (bf16[2432,128]{1,0:T(8,128)(2,1)S(1)}, bf16[2432,128]{1,0:T(8,128)(2,1)S(1)}, u32[]{:S(2)}, u32[]{:S(2)}) collective-permute-start(bf16[2432,128]{1,0:T(8,128)(2,1)S(1)} %get-tuple-element.285.refs_3_), channel_id=1, source_target_pairs={{8,16},{16,8},{9,17},{17,9},{10,18},{18,10},{11,19},{19,11},{12,20... | collective-permute-start | bytes 1867784 | tf_op jit(solution)/shard_map/cross_u2/ppermute | solution.py:83
  230.0 20.7 %collective-permute-start.57 = (bf16[1904,128]{1,0:T(8,128)(2,1)S(1)}, bf16[1904,128]{1,0:T(8,128)(2,1)S(1)}, u32[]{:S(2)}, u32[]{:S(2)}) collective-permute-start(bf16[1904,128]{1,0:T(8,128)(2,1)S(1)} %get-tuple-element.286.refs_5_), channel_id=1, source_target_pairs={{0,8},{8,0},{16,24},{24,16},{1,9},{9,1},{17,25},{25,17},{2,10},{10... | collective-permute-start | bytes 1462280 | tf_op jit(solution)/shard_map/swap_share/ppermute | solution.py:78
  233.7 17.0 %collective-permute-start.55 = (bf16[1824,128]{1,0:T(8,128)(2,1)S(1)}, bf16[1824,128]{1,0:T(8,128)(2,1)S(1)}, u32[]{:S(2)}, u32[]{:S(2)}) collective-permute-start(bf16[1824,128]{1,0:T(8,128)(2,1)S(1)} %get-tuple-element.284.refs_2_), channel_id=1, source_target_pairs={{0,8},{8,0},{16,24},{24,16},{1,9},{9,1},{17,25},{25,17},{2,10},{10... | collective-permute-start | bytes 1400840 | tf_op jit(solution)/shard_map/swap_u1/ppermute | solution.py:78
  252.1 21.5 %collective-permute-start.62 = (bf16[3040,128]{1,0:T(8,128)(2,1)S(1)}, bf16[3040,128]{1,0:T(8,128)(2,1)S(1)}, u32[]{:S(2)}, u32[]{:S(2)}) collective-permute-start(bf16[3040,128]{1,0:T(8,128)(2,1)S(1)} %get-tuple-element.293), channel_id=1, source_target_pairs={{0,4},{2,6},{4,0},{6,2},{1,5},{3,7},{5,1},{7,3},{8,12},{10,14},{12... | collective-permute-start | bytes 2334728 | tf_op jit(solution)/shard_map/u1_y/ppermute | solution.py:37
  252.9 20.7 %collective-permute-start.63 = (bf16[3040,128]{1,0:T(8,128)(2,1)S(1)}, bf16[3040,128]{1,0:T(8,128)(2,1)S(1)}, u32[]{:S(2)}, u32[]{:S(2)}) collective-permute-start(bf16[3040,128]{1,0:T(8,128)(2,1)S(1)} %get-tuple-element.294), channel_id=1, source_target_pairs={{0,2},{2,0},{4,6},{6,4},{1,3},{3,1},{5,7},{7,5},{8,10},{10,8},{12,... | collective-permute-start | bytes 2334728 | tf_op jit(solution)/shard_map/u1_x/ppermute | solution.py:37
  252.9 20.6 %collective-permute-start.60 = (bf16[2432,128]{1,0:T(8,128)(2,1)S(1)}, bf16[2432,128]{1,0:T(8,128)(2,1)S(1)}, u32[]{:S(2)}, u32[]{:S(2)}) collective-permute-start(bf16[2432,128]{1,0:T(8,128)(2,1)S(1)} %get-tuple-element.291.refs_2_), channel_id=1, source_target_pairs={{0,8},{8,0},{16,24},{24,16},{1,9},{9,1},{17,25},{25,17},{2,10},{10... | collective-permute-start | bytes 1867784 | tf_op jit(solution)/shard_map/swap_u2/ppermute | solution.py:78
  254.9 17.9 %collective-permute-start.61 = (bf16[1904,128]{1,0:T(8,128)(2,1)S(1)}, bf16[1904,128]{1,0:T(8,128)(2,1)S(1)}, u32[]{:S(2)}, u32[]{:S(2)}) collective-permute-start(bf16[1904,128]{1,0:T(8,128)(2,1)S(1)} %get-tuple-element.292.refs_3_), channel_id=1, source_target_pairs={{0,16},{8,24},{16,0},{24,8},{1,17},{9,25},{17,1},{25,9},{2,18},{10... | collective-permute-start | bytes 1462280 | tf_op jit(solution)/shard_map/share_far/ppermute | solution.py:37
  274.7 30.0 %collective-permute-start.64 = (bf16[5248,128]{1,0:T(8,128)(2,1)S(1)}, bf16[5248,128]{1,0:T(8,128)(2,1)S(1)}, u32[]{:S(2)}, u32[]{:S(2)}) collective-permute-start(bf16[5248,128]{1,0:T(8,128)(2,1)S(1)} %get-tuple-element.298), channel_id=1, source_target_pairs={{0,2},{2,0},{4,6},{6,4},{1,3},{3,1},{5,7},{7,5},{8,10},{10,8},{12,... | collective-permute-start | bytes 4030472 | tf_op jit(solution)/shard_map/u2_x/ppermute | solution.py:37
  275.0 29.7 %collective-permute-start.65 = (bf16[5248,128]{1,0:T(8,128)(2,1)S(1)}, bf16[5248,128]{1,0:T(8,128)(2,1)S(1)}, u32[]{:S(2)}, u32[]{:S(2)}) collective-permute-start(bf16[5248,128]{1,0:T(8,128)(2,1)S(1)} %get-tuple-element.299), channel_id=1, source_target_pairs={{0,4},{2,6},{4,0},{6,2},{1,5},{3,7},{5,1},{7,3},{8,12},{10,14},{12... | collective-permute-start | bytes 4030472 | tf_op jit(solution)/shard_map/u2_y/ppermute | solution.py:37
  305.4 9.9 %collective-permute-start.67 = (bf16[960,128]{1,0:T(8,128)(2,1)S(1)}, bf16[960,128]{1,0:T(8,128)(2,1)S(1)}, u32[]{:S(2)}, u32[]{:S(2)}) collective-permute-start(bf16[960,128]{1,0:T(8,128)(2,1)S(1)} %get-tuple-element.302.refs_8_), channel_id=1, source_target_pairs={{0,2},{2,0},{4,6},{6,4},{1,3},{3,1},{5,7},{7,5},{8,10},{10,8},{12,... | collective-permute-start | bytes 737288 | tf_op jit(solution)/shard_map/far_share_x/ppermute | solution.py:37
  307.1 8.2 %collective-permute-start.66 = (bf16[944,128]{1,0:T(8,128)(2,1)S(1)}, bf16[944,128]{1,0:T(8,128)(2,1)S(1)}, u32[]{:S(2)}, u32[]{:S(2)}) collective-permute-start(bf16[944,128]{1,0:T(8,128)(2,1)S(1)} %get-tuple-element.301), channel_id=1, source_target_pairs={{0,4},{2,6},{4,0},{6,2},{1,5},{3,7},{5,1},{7,3},{8,12},{10,14},{12... | collective-permute-start | bytes 725000 | tf_op jit(solution)/shard_map/far_share_y/ppermute | solution.py:37
  307.5 12.4 %collective-permute-start.69 = (bf16[1216,128]{1,0:T(8,128)(2,1)S(1)}, bf16[1216,128]{1,0:T(8,128)(2,1)S(1)}, u32[]{:S(2)}, u32[]{:S(2)}) collective-permute-start(bf16[1216,128]{1,0:T(8,128)(2,1)S(1)} %get-tuple-element.313), channel_id=1, source_target_pairs={{0,4},{2,6},{4,0},{6,2},{1,5},{3,7},{5,1},{7,3},{8,12},{10,14},{12... | collective-permute-start | bytes 933896 | tf_op jit(solution)/shard_map/far_u2_y/ppermute | solution.py:37
  309.1 10.8 %collective-permute-start.70 = (bf16[1216,128]{1,0:T(8,128)(2,1)S(1)}, bf16[1216,128]{1,0:T(8,128)(2,1)S(1)}, u32[]{:S(2)}, u32[]{:S(2)}) collective-permute-start(bf16[1216,128]{1,0:T(8,128)(2,1)S(1)} %get-tuple-element.314), channel_id=1, source_target_pairs={{0,2},{2,0},{4,6},{6,4},{1,3},{3,1},{5,7},{7,5},{8,10},{10,8},{12,... | collective-permute-start | bytes 933896 | tf_op jit(solution)/shard_map/far_u2_x/ppermute | solution.py:37
  (52 other events, 279.4 us)
